TPU v7x, 256 devices: a whole 4x4x8 slice. The times are simulated.
256 devices in a mesh: band: 64 (over z, y, core), pw: 4 (over x).
Axes of the slice: x: 4, y: 4, z: 8, core: 2. Of those that a mesh axis runs over, the one named last changes fastest.
Arguments:
- densities: float32 [2, 1024, 10240], P(None, 'band', 'pw'), may hold values from -6 to 6
- screened: float32 [2, 4, 2560, 10240], P(None, None, 'band', 'pw'), may hold values from -0.0625 to 0.0625
- pairs: int32 [256, 2], replicated, may hold values from 0 to 63, as said below
- owners: int32 [256], replicated, may hold values from 0 to 63, as said below
Outputs:
- kernel_panel: float32 [64, 12, 2, 16, 16], P('band', None, None, 'pw')
Inputs may be any that keep to these rules, and one draw needn't show every extreme that they name: `pairs`: every block number is some slot's left block; the right blocks take exactly 32 distinct values. `owners`: at most 12 slots share an owner and some owner has exactly 12; every block number owns some slot.
All inputs are finite; a program needn't handle non-finite values.
Results may differ from a plain program's by a relative error of at most 0.000096.
Values sent between devices are 32-bit elements; how exact they have to be, the bound alone decides.
No kernel may reach another device: no remote copies, remote signals or barrier semaphores. Data moves between devices by JAX's collectives and lax.ppermute only.
A program may use at most 128 MiB of HBM per device.

v0:
```python
import jax
import jax.numpy as jnp
from jax import lax
from jax.sharding import PartitionSpec as P

NG = 10240
CAP = 12


PRECISE = lax.Precision.HIGHEST


def contract_last(former, latter):
    return lax.dot_general(
        former,
        latter,
        (((1,), (1,)), ((), ())),
        precision=PRECISE,
        preferred_element_type=jnp.float32,
    )


def apply_tile(screen_tile, dens_rows):
    applied_real = contract_last(screen_tile[0], dens_rows[0]) - contract_last(
        screen_tile[1], dens_rows[1]
    )
    applied_imag = contract_last(screen_tile[1], dens_rows[0]) + contract_last(
        screen_tile[0], dens_rows[1]
    )
    return jnp.stack([applied_real, applied_imag])


def pair_product(former, latter):
    return jnp.einsum(
        "nak,knc->nac", former, latter, precision=PRECISE, preferred_element_type=jnp.float32
    )


def slot_ranks(owners, blocks):
    member = (owners[:, None] == jnp.arange(blocks, dtype=jnp.int32)[None, :]).astype(jnp.int32)
    before = jnp.cumsum(member, axis=0) - member
    return jnp.sum(before * member, axis=1)


def shards(densities, screened, pairs, owners):
    blocks = lax.axis_size("band")
    band_index = lax.axis_index("band")
    pair_blk = densities.shape[1]
    shard_count = screened.shape[1]
    slice_width = screened.shape[2]
    screen_tile = screened.reshape(2, shard_count * slice_width, screened.shape[3])
    valence = pairs[:, 0]
    conduction = pairs[:, 1]
    gathered = lax.all_gather(densities, "band", axis=1, tiled=True)
    column_rows = lax.dynamic_slice_in_dim(gathered, band_index * slice_width, slice_width, 2)
    partial_applied = apply_tile(screen_tile, gathered).reshape(2, shard_count, slice_width, -1)
    applied = lax.psum_scatter(partial_applied, "pw", scatter_dimension=1, tiled=True)
    applied = applied.reshape(2, slice_width, -1, pair_blk)
    right_part = jnp.take(applied, conduction, axis=2)
    left_part = jnp.take(column_rows.reshape(2, blocks, pair_blk, slice_width), valence, axis=1)
    kernel_real = pair_product(left_part[0], right_part[0]) + pair_product(
        left_part[1], right_part[1]
    )
    kernel_imag = pair_product(left_part[0], right_part[1]) - pair_product(
        left_part[1], right_part[0]
    )
    partial_kernel = jnp.stack([kernel_real, kernel_imag], axis=1) * NG ** (-0.5)
    slot_rank = slot_ranks(owners, blocks)
    slot_count = pairs.shape[0]
    target = owners * CAP + slot_rank
    placing = (jnp.arange(blocks * CAP, dtype=jnp.int32)[:, None] == target[None, :]).astype(
        jnp.float32
    )
    flat_kernels = partial_kernel.reshape(slot_count, -1)
    padded = jnp.dot(placing, flat_kernels, precision=PRECISE, preferred_element_type=jnp.float32)
    padded = padded.reshape((blocks, CAP) + partial_kernel.shape[1:])
    shares = lax.psum_scatter(padded, "pw", scatter_dimension=3, tiled=True)
    result = lax.psum_scatter(shares, "band", scatter_dimension=0, tiled=True)
    return result


def solution(mesh):
    in_specs = (P(None, "band", "pw"), P(None, None, "band", "pw"), P(), P())
    out_specs = P("band", None, None, "pw", None)
    return jax.shard_map(shards, mesh=mesh, in_specs=in_specs, out_specs=out_specs, check_vma=False)
```

profile of v0, /device:TPU:2, one launch (start us, length us, event | category | flops | bytes accessed | tf_op | source)
XLA Modules:
  0.0 548.7 jit_solution(5030726286858361277)
XLA Ops:
  6.5 0.7 all-gather.2.cloned.1.call-update
  7.3 0.7 fusion.25
  8.0 0.6 reduce-window.6
  8.6 0.8 and_reduce_fusion
  9.4 2.2 fusion.28
  11.6 112.0 %all-gather.2.cloned.1.call-done = f32[2,1024,2560]{2,1,0:T(8,128)} async-done(((f32[2,16,2560]{2,1,0:T(8,128)}), f32[2,1024,2560]{2,1,0:T(8,128)}) %all-gather.2.cloned.1.call-update) | async-done | bytes 20971536 | tf_op jit(solution)/shard_map/all_gather | solution.py:54
  123.6 14.5 %fusion.1 = f32[160,1024]{1,0:T(8,128)S(1)} fusion(f32[160,2560]{1,0:T(8,128)S(1)} %bitcast.102, f32[2,1024,2560]{2,1,0:T(8,128)} %all-gather.2.cloned.1.call-done), kind=kOutput, calls=%fused_computation.5 | convolution fusion | flops 5033164800 | bytes 12779520 | tf_op jit(solution)/shard_map/dot_general | solution.py:14
  138.1 13.6 %fusion = f32[160,1024]{1,0:T(8,128)S(1)} fusion(f32[160,2560]{1,0:T(8,128)S(1)} %bitcast.104, f32[2,1024,2560]{2,1,0:T(8,128)} %all-gather.2.cloned.1.call-done), kind=kOutput, calls=%fused_computation.4 | convolution fusion | flops 5033164800 | bytes 12779520 | tf_op jit(solution)/shard_map/dot_general | solution.py:14
  151.7 11.0 %fusion.10 = f32[160,1024]{1,0:T(8,128)S(1)} fusion(f32[160,1024]{1,0:T(8,128)S(1)} %fusion.1, f32[160,2560]{1,0:T(8,128)S(1)} %bitcast.105, f32[2,1024,2560]{2,1,0:T(8,128)S(1)} %copy-done), kind=kOutput, calls=%fused_computation.23 | convolution fusion | flops 5033328640 | bytes 13434880 | tf_op jit(solution)/shard_map/dot_general | solution.py:14
  162.7 11.2 %fusion.11 = f32[160,1024]{1,0:T(8,128)S(1)} fusion(f32[160,1024]{1,0:T(8,128)S(1)} %fusion, f32[160,2560]{1,0:T(8,128)S(1)} %bitcast.103, f32[2,1024,2560]{2,1,0:T(8,128)S(1)} %copy-done), kind=kOutput, calls=%fused_computation.24 | convolution fusion | flops 5033328640 | bytes 13434880 | tf_op jit(solution)/shard_map/dot_general | solution.py:14
  173.9 1.2 pad_maximum_fusion
  175.4 0.6 dynamic-slice
  176.2 1.9 constant_dynamic-slice_fusion.3
  178.1 2.8 gather_fusion
  180.9 4.0 fusion.5
  184.9 39.3 %all-reduce.7.cloned.1.call-done = f32[2,4,40,1024]{3,2,1,0:T(8,128)} async-done(((f32[2,4,40,1024]{3,2,1,0:T(8,128)}), f32[2,4,40,1024]{3,2,1,0:T(8,128)}) %all-reduce.7.cloned.1.call-update) | async-done | bytes 1310736
  224.2 1.6 constant_dynamic-slice_fusion.2
  226.2 2.8 gather_fusion.1
  229.0 3.3 fusion.4
  232.5 3.4 fusion.7
  235.9 3.4 fusion.6
  239.4 4.9 add_bitcast_fusion
  244.3 2.5 copy.24
  246.7 7.2 %subtract_bitcast_fusion = f32[256,1,16,16]{3,2,0,1:T(8,128)} fusion(f32[256,16,16]{2,1,0:T(8,128)S(1)} %fusion.6, f32[2,40,256,16]{1,3,2,0:T(8,128)} %copy-done.2, f32[2,256,16,40]{3,2,1,0:T(8,128)} %fusion.5), kind=kOutput, calls=%fused_computation.16 | convolution fusion | flops 31522816 | bytes 4718592 | tf_op jit(solution)/shard_map/nak,knc->nac/dot_general | solution.py:34
  253.9 2.5 copy.25
  256.4 3.2 fusion.12
  260.3 80.7 %all-reduce.9.cloned.1.call-done = f32[64,12,2,16,16]{0,4,3,2,1:T(8,128)} async-done(((f32[64,12,2,16,16]{0,4,3,2,1:T(8,128)}), f32[64,12,2,16,16]{0,4,3,2,1:T(8,128)}) %all-reduce.9.cloned.1.call-update) | async-done | bytes 1572880
  341.1 1.2 constant_dynamic-slice_fusion.1
  342.3 3.7 copy.26
  346.0 0.6 dynamic-slice.4
  346.6 193.4 %all-reduce.11.cloned.1.call-done = f32[64,12,2,4,16]{4,3,2,1,0:T(4,128)} async-done(((f32[64,12,2,4,16]{4,3,2,1,0:T(4,128)}), f32[64,12,2,4,16]{4,3,2,1,0:T(4,128)}) %all-reduce.11.cloned.1.call-update) | async-done | bytes 393232
  540.0 2.0 constant_dynamic-slice_fusion
  (28 shorter events, 1.1 us)
Async XLA Ops:
  6.5 117.1 %all-gather.2.cloned.1.call-start = ((), (), s32[]{:S(2)}) async-start(), calls=%async_computation | async-start | bytes 21299200 | tf_op jit(solution)/shard_map/all_gather | solution.py:54
  7.3 217.0 %all-reduce.7.cloned.1.call-start = ((), (), s32[]{:S(2)}) async-start(), calls=%async_computation.1 | async-start | bytes 2621440
  123.6 28.1 %copy-start = (f32[2,1024,2560]{2,1,0:T(8,128)S(1)}, f32[2,1024,2560]{2,1,0:T(8,128)}, u32[]{:S(2)}) copy-start(f32[2,1024,2560]{2,1,0:T(8,128)} %all-gather.2.cloned.1.call-done) | copy-start | bytes 62914564
  173.9 1.5 copy-start.5
  173.9 2.1 copy-start.3
  175.2 165.9 %all-reduce.9.cloned.1.call-start = ((), (), s32[]{:S(2)}) async-start(), calls=%async_computation.2 | async-start | bytes 6291456
  229.0 3.4 copy-start.1
  232.5 6.9 %copy-start.2 = (f32[2,40,256,16]{1,3,2,0:T(8,128)}, f32[2,40,256,16]{1,3,2,0:T(8,128)S(1)}, u32[]{:S(2)}) copy-start(f32[2,40,256,16]{1,3,2,0:T(8,128)S(1)} %fusion.4) | copy-start | bytes 3932164
  259.7 280.4 %all-reduce.11.cloned.1.call-start = ((), (), s32[]{:S(2)}) async-start(), calls=%async_computation.3 | async-start | bytes 6291456
  342.3 3.7 copy-start.4
Sparse Core Ops, SparseCore 0:
  10.0 113.5 all-gather.1
  175.3 48.8 all-reduce.6
  259.8 81.2 all-reduce.8
  346.1 193.8 all-reduce.10
where the time goes:
time: 556 us; the launch traced here: 549 us
  waiting for transfers between devices  426 us (77%)
  matrix products  72.4 us (13%)
  local copies, waits for them, and re-layouts  25.1 us (5%)
  between operations  14.1 us (3%)
  other arithmetic  10.7 us (2%)
    unnamed x7, waiting for transfers between devices  314 us
    all_gather x1, waiting for transfers between devices, shards(): gathered = lax.all_gather(densities, 'band', axis=1, tiled=True)  112 us
    dot_general x4, matrix products, contract_last(): lax.dot_general(former, latter, (((1,), (1,)), ((), ())), precision=PRECI...  50.2 us
    dot_general x4, matrix products, pair_product(): jnp.einsum('nak,knc->nac', former, latter, precision=PRECISE, preferred_e...  19 us
  transfers between devices with their start and end apart: 4, of which 4 were waited for; matrix products, arithmetic and copies ran while one was open for 3% of the time, Pallas kernels for 0%

commit v1 on v0

v1 whole, which is shorter than its diff:
```python
import functools

import jax
import jax.numpy as jnp
from jax import lax
from jax.experimental import pallas as pl
from jax.experimental.pallas import tpu as pltpu
from jax.sharding import Mesh
from jax.sharding import PartitionSpec as P

NG = 10240
CAP = 12
BLK = 16
USED = 32
HALF = USED // 2 * BLK
BAND = ("z", "y", "core")
SWAP = ((0, 1), (1, 0))
VMEM_LIMIT = 56 * 1024 * 1024


def ring(n, shift):
    return [(i, (i + shift) % n) for i in range(n)]


def split(x):
    high = lax.reduce_precision(x, 8, 7)
    return high.astype(jnp.bfloat16), (x - high).astype(jnp.bfloat16)


def dot(former, latter):
    return jnp.dot(former, latter, preferred_element_type=jnp.float32)


def plan(pairs, owners):
    blocks = 64
    ids = jnp.arange(blocks, dtype=jnp.int32)
    left, right = pairs[:, 0], pairs[:, 1]
    used = jnp.any(right[:, None] == ids[None, :], axis=0).astype(jnp.int32)
    rank = jnp.sum(used[None, :] * (ids[None, :] < ids[:, None]), axis=1)
    slots = jnp.arange(USED, dtype=jnp.int32)
    used_list = jnp.sum(
        jnp.where((rank[None, :] == slots[:, None]) & (used[None, :] > 0), ids[None, :], 0), axis=1
    )
    right_rank = jnp.sum(used[None, :] * (ids[None, :] < right[:, None]), axis=1)
    count = jnp.sum((owners[:, None] == ids[None, :]).astype(jnp.int32), axis=0)
    offset = jnp.sum(count[None, :] * (ids[None, :] < ids[:, None]), axis=1)
    order = jnp.arange(owners.shape[0], dtype=jnp.int32)
    ahead = (owners[None, :] < owners[:, None]) | (
        (owners[None, :] == owners[:, None]) & (order[None, :] < order[:, None])
    )
    place = jnp.sum(ahead.astype(jnp.int32), axis=1)
    hit = place[None, :] == order[:, None]
    left_at = jnp.sum(jnp.where(hit, left[None, :], 0), axis=1)
    right_at = jnp.sum(jnp.where(hit, right_rank[None, :], 0), axis=1)
    return used_list, left_at, right_at, offset, count


def main_kernel(table, right_ref, high_ref, low_ref, left_high, left_low, out_ref, rh, rl, kern):
    chips, span = right_ref.shape[0], right_ref.shape[1] // 2
    for chip in range(chips):
        for part in range(2):
            block = right_ref[chip, part * span : (part + 1) * span, :]
            top = block.astype(jnp.bfloat16)
            rest = (block - top.astype(jnp.float32)).astype(jnp.bfloat16)
            rows, cols = pl.ds(chip * span, span), pl.ds(part * HALF, HALF)
            rh[rows, cols] = top
            rl[rows, cols] = rest
    right_high, right_low = rh[...], rl[...]
    product = (
        dot(high_ref[...], right_high) + dot(high_ref[...], right_low) + dot(low_ref[...], right_high)
    )
    mid = product.shape[0] // 2
    real = product[:mid, :HALF] - product[mid:, HALF:]
    imag = product[mid:, :HALF] + product[:mid, HALF:]
    scale = NG ** (-0.5)
    applied = scale * jnp.concatenate(
        [jnp.concatenate([real, imag], axis=0), jnp.concatenate([imag, -real], axis=0)], axis=1
    )
    top = applied.astype(jnp.bfloat16)
    rest = (applied - top.astype(jnp.float32)).astype(jnp.bfloat16)
    kern[...] = dot(left_high[...], top) + dot(left_high[...], rest) + dot(left_low[...], top)

    lane = lax.broadcasted_iota(jnp.int32, (8, 128), 1) // BLK

    def group(g, carry):
        tiles = [[jnp.zeros((8, 128), jnp.float32) for _ in range(2)] for _ in range(2)]
        for u in range(8):
            row = pl.multiple_of(table[0, g * 8 + u] * BLK, BLK)
            column = pl.multiple_of(table[1, g * 8 + u] * 128, 128)
            shift = table[2, g * 8 + u]
            target = table[3, g * 8 + u]
            for part in range(2):
                for half in range(2):
                    tile = kern[pl.ds(row + half * 8, 8), pl.ds(column + part * HALF, 128)]
                    tile = pltpu.roll(tile, shift, 1)
                    tiles[part][half] = jnp.where(lane == target, tile, tiles[part][half])
        for part in range(2):
            for half in range(2):
                out_ref[part, half, :, pl.ds(pl.multiple_of(g * 128, 128), 128)] = tiles[part][half]
        return carry

    lax.fori_loop(0, table.shape[1] // 8, group, 0)


def main_call(table, right_all, screen_high, screen_low, left_high, left_low):
    slots = table.shape[1]
    depth = right_all.shape[0] * right_all.shape[1] // 2
    return pl.pallas_call(
        main_kernel,
        out_shape=jax.ShapeDtypeStruct((2, 2, 8, slots * BLK), jnp.float32),
        in_specs=[pl.BlockSpec(memory_space=pltpu.SMEM)] + [pl.BlockSpec(memory_space=pltpu.VMEM)] * 5,
        out_specs=pl.BlockSpec(memory_space=pltpu.VMEM),
        scratch_shapes=[
            pltpu.VMEM((depth, 2 * HALF), jnp.bfloat16),
            pltpu.VMEM((depth, 2 * HALF), jnp.bfloat16),
            pltpu.VMEM((left_high.shape[0], 2 * HALF), jnp.float32),
        ],
        compiler_params=pltpu.CompilerParams(vmem_limit_bytes=VMEM_LIMIT),
    )(table, right_all, screen_high, screen_low, left_high, left_low)


def shards(densities, screened, pairs, owners):
    core, x = lax.axis_index("core"), lax.axis_index("x")
    chip = lax.axis_index("z") * lax.axis_size("y") + lax.axis_index("y")
    span = screened.shape[2]
    used_list, left_at, right_at, offset, count = plan(pairs, owners)

    other = lax.ppermute(screened, "core", SWAP)
    screen = jnp.stack([screened, other], axis=1).reshape(2 * 2 * 4 * span, -1)
    screen_high, screen_low = split(screen)

    pieces = densities.reshape(2, BLK, 64, span).transpose(2, 3, 0, 1).reshape(64, 1, -1)
    mine = lax.all_to_all(pieces, BAND, 0, 0, tiled=True)
    mine = mine.reshape(64, span, 2, BLK)

    def rows_of(which):
        chosen = jnp.take(mine, lax.dynamic_slice_in_dim(used_list, which * (USED // 2), USED // 2), axis=0)
        return chosen.transpose(2, 1, 0, 3).reshape(2, span, HALF)

    keep, give = rows_of(core), rows_of(1 - core)
    take = lax.ppermute(give, "core", SWAP)
    first = jnp.where(core == 0, keep, take)
    second = jnp.where(core == 0, take, keep)
    shard = jnp.concatenate([first, second], axis=1).reshape(2 * 2 * span, HALF)
    right_all = lax.all_gather(shard, ("z", "y"), axis=0, tiled=False)

    flat = mine.reshape(64 * span * 2 * BLK // 128, 128)
    around = jnp.stack([flat] + [lax.ppermute(flat, "x", ring(4, s)) for s in (1, 2, 3)])
    at = (x - jnp.arange(4)) % 4
    around = jnp.take(around, at, axis=0)
    both = jnp.stack([around, lax.ppermute(around, "core", SWAP)])
    left = both.reshape(8, 64, span, 2, BLK).transpose(1, 4, 3, 0, 2).reshape(64 * BLK, -1)
    left_high, left_low = split(left)

    local = right_at - core * (USED // 2)
    valid = (local >= 0) & (local < USED // 2)
    local = jnp.where(valid, local, 0)
    lane = jnp.arange(local.shape[0], dtype=jnp.int32) % 8
    table = jnp.stack(
        [left_at, local // 8, (lane - local % 8) % 8 * BLK, jnp.where(valid, lane, -1)]
    ).astype(jnp.int32)
    kern = main_call(table, right_all, screen_high, screen_low, left_high, left_low)

    own = lax.dynamic_index_in_dim(kern, core, 0, keepdims=False)
    sent = lax.dynamic_index_in_dim(kern, 1 - core, 0, keepdims=False)
    own = own + lax.ppermute(sent, "core", SWAP)
    own = own.reshape(4, 4, -1)
    own = jnp.sum(lax.all_to_all(own, "x", 0, 0, tiled=True).reshape(4, 4, -1), axis=0)
    own = own.reshape(4, -1, BLK)
    at = (offset[:, None] + jnp.arange(CAP)[None, :]).reshape(-1)
    spread = jnp.take(own, jnp.minimum(at, own.shape[1] - 1), axis=1)
    spread = spread.reshape(4, 32, 2, CAP, BLK).transpose(1, 2, 3, 0, 4).reshape(32, 1, -1)
    gathered = lax.all_to_all(spread, ("z", "y"), 0, 0, tiled=True)
    total = jnp.sum(gathered.reshape(32, 2, CAP, 4, BLK), axis=0)
    own = lax.dynamic_index_in_dim(total, core, 0, keepdims=False)
    sent = lax.dynamic_index_in_dim(total, 1 - core, 0, keepdims=False)
    come = lax.ppermute(sent, "core", SWAP)
    real = jnp.where(core == 0, own, come)
    imag = jnp.where(core == 0, come, own)
    result = jnp.stack([real, imag], axis=1)
    held = lax.dynamic_index_in_dim(count, chip * 2 + core, 0, keepdims=False)
    result = jnp.where(jnp.arange(CAP)[:, None, None, None] < held, result, 0.0)
    return result[None]


def solution(mesh):
    fine = Mesh(mesh.devices.reshape(8, 4, 2, 4), ("z", "y", "core", "x"))
    in_specs = (P(None, BAND, "x"), P(None, None, BAND, "x"), P(), P())
    out_specs = P(BAND, None, None, "x", None)
    return jax.shard_map(shards, mesh=fine, in_specs=in_specs, out_specs=out_specs, check_vma=False)
```

time: 556 us -> 218 us (0.39)
  waiting for transfers between devices: 426 us -> 47.4 us
  matrix products: 72.4 us -> 0 us
  local copies, waits for them, and re-layouts: 25.1 us -> 83.7 us
  starting transfers between devices: 0.12 us -> 27.4 us
  Pallas kernels: 0 us -> 23.2 us
  other arithmetic: 10.7 us -> 19.3 us
    unnamed x7 -> x1, waiting for transfers between devices: 314 us -> 0.02 us
    all_gather x1, waiting for transfers between devices: 112 us -> 0.01 us  [shards(): right_all = lax.all_gather(shard, ('z', 'y'), axis=0, tiled=False)]
    dot_general x9 -> x0, matrix products: 72.4 us -> none  [the longest x4 50.2 us: contract_last(): lax.dot_general(former, latter, (((1,), (1,)), ((), ())), precision=PRECI...]
    reshape x0 -> x9, local copies, waits for them, and re-layouts: none -> 41.3 us  [the longest x2 35.3 us: shards(): both.reshape(8, 64, span, 2, BLK).transpose(1, 4, 3, 0, 2)]
    all_to_all x0 -> x3, waiting for transfers between devices: none -> 29.4 us  [the longest x1 13.4 us: shards(): mine = lax.all_to_all(pieces, BAND, 0, 0, tiled=True)]
    transpose x0 -> x5, local copies, waits for them, and re-layouts: none -> 28.6 us  [the longest x1 25 us: shards(): both.reshape(8, 64, span, 2, BLK).transpose(1, 4, 3, 0, 2)]
    pallas_call x0 -> x1, Pallas kernels: none -> 23.2 us  [main_call(): pl.pallas_call(main_kernel, out_shape=jax.ShapeDtypeStruct((2, 2, 8, slot...]
    all_to_all x0 -> x3, starting transfers between devices: none -> 21.4 us  [the longest x1 12.1 us: shards(): mine = lax.all_to_all(pieces, BAND, 0, 0, tiled=True)]
  transfers between devices with their start and end apart: 4 -> 12, of which waited for: 4 -> 10; matrix products, arithmetic and copies ran while one was open for 3% -> 36% of each run, Pallas kernels for 0% -> 0%
where the time goes in v1:
time: 218 us; the launch traced here: 215 us
  local copies, waits for them, and re-layouts  83.7 us (38%)
  waiting for transfers between devices  47.4 us (22%)
  starting transfers between devices  27.4 us (13%)
  Pallas kernels  23.2 us (11%)
  other arithmetic  19.3 us (9%)
  between operations  13.8 us (6%)
    reshape x2, local copies, waits for them, and re-layouts, shards(): both.reshape(8, 64, span, 2, BLK).transpose(1, 4, 3, 0, 2)  35.3 us
    transpose x1, local copies, waits for them, and re-layouts, shards(): both.reshape(8, 64, span, 2, BLK).transpose(1, 4, 3, 0, 2)  25 us
    pallas_call x1, Pallas kernels, main_call(): pl.pallas_call(main_kernel, out_shape=jax.ShapeDtypeStruct((2, 2, 8, slot...  23.2 us
    ppermute x3, waiting for transfers between devices, shards(): lax.ppermute(flat, 'x', ring(4, s))  13.8 us
    all_to_all x1, waiting for transfers between devices, shards(): mine = lax.all_to_all(pieces, BAND, 0, 0, tiled=True)  13.4 us
    all_to_all x1, starting transfers between devices, shards(): mine = lax.all_to_all(pieces, BAND, 0, 0, tiled=True)  12.1 us
    all_to_all x1, waiting for transfers between devices, shards(): gathered = lax.all_to_all(spread, ('z', 'y'), 0, 0, tiled=True)  10.6 us
    gather x2, local copies, waits for them, and re-layouts, shards(): spread = jnp.take(own, jnp.minimum(at, own.shape[1] - 1), axis=1)  7.28 us
  transfers between devices with their start and end apart: 12, of which 10 were waited for; matrix products, arithmetic and copies ran while one was open for 36% of the time, Pallas kernels for 0%

profile of v1, /device:TPU:2, one launch (start us, length us, event | category | flops | bytes accessed | tf_op | source)
XLA Modules:
  0.0 214.8 jit_solution(5683640799195717088)
XLA Ops:
  6.5 1.8 reshape.362
  9.0 1.0 copy.63
  10.0 12.1 %all-to-all-start = ((f32[64,1,1280]{2,1,0:T(1,128)}), f32[64,1,1280]{2,1,0:T(1,128)S(1)}, u32[]{:S(2)}, u32[]{:S(2)}) async-start(f32[64,1,1280]{2,1,0:T(1,128)} %copy.63), calls=%async_computation | async-start | bytes 655360 | tf_op jit(solution)/shard_map/all_to_all | solution.py:133
  22.7 13.4 %all-to-all-done = f32[64,1,1280]{2,1,0:T(1,128)S(1)} async-done(((f32[64,1,1280]{2,1,0:T(1,128)}), f32[64,1,1280]{2,1,0:T(1,128)S(1)}, u32[]{:S(2)}, u32[]{:S(2)}) %all-to-all-start) | async-done | bytes 327712 | tf_op jit(solution)/shard_map/all_to_all | solution.py:133
  41.2 1.6 collective-permute-start.2
  42.7 1.1 collective-permute-start.3
  43.8 2.2 %collective-permute-start.4 = (f32[640,128]{1,0:T(8,128)S(1)}, f32[640,128]{1,0:T(8,128)S(1)}, u32[]{:S(2)}, u32[]{:S(2)}) collective-permute-start(f32[640,128]{1,0:T(8,128)S(1)} %bitcast.68), channel_id=1, source_target_pairs={{0,3},{1,0},{2,1},{3,2},{4,7},{5,4},{6,5},{7,6},{8,11},{9,8},{10,9... | collective-permute-start | bytes 983048 | tf_op jit(solution)/shard_map/ppermute | solution.py:148
  46.3 5.5 %collective-permute-done.2 = f32[640,128]{1,0:T(8,128)S(1)} collective-permute-done((f32[640,128]{1,0:T(8,128)S(1)}, f32[640,128]{1,0:T(8,128)S(1)}, u32[]{:S(2)}, u32[]{:S(2)}) %collective-permute-start.2) | collective-permute-done | bytes 327712 | tf_op jit(solution)/shard_map/ppermute | solution.py:148
  51.8 3.0 %collective-permute-done.3 = f32[640,128]{1,0:T(8,128)S(1)} collective-permute-done((f32[640,128]{1,0:T(8,128)S(1)}, f32[640,128]{1,0:T(8,128)S(1)}, u32[]{:S(2)}, u32[]{:S(2)}) %collective-permute-start.3) | collective-permute-done | bytes 327712 | tf_op jit(solution)/shard_map/ppermute | solution.py:148
  54.8 5.3 %collective-permute-done.4 = f32[640,128]{1,0:T(8,128)S(1)} collective-permute-done((f32[640,128]{1,0:T(8,128)S(1)}, f32[640,128]{1,0:T(8,128)S(1)}, u32[]{:S(2)}, u32[]{:S(2)}) %collective-permute-start.4) | collective-permute-done | bytes 327712 | tf_op jit(solution)/shard_map/ppermute | solution.py:148
  60.8 1.2 broadcast_select_fusion
  63.3 2.0 collective-permute-done.5
  65.3 1.1 copy-done
  66.4 1.5 pad_maximum_fusion.1
  67.9 28.4 %reshape.368 = f32[8,64,40,2,16]{4,3,2,1,0:T(2,128)} reshape(f32[2,4,640,128]{3,2,1,0:T(8,128)S(1)} %pad_maximum_fusion.1) | data formatting | bytes 5242880 | tf_op jit(solution)/shard_map/reshape | solution.py:152
  96.3 25.0 %copy.71 = f32[64,16,2,8,40]{4,3,2,1,0:T(8,128)} copy(f32[64,16,2,8,40]{1,2,4,0,3:T(2,128)} %bitcast.62) | data formatting | bytes 5242880 | tf_op jit(solution)/shard_map/transpose | solution.py:152
  121.3 6.9 %reshape.369 = f32[1024,640]{1,0:T(8,128)S(1)} reshape(f32[64,16,2,8,40]{4,3,2,1,0:T(8,128)} %copy.71) | data formatting | bytes 5242880 | tf_op jit(solution)/shard_map/reshape | solution.py:152
  128.1 1.9 fusion.1
  130.0 3.4 %pad_maximum_fusion = f32[2,2,4,40,2560]{4,3,2,0,1:T(8,128)S(1)} fusion(f32[2,1,4,40,2560]{4,3,2,0,1:T(8,128)} %bitcast.14, f32[2,1,4,40,2560]{4,3,2,0,1:T(8,128)} %bitcast.13), kind=kLoop, calls=%fused_computation.7 | loop fusion | flops 1638400 | bytes 13107200 | tf_op jit(solution)/shard_map/stack | solution.py:129
  134.1 3.7 %fusion = (bf16[640,2560]{1,0:T(8,128)(2,1)}, bf16[640,2560]{1,0:T(8,128)(2,1)}) fusion(f32[2,2,4,40,2560]{4,3,2,1,0:T(8,128)S(1)} %copy.70), kind=kLoop, calls=%fused_computation.6 | loop fusion | flops 6553600 | bytes 13107200 | tf_op jit(solution)/shard_map/convert_element_type | solution.py:27
  137.9 23.2 %shard_map.46 = f32[2,2,8,4096]{3,2,1,0:T(8,128)} custom-call(s32[4,256]{1,0:T(4,128)} %pad_add_fusion.table, f32[32,160,256]{2,1,0:T(8,128)} %all-gather.2.cloned.1.call-done.right_ref, bf16[640,2560]{1,0:T(8,128)(2,1)} %get-tuple-element.15.high_ref, bf16[640,2560]{1,0:T(8,128)(2,1)} %get-tuple-element.14.low_ref, ...), custom_call_target="tpu_custom_call" | custom-call | tf_op jit(solution)/shard_map/pallas_call | solution.py:108
  161.1 1.0 dynamic-slice_bitcast_fusion
  162.6 1.1 collective-permute-done.6
  163.7 1.0 bitcast_add_fusion
  165.4 4.6 %all-to-all-start.1 = ((f32[4,4,4096]{2,1,0:T(4,128)}), f32[4,4,4096]{2,1,0:T(4,128)S(1)}, u32[]{:S(2)}, u32[]{:S(2)}) async-start(f32[4,4,4096]{2,1,0:T(4,128)} %reshape.370), calls=%async_computation.1 | async-start | bytes 524288 | tf_op jit(solution)/shard_map/all_to_all | solution.py:168
  170.2 5.4 %all-to-all-done.1 = f32[4,4,4096]{2,1,0:T(4,128)S(1)} async-done(((f32[4,4,4096]{2,1,0:T(4,128)}), f32[4,4,4096]{2,1,0:T(4,128)S(1)}, u32[]{:S(2)}, u32[]{:S(2)}) %all-to-all-start.1) | async-done | bytes 262176 | tf_op jit(solution)/shard_map/all_to_all | solution.py:168
  176.2 3.4 %gather_fusion.1 = f32[768,4,16]{2,1,0:T(4,128)} fusion(f32[4,256,16]{2,0,1:T(4,128)S(1)} %copy.72, s32[1024]{0:T(1024)S(1)} %pad_clamp_fusion), kind=kCustom, calls=%fused_computation.3 | custom fusion | bytes 396288 | tf_op jit(solution)/shard_map/jit(_take)/gather | solution.py:171
  179.6 3.8 %copy.77 = f32[4,32,2,12,16]{3,2,1,4,0:T(2,128)S(1)} copy(f32[4,32,2,12,16]{4,0,3,2,1:T(4,128)} %bitcast.63) | data formatting | bytes 393216 | tf_op jit(solution)/shard_map/jit(_take)/gather | solution.py:171
  183.5 2.4 %select_bitcast_fusion = f32[32,2,12,4,16]{2,1,0,4,3:T(2,128)} fusion(f32[4,32,2,12,16]{3,2,1,4,0:T(2,128)S(1)} %copy.77, pred[32,2,12]{2,1,0:T(4,128)(4,1)S(1)} %compare_and_fusion), kind=kLoop, calls=%fused_computation.12 | loop fusion | flops 49152 | bytes 393984 | tf_op jit(solution)/shard_map/transpose | solution.py:172
  185.9 3.0 %copy.74 = f32[32,2,12,4,16]{0,4,3,2,1:T(8,128)S(1)} copy(f32[32,2,12,4,16]{2,1,0,4,3:T(2,128)} %select_bitcast_fusion) | data formatting | bytes 393216 | tf_op jit(solution)/shard_map/transpose | solution.py:172
  189.8 4.7 %all-to-all-start.2 = ((f32[32,1,1536]{2,1,0:T(1,128)}), f32[32,1,1536]{2,1,0:T(1,128)S(1)}, u32[]{:S(2)}, u32[]{:S(2)}) async-start(f32[32,1,1536]{2,1,0:T(1,128)} %copy.75), calls=%async_computation.2 | async-start | bytes 393216 | tf_op jit(solution)/shard_map/all_to_all | solution.py:173
  195.1 10.6 %all-to-all-done.2 = f32[32,1,1536]{2,1,0:T(1,128)S(1)} async-done(((f32[32,1,1536]{2,1,0:T(1,128)}), f32[32,1,1536]{2,1,0:T(1,128)S(1)}, u32[]{:S(2)}, u32[]{:S(2)}) %all-to-all-start.2) | async-done | bytes 196640 | tf_op jit(solution)/shard_map/all_to_all | solution.py:173
  (69 shorter events, 14.7 us)
Async XLA Ops:
  6.5 15.6 %copy-start.2 = (s32[256,2]{0,1:T(2,128)S(1)}, s32[256,2]{0,1:T(2,128)}, u32[]{:S(2)}) copy-start(s32[256,2]{0,1:T(2,128)} %param.8) | copy-start | bytes 6148
  10.0 26.0 %all-to-all-start = ((f32[64,1,1280]{2,1,0:T(1,128)}), f32[64,1,1280]{2,1,0:T(1,128)S(1)}, u32[]{:S(2)}, u32[]{:S(2)}) async-start(f32[64,1,1280]{2,1,0:T(1,128)} %copy.63), calls=%async_computation | async-start | bytes 655360 | tf_op jit(solution)/shard_map/all_to_all | solution.py:133
  22.1 115.7 %all-gather.2.cloned.1.call-start = ((), (), s32[]{:S(2)}) async-start(), calls=%async_computation.3 | async-start | bytes 5406720 | tf_op jit(solution)/shard_map/all_gather | solution.py:145
  38.1 1.6 collective-permute-start
  38.5 7.6 %copy-start.1 = (s32[256]{0:T(256)S(1)}, s32[256]{0:T(256)}, u32[]{:S(2)}) copy-start(s32[256]{0:T(256)} %param.9) | copy-start | bytes 3076
  40.7 89.3 %collective-permute-start.1 = (f32[2,4,40,2560]{3,2,1,0:T(8,128)}, f32[2,4,40,2560]{3,2,1,0:T(8,128)}, u32[]{:S(2)}, u32[]{:S(2)}) collective-permute-start(f32[2,4,40,2560]{3,2,1,0:T(8,128)} %param.7), channel_id=1, source_target_pairs={{0,4},{4,0},{1,5},{5,1},{2,6},{6,2},{3,7},{7,3},{8,12},{12,8},{9,1... | collective-permute-start | bytes 9830408 | tf_op jit(solution)/shard_map/ppermute | solution.py:128
  41.2 10.6 %collective-permute-start.2 = (f32[640,128]{1,0:T(8,128)S(1)}, f32[640,128]{1,0:T(8,128)S(1)}, u32[]{:S(2)}, u32[]{:S(2)}) collective-permute-start(f32[640,128]{1,0:T(8,128)S(1)} %bitcast.66), channel_id=1, source_target_pairs={{0,1},{1,2},{2,3},{3,0},{4,5},{5,6},{6,7},{7,4},{8,9},{9,10},{10,1... | collective-permute-start | bytes 983048 | tf_op jit(solution)/shard_map/ppermute | solution.py:148
  42.7 12.1 %collective-permute-start.3 = (f32[640,128]{1,0:T(8,128)S(1)}, f32[640,128]{1,0:T(8,128)S(1)}, u32[]{:S(2)}, u32[]{:S(2)}) collective-permute-start(f32[640,128]{1,0:T(8,128)S(1)} %bitcast.67), channel_id=1, source_target_pairs={{0,2},{1,3},{2,0},{3,1},{4,6},{5,7},{6,4},{7,5},{8,10},{9,11},{10,... | collective-permute-start | bytes 983048 | tf_op jit(solution)/shard_map/ppermute | solution.py:148
  43.8 16.3 %collective-permute-start.4 = (f32[640,128]{1,0:T(8,128)S(1)}, f32[640,128]{1,0:T(8,128)S(1)}, u32[]{:S(2)}, u32[]{:S(2)}) collective-permute-start(f32[640,128]{1,0:T(8,128)S(1)} %bitcast.68), channel_id=1, source_target_pairs={{0,3},{1,0},{2,1},{3,2},{4,7},{5,4},{6,5},{7,6},{8,11},{9,8},{10,9... | collective-permute-start | bytes 983048 | tf_op jit(solution)/shard_map/ppermute | solution.py:148
  62.0 3.2 %collective-permute-start.5 = (f32[4,640,128]{2,1,0:T(8,128)}, f32[4,640,128]{2,1,0:T(8,128)S(1)}, u32[]{:S(2)}, u32[]{:S(2)}) collective-permute-start(f32[4,640,128]{2,1,0:T(8,128)} %broadcast_select_fusion), channel_id=1, source_target_pairs={{0,4},{4,0},{1,5},{5,1},{2,6},{6,2},{3,7},{7,3},{8,12},{12,8},{9,1... | collective-permute-start | bytes 3932168 | tf_op jit(solution)/shard_map/ppermute | solution.py:151
  65.3 1.1 copy-start
  162.1 1.6 collective-permute-start.6
  165.4 10.1 %all-to-all-start.1 = ((f32[4,4,4096]{2,1,0:T(4,128)}), f32[4,4,4096]{2,1,0:T(4,128)S(1)}, u32[]{:S(2)}, u32[]{:S(2)}) async-start(f32[4,4,4096]{2,1,0:T(4,128)} %reshape.370), calls=%async_computation.1 | async-start | bytes 524288 | tf_op jit(solution)/shard_map/all_to_all | solution.py:168
  189.8 15.9 %all-to-all-start.2 = ((f32[32,1,1536]{2,1,0:T(1,128)}), f32[32,1,1536]{2,1,0:T(1,128)S(1)}, u32[]{:S(2)}, u32[]{:S(2)}) async-start(f32[32,1,1536]{2,1,0:T(1,128)} %copy.75), calls=%async_computation.2 | async-start | bytes 393216 | tf_op jit(solution)/shard_map/all_to_all | solution.py:173
  206.0 1.3 collective-permute-start.7
Sparse Core Ops, SparseCore 0:
  40.8 81.4 all-gather.1

commit v2 on v1

v2 whole, which is shorter than its diff:
```python
import functools

import jax
import jax.numpy as jnp
from jax import lax
from jax.experimental import pallas as pl
from jax.experimental.pallas import tpu as pltpu
from jax.sharding import Mesh
from jax.sharding import PartitionSpec as P

NG = 10240
CAP = 12
BLK = 16
USED = 32
HALF = USED // 2 * BLK
BAND = ("z", "y", "core")
SWAP = ((0, 1), (1, 0))
SMEM = pl.BlockSpec(memory_space=pltpu.SMEM)
VMEM = pl.BlockSpec(memory_space=pltpu.VMEM)
PLANE = 320
PAIR = 2 * PLANE


def ring(n, shift):
    return [(i, (i + shift) % n) for i in range(n)]


def params(mib):
    return pltpu.CompilerParams(vmem_limit_bytes=mib * 1024 * 1024)


def split(x):
    high = x.astype(jnp.bfloat16)
    return high, (x - high.astype(jnp.float32)).astype(jnp.bfloat16)


def dot(former, latter):
    return jnp.dot(former, latter, preferred_element_type=jnp.float32)


def dot3(high, low, former, latter):
    return dot(high, former) + dot(high, latter) + dot(low, former)


def plan(pairs, owners):
    blocks = 64
    ids = jnp.arange(blocks, dtype=jnp.int32)
    left, right = pairs[:, 0], pairs[:, 1]
    used = jnp.any(right[:, None] == ids[None, :], axis=0).astype(jnp.int32)
    rank = jnp.sum(used[None, :] * (ids[None, :] < ids[:, None]), axis=1)
    slots = jnp.arange(USED, dtype=jnp.int32)
    used_list = jnp.sum(
        jnp.where((rank[None, :] == slots[:, None]) & (used[None, :] > 0), ids[None, :], 0), axis=1
    )
    right_rank = jnp.sum(used[None, :] * (ids[None, :] < right[:, None]), axis=1)
    count = jnp.sum((owners[:, None] == ids[None, :]).astype(jnp.int32), axis=0)
    offset = jnp.sum(count[None, :] * (ids[None, :] < ids[:, None]), axis=1)
    order = jnp.arange(owners.shape[0], dtype=jnp.int32)
    ahead = (owners[None, :] < owners[:, None]) | (
        (owners[None, :] == owners[:, None]) & (order[None, :] < order[:, None])
    )
    place = jnp.sum(ahead.astype(jnp.int32), axis=1)
    hit = place[None, :] == order[:, None]
    left_at = jnp.sum(jnp.where(hit, left[None, :], 0), axis=1)
    right_at = jnp.sum(jnp.where(hit, right_rank[None, :], 0), axis=1)
    return used_list, left_at, right_at, offset, count


def screen_kernel(place, own_ref, other_ref, high_ref, low_ref):
    z = place[0]
    rows = 16
    lane = lax.broadcasted_iota(jnp.int32, (rows, 128), 1)
    for source, ref in enumerate((own_ref, other_ref)):

        def body(step, carry):
            part = step // 10
            start = pl.multiple_of(step * rows, rows)
            target = pl.multiple_of(part * PLANE + source * (PLANE // 2) + (step - part * 10) * rows, rows)
            for pair, (one, two) in enumerate(((7, 1), (6, 2), (5, 3), (0, 4))):
                parts = []
                for place_in, delta in ((0, one), (64, two)):
                    plane = lax.rem(z + delta, 8)
                    odd = lax.rem(plane, 2)
                    column = pl.multiple_of(plane * PLANE - odd * 64, 128)
                    window = ref[pl.ds(start, rows), pl.ds(column, 384)]
                    turned = pltpu.roll(window, 320 if place_in == 0 else 64, 1)
                    plain = (odd == 0) if place_in == 0 else (odd == 1)
                    parts.append(jnp.where(plain, window, turned))
                a, b = parts
                middle = jnp.where(lane < 64, a[:, 256:], b[:, :128])
                whole = jnp.concatenate([a[:, :256], middle, b[:, 128:]], axis=1)
                top, rest = split(whole)
                high_ref[pl.ds(target, rows), pair * PAIR : (pair + 1) * PAIR] = top
                low_ref[pl.ds(target, rows), pair * PAIR : (pair + 1) * PAIR] = rest
            return carry

        lax.fori_loop(0, 20, body, 0)


def screen_call(place, own, other):
    shape = jax.ShapeDtypeStruct((2 * own.shape[0], own.shape[1]), jnp.bfloat16)
    return pl.pallas_call(
        screen_kernel,
        out_shape=(shape, shape),
        in_specs=[SMEM, VMEM, VMEM],
        out_specs=(VMEM, VMEM),
        compiler_params=params(20),
        name="screen",
    )(place, own, other)


def left_kernel(place, *refs):
    pieces, (high_ref, low_ref, work) = refs[:8], refs[8:]
    x = place[1]
    span = pieces[0].shape[0] // 2
    for core in range(2):
        for shift in range(4):
            shard = lax.rem(x - shift + 4, 4)
            for part in range(2):
                row = pl.multiple_of(part * 8 * span + core * 4 * span + shard * span, 8)
                work[pl.ds(row, span), :] = pieces[core * 4 + shift][part * span : (part + 1) * span, :]
    for block in range(work.shape[1] // 128):
        turned = work[:, block * 128 : (block + 1) * 128].T
        top, rest = split(turned)
        high_ref[block * 128 : (block + 1) * 128, :] = top
        low_ref[block * 128 : (block + 1) * 128, :] = rest


def left_call(place, pieces):
    depth, width = pieces[0].shape
    shape = jax.ShapeDtypeStruct((width, 8 * depth), jnp.bfloat16)
    return pl.pallas_call(
        left_kernel,
        out_shape=(shape, shape),
        in_specs=[SMEM] + [VMEM] * 8,
        out_specs=(VMEM, VMEM),
        scratch_shapes=[pltpu.VMEM((8 * depth, width), jnp.float32)],
        compiler_params=params(20),
        name="left",
    )(place, *pieces)


def load_right(place, refs, high, low):
    y = place[2]
    span = refs[0].shape[0] // 8
    for plane, ref in enumerate(refs):
        for at, delta in enumerate((0, 3, 1, 2)):
            row = pl.multiple_of(plane * PLANE + lax.rem(y + delta, 4) * span, 16)
            for part in range(2):
                start = (at * 2 + part) * span
                top, rest = split(ref[start : start + span, :])
                high[pl.ds(row, span), part * HALF : (part + 1) * HALF] = top
                low[pl.ds(row, span), part * HALF : (part + 1) * HALF] = rest


def group_kernel(first, place, one_ref, two_ref, high_ref, low_ref, *refs):
    sum_ref, (out_ref, rh, rl) = (None if first else refs[0]), refs[-3:]
    load_right(place, (one_ref, two_ref), rh, rl)
    value = dot3(high_ref[...], low_ref[...], rh[...], rl[...])
    out_ref[...] = value if first else value + sum_ref[...]


def screen_spec(index):
    return pl.BlockSpec((PAIR, PAIR), lambda i: (0, index))


def group_call(index, place, one, two, screen_high, screen_low, total):
    whole = lambda shape: pl.BlockSpec(shape, lambda i: (0, 0))
    first = total is None
    return pl.pallas_call(
        functools.partial(group_kernel, first),
        grid=(1,),
        out_shape=jax.ShapeDtypeStruct((PAIR, 2 * HALF), jnp.float32),
        in_specs=[SMEM, whole(one.shape), whole(two.shape), screen_spec(index), screen_spec(index)]
        + ([] if first else [whole((PAIR, 2 * HALF))]),
        out_specs=whole((PAIR, 2 * HALF)),
        scratch_shapes=[pltpu.VMEM((PAIR, 2 * HALF), jnp.bfloat16)] * 2,
        compiler_params=params(24),
        name="group",
    )(place, one, two, screen_high, screen_low, *([] if first else [total]))


def pair_kernel(place, table, one_ref, two_ref, high_ref, low_ref, sum_ref, left_high, left_low, keep_ref, give_ref, rh, rl, kern):
    load_right(place, (one_ref, two_ref), rh, rl)
    product = sum_ref[...] + dot3(high_ref[...], low_ref[...], rh[...], rl[...])
    mid = product.shape[0] // 2
    real = product[:mid, :HALF] - product[mid:, HALF:]
    imag = product[mid:, :HALF] + product[:mid, HALF:]
    applied = NG ** (-0.5) * jnp.concatenate(
        [jnp.concatenate([real, imag], axis=0), jnp.concatenate([imag, -real], axis=0)], axis=1
    )
    kern[...] = dot3(left_high[...], left_low[...], *split(applied))

    lane = lax.broadcasted_iota(jnp.int32, (8, 128), 1) // BLK
    core = place[3]

    def group(g, carry):
        tiles = [[jnp.zeros((8, 128), jnp.float32) for _ in range(2)] for _ in range(2)]
        for u in range(8):
            row = pl.multiple_of(table[0, g * 8 + u] * BLK, BLK)
            column = pl.multiple_of(table[1, g * 8 + u] * 128, 128)
            shift = table[2, g * 8 + u]
            target = table[3, g * 8 + u]
            for part in range(2):
                for half in range(2):
                    tile = kern[pl.ds(row + half * 8, 8), pl.ds(column + part * HALF, 128)]
                    tile = pltpu.roll(tile, shift, 1)
                    tiles[part][half] = jnp.where(lane == target, tile, tiles[part][half])
        lanes = pl.ds(pl.multiple_of(g * 128, 128), 128)
        for half in range(2):
            keep_ref[half, :, lanes] = jnp.where(core == 0, tiles[0][half], tiles[1][half])
            give_ref[half, :, lanes] = jnp.where(core == 0, tiles[1][half], tiles[0][half])
        return carry

    lax.fori_loop(0, table.shape[1] // 8, group, 0)


def pair_call(place, table, one, two, screen_high, screen_low, total, left_high, left_low):
    whole = lambda array: pl.BlockSpec(array.shape, lambda i: (0, 0))
    shape = jax.ShapeDtypeStruct((2, 8, table.shape[1] * BLK), jnp.float32)
    out = pl.BlockSpec(shape.shape, lambda i: (0, 0, 0))
    return pl.pallas_call(
        pair_kernel,
        grid=(1,),
        out_shape=(shape, shape),
        in_specs=[SMEM, SMEM, whole(one), whole(two), screen_spec(3), screen_spec(3)]
        + [whole(total), whole(left_high), whole(left_low)],
        out_specs=(out, out),
        scratch_shapes=[pltpu.VMEM((PAIR, 2 * HALF), jnp.bfloat16)] * 2
        + [pltpu.VMEM((left_high.shape[0], 2 * HALF), jnp.float32)],
        compiler_params=params(36),
        name="pair",
    )(place, table, one, two, screen_high, screen_low, total, left_high, left_low)


def rows_kernel(keep_ref, come_ref, out_ref):
    upper = lax.broadcasted_iota(jnp.int32, out_ref.shape[1:], 0) < 4
    width = out_ref.shape[2]
    for half in range(2):
        total = keep_ref[half] + come_ref[half]
        top, bottom = total[:, :width], total[:, width:]
        out_ref[2 * half] = jnp.where(upper, top, pltpu.roll(bottom, 4, 0))
        out_ref[2 * half + 1] = jnp.where(upper, pltpu.roll(top, 4, 0), bottom)


def rows_call(keep, come):
    return pl.pallas_call(
        rows_kernel,
        out_shape=jax.ShapeDtypeStruct((4, 8, keep.shape[2] // 2), jnp.float32),
        in_specs=[VMEM, VMEM],
        out_specs=VMEM,
        name="rows",
    )(keep, come)


def owner_kernel(offset, parts_ref, out_ref, work):
    total = parts_ref[0] + parts_ref[1] + parts_ref[2] + parts_ref[3]
    width = total.shape[1]
    upper = lax.broadcasted_iota(jnp.int32, total.shape, 0) < 4
    turned = pltpu.roll(total, 4, 0)
    work[:, :width] = jnp.where(upper, total, turned)
    work[:, width : 2 * width] = jnp.where(upper, turned, total)
    work[:, 2 * width :] = jnp.zeros((8, work.shape[1] - 2 * width), jnp.float32)
    first = lax.broadcasted_iota(jnp.int32, (8, 384), 0) < 4

    def body(chip, carry):
        windows = []
        for core in range(2):
            start = offset[chip * 2 + core]
            column = pl.multiple_of(start // 8 * 128, 128)
            shift = lax.rem(384 - lax.rem(start, 8) * BLK, 384)
            windows.append(pltpu.roll(work[:, pl.ds(column, 384)], shift, 1))
        out_ref[chip] = jnp.where(first, *windows)[:, :256]
        return carry

    lax.fori_loop(0, out_ref.shape[0], body, 0)


def owner_call(offset, parts):
    return pl.pallas_call(
        owner_kernel,
        out_shape=jax.ShapeDtypeStruct((32, 8, 256), jnp.float32),
        in_specs=[SMEM, VMEM],
        out_specs=VMEM,
        scratch_shapes=[pltpu.VMEM((8, 2 * parts.shape[2] + 384), jnp.float32)],
        name="owner",
    )(offset, parts)


def sum_kernel(in_ref, out_ref):
    total = in_ref[0]
    for chip in range(1, in_ref.shape[0]):
        total = total + in_ref[chip]
    out_ref[...] = total


def sum_call(parts):
    return pl.pallas_call(
        sum_kernel,
        out_shape=jax.ShapeDtypeStruct(parts.shape[1:], jnp.float32),
        in_specs=[VMEM],
        out_specs=VMEM,
        name="total",
    )(parts)


def last_kernel(place, own_ref, come_ref, out_ref):
    core, held = place[3], place[4]
    own, come = own_ref[...], come_ref[...]
    real = jnp.where(core == 0, own, come)
    imag = jnp.where(core == 0, come, own)
    upper = lax.broadcasted_iota(jnp.int32, own.shape, 0) < 4
    mine = jnp.where(
        core == 0,
        jnp.where(upper, real, pltpu.roll(imag, 4, 0)),
        jnp.where(upper, pltpu.roll(real, 4, 0), imag),
    )
    for slot in range(CAP):
        tile = mine[:, slot // 8 * 128 : slot // 8 * 128 + 128]
        tile = pltpu.roll(tile, (128 - slot % 8 * BLK) % 128, 1)
        out_ref[slot] = jnp.where(slot < held, tile[:, :BLK], 0.0)


def last_call(place, own, come):
    return pl.pallas_call(
        last_kernel,
        out_shape=jax.ShapeDtypeStruct((CAP, 8, BLK), jnp.float32),
        in_specs=[SMEM, VMEM, VMEM],
        out_specs=VMEM,
        name="last",
    )(place, own, come)


def shards(densities, screened, pairs, owners):
    core, x = lax.axis_index("core"), lax.axis_index("x")
    z, y = lax.axis_index("z"), lax.axis_index("y")
    chip = z * lax.axis_size("y") + y
    span = screened.shape[2]
    used_list, left_at, right_at, offset, count = plan(pairs, owners)
    held = lax.dynamic_index_in_dim(count, chip * 2 + core, 0, keepdims=False)
    place = jnp.stack([z, x, y, core, held]).astype(jnp.int32)

    screen = screened.reshape(2 * 4 * span, -1)
    other = lax.ppermute(screen, "core", SWAP)
    screen_high, screen_low = screen_call(place, screen, other)

    pieces = densities.reshape(2, BLK, 64, span).transpose(2, 3, 0, 1).reshape(64, 1, -1)
    mine = lax.all_to_all(pieces, BAND, 0, 0, tiled=True)
    mine = mine.reshape(64, span, 2, BLK)

    def rows_of(which):
        chosen = jnp.take(
            mine, lax.dynamic_slice_in_dim(used_list, which * (USED // 2), USED // 2), axis=0, mode="clip"
        )
        return chosen.transpose(2, 1, 0, 3).reshape(2, span, HALF)

    keep, give = rows_of(core), rows_of(1 - core)
    take = lax.ppermute(give, "core", SWAP)
    first = jnp.where(core == 0, keep, take)
    second = jnp.where(core == 0, take, keep)
    shard = jnp.concatenate([first, second], axis=1).reshape(2 * 2 * span, HALF)

    shift = lambda array, axis, by: lax.ppermute(array, axis, ring(lax.axis_size(axis), by))
    from_below, from_above = shift(shard, "y", 1), shift(shard, "y", -1)
    across = shift(from_below, "y", 1)
    plane = jnp.concatenate([shard, from_below, from_above, across], axis=0)
    below = [plane]
    above = [plane]
    for step in range(3):
        below.append(shift(below[-1], "z", 1))
        above.append(shift(above[-1], "z", -1))
    far = shift(below[-1], "z", 1)

    columns = mine.transpose(2, 1, 0, 3).reshape(2 * span, -1)
    around = [columns] + [shift(columns, "x", by) for by in (1, 2, 3)]
    swapped = lax.ppermute(jnp.concatenate(around, axis=0), "core", SWAP)
    swapped = [swapped[at * 2 * span : (at + 1) * 2 * span] for at in range(4)]
    left_high, left_low = left_call(place, around + swapped)

    local = right_at - core * (USED // 2)
    valid = (local >= 0) & (local < USED // 2)
    local = jnp.where(valid, local, 0)
    lane = jnp.arange(local.shape[0], dtype=jnp.int32) % 8
    table = jnp.stack(
        [left_at, local // 8, (lane - local % 8) % 8 * BLK, jnp.where(valid, lane, -1)]
    ).astype(jnp.int32)

    total = None
    for index in range(3):
        total = group_call(index, place, below[index + 1], above[index + 1], screen_high, screen_low, total)
    keep, give = pair_call(place, table, plane, far, screen_high, screen_low, total, left_high, left_low)

    parts = rows_call(keep, lax.ppermute(give, "core", SWAP))
    parts = lax.all_to_all(parts, "x", 0, 0, tiled=True)
    parts = owner_call(offset, parts)
    parts = lax.all_to_all(parts, ("z", "y"), 0, 0, tiled=True)
    own = sum_call(parts)
    result = last_call(place, own, lax.ppermute(own, "core", SWAP))
    return result.reshape(1, CAP, 2, 4, BLK)


def solution(mesh):
    fine = Mesh(mesh.devices.reshape(8, 4, 2, 4), ("z", "y", "core", "x"))
    in_specs = (P(None, BAND, "x"), P(None, None, BAND, "x"), P(), P())
    out_specs = P(BAND, None, None, "x", None)
    return jax.shard_map(shards, mesh=fine, in_specs=in_specs, out_specs=out_specs, check_vma=False)
```

time: 218 us -> 193 us (0.89)
  local copies, waits for them, and re-layouts: 83.7 us -> 27.5 us
  blocking collectives: 0 us -> 17.1 us
  Pallas kernels: 23.2 us -> 40.2 us
  waiting for transfers between devices: 47.4 us -> 63 us
  between operations: 13.8 us -> 0.39 us
  other arithmetic: 19.3 us -> 6.74 us
  starting transfers between devices: 27.4 us -> 35.7 us
    reshape x6 -> x2, local copies, waits for them, and re-layouts: 37.5 us -> 4.6 us  [shards(): columns = mine.transpose(2, 1, 0, 3).reshape(2 * span, -1)]
    ppermute x7 -> x17, waiting for transfers between devices: 17.4 us -> 45.1 us  [the longest x13 42.1 us: shards(): lax.ppermute(array, axis, ring(lax.axis_size(axis), by))]
    transpose x2 -> x1, local copies, waits for them, and re-layouts: 27.9 us -> 2.35 us  [shards(): columns = mine.transpose(2, 1, 0, 3).reshape(2 * span, -1)]
    all_to_all x0 -> x1, blocking collectives: none -> 17.1 us  [shards(): parts = lax.all_to_all(parts, ('z', 'y'), 0, 0, tiled=True)]
    pallas_call x1 -> x10, Pallas kernels: 23.2 us -> 40.2 us  [the longest x1 13 us: pair_call(): pl.pallas_call(pair_kernel, grid=(1,), out_shape=(shape, shape), in_specs...]
    ppermute x7 -> x17, starting transfers between devices: 5.57 us -> 18.7 us  [the longest x13 18.4 us: shards(): lax.ppermute(array, axis, ring(lax.axis_size(axis), by))]
    all_to_all x2 -> x1, waiting for transfers between devices: 16 us -> 4.89 us  [shards(): parts = lax.all_to_all(parts, 'x', 0, 0, tiled=True)]
    gather x3 -> x0, local copies, waits for them, and re-layouts: 7.92 us -> none  [the longest x2 7.28 us: shards(): spread = jnp.take(own, jnp.minimum(at, own.shape[1] - 1), axis=1)]
  transfers between devices with their start and end apart: 12 -> 20, of which waited for: 10 -> 11; matrix products, arithmetic and copies ran while one was open for 36% -> 10% of each run, Pallas kernels for 0% -> 10%
where the time goes in v2:
time: 193 us; the launch traced here: 190 us
  waiting for transfers between devices  63 us (33%)
  Pallas kernels  40.2 us (21%)
  starting transfers between devices  35.7 us (18%)
  local copies, waits for them, and re-layouts  27.5 us (14%)
  blocking collectives  17.1 us (9%)
  other arithmetic  6.74 us (3%)
    ppermute x13, waiting for transfers between devices, shards(): lax.ppermute(array, axis, ring(lax.axis_size(axis), by))  42.1 us
    ppermute x13, starting transfers between devices, shards(): lax.ppermute(array, axis, ring(lax.axis_size(axis), by))  18.4 us
    all_to_all x1, blocking collectives, shards(): parts = lax.all_to_all(parts, ('z', 'y'), 0, 0, tiled=True)  17.1 us
    pallas_call x1, Pallas kernels, pair_call(): pl.pallas_call(pair_kernel, grid=(1,), out_shape=(shape, shape), in_specs...  13 us
    all_to_all x1, waiting for transfers between devices, shards(): mine = lax.all_to_all(pieces, BAND, 0, 0, tiled=True)  13 us
    all_to_all x1, starting transfers between devices, shards(): mine = lax.all_to_all(pieces, BAND, 0, 0, tiled=True)  12.1 us
    pallas_call x3, Pallas kernels, group_call(): pl.pallas_call(functools.partial(group_kernel, first), grid=(1,), out_sha...  8.97 us
    pallas_call x1, Pallas kernels, screen_call(): pl.pallas_call(screen_kernel, out_shape=(shape, shape), in_specs=[SMEM, V...  7.39 us
  transfers between devices with their start and end apart: 20, of which 11 were waited for; matrix products, arithmetic and copies ran while one was open for 10% of the time, Pallas kernels for 10%

profile of v2, /device:TPU:2, one launch (start us, length us, event | category | flops | bytes accessed | tf_op | source)
XLA Modules:
  0.0 190.5 jit_solution(3809032333924351008)
XLA Ops:
  0.0 1.8 reshape.199
  3.5 12.1 %all-to-all-start = ((f32[64,1,1280]{2,1,0:T(1,128)}), f32[64,1,1280]{2,1,0:T(1,128)S(1)}, u32[]{:S(2)}, u32[]{:S(2)}) async-start(f32[64,1,1280]{2,1,0:T(1,128)} %copy.32), calls=%async_computation | async-start | bytes 655360 | tf_op jit(solution)/shard_map/all_to_all | solution.py:348
  16.4 13.0 %all-to-all-done = f32[64,1,1280]{2,1,0:T(1,128)S(1)} async-done(((f32[64,1,1280]{2,1,0:T(1,128)}), f32[64,1,1280]{2,1,0:T(1,128)S(1)}, u32[]{:S(2)}, u32[]{:S(2)}) %all-to-all-start) | async-done | bytes 327712 | tf_op jit(solution)/shard_map/all_to_all | solution.py:348
  30.6 3.0 %copy.34 = f32[64,40,2,16]{1,3,2,0:T(8,128)} copy(f32[64,40,2,16]{0,3,2,1:T(8,128)} %bitcast.26) | data formatting | bytes 655360 | tf_op jit(solution)/shard_map/reshape | solution.py:349
  33.7 1.8 gather_fusion.1
  36.7 1.8 gather_fusion
  41.5 2.1 %collective-permute-start.2 = (f32[160,256]{1,0:T(8,128)}, f32[160,256]{1,0:T(8,128)S(1)}, u32[]{:S(2)}, u32[]{:S(2)}) collective-permute-start(f32[160,256]{1,0:T(8,128)} %bitcast.33), channel_id=1, source_target_pairs={{0,24},{8,0},{16,8},{24,16},{1,25},{9,1},{17,9},{25,17},{2,26},{10... | collective-permute-start | bytes 491528 | tf_op jit(solution)/shard_map/ppermute | solution.py:363
  43.7 4.6 %collective-permute-done.1 = f32[160,256]{1,0:T(8,128)S(1)} collective-permute-done((f32[160,256]{1,0:T(8,128)}, f32[160,256]{1,0:T(8,128)S(1)}, u32[]{:S(2)}, u32[]{:S(2)}) %collective-permute-start.1) | collective-permute-done | bytes 163872 | tf_op jit(solution)/shard_map/ppermute | solution.py:363
  48.3 6.8 %collective-permute-done.3 = f32[160,256]{1,0:T(8,128)S(1)} collective-permute-done((f32[160,256]{1,0:T(8,128)S(1)}, f32[160,256]{1,0:T(8,128)S(1)}, u32[]{:S(2)}, u32[]{:S(2)}) %collective-permute-start.3) | collective-permute-done | bytes 163872 | tf_op jit(solution)/shard_map/ppermute | solution.py:363
  55.1 1.8 pad_maximum_fusion.1.one_ref
  58.2 2.3 %copy.39 = f32[2,40,64,16]{1,0,3,2:T(2,128)} copy(f32[2,40,64,16]{2,3,0,1:T(8,128)} %bitcast.27) | data formatting | bytes 655360 | tf_op jit(solution)/shard_map/transpose | solution.py:374
  60.5 2.6 %reshape.206 = f32[80,1024]{0,1:T(8,128)} reshape(f32[2,40,64,16]{1,0,3,2:T(2,128)} %copy.39) | data formatting | bytes 655360 | tf_op jit(solution)/shard_map/reshape | solution.py:374
  63.2 2.0 %copy.44.refs_0_ = f32[80,1024]{1,0:T(8,128)} copy(f32[80,1024]{0,1:T(8,128)} %reshape.206) | data formatting | bytes 655360 | tf_op jit(solution)/shard_map/reshape | solution.py:374
  66.6 2.0 %collective-permute-start.9 = (f32[640,256]{1,0:T(8,128)}, f32[640,256]{1,0:T(8,128)S(1)}, u32[]{:S(2)}, u32[]{:S(2)}) collective-permute-start(f32[640,256]{1,0:T(8,128)} %pad_maximum_fusion.1.one_ref), channel_id=1, source_target_pairs={{0,224},{32,0},{64,32},{96,64},{128,96},{160,128},{192,160},{224,1... | collective-permute-start | bytes 1966088 | tf_op jit(solution)/shard_map/ppermute | solution.py:363
  68.6 5.1 %collective-permute-done.4.one_ref = f32[640,256]{1,0:T(8,128)} collective-permute-done((f32[640,256]{1,0:T(8,128)}, f32[640,256]{1,0:T(8,128)}, u32[]{:S(2)}, u32[]{:S(2)}) %collective-permute-start.4) | collective-permute-done | bytes 655392 | tf_op jit(solution)/shard_map/ppermute | solution.py:363
  74.0 2.1 %collective-permute-start.13 = (f32[80,1024]{1,0:T(8,128)}, f32[80,1024]{1,0:T(8,128)S(1)}, u32[]{:S(2)}, u32[]{:S(2)}) collective-permute-start(f32[80,1024]{1,0:T(8,128)} %copy.44.refs_0_), channel_id=1, source_target_pairs={{0,2},{1,3},{2,0},{3,1},{4,6},{5,7},{6,4},{7,5},{8,10},{9,11},{10,... | collective-permute-start | bytes 983048 | tf_op jit(solution)/shard_map/ppermute | solution.py:363
  77.5 8.8 %collective-permute-done.13.refs_2_ = f32[80,1024]{1,0:T(8,128)S(1)} collective-permute-done((f32[80,1024]{1,0:T(8,128)}, f32[80,1024]{1,0:T(8,128)S(1)}, u32[]{:S(2)}, u32[]{:S(2)}) %collective-permute-start.13) | collective-permute-done | bytes 327712 | tf_op jit(solution)/shard_map/ppermute | solution.py:363
  86.3 3.6 %collective-permute-done.14.refs_3_ = f32[80,1024]{1,0:T(8,128)S(1)} collective-permute-done((f32[80,1024]{1,0:T(8,128)}, f32[80,1024]{1,0:T(8,128)S(1)}, u32[]{:S(2)}, u32[]{:S(2)}) %collective-permute-start.14) | collective-permute-done | bytes 327712 | tf_op jit(solution)/shard_map/ppermute | solution.py:363
  89.9 2.2 %pad_maximum_fusion = f32[320,1024]{1,0:T(8,128)} fusion(f32[80,1024]{1,0:T(8,128)S(1)} %collective-permute-done.14.refs_3_, f32[80,1024]{1,0:T(8,128)S(1)} %collective-permute-done.13.refs_2_, f32[80,1024]{1,0:T(8,128)S(1)} %collective-permute-done.12.refs_1_, f32[80,1024]{1,0:T(8,128)} %copy.44.refs_0_), kind=kLoop, calls=%fused_computation.2 | loop fusion | flops 983040 | bytes 2621440 | tf_op jit(solution)/shard_map/concatenate | solution.py:376
  92.5 2.8 %collective-permute-start.10 = (f32[640,256]{1,0:T(8,128)S(1)}, f32[640,256]{1,0:T(8,128)}, u32[]{:S(2)}, u32[]{:S(2)}) collective-permute-start(f32[640,256]{1,0:T(8,128)S(1)} %collective-permute-done.9.two_ref), channel_id=1, source_target_pairs={{0,224},{32,0},{64,32},{96,64},{128,96},{160,128},{192,160},{224,1... | collective-permute-start | bytes 1966088 | tf_op jit(solution)/shard_map/ppermute | solution.py:363
  97.3 12.6 %collective-permute-done.10.two_ref = f32[640,256]{1,0:T(8,128)} collective-permute-done((f32[640,256]{1,0:T(8,128)S(1)}, f32[640,256]{1,0:T(8,128)}, u32[]{:S(2)}, u32[]{:S(2)}) %collective-permute-start.10) | collective-permute-done | bytes 655392 | tf_op jit(solution)/shard_map/ppermute | solution.py:363
  110.0 3.8 %collective-permute-start.11 = (f32[640,256]{1,0:T(8,128)}, f32[640,256]{1,0:T(8,128)}, u32[]{:S(2)}, u32[]{:S(2)}) collective-permute-start(f32[640,256]{1,0:T(8,128)} %collective-permute-done.10.two_ref), channel_id=1, source_target_pairs={{0,224},{32,0},{64,32},{96,64},{128,96},{160,128},{192,160},{224,1... | collective-permute-start | bytes 1966088 | tf_op jit(solution)/shard_map/ppermute | solution.py:363
  117.5 1.8 left.1
  119.3 7.4 %screen.1 = (bf16[640,2560]{1,0:T(8,128)(2,1)S(1)}, bf16[640,2560]{1,0:T(8,128)(2,1)S(1)}) custom-call(s32[5]{0:T(128)S(1)} %stack.29.place, f32[320,2560]{1,0:T(8,128)S(1)} %bitcast.25, f32[320,2560]{1,0:T(8,128)} %collective-permute-done.8.other_ref), custom_call_target="tpu_custom_call" | custom-call | tf_op jit(solution)/shard_map/screen/pallas_call | solution.py:102
  126.7 3.0 %group.3.refs_0_ = f32[640,512]{1,0:T(8,128)S(1)} custom-call(s32[5]{0:T(128)S(1)} %stack.29.place, f32[640,256]{1,0:T(8,128)} %collective-permute-done.4.one_ref, f32[640,256]{1,0:T(8,128)S(1)} %copy-done.9, bf16[640,2560]{1,0:T(8,128)(2,1)S(1)} %get-tuple-element.11.high_ref, bf16[640,2560]{1,0:T(8,128)(2,1)S(1)} %get-tuple-element.12.low_ref), custom_call_target="tpu_custom_call" | custom-call | tf_op jit(solution)/shard_map/group/pallas_call | solution.py:170
  129.7 2.9 %group.4.refs_0_ = f32[640,512]{1,0:T(8,128)S(1)} custom-call(s32[5]{0:T(128)S(1)} %stack.29.place, f32[640,256]{1,0:T(8,128)S(1)} %copy-done.11, f32[640,256]{1,0:T(8,128)} %collective-permute-done.10.two_ref, bf16[640,2560]{1,0:T(8,128)(2,1)S(1)} %get-tuple-element.11.high_ref, bf16[640,2560]{1,0:T(8,128)(2,1)S(1)} %get-tuple-element.12.low_ref, ...), custom_call_target="tpu_custom_call" | custom-call | tf_op jit(solution)/shard_map/group/pallas_call | solution.py:170
  132.6 3.1 %group.5.sum_ref = f32[640,512]{1,0:T(8,128)S(1)} custom-call(s32[5]{0:T(128)S(1)} %stack.29.place, f32[640,256]{1,0:T(8,128)} %collective-permute-done.6.one_ref, f32[640,256]{1,0:T(8,128)} %collective-permute-done.11.two_ref, bf16[640,2560]{1,0:T(8,128)(2,1)S(1)} %get-tuple-element.11.high_ref, bf16[640,2560]{1,0:T(8,128)(2,1)S(1)} %get-tuple-element.12.low_ref, ...), custom_call_target="tpu_custom_call" | custom-call | tf_op jit(solution)/shard_map/group/pallas_call | solution.py:170
  135.7 13.0 %pair.1 = (f32[2,8,4096]{2,1,0:T(8,128)S(1)}, f32[2,8,4096]{2,1,0:T(8,128)S(1)}) custom-call(s32[5]{0:T(128)S(1)} %stack.29.place, s32[4,256]{1,0:T(4,128)S(1)} %pad_add_fusion.table, f32[640,256]{1,0:T(8,128)} %pad_maximum_fusion.1.one_ref, f32[640,256]{1,0:T(8,128)} %collective-permute-done.7.two_ref, bf16[640,2560]{1,0:T(8,128)(2,1)S(1)} %get-tuple-element.11.high_ref, ...), custom_call_target="tpu_custom_call" | custom-call | tf_op jit(solution)/shard_map/pair/pallas_call | solution.py:222
  153.5 4.6 %all-to-all-start.1 = ((f32[4,8,2048]{2,1,0:T(8,128)}), f32[4,8,2048]{2,1,0:T(8,128)S(1)}, u32[]{:S(2)}, u32[]{:S(2)}) async-start(f32[4,8,2048]{2,1,0:T(8,128)} %rows.1), calls=%async_computation.1 | async-start | bytes 524288 | tf_op jit(solution)/shard_map/all_to_all | solution.py:394
  158.7 4.9 %all-to-all-done.1.parts_ref = f32[4,8,2048]{2,1,0:T(8,128)S(1)} async-done(((f32[4,8,2048]{2,1,0:T(8,128)}), f32[4,8,2048]{2,1,0:T(8,128)S(1)}, u32[]{:S(2)}, u32[]{:S(2)}) %all-to-all-start.1) | async-done | bytes 262176 | tf_op jit(solution)/shard_map/all_to_all | solution.py:394
  164.2 4.2 %owner.1 = f32[32,8,256]{2,1,0:T(8,128)} custom-call(s32[64]{0:T(128)} %select_reduce_fusion.4.offset, f32[4,8,2048]{2,1,0:T(8,128)} %copy-done.14), custom_call_target="tpu_custom_call" | custom-call | tf_op jit(solution)/shard_map/owner/pallas_call | solution.py:280
  168.4 17.1 %all_to_all.15.in_ref = f32[32,8,256]{2,1,0:T(8,128)} all-to-all(f32[32,8,256]{2,1,0:T(8,128)} %owner.1), channel_id=1, replica_groups=mesh['z'=8,'y'=4,'core'=2,'x'=4] {'z','y'}, dimensions={0} | all-to-all | bytes 524288 | tf_op jit(solution)/shard_map/all_to_all | solution.py:396
  (97 shorter events, 29.2 us)
Async XLA Ops:
  1.8 13.8 %copy-start.18 = (s32[256,2]{0,1:T(2,128)S(1)}, s32[256,2]{0,1:T(2,128)}, u32[]{:S(2)}) copy-start(s32[256,2]{0,1:T(2,128)} %param.6) | copy-start | bytes 6148
  3.5 26.0 %all-to-all-start = ((f32[64,1,1280]{2,1,0:T(1,128)}), f32[64,1,1280]{2,1,0:T(1,128)S(1)}, u32[]{:S(2)}, u32[]{:S(2)}) async-start(f32[64,1,1280]{2,1,0:T(1,128)} %copy.32), calls=%async_computation | async-start | bytes 655360 | tf_op jit(solution)/shard_map/all_to_all | solution.py:348
  30.6 5.9 %copy-start = (f32[2,4,40,2560]{3,2,1,0:T(8,128)S(1)}, f32[2,4,40,2560]{3,2,1,0:T(8,128)}, u32[]{:S(2)}) copy-start(f32[2,4,40,2560]{3,2,1,0:T(8,128)} %param.5) | copy-start | bytes 9830404
  36.2 2.3 %collective-permute-start = (f32[2,40,256]{1,2,0:T(8,128)}, f32[2,40,256]{1,2,0:T(8,128)}, u32[]{:S(2)}, u32[]{:S(2)}) collective-permute-start(f32[2,40,256]{1,2,0:T(8,128)} %bitcast.14), channel_id=1, source_target_pairs={{0,4},{4,0},{1,5},{5,1},{2,6},{6,2},{3,7},{7,3},{8,12},{12,8},{9,1... | collective-permute-start | bytes 245768 | tf_op jit(solution)/shard_map/ppermute | solution.py:358
  36.5 82.8 %collective-permute-start.8 = (f32[320,2560]{1,0:T(8,128)S(1)}, f32[320,2560]{1,0:T(8,128)}, u32[]{:S(2)}, u32[]{:S(2)}) collective-permute-start(f32[320,2560]{1,0:T(8,128)S(1)} %bitcast.24), channel_id=1, source_target_pairs={{0,4},{4,0},{1,5},{5,1},{2,6},{6,2},{3,7},{7,3},{8,12},{12,8},{9,1... | collective-permute-start | bytes 9830408 | tf_op jit(solution)/shard_map/ppermute | solution.py:344
  40.5 7.8 %collective-permute-start.1 = (f32[160,256]{1,0:T(8,128)}, f32[160,256]{1,0:T(8,128)S(1)}, u32[]{:S(2)}, u32[]{:S(2)}) collective-permute-start(f32[160,256]{1,0:T(8,128)} %bitcast.32), channel_id=1, source_target_pairs={{0,8},{8,16},{16,24},{24,0},{1,9},{9,17},{17,25},{25,1},{2,10},{10... | collective-permute-start | bytes 491528 | tf_op jit(solution)/shard_map/ppermute | solution.py:363
  41.5 6.8 %collective-permute-start.2 = (f32[160,256]{1,0:T(8,128)}, f32[160,256]{1,0:T(8,128)S(1)}, u32[]{:S(2)}, u32[]{:S(2)}) collective-permute-start(f32[160,256]{1,0:T(8,128)} %bitcast.33), channel_id=1, source_target_pairs={{0,24},{8,0},{16,8},{24,16},{1,25},{9,1},{17,9},{25,17},{2,26},{10... | collective-permute-start | bytes 491528 | tf_op jit(solution)/shard_map/ppermute | solution.py:363
  48.3 6.8 %collective-permute-start.3 = (f32[160,256]{1,0:T(8,128)S(1)}, f32[160,256]{1,0:T(8,128)S(1)}, u32[]{:S(2)}, u32[]{:S(2)}) collective-permute-start(f32[160,256]{1,0:T(8,128)S(1)} %collective-permute-done.1), channel_id=1, source_target_pairs={{0,8},{8,16},{16,24},{24,0},{1,9},{9,17},{17,25},{25,1},{2,10},{10... | collective-permute-start | bytes 491528 | tf_op jit(solution)/shard_map/ppermute | solution.py:363
  56.9 16.8 %collective-permute-start.4 = (f32[640,256]{1,0:T(8,128)}, f32[640,256]{1,0:T(8,128)}, u32[]{:S(2)}, u32[]{:S(2)}) collective-permute-start(f32[640,256]{1,0:T(8,128)} %pad_maximum_fusion.1.one_ref), channel_id=1, source_target_pairs={{0,32},{32,64},{64,96},{96,128},{128,160},{160,192},{192,224},{224... | collective-permute-start | bytes 1966088 | tf_op jit(solution)/shard_map/ppermute | solution.py:363
  65.1 27.2 %copy-start.17 = (s32[256]{0:T(256)S(1)}, s32[256]{0:T(256)}, u32[]{:S(2)}) copy-start(s32[256]{0:T(256)} %param.7) | copy-start | bytes 3076
  65.1 31.9 %copy-start.20 = (s32[64]{0:T(128)S(1)}, s32[64]{0:T(128)}, u32[]{:S(2)}) copy-start(s32[64]{0:T(128)} %copy-done.19) | copy-start | bytes 772
  65.1 11.0 %collective-permute-start.12 = (f32[80,1024]{1,0:T(8,128)}, f32[80,1024]{1,0:T(8,128)S(1)}, u32[]{:S(2)}, u32[]{:S(2)}) collective-permute-start(f32[80,1024]{1,0:T(8,128)} %copy.44.refs_0_), channel_id=1, source_target_pairs={{0,1},{1,2},{2,3},{3,0},{4,5},{5,6},{6,7},{7,4},{8,9},{9,10},{10,1... | collective-permute-start | bytes 983048 | tf_op jit(solution)/shard_map/ppermute | solution.py:363
  66.6 25.9 %collective-permute-start.9 = (f32[640,256]{1,0:T(8,128)}, f32[640,256]{1,0:T(8,128)S(1)}, u32[]{:S(2)}, u32[]{:S(2)}) collective-permute-start(f32[640,256]{1,0:T(8,128)} %pad_maximum_fusion.1.one_ref), channel_id=1, source_target_pairs={{0,224},{32,0},{64,32},{96,64},{128,96},{160,128},{192,160},{224,1... | collective-permute-start | bytes 1966088 | tf_op jit(solution)/shard_map/ppermute | solution.py:363
  73.7 22.5 %collective-permute-start.5 = (f32[640,256]{1,0:T(8,128)}, f32[640,256]{1,0:T(8,128)S(1)}, u32[]{:S(2)}, u32[]{:S(2)}) collective-permute-start(f32[640,256]{1,0:T(8,128)} %collective-permute-done.4.one_ref), channel_id=1, source_target_pairs={{0,32},{32,64},{64,96},{96,128},{128,160},{160,192},{192,224},{224... | collective-permute-start | bytes 1966088 | tf_op jit(solution)/shard_map/ppermute | solution.py:363
  74.0 12.4 %collective-permute-start.13 = (f32[80,1024]{1,0:T(8,128)}, f32[80,1024]{1,0:T(8,128)S(1)}, u32[]{:S(2)}, u32[]{:S(2)}) collective-permute-start(f32[80,1024]{1,0:T(8,128)} %copy.44.refs_0_), channel_id=1, source_target_pairs={{0,2},{1,3},{2,0},{3,1},{4,6},{5,7},{6,4},{7,5},{8,10},{9,11},{10,... | collective-permute-start | bytes 983048 | tf_op jit(solution)/shard_map/ppermute | solution.py:363
  76.1 16.1 %copy-start.2 = (f32[80,1024]{1,0:T(8,128)}, f32[80,1024]{1,0:T(8,128)S(1)}, u32[]{:S(2)}) copy-start(f32[80,1024]{1,0:T(8,128)S(1)} %collective-permute-done.12.refs_1_) | copy-start | bytes 983044
  76.1 13.9 %collective-permute-start.14 = (f32[80,1024]{1,0:T(8,128)}, f32[80,1024]{1,0:T(8,128)S(1)}, u32[]{:S(2)}, u32[]{:S(2)}) collective-permute-start(f32[80,1024]{1,0:T(8,128)} %copy.44.refs_0_), channel_id=1, source_target_pairs={{0,3},{1,0},{2,1},{3,2},{4,7},{5,4},{6,5},{7,6},{8,11},{9,8},{10,9... | collective-permute-start | bytes 983048 | tf_op jit(solution)/shard_map/ppermute | solution.py:363
  86.3 5.9 %copy-start.4 = (f32[80,1024]{1,0:T(8,128)}, f32[80,1024]{1,0:T(8,128)S(1)}, u32[]{:S(2)}) copy-start(f32[80,1024]{1,0:T(8,128)S(1)} %collective-permute-done.13.refs_2_) | copy-start | bytes 983044
  89.9 2.3 %copy-start.6 = (f32[80,1024]{1,0:T(8,128)}, f32[80,1024]{1,0:T(8,128)S(1)}, u32[]{:S(2)}) copy-start(f32[80,1024]{1,0:T(8,128)S(1)} %collective-permute-done.14.refs_3_) | copy-start | bytes 983044
  92.2 23.6 %collective-permute-start.15 = (f32[320,1024]{1,0:T(8,128)}, f32[320,1024]{1,0:T(8,128)}, u32[]{:S(2)}, u32[]{:S(2)}) collective-permute-start(f32[320,1024]{1,0:T(8,128)} %pad_maximum_fusion), channel_id=1, source_target_pairs={{0,4},{4,0},{1,5},{5,1},{2,6},{6,2},{3,7},{7,3},{8,12},{12,8},{9,1... | collective-permute-start | bytes 3932168 | tf_op jit(solution)/shard_map/ppermute | solution.py:376
  92.5 17.5 %collective-permute-start.10 = (f32[640,256]{1,0:T(8,128)S(1)}, f32[640,256]{1,0:T(8,128)}, u32[]{:S(2)}, u32[]{:S(2)}) collective-permute-start(f32[640,256]{1,0:T(8,128)S(1)} %collective-permute-done.9.two_ref), channel_id=1, source_target_pairs={{0,224},{32,0},{64,32},{96,64},{128,96},{160,128},{192,160},{224,1... | collective-permute-start | bytes 1966088 | tf_op jit(solution)/shard_map/ppermute | solution.py:363
  96.2 18.2 %collective-permute-start.6 = (f32[640,256]{1,0:T(8,128)S(1)}, f32[640,256]{1,0:T(8,128)}, u32[]{:S(2)}, u32[]{:S(2)}) collective-permute-start(f32[640,256]{1,0:T(8,128)S(1)} %collective-permute-done.5.one_ref), channel_id=1, source_target_pairs={{0,32},{32,64},{64,96},{96,128},{128,160},{160,192},{192,224},{224... | collective-permute-start | bytes 1966088 | tf_op jit(solution)/shard_map/ppermute | solution.py:363
  110.0 22.6 %collective-permute-start.11 = (f32[640,256]{1,0:T(8,128)}, f32[640,256]{1,0:T(8,128)}, u32[]{:S(2)}, u32[]{:S(2)}) collective-permute-start(f32[640,256]{1,0:T(8,128)} %collective-permute-done.10.two_ref), channel_id=1, source_target_pairs={{0,224},{32,0},{64,32},{96,64},{128,96},{160,128},{192,160},{224,1... | collective-permute-start | bytes 1966088 | tf_op jit(solution)/shard_map/ppermute | solution.py:363
  114.3 21.4 %collective-permute-start.7 = (f32[640,256]{1,0:T(8,128)}, f32[640,256]{1,0:T(8,128)}, u32[]{:S(2)}, u32[]{:S(2)}) collective-permute-start(f32[640,256]{1,0:T(8,128)} %collective-permute-done.6.one_ref), channel_id=1, source_target_pairs={{0,32},{32,64},{64,96},{96,128},{128,160},{160,192},{192,224},{224... | collective-permute-start | bytes 1966088 | tf_op jit(solution)/shard_map/ppermute | solution.py:363
  115.8 20.0 %copy-start.13 = (s32[5]{0:T(128)}, s32[5]{0:T(128)S(1)}, u32[]{:S(2)}) copy-start(s32[5]{0:T(128)S(1)} %stack.29.place) | copy-start | bytes 64
  115.8 1.6 copy-start.1
  115.8 1.6 copy-start.7
  119.3 7.4 %copy-start.9 = (f32[640,256]{1,0:T(8,128)S(1)}, f32[640,256]{1,0:T(8,128)}, u32[]{:S(2)}) copy-start(f32[640,256]{1,0:T(8,128)} %copy-done.8) | copy-start | bytes 1966084
  126.7 3.0 %copy-start.11 = (f32[640,256]{1,0:T(8,128)S(1)}, f32[640,256]{1,0:T(8,128)}, u32[]{:S(2)}) copy-start(f32[640,256]{1,0:T(8,128)} %copy-done.10) | copy-start | bytes 1966084
  149.5 1.5 collective-permute-start.16
  153.5 10.1 %all-to-all-start.1 = ((f32[4,8,2048]{2,1,0:T(8,128)}), f32[4,8,2048]{2,1,0:T(8,128)S(1)}, u32[]{:S(2)}, u32[]{:S(2)}) async-start(f32[4,8,2048]{2,1,0:T(8,128)} %rows.1), calls=%async_computation.1 | async-start | bytes 524288 | tf_op jit(solution)/shard_map/all_to_all | solution.py:394
  187.1 1.4 collective-permute-start.17
  (9 other events, 8.0 us)

commit v3 on v2

--- a/solution.py
+++ b/solution.py
@@ -263,7 +263,7 @@
     work[:, 2 * width :] = jnp.zeros((8, work.shape[1] - 2 * width), jnp.float32)
     first = lax.broadcasted_iota(jnp.int32, (8, 384), 0) < 4
 
-    def body(chip, carry):
+    for chip in range(out_ref.shape[0]):
         windows = []
         for core in range(2):
             start = offset[chip * 2 + core]
@@ -271,9 +271,6 @@
             shift = lax.rem(384 - lax.rem(start, 8) * BLK, 384)
             windows.append(pltpu.roll(work[:, pl.ds(column, 384)], shift, 1))
         out_ref[chip] = jnp.where(first, *windows)[:, :256]
-        return carry
-
-    lax.fori_loop(0, out_ref.shape[0], body, 0)
 
 
 def owner_call(offset, parts):
@@ -331,6 +328,108 @@
     )(place, own, come)
 
 
+def pack_kernel(place, own_ref, other_ref, out_ref, work):
+    core = place[3]
+    width = own_ref.shape[2]
+    for block in range(width // 128):
+        lanes = pl.ds(block * 128, 128)
+        rows = []
+        for part in range(2):
+            own, other = own_ref[part, :, lanes], other_ref[part, :, lanes]
+            rows += [jnp.where(core == 0, own, other), jnp.where(core == 0, other, own)]
+        rows = jnp.concatenate(rows + rows, axis=0)
+        work[block * 128 : (block + 1) * 128, :] = rows.T
+    half = lax.broadcasted_iota(jnp.int32, (8, 128), 1) < 64
+    for chip in range(32):
+        at = pl.multiple_of(chip * 80 + core * 40, 8)
+        tiles = [work[pl.ds(at + 8 * t, 8), :] for t in range(5)]
+        out_ref[chip * 20 : chip * 20 + 8, :] = jnp.where(half, tiles[0], tiles[1])
+        out_ref[chip * 20 + 8 : chip * 20 + 16, :] = jnp.where(half, tiles[2], tiles[3])
+        last = jnp.where(half, tiles[4], pltpu.roll(tiles[4], 4, 0))
+        out_ref[chip * 20 + 16 : chip * 20 + 20, :] = last[:4]
+
+
+def pack_call(place, own, other):
+    width = own.shape[2]
+    return pl.pallas_call(
+        pack_kernel,
+        out_shape=jax.ShapeDtypeStruct((32 * 20, 128), jnp.float32),
+        in_specs=[SMEM, VMEM, VMEM],
+        out_specs=VMEM,
+        scratch_shapes=[pltpu.VMEM((width, 128), jnp.float32)],
+        name="pack",
+    )(place, own, other)
+
+
+def unpack_kernel(place, used, in_ref, columns_ref, keep_ref, give_ref):
+    core = place[3]
+    quarter = lax.broadcasted_iota(jnp.int32, (8, 128), 1) // 32
+    upper = lax.broadcasted_iota(jnp.int32, (8, 128), 0) < 4
+    for group in range(8):
+        tiles = [[None] * 5 for _ in range(2)]
+        for u in range(4):
+            at = (group * 4 + u) * 20
+            one, two = in_ref[at : at + 8, :], in_ref[at + 8 : at + 16, :]
+            end = in_ref[at + 12 : at + 20, :]
+            end = jnp.where(upper, pltpu.roll(end, 4, 0), pltpu.roll(end, 64, 1))
+            for t, (source, first) in enumerate(((one, 0), (one, 64), (two, 0), (two, 64), (end, 0))):
+                for part in range(2):
+                    by = (u * 32 - first - part * 32) % 128
+                    turned = pltpu.roll(source, by, 1) if by else source
+                    old = tiles[part][t]
+                    tiles[part][t] = turned if old is None else jnp.where(quarter == u, turned, old)
+        for part in range(2):
+            for t in range(5):
+                row = part * 40 + t * 8
+                columns_ref[row : row + 8, group * 128 : (group + 1) * 128] = tiles[part][t]
+    eighth = lax.broadcasted_iota(jnp.int32, (80, 128), 1) // BLK
+    for ref, which in ((give_ref, 1 - core), (keep_ref, core)):
+        for group in range(2):
+            slab = None
+            for u in range(8):
+                block = used[which * (USED // 2) + group * 8 + u]
+                column = pl.multiple_of(block // 8 * 128, 128)
+                by = lax.rem(u * BLK + 128 - lax.rem(block, 8) * BLK, 128)
+                turned = pltpu.roll(columns_ref[:, pl.ds(column, 128)], by, 1)
+                slab = turned if slab is None else jnp.where(eighth == u, turned, slab)
+            ref[:, group * 128 : (group + 1) * 128] = slab
+
+
+def unpack_call(place, used, pieces):
+    return pl.pallas_call(
+        unpack_kernel,
+        out_shape=(
+            jax.ShapeDtypeStruct((80, 1024), jnp.float32),
+            jax.ShapeDtypeStruct((80, HALF), jnp.float32),
+            jax.ShapeDtypeStruct((80, HALF), jnp.float32),
+        ),
+        in_specs=[SMEM, SMEM, VMEM],
+        out_specs=(VMEM, VMEM, VMEM),
+        name="unpack",
+    )(place, used, pieces)
+
+
+def shard_kernel(place, keep_ref, take_ref, out_ref):
+    core = place[3]
+    for part in range(2):
+        out_ref[pl.ds(pl.multiple_of(part * 80 + core * 40, 8), 40), :] = keep_ref[part * 40 : part * 40 + 40, :]
+        out_ref[pl.ds(pl.multiple_of(part * 80 + 40 - core * 40, 8), 40), :] = take_ref[part * 40 : part * 40 + 40, :]
+
+
+def shard_call(place, keep, take):
+    return pl.pallas_call(
+        shard_kernel,
+        out_shape=jax.ShapeDtypeStruct((160, HALF), jnp.float32),
+        in_specs=[SMEM, VMEM, VMEM],
+        out_specs=VMEM,
+        name="shard",
+    )(place, keep, take)
+
+
+def after(array, *others):
+    return lax.optimization_barrier((array, *others))[0]
+
+
 def shards(densities, screened, pairs, owners):
     core, x = lax.axis_index("core"), lax.axis_index("x")
     z, y = lax.axis_index("z"), lax.axis_index("y")
@@ -340,43 +439,6 @@
     held = lax.dynamic_index_in_dim(count, chip * 2 + core, 0, keepdims=False)
     place = jnp.stack([z, x, y, core, held]).astype(jnp.int32)
 
-    screen = screened.reshape(2 * 4 * span, -1)
-    other = lax.ppermute(screen, "core", SWAP)
-    screen_high, screen_low = screen_call(place, screen, other)
-
-    pieces = densities.reshape(2, BLK, 64, span).transpose(2, 3, 0, 1).reshape(64, 1, -1)
-    mine = lax.all_to_all(pieces, BAND, 0, 0, tiled=True)
-    mine = mine.reshape(64, span, 2, BLK)
-
-    def rows_of(which):
-        chosen = jnp.take(
-            mine, lax.dynamic_slice_in_dim(used_list, which * (USED // 2), USED // 2), axis=0, mode="clip"
-        )
-        return chosen.transpose(2, 1, 0, 3).reshape(2, span, HALF)
-
-    keep, give = rows_of(core), rows_of(1 - core)
-    take = lax.ppermute(give, "core", SWAP)
-    first = jnp.where(core == 0, keep, take)
-    second = jnp.where(core == 0, take, keep)
-    shard = jnp.concatenate([first, second], axis=1).reshape(2 * 2 * span, HALF)
-
-    shift = lambda array, axis, by: lax.ppermute(array, axis, ring(lax.axis_size(axis), by))
-    from_below, from_above = shift(shard, "y", 1), shift(shard, "y", -1)
-    across = shift(from_below, "y", 1)
-    plane = jnp.concatenate([shard, from_below, from_above, across], axis=0)
-    below = [plane]
-    above = [plane]
-    for step in range(3):
-        below.append(shift(below[-1], "z", 1))
-        above.append(shift(above[-1], "z", -1))
-    far = shift(below[-1], "z", 1)
-
-    columns = mine.transpose(2, 1, 0, 3).reshape(2 * span, -1)
-    around = [columns] + [shift(columns, "x", by) for by in (1, 2, 3)]
-    swapped = lax.ppermute(jnp.concatenate(around, axis=0), "core", SWAP)
-    swapped = [swapped[at * 2 * span : (at + 1) * 2 * span] for at in range(4)]
-    left_high, left_low = left_call(place, around + swapped)
-
     local = right_at - core * (USED // 2)
     valid = (local >= 0) & (local < USED // 2)
     local = jnp.where(valid, local, 0)
@@ -385,9 +447,41 @@
         [left_at, local // 8, (lane - local % 8) % 8 * BLK, jnp.where(valid, lane, -1)]
     ).astype(jnp.int32)
 
-    total = None
-    for index in range(3):
-        total = group_call(index, place, below[index + 1], above[index + 1], screen_high, screen_low, total)
+    pieces = pack_call(place, densities, lax.ppermute(densities, "core", SWAP))
+    mine = lax.all_to_all(pieces.reshape(32, 1, -1), ("z", "y"), 0, 0, tiled=True).reshape(pieces.shape)
+    mine, table, offset = lax.optimization_barrier((mine, table, offset))
+
+    screen = screened.reshape(2 * 4 * span, -1)
+    other = lax.ppermute(after(screen, pieces), "core", SWAP)
+    screen_high, screen_low = screen_call(place, screen, other)
+
+    columns, keep, give = unpack_call(place, used_list, mine)
+    shard = shard_call(place, keep, lax.ppermute(give, "core", SWAP))
+
+    shift = lambda array, axis, by: lax.ppermute(array, axis, ring(lax.axis_size(axis), by))
+    from_below, from_above = shift(shard, "y", 1), shift(shard, "y", -1)
+    across = shift(from_below, "y", 1)
+    plane = jnp.concatenate([shard, from_below, from_above, across], axis=0)
+    below, above = shift(plane, "z", 1), shift(plane, "z", -1)
+
+    columns = after(columns, plane)
+    around = [columns] + [shift(columns, "x", by) for by in (1, 2, 3)]
+    swapped = lax.ppermute(jnp.concatenate(around, axis=0), "core", SWAP)
+    swapped = [swapped[at * 2 * span : (at + 1) * 2 * span] for at in range(4)]
+
+    below, above, screen_high, screen_low = lax.optimization_barrier((below, above, screen_high, screen_low))
+    below2, above2 = shift(below, "z", 1), shift(above, "z", -1)
+    left_high, left_low = left_call(place, around + swapped)
+    total = group_call(0, place, below, above, screen_high, screen_low, None)
+    below2, above2, total, left_high, left_low = lax.optimization_barrier(
+        (below2, above2, total, left_high, left_low)
+    )
+    below3, above3 = shift(below2, "z", 1), shift(above2, "z", -1)
+    total = group_call(1, place, below2, above2, screen_high, screen_low, total)
+    below3, above3, total = lax.optimization_barrier((below3, above3, total))
+    far = shift(below3, "z", 1)
+    total = group_call(2, place, below3, above3, screen_high, screen_low, total)
+    far, total = lax.optimization_barrier((far, total))
     keep, give = pair_call(place, table, plane, far, screen_high, screen_low, total, left_high, left_low)
 
     parts = rows_call(keep, lax.ppermute(give, "core", SWAP))

time: 193 us -> 199 us (1.031)
  local copies, waits for them, and re-layouts: 27.5 us -> 6.09 us
  waiting for transfers between devices: 63 us -> 82.3 us
  blocking collectives: 17.1 us -> 30.5 us
  starting transfers between devices: 35.7 us -> 30.5 us
    ppermute x13, waiting for transfers between devices: 42.1 us -> 65.2 us  [shards(): lax.ppermute(array, axis, ring(lax.axis_size(axis), by))]
    all_to_all x0 -> x1, blocking collectives: none -> 12.6 us  [shards(): parts = lax.all_to_all(parts, 'x', 0, 0, tiled=True)]
    reshape x5 -> x0, local copies, waits for them, and re-layouts: 10.5 us -> none  [the longest x2 4.6 us: shards(): columns = mine.transpose(2, 1, 0, 3).reshape(2 * span, -1)]
    pallas_call x0 -> x3, Pallas kernels: none -> 7.08 us  [the longest x1 3.21 us: unpack_call(): pl.pallas_call(unpack_kernel, out_shape=(jax.ShapeDtypeStruct((80, 1024),...]
    all_to_all x2 -> x1, waiting for transfers between devices: 17.9 us -> 12.8 us  [shards(): lax.all_to_all(pieces.reshape(32, 1, -1), ('z', 'y'), 0, 0, tiled=True)]
    all_to_all x2 -> x1, starting transfers between devices: 16.7 us -> 11.6 us  [shards(): lax.all_to_all(pieces.reshape(32, 1, -1), ('z', 'y'), 0, 0, tiled=True)]
    transpose x4 -> x0, local copies, waits for them, and re-layouts: 3.7 us -> none  [the longest x1 2.35 us: shards(): columns = mine.transpose(2, 1, 0, 3).reshape(2 * span, -1)]
    gather x2 -> x0, local copies, waits for them, and re-layouts: 3.57 us -> none  [rows_of(): jnp.take(mine, lax.dynamic_slice_in_dim(used_list, which * (USED // 2), U...]
  transfers between devices with their start and end apart: 20 -> 20, of which waited for: 11 -> 14; matrix products, arithmetic and copies ran while one was open for 10% -> 4% of each run, Pallas kernels for 10% -> 10%
where the time goes in v3:
time: 199 us; the launch traced here: 196 us
  waiting for transfers between devices  82.3 us (41%)
  Pallas kernels  41.4 us (21%)
  starting transfers between devices  30.5 us (15%)
  blocking collectives  30.5 us (15%)
  local copies, waits for them, and re-layouts  6.09 us (3%)
  other arithmetic  4.84 us (2%)
    ppermute x13, waiting for transfers between devices, shards(): lax.ppermute(array, axis, ring(lax.axis_size(axis), by))  65.2 us
    ppermute x13, starting transfers between devices, shards(): lax.ppermute(array, axis, ring(lax.axis_size(axis), by))  18.3 us
    all_to_all x1, blocking collectives, shards(): parts = lax.all_to_all(parts, ('z', 'y'), 0, 0, tiled=True)  17.9 us
    all_to_all x1, waiting for transfers between devices, shards(): lax.all_to_all(pieces.reshape(32, 1, -1), ('z', 'y'), 0, 0, tiled=True)  12.8 us
    all_to_all x1, blocking collectives, shards(): parts = lax.all_to_all(parts, 'x', 0, 0, tiled=True)  12.6 us
    pallas_call x1, Pallas kernels, pair_call(): pl.pallas_call(pair_kernel, grid=(1,), out_shape=(shape, shape), in_specs...  12.4 us
    all_to_all x1, starting transfers between devices, shards(): lax.all_to_all(pieces.reshape(32, 1, -1), ('z', 'y'), 0, 0, tiled=True)  11.6 us
    pallas_call x3, Pallas kernels, group_call(): pl.pallas_call(functools.partial(group_kernel, first), grid=(1,), out_sha...  7.04 us
  transfers between devices with their start and end apart: 20, of which 14 were waited for; matrix products, arithmetic and copies ran while one was open for 4% of the time, Pallas kernels for 10%

profile of v3, /device:TPU:2, one launch (start us, length us, event | category | flops | bytes accessed | tf_op | source)
XLA Modules:
  0.0 195.9 jit_solution(9392181855337402298)
XLA Ops:
  5.2 2.2 %pack.1 = f32[640,128]{1,0:T(8,128)} custom-call(s32[5]{0:T(128)} %stack.29.place, f32[2,16,2560]{2,1,0:T(8,128)} %own_ref.1, f32[2,16,2560]{2,1,0:T(8,128)} %copy-done.4), custom_call_target="tpu_custom_call" | custom-call | tf_op jit(solution)/shard_map/pack/pallas_call | solution.py:354
  8.3 11.6 %all-to-all-start = ((f32[32,1,2560]{2,1,0:T(1,128)}), f32[32,1,2560]{2,1,0:T(1,128)}, u32[]{:S(2)}, u32[]{:S(2)}) async-start(f32[32,1,2560]{2,1,0:T(1,128)} %bitcast.14), calls=%async_computation | async-start | bytes 655360 | tf_op jit(solution)/shard_map/all_to_all | solution.py:451
  21.4 12.8 %all-to-all-done = f32[32,1,2560]{2,1,0:T(1,128)} async-done(((f32[32,1,2560]{2,1,0:T(1,128)}), f32[32,1,2560]{2,1,0:T(1,128)}, u32[]{:S(2)}, u32[]{:S(2)}) %all-to-all-start) | async-done | bytes 327712 | tf_op jit(solution)/shard_map/all_to_all | solution.py:451
  34.1 3.2 %unpack.1 = (f32[80,1024]{1,0:T(8,128)}, f32[80,256]{1,0:T(8,128)}, f32[80,256]{1,0:T(8,128)}) custom-call(s32[5]{0:T(128)} %stack.29.place, s32[32]{0:T(128)} %select_reduce_fusion.5.used, f32[640,128]{1,0:T(8,128)} %bitcast.5.in_ref), custom_call_target="tpu_custom_call" | custom-call | tf_op jit(solution)/shard_map/unpack/pallas_call | solution.py:399
  39.5 1.6 shard.1
  41.4 2.9 %collective-permute-start.3 = (f32[160,256]{1,0:T(8,128)}, f32[160,256]{1,0:T(8,128)S(1)}, u32[]{:S(2)}, u32[]{:S(2)}) collective-permute-start(f32[160,256]{1,0:T(8,128)} %shard.1), channel_id=1, source_target_pairs={{0,24},{8,0},{16,8},{24,16},{1,25},{9,1},{17,9},{25,17},{2,26},{10... | collective-permute-start | bytes 491528 | tf_op jit(solution)/shard_map/ppermute | solution.py:461
  44.3 4.4 %collective-permute-done.2 = f32[160,256]{1,0:T(8,128)S(1)} collective-permute-done((f32[160,256]{1,0:T(8,128)}, f32[160,256]{1,0:T(8,128)S(1)}, u32[]{:S(2)}, u32[]{:S(2)}) %collective-permute-start.2) | collective-permute-done | bytes 163872 | tf_op jit(solution)/shard_map/ppermute | solution.py:461
  48.8 6.6 %collective-permute-done.4 = f32[160,256]{1,0:T(8,128)S(1)} collective-permute-done((f32[160,256]{1,0:T(8,128)S(1)}, f32[160,256]{1,0:T(8,128)S(1)}, u32[]{:S(2)}, u32[]{:S(2)}) %collective-permute-start.4) | collective-permute-done | bytes 163872 | tf_op jit(solution)/shard_map/ppermute | solution.py:461
  57.2 2.4 %collective-permute-start.11 = (f32[80,1024]{1,0:T(8,128)S(1)}, f32[80,1024]{1,0:T(8,128)S(1)}, u32[]{:S(2)}, u32[]{:S(2)}) collective-permute-start(f32[80,1024]{1,0:T(8,128)S(1)} %copy-done.1), channel_id=1, source_target_pairs={{0,2},{1,3},{2,0},{3,1},{4,6},{5,7},{6,4},{7,5},{8,10},{9,11},{10,... | collective-permute-start | bytes 983048 | tf_op jit(solution)/shard_map/ppermute | solution.py:461
  59.6 1.8 collective-permute-start.10
  61.4 5.0 %collective-permute-done.12.refs_3_ = f32[80,1024]{1,0:T(8,128)S(1)} collective-permute-done((f32[80,1024]{1,0:T(8,128)S(1)}, f32[80,1024]{1,0:T(8,128)S(1)}, u32[]{:S(2)}, u32[]{:S(2)}) %collective-permute-start.12) | collective-permute-done | bytes 327712 | tf_op jit(solution)/shard_map/ppermute | solution.py:461
  66.3 6.3 %collective-permute-done.11.refs_2_ = f32[80,1024]{1,0:T(8,128)S(1)} collective-permute-done((f32[80,1024]{1,0:T(8,128)S(1)}, f32[80,1024]{1,0:T(8,128)S(1)}, u32[]{:S(2)}, u32[]{:S(2)}) %collective-permute-start.11) | collective-permute-done | bytes 327712 | tf_op jit(solution)/shard_map/ppermute | solution.py:461
  74.2 1.7 collective-permute-start.5
  75.9 5.9 %screen.1 = (bf16[640,2560]{1,0:T(8,128)(2,1)S(1)}, bf16[640,2560]{1,0:T(8,128)(2,1)S(1)}) custom-call(s32[5]{0:T(128)S(1)} %copy-done.3, f32[320,2560]{1,0:T(8,128)S(1)} %bitcast.13, f32[320,2560]{1,0:T(8,128)S(1)} %collective-permute-done.7.other_ref), custom_call_target="tpu_custom_call" | custom-call | tf_op jit(solution)/shard_map/screen/pallas_call | solution.py:102
  81.8 9.1 %collective-permute-done.6.two_ref = f32[640,256]{1,0:T(8,128)S(1)} collective-permute-done((f32[640,256]{1,0:T(8,128)S(1)}, f32[640,256]{1,0:T(8,128)S(1)}, u32[]{:S(2)}, u32[]{:S(2)}) %collective-permute-start.6) | collective-permute-done | bytes 655392 | tf_op jit(solution)/shard_map/ppermute | solution.py:461
  92.6 2.8 %collective-permute-start.9 = (f32[640,256]{1,0:T(8,128)S(1)}, f32[640,256]{1,0:T(8,128)S(1)}, u32[]{:S(2)}, u32[]{:S(2)}) collective-permute-start(f32[640,256]{1,0:T(8,128)S(1)} %collective-permute-done.6.two_ref), channel_id=1, source_target_pairs={{0,224},{32,0},{64,32},{96,64},{128,96},{160,128},{192,160},{224,1... | collective-permute-start | bytes 1966088 | tf_op jit(solution)/shard_map/ppermute | solution.py:461
  95.6 1.8 left.1
  97.4 2.3 %group.3.refs_0_ = f32[640,512]{1,0:T(8,128)S(1)} custom-call(s32[5]{0:T(128)S(1)} %copy-done.3, f32[640,256]{1,0:T(8,128)S(1)} %collective-permute-done.5.one_ref, f32[640,256]{1,0:T(8,128)S(1)} %collective-permute-done.6.two_ref, bf16[640,2560]{1,0:T(8,128)(2,1)S(1)} %get-tuple-element.43.high_ref, bf16[640,2560]{1,0:T(8,128)(2,1)S(1)} %get-tuple-element.44.low_ref), custom_call_target="tpu_custom_call" | custom-call | tf_op jit(solution)/shard_map/group/pallas_call | solution.py:170
  99.7 9.6 %collective-permute-done.8.one_ref = f32[640,256]{1,0:T(8,128)S(1)} collective-permute-done((f32[640,256]{1,0:T(8,128)S(1)}, f32[640,256]{1,0:T(8,128)S(1)}, u32[]{:S(2)}, u32[]{:S(2)}) %collective-permute-start.8) | collective-permute-done | bytes 655392 | tf_op jit(solution)/shard_map/ppermute | solution.py:461
  109.4 3.2 %collective-permute-start.15 = (f32[640,256]{1,0:T(8,128)S(1)}, f32[640,256]{1,0:T(8,128)S(1)}, u32[]{:S(2)}, u32[]{:S(2)}) collective-permute-start(f32[640,256]{1,0:T(8,128)S(1)} %collective-permute-done.9.two_ref), channel_id=1, source_target_pairs={{0,224},{32,0},{64,32},{96,64},{128,96},{160,128},{192,160},{224,1... | collective-permute-start | bytes 1966088 | tf_op jit(solution)/shard_map/ppermute | solution.py:461
  112.6 2.3 %group.4.refs_0_ = f32[640,512]{1,0:T(8,128)S(1)} custom-call(s32[5]{0:T(128)S(1)} %copy-done.3, f32[640,256]{1,0:T(8,128)S(1)} %collective-permute-done.8.one_ref, f32[640,256]{1,0:T(8,128)S(1)} %collective-permute-done.9.two_ref, bf16[640,2560]{1,0:T(8,128)(2,1)S(1)} %get-tuple-element.43.high_ref, bf16[640,2560]{1,0:T(8,128)(2,1)S(1)} %get-tuple-element.44.low_ref, ...), custom_call_target="tpu_custom_call" | custom-call | tf_op jit(solution)/shard_map/group/pallas_call | solution.py:170
  114.9 10.7 %collective-permute-done.14.one_ref = f32[640,256]{1,0:T(8,128)S(1)} collective-permute-done((f32[640,256]{1,0:T(8,128)S(1)}, f32[640,256]{1,0:T(8,128)S(1)}, u32[]{:S(2)}, u32[]{:S(2)}) %collective-permute-start.14) | collective-permute-done | bytes 655392 | tf_op jit(solution)/shard_map/ppermute | solution.py:461
  125.6 1.6 collective-permute-start.16
  127.3 2.3 %group.5.sum_ref = f32[640,512]{1,0:T(8,128)S(1)} custom-call(s32[5]{0:T(128)S(1)} %copy-done.3, f32[640,256]{1,0:T(8,128)S(1)} %collective-permute-done.14.one_ref, f32[640,256]{1,0:T(8,128)S(1)} %collective-permute-done.15.two_ref, bf16[640,2560]{1,0:T(8,128)(2,1)S(1)} %get-tuple-element.43.high_ref, bf16[640,2560]{1,0:T(8,128)(2,1)S(1)} %get-tuple-element.44.low_ref, ...), custom_call_target="tpu_custom_call" | custom-call | tf_op jit(solution)/shard_map/group/pallas_call | solution.py:170
  129.6 11.3 %collective-permute-done.16.two_ref = f32[640,256]{1,0:T(8,128)S(1)} collective-permute-done((f32[640,256]{1,0:T(8,128)S(1)}, f32[640,256]{1,0:T(8,128)S(1)}, u32[]{:S(2)}, u32[]{:S(2)}) %collective-permute-start.16) | collective-permute-done | bytes 655392 | tf_op jit(solution)/shard_map/ppermute | solution.py:461
  140.9 12.4 %pair.1 = (f32[2,8,4096]{2,1,0:T(8,128)S(1)}, f32[2,8,4096]{2,1,0:T(8,128)S(1)}) custom-call(s32[5]{0:T(128)S(1)} %copy-done.3, s32[4,256]{1,0:T(4,128)S(1)} %pad_add_fusion.table, f32[640,256]{1,0:T(8,128)S(1)} %pad_maximum_fusion.1.one_ref, f32[640,256]{1,0:T(8,128)S(1)} %collective-permute-done.16.two_ref, ...), custom_call_target="tpu_custom_call" | custom-call | tf_op jit(solution)/shard_map/pair/pallas_call | solution.py:222
  154.0 1.5 collective-permute-done.17.come_ref
  156.2 1.8 rows.1
  158.0 12.6 %all_to_all.15.parts_ref = f32[4,8,2048]{2,1,0:T(8,128)} all-to-all(f32[4,8,2048]{2,1,0:T(8,128)} %rows.1), channel_id=1, replica_groups=mesh['z'=8,'y'=4,'core'=2,'x'=4] {'x'}, dimensions={0} | all-to-all | bytes 524288 | tf_op jit(solution)/shard_map/all_to_all | solution.py:488
  170.6 2.4 %owner.1 = f32[32,8,256]{2,1,0:T(8,128)} custom-call(s32[64]{0:T(128)} %select_reduce_fusion.4.offset, f32[4,8,2048]{2,1,0:T(8,128)} %all_to_all.15.parts_ref), custom_call_target="tpu_custom_call" | custom-call | tf_op jit(solution)/shard_map/owner/pallas_call | solution.py:277
  173.0 17.9 %all_to_all.16.in_ref = f32[32,8,256]{2,1,0:T(8,128)} all-to-all(f32[32,8,256]{2,1,0:T(8,128)} %owner.1), channel_id=1, replica_groups=mesh['z'=8,'y'=4,'core'=2,'x'=4] {'z','y'}, dimensions={0} | all-to-all | bytes 524288 | tf_op jit(solution)/shard_map/all_to_all | solution.py:490
  190.9 1.6 total.1.own_ref
  (58 shorter events, 19.9 us)
Async XLA Ops:
  0.0 4.5 %collective-permute-start = (f32[2,16,2560]{2,1,0:T(8,128)}, f32[2,16,2560]{2,1,0:T(8,128)S(1)}, u32[]{:S(2)}, u32[]{:S(2)}) collective-permute-start(f32[2,16,2560]{2,1,0:T(8,128)} %own_ref.1), channel_id=1, source_target_pairs={{0,4},{4,0},{1,5},{5,1},{2,6},{6,2},{3,7},{7,3},{8,12},{12,8},{9,1... | collective-permute-start | bytes 983048 | tf_op jit(solution)/shard_map/ppermute | solution.py:450
  4.5 0.7 copy-start.4
  7.5 68.4 %collective-permute-start.7 = (f32[320,2560]{1,0:T(8,128)}, f32[320,2560]{1,0:T(8,128)S(1)}, u32[]{:S(2)}, u32[]{:S(2)}) collective-permute-start(f32[320,2560]{1,0:T(8,128)} %bitcast.12), channel_id=1, source_target_pairs={{0,4},{4,0},{1,5},{5,1},{2,6},{6,2},{3,7},{7,3},{8,12},{12,8},{9,1... | collective-permute-start | bytes 9830408 | tf_op jit(solution)/shard_map/ppermute | solution.py:455
  8.3 25.9 %all-to-all-start = ((f32[32,1,2560]{2,1,0:T(1,128)}), f32[32,1,2560]{2,1,0:T(1,128)}, u32[]{:S(2)}, u32[]{:S(2)}) async-start(f32[32,1,2560]{2,1,0:T(1,128)} %bitcast.14), calls=%async_computation | async-start | bytes 655360 | tf_op jit(solution)/shard_map/all_to_all | solution.py:451
  37.4 1.5 collective-permute-start.1
  38.8 0.6 copy-start.6
  41.1 15.4 %copy-start.1 = (f32[80,1024]{1,0:T(8,128)S(1)}, f32[80,1024]{1,0:T(8,128)}, u32[]{:S(2)}) copy-start(f32[80,1024]{1,0:T(8,128)} %get-tuple-element.46.refs_0_) | copy-start | bytes 983044
  41.1 7.7 %collective-permute-start.2 = (f32[160,256]{1,0:T(8,128)}, f32[160,256]{1,0:T(8,128)S(1)}, u32[]{:S(2)}, u32[]{:S(2)}) collective-permute-start(f32[160,256]{1,0:T(8,128)} %shard.1), channel_id=1, source_target_pairs={{0,8},{8,16},{16,24},{24,0},{1,9},{9,17},{17,25},{25,1},{2,10},{10... | collective-permute-start | bytes 491528 | tf_op jit(solution)/shard_map/ppermute | solution.py:461
  41.4 7.4 %collective-permute-start.3 = (f32[160,256]{1,0:T(8,128)}, f32[160,256]{1,0:T(8,128)S(1)}, u32[]{:S(2)}, u32[]{:S(2)}) collective-permute-start(f32[160,256]{1,0:T(8,128)} %shard.1), channel_id=1, source_target_pairs={{0,24},{8,0},{16,8},{24,16},{1,25},{9,1},{17,9},{25,17},{2,26},{10... | collective-permute-start | bytes 491528 | tf_op jit(solution)/shard_map/ppermute | solution.py:461
  48.8 6.6 %collective-permute-start.4 = (f32[160,256]{1,0:T(8,128)S(1)}, f32[160,256]{1,0:T(8,128)S(1)}, u32[]{:S(2)}, u32[]{:S(2)}) collective-permute-start(f32[160,256]{1,0:T(8,128)S(1)} %collective-permute-done.2), channel_id=1, source_target_pairs={{0,8},{8,16},{16,24},{24,0},{1,9},{9,17},{17,25},{25,1},{2,10},{10... | collective-permute-start | bytes 491528 | tf_op jit(solution)/shard_map/ppermute | solution.py:461
  55.4 20.4 %copy-start = (f32[2,4,40,2560]{3,2,1,0:T(8,128)S(1)}, f32[2,4,40,2560]{3,2,1,0:T(8,128)}, u32[]{:S(2)}) copy-start(f32[2,4,40,2560]{3,2,1,0:T(8,128)} %param.5) | copy-start | bytes 9830404
  56.5 19.3 %copy-start.3 = (s32[5]{0:T(128)S(1)}, s32[5]{0:T(128)}, u32[]{:S(2)}) copy-start(s32[5]{0:T(128)} %stack.29.place) | copy-start | bytes 64
  56.5 9.8 %collective-permute-start.12 = (f32[80,1024]{1,0:T(8,128)S(1)}, f32[80,1024]{1,0:T(8,128)S(1)}, u32[]{:S(2)}, u32[]{:S(2)}) collective-permute-start(f32[80,1024]{1,0:T(8,128)S(1)} %copy-done.1), channel_id=1, source_target_pairs={{0,3},{1,0},{2,1},{3,2},{4,7},{5,4},{6,5},{7,6},{8,11},{9,8},{10,9... | collective-permute-start | bytes 983048 | tf_op jit(solution)/shard_map/ppermute | solution.py:461
  57.2 15.4 %collective-permute-start.11 = (f32[80,1024]{1,0:T(8,128)S(1)}, f32[80,1024]{1,0:T(8,128)S(1)}, u32[]{:S(2)}, u32[]{:S(2)}) collective-permute-start(f32[80,1024]{1,0:T(8,128)S(1)} %copy-done.1), channel_id=1, source_target_pairs={{0,2},{1,3},{2,0},{3,1},{4,6},{5,7},{6,4},{7,5},{8,10},{9,11},{10,... | collective-permute-start | bytes 983048 | tf_op jit(solution)/shard_map/ppermute | solution.py:461
  59.6 13.9 %collective-permute-start.10 = (f32[80,1024]{1,0:T(8,128)S(1)}, f32[80,1024]{1,0:T(8,128)S(1)}, u32[]{:S(2)}, u32[]{:S(2)}) collective-permute-start(f32[80,1024]{1,0:T(8,128)S(1)} %copy-done.1), channel_id=1, source_target_pairs={{0,1},{1,2},{2,3},{3,0},{4,5},{5,6},{6,7},{7,4},{8,9},{9,10},{10,1... | collective-permute-start | bytes 983048 | tf_op jit(solution)/shard_map/ppermute | solution.py:461
  73.6 21.8 %collective-permute-start.13 = (f32[320,1024]{1,0:T(8,128)S(1)}, f32[320,1024]{1,0:T(8,128)S(1)}, u32[]{:S(2)}, u32[]{:S(2)}) collective-permute-start(f32[320,1024]{1,0:T(8,128)S(1)} %pad_maximum_fusion), channel_id=1, source_target_pairs={{0,4},{4,0},{1,5},{5,1},{2,6},{6,2},{3,7},{7,3},{8,12},{12,8},{9,1... | collective-permute-start | bytes 3932168 | tf_op jit(solution)/shard_map/ppermute | solution.py:469
  73.7 17.1 %collective-permute-start.6 = (f32[640,256]{1,0:T(8,128)S(1)}, f32[640,256]{1,0:T(8,128)S(1)}, u32[]{:S(2)}, u32[]{:S(2)}) collective-permute-start(f32[640,256]{1,0:T(8,128)S(1)} %pad_maximum_fusion.1.one_ref), channel_id=1, source_target_pairs={{0,224},{32,0},{64,32},{96,64},{128,96},{160,128},{192,160},{224,1... | collective-permute-start | bytes 1966088 | tf_op jit(solution)/shard_map/ppermute | solution.py:461
  74.2 18.0 %collective-permute-start.5 = (f32[640,256]{1,0:T(8,128)S(1)}, f32[640,256]{1,0:T(8,128)S(1)}, u32[]{:S(2)}, u32[]{:S(2)}) collective-permute-start(f32[640,256]{1,0:T(8,128)S(1)} %pad_maximum_fusion.1.one_ref), channel_id=1, source_target_pairs={{0,32},{32,64},{64,96},{96,128},{128,160},{160,192},{192,224},{224... | collective-permute-start | bytes 1966088 | tf_op jit(solution)/shard_map/ppermute | solution.py:461
  92.2 17.2 %collective-permute-start.8 = (f32[640,256]{1,0:T(8,128)S(1)}, f32[640,256]{1,0:T(8,128)S(1)}, u32[]{:S(2)}, u32[]{:S(2)}) collective-permute-start(f32[640,256]{1,0:T(8,128)S(1)} %collective-permute-done.5.one_ref), channel_id=1, source_target_pairs={{0,32},{32,64},{64,96},{96,128},{128,160},{160,192},{192,224},{224... | collective-permute-start | bytes 1966088 | tf_op jit(solution)/shard_map/ppermute | solution.py:461
  92.6 16.7 %collective-permute-start.9 = (f32[640,256]{1,0:T(8,128)S(1)}, f32[640,256]{1,0:T(8,128)S(1)}, u32[]{:S(2)}, u32[]{:S(2)}) collective-permute-start(f32[640,256]{1,0:T(8,128)S(1)} %collective-permute-done.6.two_ref), channel_id=1, source_target_pairs={{0,224},{32,0},{64,32},{96,64},{128,96},{160,128},{192,160},{224,1... | collective-permute-start | bytes 1966088 | tf_op jit(solution)/shard_map/ppermute | solution.py:461
  109.4 16.3 %collective-permute-start.14 = (f32[640,256]{1,0:T(8,128)S(1)}, f32[640,256]{1,0:T(8,128)S(1)}, u32[]{:S(2)}, u32[]{:S(2)}) collective-permute-start(f32[640,256]{1,0:T(8,128)S(1)} %collective-permute-done.8.one_ref), channel_id=1, source_target_pairs={{0,32},{32,64},{64,96},{96,128},{128,160},{160,192},{192,224},{224... | collective-permute-start | bytes 1966088 | tf_op jit(solution)/shard_map/ppermute | solution.py:461
  109.4 16.2 %collective-permute-start.15 = (f32[640,256]{1,0:T(8,128)S(1)}, f32[640,256]{1,0:T(8,128)S(1)}, u32[]{:S(2)}, u32[]{:S(2)}) collective-permute-start(f32[640,256]{1,0:T(8,128)S(1)} %collective-permute-done.9.two_ref), channel_id=1, source_target_pairs={{0,224},{32,0},{64,32},{96,64},{128,96},{160,128},{192,160},{224,1... | collective-permute-start | bytes 1966088 | tf_op jit(solution)/shard_map/ppermute | solution.py:461
  125.6 15.3 %collective-permute-start.16 = (f32[640,256]{1,0:T(8,128)S(1)}, f32[640,256]{1,0:T(8,128)S(1)}, u32[]{:S(2)}, u32[]{:S(2)}) collective-permute-start(f32[640,256]{1,0:T(8,128)S(1)} %collective-permute-done.14.one_ref), channel_id=1, source_target_pairs={{0,32},{32,64},{64,96},{96,128},{128,160},{160,192},{192,224},{224... | collective-permute-start | bytes 1966088 | tf_op jit(solution)/shard_map/ppermute | solution.py:461
  153.3 0.7 copy-start.2
  154.0 1.5 collective-permute-start.17
  155.5 0.7 copy-start.5
  192.5 1.4 collective-permute-start.18
  193.8 0.6 copy-start.7

commit v4 on v3

--- a/solution.py
+++ b/solution.py
@@ -140,22 +140,23 @@
     )(place, *pieces)
 
 
-def load_right(place, refs, high, low):
+def load_right(place, planes, high, low):
     y = place[2]
-    span = refs[0].shape[0] // 8
-    for plane, ref in enumerate(refs):
+    span = PLANE // 4
+    for plane, refs in enumerate(planes):
+        each = 4 // len(refs)
         for at, delta in enumerate((0, 3, 1, 2)):
             row = pl.multiple_of(plane * PLANE + lax.rem(y + delta, 4) * span, 16)
             for part in range(2):
-                start = (at * 2 + part) * span
-                top, rest = split(ref[start : start + span, :])
+                start = (at % each * 2 + part) * span
+                top, rest = split(refs[at // each][start : start + span, :])
                 high[pl.ds(row, span), part * HALF : (part + 1) * HALF] = top
                 low[pl.ds(row, span), part * HALF : (part + 1) * HALF] = rest
 
 
 def group_kernel(first, place, one_ref, two_ref, high_ref, low_ref, *refs):
     sum_ref, (out_ref, rh, rl) = (None if first else refs[0]), refs[-3:]
-    load_right(place, (one_ref, two_ref), rh, rl)
+    load_right(place, ((one_ref,), (two_ref,)), rh, rl)
     value = dot3(high_ref[...], low_ref[...], rh[...], rl[...])
     out_ref[...] = value if first else value + sum_ref[...]
 
@@ -180,8 +181,8 @@
     )(place, one, two, screen_high, screen_low, *([] if first else [total]))
 
 
-def pair_kernel(place, table, one_ref, two_ref, high_ref, low_ref, sum_ref, left_high, left_low, keep_ref, give_ref, rh, rl, kern):
-    load_right(place, (one_ref, two_ref), rh, rl)
+def pair_kernel(place, table, one_ref, two_ref, three_ref, high_ref, low_ref, sum_ref, left_high, left_low, keep_ref, give_ref, rh, rl, kern):
+    load_right(place, ((one_ref,), (two_ref, three_ref)), rh, rl)
     product = sum_ref[...] + dot3(high_ref[...], low_ref[...], rh[...], rl[...])
     mid = product.shape[0] // 2
     real = product[:mid, :HALF] - product[mid:, HALF:]
@@ -215,7 +216,7 @@
     lax.fori_loop(0, table.shape[1] // 8, group, 0)
 
 
-def pair_call(place, table, one, two, screen_high, screen_low, total, left_high, left_low):
+def pair_call(place, table, one, two, three, screen_high, screen_low, total, left_high, left_low):
     whole = lambda array: pl.BlockSpec(array.shape, lambda i: (0, 0))
     shape = jax.ShapeDtypeStruct((2, 8, table.shape[1] * BLK), jnp.float32)
     out = pl.BlockSpec(shape.shape, lambda i: (0, 0, 0))
@@ -223,14 +224,14 @@
         pair_kernel,
         grid=(1,),
         out_shape=(shape, shape),
-        in_specs=[SMEM, SMEM, whole(one), whole(two), screen_spec(3), screen_spec(3)]
+        in_specs=[SMEM, SMEM, whole(one), whole(two), whole(three), screen_spec(3), screen_spec(3)]
         + [whole(total), whole(left_high), whole(left_low)],
         out_specs=(out, out),
         scratch_shapes=[pltpu.VMEM((PAIR, 2 * HALF), jnp.bfloat16)] * 2
         + [pltpu.VMEM((left_high.shape[0], 2 * HALF), jnp.float32)],
         compiler_params=params(36),
         name="pair",
-    )(place, table, one, two, screen_high, screen_low, total, left_high, left_low)
+    )(place, table, one, two, three, screen_high, screen_low, total, left_high, left_low)
 
 
 def rows_kernel(keep_ref, come_ref, out_ref):
@@ -301,8 +302,8 @@
     )(parts)
 
 
-def last_kernel(place, own_ref, come_ref, out_ref):
-    core, held = place[3], place[4]
+def last_kernel(place, held_ref, own_ref, come_ref, out_ref):
+    core, held = place[3], held_ref[0]
     own, come = own_ref[...], come_ref[...]
     real = jnp.where(core == 0, own, come)
     imag = jnp.where(core == 0, come, own)
@@ -318,14 +319,14 @@
         out_ref[slot] = jnp.where(slot < held, tile[:, :BLK], 0.0)
 
 
-def last_call(place, own, come):
+def last_call(place, held, own, come):
     return pl.pallas_call(
         last_kernel,
         out_shape=jax.ShapeDtypeStruct((CAP, 8, BLK), jnp.float32),
-        in_specs=[SMEM, VMEM, VMEM],
+        in_specs=[SMEM, SMEM, VMEM, VMEM],
         out_specs=VMEM,
         name="last",
-    )(place, own, come)
+    )(place, held, own, come)
 
 
 def pack_kernel(place, own_ref, other_ref, out_ref, work):
@@ -436,8 +437,8 @@
     chip = z * lax.axis_size("y") + y
     span = screened.shape[2]
     used_list, left_at, right_at, offset, count = plan(pairs, owners)
-    held = lax.dynamic_index_in_dim(count, chip * 2 + core, 0, keepdims=False)
-    place = jnp.stack([z, x, y, core, held]).astype(jnp.int32)
+    held = lax.dynamic_slice_in_dim(count, chip * 2 + core, 1)
+    place = jnp.stack([z, x, y, core]).astype(jnp.int32)
 
     local = right_at - core * (USED // 2)
     valid = (local >= 0) & (local < USED // 2)
@@ -449,7 +450,7 @@
 
     pieces = pack_call(place, densities, lax.ppermute(densities, "core", SWAP))
     mine = lax.all_to_all(pieces.reshape(32, 1, -1), ("z", "y"), 0, 0, tiled=True).reshape(pieces.shape)
-    mine, table, offset = lax.optimization_barrier((mine, table, offset))
+    mine, table, offset, held = lax.optimization_barrier((mine, table, offset, held))
 
     screen = screened.reshape(2 * 4 * span, -1)
     other = lax.ppermute(after(screen, pieces), "core", SWAP)
@@ -464,32 +465,31 @@
     plane = jnp.concatenate([shard, from_below, from_above, across], axis=0)
     below, above = shift(plane, "z", 1), shift(plane, "z", -1)
 
-    columns = after(columns, plane)
-    around = [columns] + [shift(columns, "x", by) for by in (1, 2, 3)]
-    swapped = lax.ppermute(jnp.concatenate(around, axis=0), "core", SWAP)
-    swapped = [swapped[at * 2 * span : (at + 1) * 2 * span] for at in range(4)]
-
     below, above, screen_high, screen_low = lax.optimization_barrier((below, above, screen_high, screen_low))
     below2, above2 = shift(below, "z", 1), shift(above, "z", -1)
-    left_high, left_low = left_call(place, around + swapped)
+    columns = after(columns, screen_high)
+    around = [columns] + [shift(columns, "x", by) for by in (1, 2, 3)]
     total = group_call(0, place, below, above, screen_high, screen_low, None)
-    below2, above2, total, left_high, left_low = lax.optimization_barrier(
-        (below2, above2, total, left_high, left_low)
-    )
+    below2, above2, total = lax.optimization_barrier((below2, above2, total))
     below3, above3 = shift(below2, "z", 1), shift(above2, "z", -1)
     total = group_call(1, place, below2, above2, screen_high, screen_low, total)
     below3, above3, total = lax.optimization_barrier((below3, above3, total))
-    far = shift(below3, "z", 1)
+    around = lax.optimization_barrier((*around, total))[:4]
+    swapped = lax.ppermute(jnp.concatenate(around, axis=0), "core", SWAP)
+    swapped = [swapped[at * 2 * span : (at + 1) * 2 * span] for at in range(4)]
+    left_high, left_low = left_call(place, list(around) + swapped)
+    middle = below3.shape[0] // 2
+    far, near = shift(below3[:middle], "z", 1), shift(above3[middle:], "z", -1)
     total = group_call(2, place, below3, above3, screen_high, screen_low, total)
-    far, total = lax.optimization_barrier((far, total))
-    keep, give = pair_call(place, table, plane, far, screen_high, screen_low, total, left_high, left_low)
+    far, near, total, left_high, left_low = lax.optimization_barrier((far, near, total, left_high, left_low))
+    keep, give = pair_call(place, table, plane, far, near, screen_high, screen_low, total, left_high, left_low)
 
     parts = rows_call(keep, lax.ppermute(give, "core", SWAP))
     parts = lax.all_to_all(parts, "x", 0, 0, tiled=True)
     parts = owner_call(offset, parts)
     parts = lax.all_to_all(parts, ("z", "y"), 0, 0, tiled=True)
     own = sum_call(parts)
-    result = last_call(place, own, lax.ppermute(own, "core", SWAP))
+    result = last_call(place, held, own, lax.ppermute(own, "core", SWAP))
     return result.reshape(1, CAP, 2, 4, BLK)
 
 

time: 199 us -> 176 us (0.88)
  waiting for transfers between devices: 82.3 us -> 60.2 us
  Pallas kernels: 41.4 us -> 43.5 us
    ppermute x13 -> x14, waiting for transfers between devices: 65.2 us -> 41.1 us  [shards(): lax.ppermute(array, axis, ring(lax.axis_size(axis), by))]
    ppermute x13 -> x14, starting transfers between devices: 18.3 us -> 18.7 us  [shards(): lax.ppermute(array, axis, ring(lax.axis_size(axis), by))]
  transfers between devices with their start and end apart: 20 -> 21, of which waited for: 14 -> 15; matrix products, arithmetic and copies ran while one was open for 4% -> 4% of each run, Pallas kernels for 10% -> 12%
where the time goes in v4:
time: 176 us; the launch traced here: 174 us
  waiting for transfers between devices  60.2 us (34%)
  Pallas kernels  43.5 us (25%)
  starting transfers between devices  30.5 us (17%)
  blocking collectives  29.9 us (17%)
  other arithmetic  5.27 us (3%)
  local copies, waits for them, and re-layouts  4.16 us (2%)
    ppermute x14, waiting for transfers between devices, shards(): lax.ppermute(array, axis, ring(lax.axis_size(axis), by))  41.1 us
    ppermute x14, starting transfers between devices, shards(): lax.ppermute(array, axis, ring(lax.axis_size(axis), by))  18.7 us
    all_to_all x1, blocking collectives, shards(): parts = lax.all_to_all(parts, ('z', 'y'), 0, 0, tiled=True)  17.4 us
    all_to_all x1, waiting for transfers between devices, shards(): lax.all_to_all(pieces.reshape(32, 1, -1), ('z', 'y'), 0, 0, tiled=True)  13.4 us
    all_to_all x1, blocking collectives, shards(): parts = lax.all_to_all(parts, 'x', 0, 0, tiled=True)  12.5 us
    pallas_call x1, Pallas kernels, pair_call(): pl.pallas_call(pair_kernel, grid=(1,), out_shape=(shape, shape), in_specs...  12.3 us
    all_to_all x1, starting transfers between devices, shards(): lax.all_to_all(pieces.reshape(32, 1, -1), ('z', 'y'), 0, 0, tiled=True)  11.6 us
    pallas_call x1, Pallas kernels, screen_call(): pl.pallas_call(screen_kernel, out_shape=(shape, shape), in_specs=[SMEM, V...  7.33 us
  transfers between devices with their start and end apart: 21, of which 15 were waited for; matrix products, arithmetic and copies ran while one was open for 4% of the time, Pallas kernels for 12%

profile of v4, /device:TPU:2, one launch (start us, length us, event | category | flops | bytes accessed | tf_op | source)
XLA Modules:
  0.0 173.8 jit_solution(10249564479686906853)
XLA Ops:
  2.0 2.4 %pack.1 = f32[640,128]{1,0:T(8,128)} custom-call(s32[4]{0:T(128)} %pad_add_fusion.1.place, f32[2,16,2560]{2,1,0:T(8,128)} %own_ref.1, f32[2,16,2560]{2,1,0:T(8,128)} %collective-permute-done.other_ref), custom_call_target="tpu_custom_call" | custom-call | tf_op jit(solution)/shard_map/pack/pallas_call | solution.py:355
  8.0 11.6 %all-to-all-start = ((f32[32,1,2560]{2,1,0:T(1,128)}), f32[32,1,2560]{2,1,0:T(1,128)}, u32[]{:S(2)}, u32[]{:S(2)}) async-start(f32[32,1,2560]{2,1,0:T(1,128)} %bitcast.14), calls=%async_computation | async-start | bytes 655360 | tf_op jit(solution)/shard_map/all_to_all | solution.py:452
  21.1 13.4 %all-to-all-done = f32[32,1,2560]{2,1,0:T(1,128)} async-done(((f32[32,1,2560]{2,1,0:T(1,128)}), f32[32,1,2560]{2,1,0:T(1,128)}, u32[]{:S(2)}, u32[]{:S(2)}) %all-to-all-start) | async-done | bytes 327712 | tf_op jit(solution)/shard_map/all_to_all | solution.py:452
  34.5 3.2 %unpack.1 = (f32[80,1024]{1,0:T(8,128)}, f32[80,256]{1,0:T(8,128)}, f32[80,256]{1,0:T(8,128)}) custom-call(s32[4]{0:T(128)} %pad_add_fusion.1.place, s32[32]{0:T(128)} %select_reduce_fusion.5.used, f32[640,128]{1,0:T(8,128)} %bitcast.5.in_ref), custom_call_target="tpu_custom_call" | custom-call | tf_op jit(solution)/shard_map/unpack/pallas_call | solution.py:400
  39.8 1.6 shard.1
  41.5 3.1 %collective-permute-start.3 = (f32[160,256]{1,0:T(8,128)}, f32[160,256]{1,0:T(8,128)S(1)}, u32[]{:S(2)}, u32[]{:S(2)}) collective-permute-start(f32[160,256]{1,0:T(8,128)} %shard.1), channel_id=1, source_target_pairs={{0,24},{8,0},{16,8},{24,16},{1,25},{9,1},{17,9},{25,17},{2,26},{10... | collective-permute-start | bytes 491528 | tf_op jit(solution)/shard_map/ppermute | solution.py:462
  44.6 4.4 %collective-permute-done.2 = f32[160,256]{1,0:T(8,128)S(1)} collective-permute-done((f32[160,256]{1,0:T(8,128)}, f32[160,256]{1,0:T(8,128)S(1)}, u32[]{:S(2)}, u32[]{:S(2)}) %collective-permute-start.2) | collective-permute-done | bytes 163872 | tf_op jit(solution)/shard_map/ppermute | solution.py:462
  49.1 6.6 %collective-permute-done.4 = f32[160,256]{1,0:T(8,128)S(1)} collective-permute-done((f32[160,256]{1,0:T(8,128)S(1)}, f32[160,256]{1,0:T(8,128)S(1)}, u32[]{:S(2)}, u32[]{:S(2)}) %collective-permute-start.4) | collective-permute-done | bytes 163872 | tf_op jit(solution)/shard_map/ppermute | solution.py:462
  56.9 1.8 %collective-permute-start.5 = (f32[640,256]{1,0:T(8,128)S(1)}, f32[640,256]{1,0:T(8,128)S(1)}, u32[]{:S(2)}, u32[]{:S(2)}) collective-permute-start(f32[640,256]{1,0:T(8,128)S(1)} %pad_maximum_fusion.1.one_ref), channel_id=1, source_target_pairs={{0,32},{32,64},{64,96},{96,128},{128,160},{160,192},{192,224},{224... | collective-permute-start | bytes 1966088 | tf_op jit(solution)/shard_map/ppermute | solution.py:462
  58.8 7.3 %screen.1 = (bf16[640,2560]{1,0:T(8,128)(2,1)S(1)}, bf16[640,2560]{1,0:T(8,128)(2,1)S(1)}) custom-call(s32[4]{0:T(128)S(1)} %copy-done.3, f32[320,2560]{1,0:T(8,128)S(1)} %bitcast.13, f32[320,2560]{1,0:T(8,128)} %collective-permute-done.7.other_ref), custom_call_target="tpu_custom_call" | custom-call | tf_op jit(solution)/shard_map/screen/pallas_call | solution.py:102
  66.1 5.7 %collective-permute-done.6.two_ref = f32[640,256]{1,0:T(8,128)S(1)} collective-permute-done((f32[640,256]{1,0:T(8,128)S(1)}, f32[640,256]{1,0:T(8,128)S(1)}, u32[]{:S(2)}, u32[]{:S(2)}) %collective-permute-start.6) | collective-permute-done | bytes 655392 | tf_op jit(solution)/shard_map/ppermute | solution.py:462
  73.7 2.7 %collective-permute-start.9 = (f32[640,256]{1,0:T(8,128)S(1)}, f32[640,256]{1,0:T(8,128)S(1)}, u32[]{:S(2)}, u32[]{:S(2)}) collective-permute-start(f32[640,256]{1,0:T(8,128)S(1)} %collective-permute-done.6.two_ref), channel_id=1, source_target_pairs={{0,224},{32,0},{64,32},{96,64},{128,96},{160,128},{192,160},{224,1... | collective-permute-start | bytes 1966088 | tf_op jit(solution)/shard_map/ppermute | solution.py:462
  76.3 2.3 %group.3.refs_0_ = f32[640,512]{1,0:T(8,128)S(1)} custom-call(s32[4]{0:T(128)S(1)} %copy-done.3, f32[640,256]{1,0:T(8,128)S(1)} %collective-permute-done.5.one_ref, f32[640,256]{1,0:T(8,128)S(1)} %collective-permute-done.6.two_ref, bf16[640,2560]{1,0:T(8,128)(2,1)S(1)} %get-tuple-element.50.high_ref, bf16[640,2560]{1,0:T(8,128)(2,1)S(1)} %get-tuple-element.51.low_ref), custom_call_target="tpu_custom_call" | custom-call | tf_op jit(solution)/shard_map/group/pallas_call | solution.py:171
  78.7 9.6 %collective-permute-done.8.one_ref = f32[640,256]{1,0:T(8,128)S(1)} collective-permute-done((f32[640,256]{1,0:T(8,128)S(1)}, f32[640,256]{1,0:T(8,128)S(1)}, u32[]{:S(2)}, u32[]{:S(2)}) %collective-permute-start.8) | collective-permute-done | bytes 655392 | tf_op jit(solution)/shard_map/ppermute | solution.py:462
  88.3 3.2 %collective-permute-start.11 = (f32[640,256]{1,0:T(8,128)S(1)}, f32[640,256]{1,0:T(8,128)S(1)}, u32[]{:S(2)}, u32[]{:S(2)}) collective-permute-start(f32[640,256]{1,0:T(8,128)S(1)} %collective-permute-done.9.two_ref), channel_id=1, source_target_pairs={{0,224},{32,0},{64,32},{96,64},{128,96},{160,128},{192,160},{224,1... | collective-permute-start | bytes 1966088 | tf_op jit(solution)/shard_map/ppermute | solution.py:462
  92.1 2.4 %collective-permute-start.15 = (f32[80,1024]{1,0:T(8,128)S(1)}, f32[80,1024]{1,0:T(8,128)S(1)}, u32[]{:S(2)}, u32[]{:S(2)}) collective-permute-start(f32[80,1024]{1,0:T(8,128)S(1)} %copy-done.1), channel_id=1, source_target_pairs={{0,2},{1,3},{2,0},{3,1},{4,6},{5,7},{6,4},{7,5},{8,10},{9,11},{10,... | collective-permute-start | bytes 983048 | tf_op jit(solution)/shard_map/ppermute | solution.py:462
  94.5 1.8 %collective-permute-start.14 = (f32[80,1024]{1,0:T(8,128)S(1)}, f32[80,1024]{1,0:T(8,128)S(1)}, u32[]{:S(2)}, u32[]{:S(2)}) collective-permute-start(f32[80,1024]{1,0:T(8,128)S(1)} %copy-done.1), channel_id=1, source_target_pairs={{0,1},{1,2},{2,3},{3,0},{4,5},{5,6},{6,7},{7,4},{8,9},{9,10},{10,1... | collective-permute-start | bytes 983048 | tf_op jit(solution)/shard_map/ppermute | solution.py:462
  96.3 2.3 %group.4.refs_0_ = f32[640,512]{1,0:T(8,128)S(1)} custom-call(s32[4]{0:T(128)S(1)} %copy-done.3, f32[640,256]{1,0:T(8,128)S(1)} %collective-permute-done.8.one_ref, f32[640,256]{1,0:T(8,128)S(1)} %collective-permute-done.9.two_ref, bf16[640,2560]{1,0:T(8,128)(2,1)S(1)} %get-tuple-element.50.high_ref, bf16[640,2560]{1,0:T(8,128)(2,1)S(1)} %get-tuple-element.51.low_ref, ...), custom_call_target="tpu_custom_call" | custom-call | tf_op jit(solution)/shard_map/group/pallas_call | solution.py:171
  98.7 4.0 %collective-permute-done.10.one_ref = f32[640,256]{1,0:T(8,128)S(1)} collective-permute-done((f32[640,256]{1,0:T(8,128)S(1)}, f32[640,256]{1,0:T(8,128)S(1)}, u32[]{:S(2)}, u32[]{:S(2)}) %collective-permute-start.10) | collective-permute-done | bytes 655392 | tf_op jit(solution)/shard_map/ppermute | solution.py:462
  102.6 2.4 %collective-permute-done.15.refs_2_ = f32[80,1024]{1,0:T(8,128)S(1)} collective-permute-done((f32[80,1024]{1,0:T(8,128)S(1)}, f32[80,1024]{1,0:T(8,128)S(1)}, u32[]{:S(2)}, u32[]{:S(2)}) %collective-permute-start.15) | collective-permute-done | bytes 327712 | tf_op jit(solution)/shard_map/ppermute | solution.py:462
  106.3 1.5 collective-permute-start.13
  108.4 2.3 %group.5.sum_ref = f32[640,512]{1,0:T(8,128)S(1)} custom-call(s32[4]{0:T(128)S(1)} %copy-done.3, f32[640,256]{1,0:T(8,128)S(1)} %collective-permute-done.10.one_ref, f32[640,256]{1,0:T(8,128)S(1)} %collective-permute-done.11.two_ref, bf16[640,2560]{1,0:T(8,128)(2,1)S(1)} %get-tuple-element.50.high_ref, bf16[640,2560]{1,0:T(8,128)(2,1)S(1)} %get-tuple-element.51.low_ref, ...), custom_call_target="tpu_custom_call" | custom-call | tf_op jit(solution)/shard_map/group/pallas_call | solution.py:171
  110.9 1.8 %left.1 = (bf16[1024,640]{1,0:T(8,128)(2,1)S(1)}, bf16[1024,640]{1,0:T(8,128)(2,1)S(1)}) custom-call(s32[4]{0:T(128)S(1)} %copy-done.3, f32[80,1024]{1,0:T(8,128)S(1)} %copy-done.1, f32[80,1024]{1,0:T(8,128)S(1)} %collective-permute-done.14.refs_1_, f32[80,1024]{1,0:T(8,128)S(1)} %collective-permute-done.15.refs_2_, ...), custom_call_target="tpu_custom_call" | custom-call | tf_op jit(solution)/shard_map/left/pallas_call | solution.py:132
  112.7 3.8 %collective-permute-done.13.three_ref = f32[320,256]{1,0:T(8,128)S(1)} collective-permute-done((f32[320,256]{1,0:T(8,128)S(1)}, f32[320,256]{1,0:T(8,128)S(1)}, u32[]{:S(2)}, u32[]{:S(2)}) %collective-permute-start.13) | collective-permute-done | bytes 327712 | tf_op jit(solution)/shard_map/ppermute | solution.py:462
  116.5 2.4 %collective-permute-done.12.two_ref = f32[320,256]{1,0:T(8,128)S(1)} collective-permute-done((f32[320,256]{1,0:T(8,128)S(1)}, f32[320,256]{1,0:T(8,128)S(1)}, u32[]{:S(2)}, u32[]{:S(2)}) %collective-permute-start.12) | collective-permute-done | bytes 327712 | tf_op jit(solution)/shard_map/ppermute | solution.py:462
  118.9 12.3 %pair.1 = (f32[2,8,4096]{2,1,0:T(8,128)S(1)}, f32[2,8,4096]{2,1,0:T(8,128)S(1)}) custom-call(s32[4]{0:T(128)S(1)} %copy-done.3, s32[4,256]{1,0:T(4,128)S(1)} %pad_add_fusion.table, f32[640,256]{1,0:T(8,128)S(1)} %pad_maximum_fusion.1.one_ref, f32[320,256]{1,0:T(8,128)S(1)} %collective-permute-done.12.two_ref, ...), custom_call_target="tpu_custom_call" | custom-call | tf_op jit(solution)/shard_map/pair/pallas_call | solution.py:223
  134.1 1.8 %rows.1 = f32[4,8,2048]{2,1,0:T(8,128)} custom-call(f32[2,8,4096]{2,1,0:T(8,128)} %copy-done.2, f32[2,8,4096]{2,1,0:T(8,128)} %copy-done.4), custom_call_target="tpu_custom_call" | custom-call | tf_op jit(solution)/shard_map/rows/pallas_call | solution.py:248
  135.9 12.5 %all_to_all.15.parts_ref = f32[4,8,2048]{2,1,0:T(8,128)} all-to-all(f32[4,8,2048]{2,1,0:T(8,128)} %rows.1), channel_id=1, replica_groups=mesh['z'=8,'y'=4,'core'=2,'x'=4] {'x'}, dimensions={0} | all-to-all | bytes 524288 | tf_op jit(solution)/shard_map/all_to_all | solution.py:488
  148.4 2.4 %owner.1 = f32[32,8,256]{2,1,0:T(8,128)} custom-call(s32[64]{0:T(128)} %select_reduce_fusion.4.offset, f32[4,8,2048]{2,1,0:T(8,128)} %all_to_all.15.parts_ref), custom_call_target="tpu_custom_call" | custom-call | tf_op jit(solution)/shard_map/owner/pallas_call | solution.py:278
  150.8 17.4 %all_to_all.16.in_ref = f32[32,8,256]{2,1,0:T(8,128)} all-to-all(f32[32,8,256]{2,1,0:T(8,128)} %owner.1), channel_id=1, replica_groups=mesh['z'=8,'y'=4,'core'=2,'x'=4] {'z','y'}, dimensions={0} | all-to-all | bytes 524288 | tf_op jit(solution)/shard_map/all_to_all | solution.py:490
  168.2 1.6 total.1.own_ref
  171.7 2.0 %last.1 = f32[12,8,16]{2,1,0:T(8,128)} custom-call(s32[4]{0:T(128)} %pad_add_fusion.1.place, s32[1]{0:T(128)} %dynamic_slice.3.held_ref, f32[8,256]{1,0:T(8,128)} %total.1.own_ref, f32[8,256]{1,0:T(8,128)} %copy-done.6), custom_call_target="tpu_custom_call" | custom-call | tf_op jit(solution)/shard_map/last/pallas_call | solution.py:323
  (60 shorter events, 19.7 us)
Async XLA Ops:
  0.0 2.0 %collective-permute-start = (f32[2,16,2560]{2,1,0:T(8,128)}, f32[2,16,2560]{2,1,0:T(8,128)}, u32[]{:S(2)}, u32[]{:S(2)}) collective-permute-start(f32[2,16,2560]{2,1,0:T(8,128)} %own_ref.1), channel_id=1, source_target_pairs={{0,4},{4,0},{1,5},{5,1},{2,6},{6,2},{3,7},{7,3},{8,12},{12,8},{9,1... | collective-permute-start | bytes 983048 | tf_op jit(solution)/shard_map/ppermute | solution.py:451
  2.0 56.8 %copy-start = (f32[2,4,40,2560]{3,2,1,0:T(8,128)S(1)}, f32[2,4,40,2560]{3,2,1,0:T(8,128)}, u32[]{:S(2)}) copy-start(f32[2,4,40,2560]{3,2,1,0:T(8,128)} %param.5) | copy-start | bytes 9830404
  4.4 54.4 %collective-permute-start.7 = (f32[320,2560]{1,0:T(8,128)}, f32[320,2560]{1,0:T(8,128)}, u32[]{:S(2)}, u32[]{:S(2)}) collective-permute-start(f32[320,2560]{1,0:T(8,128)} %bitcast.12), channel_id=1, source_target_pairs={{0,4},{4,0},{1,5},{5,1},{2,6},{6,2},{3,7},{7,3},{8,12},{12,8},{9,1... | collective-permute-start | bytes 9830408 | tf_op jit(solution)/shard_map/ppermute | solution.py:456
  8.0 50.8 %copy-start.3 = (s32[4]{0:T(128)S(1)}, s32[4]{0:T(128)}, u32[]{:S(2)}) copy-start(s32[4]{0:T(128)} %pad_add_fusion.1.place) | copy-start | bytes 52
  8.0 26.4 %all-to-all-start = ((f32[32,1,2560]{2,1,0:T(1,128)}), f32[32,1,2560]{2,1,0:T(1,128)}, u32[]{:S(2)}, u32[]{:S(2)}) async-start(f32[32,1,2560]{2,1,0:T(1,128)} %bitcast.14), calls=%async_computation | async-start | bytes 655360 | tf_op jit(solution)/shard_map/all_to_all | solution.py:452
  37.7 1.5 collective-permute-start.1
  39.2 0.6 copy-start.5
  41.4 7.7 %collective-permute-start.2 = (f32[160,256]{1,0:T(8,128)}, f32[160,256]{1,0:T(8,128)S(1)}, u32[]{:S(2)}, u32[]{:S(2)}) collective-permute-start(f32[160,256]{1,0:T(8,128)} %shard.1), channel_id=1, source_target_pairs={{0,8},{8,16},{16,24},{24,0},{1,9},{9,17},{17,25},{25,1},{2,10},{10... | collective-permute-start | bytes 491528 | tf_op jit(solution)/shard_map/ppermute | solution.py:462
  41.5 7.6 %collective-permute-start.3 = (f32[160,256]{1,0:T(8,128)}, f32[160,256]{1,0:T(8,128)S(1)}, u32[]{:S(2)}, u32[]{:S(2)}) collective-permute-start(f32[160,256]{1,0:T(8,128)} %shard.1), channel_id=1, source_target_pairs={{0,24},{8,0},{16,8},{24,16},{1,25},{9,1},{17,9},{25,17},{2,26},{10... | collective-permute-start | bytes 491528 | tf_op jit(solution)/shard_map/ppermute | solution.py:462
  49.1 6.6 %collective-permute-start.4 = (f32[160,256]{1,0:T(8,128)S(1)}, f32[160,256]{1,0:T(8,128)S(1)}, u32[]{:S(2)}, u32[]{:S(2)}) collective-permute-start(f32[160,256]{1,0:T(8,128)S(1)} %collective-permute-done.2), channel_id=1, source_target_pairs={{0,8},{8,16},{16,24},{24,0},{1,9},{9,17},{17,25},{25,1},{2,10},{10... | collective-permute-start | bytes 491528 | tf_op jit(solution)/shard_map/ppermute | solution.py:462
  56.7 15.1 %collective-permute-start.6 = (f32[640,256]{1,0:T(8,128)S(1)}, f32[640,256]{1,0:T(8,128)S(1)}, u32[]{:S(2)}, u32[]{:S(2)}) collective-permute-start(f32[640,256]{1,0:T(8,128)S(1)} %pad_maximum_fusion.1.one_ref), channel_id=1, source_target_pairs={{0,224},{32,0},{64,32},{96,64},{128,96},{160,128},{192,160},{224,1... | collective-permute-start | bytes 1966088 | tf_op jit(solution)/shard_map/ppermute | solution.py:462
  56.9 16.2 %collective-permute-start.5 = (f32[640,256]{1,0:T(8,128)S(1)}, f32[640,256]{1,0:T(8,128)S(1)}, u32[]{:S(2)}, u32[]{:S(2)}) collective-permute-start(f32[640,256]{1,0:T(8,128)S(1)} %pad_maximum_fusion.1.one_ref), channel_id=1, source_target_pairs={{0,32},{32,64},{64,96},{96,128},{128,160},{160,192},{192,224},{224... | collective-permute-start | bytes 1966088 | tf_op jit(solution)/shard_map/ppermute | solution.py:462
  73.1 18.5 %copy-start.1 = (f32[80,1024]{1,0:T(8,128)S(1)}, f32[80,1024]{1,0:T(8,128)}, u32[]{:S(2)}) copy-start(f32[80,1024]{1,0:T(8,128)} %get-tuple-element.60.refs_0_) | copy-start | bytes 983044
  73.1 15.2 %collective-permute-start.8 = (f32[640,256]{1,0:T(8,128)S(1)}, f32[640,256]{1,0:T(8,128)S(1)}, u32[]{:S(2)}, u32[]{:S(2)}) collective-permute-start(f32[640,256]{1,0:T(8,128)S(1)} %collective-permute-done.5.one_ref), channel_id=1, source_target_pairs={{0,32},{32,64},{64,96},{96,128},{128,160},{160,192},{192,224},{224... | collective-permute-start | bytes 1966088 | tf_op jit(solution)/shard_map/ppermute | solution.py:462
  73.7 14.7 %collective-permute-start.9 = (f32[640,256]{1,0:T(8,128)S(1)}, f32[640,256]{1,0:T(8,128)S(1)}, u32[]{:S(2)}, u32[]{:S(2)}) collective-permute-start(f32[640,256]{1,0:T(8,128)S(1)} %collective-permute-done.6.two_ref), channel_id=1, source_target_pairs={{0,224},{32,0},{64,32},{96,64},{128,96},{160,128},{192,160},{224,1... | collective-permute-start | bytes 1966088 | tf_op jit(solution)/shard_map/ppermute | solution.py:462
  88.3 14.3 %collective-permute-start.10 = (f32[640,256]{1,0:T(8,128)S(1)}, f32[640,256]{1,0:T(8,128)S(1)}, u32[]{:S(2)}, u32[]{:S(2)}) collective-permute-start(f32[640,256]{1,0:T(8,128)S(1)} %collective-permute-done.8.one_ref), channel_id=1, source_target_pairs={{0,32},{32,64},{64,96},{96,128},{128,160},{160,192},{192,224},{224... | collective-permute-start | bytes 1966088 | tf_op jit(solution)/shard_map/ppermute | solution.py:462
  88.3 14.3 %collective-permute-start.11 = (f32[640,256]{1,0:T(8,128)S(1)}, f32[640,256]{1,0:T(8,128)S(1)}, u32[]{:S(2)}, u32[]{:S(2)}) collective-permute-start(f32[640,256]{1,0:T(8,128)S(1)} %collective-permute-done.9.two_ref), channel_id=1, source_target_pairs={{0,224},{32,0},{64,32},{96,64},{128,96},{160,128},{192,160},{224,1... | collective-permute-start | bytes 1966088 | tf_op jit(solution)/shard_map/ppermute | solution.py:462
  91.6 11.1 %collective-permute-start.16 = (f32[80,1024]{1,0:T(8,128)S(1)}, f32[80,1024]{1,0:T(8,128)S(1)}, u32[]{:S(2)}, u32[]{:S(2)}) collective-permute-start(f32[80,1024]{1,0:T(8,128)S(1)} %copy-done.1), channel_id=1, source_target_pairs={{0,3},{1,0},{2,1},{3,2},{4,7},{5,4},{6,5},{7,6},{8,11},{9,8},{10,9... | collective-permute-start | bytes 983048 | tf_op jit(solution)/shard_map/ppermute | solution.py:462
  92.1 12.9 %collective-permute-start.15 = (f32[80,1024]{1,0:T(8,128)S(1)}, f32[80,1024]{1,0:T(8,128)S(1)}, u32[]{:S(2)}, u32[]{:S(2)}) collective-permute-start(f32[80,1024]{1,0:T(8,128)S(1)} %copy-done.1), channel_id=1, source_target_pairs={{0,2},{1,3},{2,0},{3,1},{4,6},{5,7},{6,4},{7,5},{8,10},{9,11},{10,... | collective-permute-start | bytes 983048 | tf_op jit(solution)/shard_map/ppermute | solution.py:462
  94.5 11.5 %collective-permute-start.14 = (f32[80,1024]{1,0:T(8,128)S(1)}, f32[80,1024]{1,0:T(8,128)S(1)}, u32[]{:S(2)}, u32[]{:S(2)}) collective-permute-start(f32[80,1024]{1,0:T(8,128)S(1)} %copy-done.1), channel_id=1, source_target_pairs={{0,1},{1,2},{2,3},{3,0},{4,5},{5,6},{6,7},{7,4},{8,9},{9,10},{10,1... | collective-permute-start | bytes 983048 | tf_op jit(solution)/shard_map/ppermute | solution.py:462
  106.1 4.6 %collective-permute-start.17 = (f32[320,1024]{1,0:T(8,128)S(1)}, f32[320,1024]{1,0:T(8,128)S(1)}, u32[]{:S(2)}, u32[]{:S(2)}) collective-permute-start(f32[320,1024]{1,0:T(8,128)S(1)} %pad_maximum_fusion), channel_id=1, source_target_pairs={{0,4},{4,0},{1,5},{5,1},{2,6},{6,2},{3,7},{7,3},{8,12},{12,8},{9,1... | collective-permute-start | bytes 3932168 | tf_op jit(solution)/shard_map/ppermute | solution.py:478
  106.3 10.2 %collective-permute-start.13 = (f32[320,256]{1,0:T(8,128)S(1)}, f32[320,256]{1,0:T(8,128)S(1)}, u32[]{:S(2)}, u32[]{:S(2)}) collective-permute-start(f32[320,256]{1,0:T(8,128)S(1)} %slice.27), channel_id=1, source_target_pairs={{0,224},{32,0},{64,32},{96,64},{128,96},{160,128},{192,160},{224,1... | collective-permute-start | bytes 983048 | tf_op jit(solution)/shard_map/ppermute | solution.py:462
  107.8 11.0 %collective-permute-start.12 = (f32[320,256]{1,0:T(8,128)S(1)}, f32[320,256]{1,0:T(8,128)S(1)}, u32[]{:S(2)}, u32[]{:S(2)}) collective-permute-start(f32[320,256]{1,0:T(8,128)S(1)} %slice.26), channel_id=1, source_target_pairs={{0,32},{32,64},{64,96},{96,128},{128,160},{160,192},{192,224},{224... | collective-permute-start | bytes 983048 | tf_op jit(solution)/shard_map/ppermute | solution.py:462
  131.2 0.7 copy-start.2
  131.9 1.5 collective-permute-start.18
  133.4 0.7 copy-start.4
  169.7 1.4 collective-permute-start.19
  171.1 0.6 copy-start.6

commit v5 on v4

--- a/solution.py
+++ b/solution.py
@@ -17,8 +17,11 @@
 SWAP = ((0, 1), (1, 0))
 SMEM = pl.BlockSpec(memory_space=pltpu.SMEM)
 VMEM = pl.BlockSpec(memory_space=pltpu.VMEM)
-PLANE = 320
-PAIR = 2 * PLANE
+SPAN = 80
+PLANE = 2 * SPAN
+ORDER = (0, 7, 1, 6, 2, 5, 3, 4)
+GROUPS = ((0, 5, 896), (5, 7, 384), (7, 8, 256))
+TURN = 2560 - 256
 
 
 def ring(n, shift):
@@ -66,59 +69,136 @@
     return used_list, left_at, right_at, offset, count
 
 
-def screen_kernel(place, own_ref, other_ref, high_ref, low_ref):
-    z = place[0]
-    rows = 16
-    lane = lax.broadcasted_iota(jnp.int32, (rows, 128), 1)
-    for source, ref in enumerate((own_ref, other_ref)):
-
-        def body(step, carry):
-            part = step // 10
-            start = pl.multiple_of(step * rows, rows)
-            target = pl.multiple_of(part * PLANE + source * (PLANE // 2) + (step - part * 10) * rows, rows)
-            for pair, (one, two) in enumerate(((7, 1), (6, 2), (5, 3), (0, 4))):
-                parts = []
-                for place_in, delta in ((0, one), (64, two)):
-                    plane = lax.rem(z + delta, 8)
-                    odd = lax.rem(plane, 2)
-                    column = pl.multiple_of(plane * PLANE - odd * 64, 128)
-                    window = ref[pl.ds(start, rows), pl.ds(column, 384)]
-                    turned = pltpu.roll(window, 320 if place_in == 0 else 64, 1)
-                    plain = (odd == 0) if place_in == 0 else (odd == 1)
-                    parts.append(jnp.where(plain, window, turned))
-                a, b = parts
-                middle = jnp.where(lane < 64, a[:, 256:], b[:, :128])
-                whole = jnp.concatenate([a[:, :256], middle, b[:, 128:]], axis=1)
-                top, rest = split(whole)
-                high_ref[pl.ds(target, rows), pair * PAIR : (pair + 1) * PAIR] = top
-                low_ref[pl.ds(target, rows), pair * PAIR : (pair + 1) * PAIR] = rest
+def stripes(ref, row, first, z, slots, count):
+    tiles = [None] * count
+    for delta, base in slots:
+        for upper in range(2):
+            source = lax.rem(z + delta, 8) * (4 * SPAN) + (first + 2 * upper) * SPAN
+            column = pl.multiple_of(jnp.minimum(source // 128 * 128, TURN), 128)
+            target = base + upper * SPAN
+            inner, at = target % 128, target // 128
+            by = lax.rem(inner + 256 - (source - column), 256)
+            window = pltpu.roll(ref[row, pl.ds(column, 256)], by, 1)
+            end = inner + SPAN
+            lane = lax.broadcasted_iota(jnp.int32, (window.shape[0], 128), 1)
+            old = jnp.zeros((window.shape[0], 128), jnp.float32) if tiles[at] is None else tiles[at]
+            tiles[at] = jnp.where((lane >= inner) & (lane < end), window[:, :128], old)
+            if end > 128:
+                tiles[at + 1] = jnp.where(lane < end - 128, window[:, 128:], 0.0)
+    return [jnp.zeros((16, 128), jnp.float32) if tile is None else tile for tile in tiles]
+
+
+def give_kernel(place, in_ref, *outs):
+    z, y = place[0], place[2]
+    first = lax.rem(y + 1, 2)
+    slots = [(delta, slot * PLANE) for slot, delta in enumerate(ORDER)]
+    start = 0
+    for out_ref in outs:
+
+        def body(step, carry, start=start, out_ref=out_ref):
+            row = pl.ds(pl.multiple_of(start + step * 16, 16), 16)
+            tiles = stripes(in_ref, row, first, z, slots, 10)
+            for at, tile in enumerate(tiles):
+                out_ref[pl.ds(pl.multiple_of(step * 16, 16), 16), at * 128 : (at + 1) * 128] = tile
             return carry
 
-        lax.fori_loop(0, 20, body, 0)
-
-
-def screen_call(place, own, other):
-    shape = jax.ShapeDtypeStruct((2 * own.shape[0], own.shape[1]), jnp.bfloat16)
-    return pl.pallas_call(
-        screen_kernel,
-        out_shape=(shape, shape),
-        in_specs=[SMEM, VMEM, VMEM],
-        out_specs=(VMEM, VMEM),
-        compiler_params=params(20),
-        name="screen",
-    )(place, own, other)
+        lax.fori_loop(0, out_ref.shape[0] // 16, body, 0)
+        start += out_ref.shape[0]
+
+
+def give_call(place, screen, chunks):
+    width = screen.shape[1] // 2
+    return pl.pallas_call(
+        give_kernel,
+        out_shape=[jax.ShapeDtypeStruct((rows, width), jnp.float32) for rows in chunks],
+        in_specs=[SMEM, VMEM],
+        out_specs=[VMEM] * len(chunks),
+        compiler_params=params(12),
+        name="give",
+    )(place, screen)
+
+
+def store_groups(outs, row, tiles):
+    column = 0
+    for group, (_, _, width) in enumerate(GROUPS):
+        block = jnp.concatenate(tiles[column // 128 : (column + width) // 128], axis=1)
+        top, rest = split(block)
+        outs[2 * group][row, :] = top
+        outs[2 * group + 1][row, :] = rest
+        column += width
+
+
+def own_kernel(place, *refs):
+    sources, outs = refs[:2], refs[2:]
+    z, y = place[0], place[2]
+    first = lax.rem(y, 2)
+    slots, base = [], 0
+    for one, two, width in GROUPS:
+        slots += [(ORDER[slot], base + (slot - one) * PLANE) for slot in range(one, two)]
+        base += width
+    for index, ref in enumerate(sources):
+        count = ref.shape[0]
+
+        def body(step, carry, index=index, ref=ref, count=count):
+            tiles = stripes(ref, pl.ds(pl.multiple_of(step * 16, 16), 16), first, z, slots, base // 128)
+            store_groups(outs, pl.ds(pl.multiple_of(index * count + step * 16, 16), 16), tiles)
+            return carry
+
+        lax.fori_loop(0, count // 16, body, 0)
+
+
+def come_kernel(*refs):
+    sources, outs = refs[:-6], refs[-6:]
+    start = 0
+    for ref in sources:
+
+        def body(step, carry, start=start, ref=ref):
+            row = pl.ds(pl.multiple_of(step * 16, 16), 16)
+            tiles = []
+            for one, two, width in GROUPS:
+                low, high = one * PLANE, two * PLANE
+                aligned = low // 128 * 128
+                block = ref[row, aligned : (high + 127) // 128 * 128]
+                if low > aligned:
+                    block = pltpu.roll(block, block.shape[1] - (low - aligned), 1)
+                if block.shape[1] < width:
+                    pad = jnp.zeros((16, width - block.shape[1]), jnp.float32)
+                    block = jnp.concatenate([block, pad], axis=1)
+                lane = lax.broadcasted_iota(jnp.int32, (16, width), 1)
+                block = jnp.where(lane < high - low, block[:, :width], 0.0)
+                tiles += [block[:, at : at + 128] for at in range(0, width, 128)]
+            store_groups(outs, pl.ds(pl.multiple_of(start + step * 16, 16), 16), tiles)
+            return carry
+
+        lax.fori_loop(0, ref.shape[0] // 16, body, 0)
+        start += ref.shape[0]
+
+
+def screen_call(place, sources):
+    kernel, first = (come_kernel, []) if place is None else (own_kernel, [place])
+    rows = sum(source.shape[0] for source in sources)
+    return pl.pallas_call(
+        kernel,
+        out_shape=[jax.ShapeDtypeStruct((rows, width), jnp.bfloat16) for _, _, width in GROUPS for _ in range(2)],
+        in_specs=[SMEM] * len(first) + [VMEM] * len(sources),
+        out_specs=[VMEM] * 6,
+        compiler_params=params(24),
+        name="come" if place is None else "own",
+    )(*first, *sources)
 
 
 def left_kernel(place, *refs):
     pieces, (high_ref, low_ref, work) = refs[:8], refs[8:]
     x = place[1]
-    span = pieces[0].shape[0] // 2
+    span = pieces[0].shape[0] // 4
     for core in range(2):
         for shift in range(4):
             shard = lax.rem(x - shift + 4, 4)
-            for part in range(2):
-                row = pl.multiple_of(part * 8 * span + core * 4 * span + shard * span, 8)
-                work[pl.ds(row, span), :] = pieces[core * 4 + shift][part * span : (part + 1) * span, :]
+            for chip in range(2):
+                for part in range(2):
+                    row = ((chip * 2 + core) * 2 + part) * 4 * span + shard * span
+                    start = (chip * 2 + part) * span
+                    work[pl.ds(pl.multiple_of(row, 8), span), :] = pieces[core * 4 + shift][start : start + span, :]
     for block in range(work.shape[1] // 128):
         turned = work[:, block * 128 : (block + 1) * 128].T
         top, rest = split(turned)
@@ -135,61 +215,68 @@
         in_specs=[SMEM] + [VMEM] * 8,
         out_specs=(VMEM, VMEM),
         scratch_shapes=[pltpu.VMEM((8 * depth, width), jnp.float32)],
-        compiler_params=params(20),
+        compiler_params=params(30),
         name="left",
     )(place, *pieces)
 
 
 def load_right(place, planes, high, low):
-    y = place[2]
-    span = PLANE // 4
+    second = place[2] // 2
     for plane, refs in enumerate(planes):
-        each = 4 // len(refs)
-        for at, delta in enumerate((0, 3, 1, 2)):
-            row = pl.multiple_of(plane * PLANE + lax.rem(y + delta, 4) * span, 16)
+        for at in range(2):
+            place_in = second if at == 0 else 1 - second
+            row = pl.multiple_of(plane * PLANE + place_in * SPAN, 16)
+            ref, base = (refs[0], at * 2 * SPAN) if len(refs) == 1 else (refs[at], 0)
             for part in range(2):
-                start = (at % each * 2 + part) * span
-                top, rest = split(refs[at // each][start : start + span, :])
-                high[pl.ds(row, span), part * HALF : (part + 1) * HALF] = top
-                low[pl.ds(row, span), part * HALF : (part + 1) * HALF] = rest
-
-
-def group_kernel(first, place, one_ref, two_ref, high_ref, low_ref, *refs):
-    sum_ref, (out_ref, rh, rl) = (None if first else refs[0]), refs[-3:]
-    load_right(place, ((one_ref,), (two_ref,)), rh, rl)
-    value = dot3(high_ref[...], low_ref[...], rh[...], rl[...])
-    out_ref[...] = value if first else value + sum_ref[...]
-
-
-def screen_spec(index):
-    return pl.BlockSpec((PAIR, PAIR), lambda i: (0, index))
-
-
-def group_call(index, place, one, two, screen_high, screen_low, total):
-    whole = lambda shape: pl.BlockSpec(shape, lambda i: (0, 0))
-    first = total is None
-    return pl.pallas_call(
-        functools.partial(group_kernel, first),
-        grid=(1,),
-        out_shape=jax.ShapeDtypeStruct((PAIR, 2 * HALF), jnp.float32),
-        in_specs=[SMEM, whole(one.shape), whole(two.shape), screen_spec(index), screen_spec(index)]
-        + ([] if first else [whole((PAIR, 2 * HALF))]),
-        out_specs=whole((PAIR, 2 * HALF)),
-        scratch_shapes=[pltpu.VMEM((PAIR, 2 * HALF), jnp.bfloat16)] * 2,
-        compiler_params=params(24),
+                start = base + part * SPAN
+                top, rest = split(ref[start : start + SPAN, :])
+                high[pl.ds(row, SPAN), part * HALF : (part + 1) * HALF] = top
+                low[pl.ds(row, SPAN), part * HALF : (part + 1) * HALF] = rest
+    used = len(planes) * PLANE
+    for ref in (high, low):
+        ref[used:, :] = jnp.zeros((ref.shape[0] - used, ref.shape[1]), ref.dtype)
+
+
+def group_kernel(planes, place, *refs):
+    rights, screens, rest = refs[:planes], refs[planes : planes + 4], refs[planes + 4 :]
+    out_ref, rh, rl = rest[-3:]
+    load_right(place, [(ref,) for ref in rights], rh, rl)
+    half = out_ref.shape[0] // 2
+    for at in range(2):
+        rows = slice(at * half, (at + 1) * half)
+        value = dot3(screens[2 * at][...], screens[2 * at + 1][...], rh[...], rl[...])
+        out_ref[rows, :] = value if len(rest) == 3 else value + rest[0][rows, :]
+
+
+def group_call(place, rights, screens, total):
+    rows, width = screens[0].shape
+    return pl.pallas_call(
+        functools.partial(group_kernel, len(rights)),
+        out_shape=jax.ShapeDtypeStruct((2 * rows, 2 * HALF), jnp.float32),
+        in_specs=[SMEM] + [VMEM] * (len(rights) + 4 + len(total)),
+        out_specs=VMEM,
+        scratch_shapes=[pltpu.VMEM((width, 2 * HALF), jnp.bfloat16)] * 2,
+        compiler_params=params(32),
         name="group",
-    )(place, one, two, screen_high, screen_low, *([] if first else [total]))
-
-
-def pair_kernel(place, table, one_ref, two_ref, three_ref, high_ref, low_ref, sum_ref, left_high, left_low, keep_ref, give_ref, rh, rl, kern):
-    load_right(place, ((one_ref,), (two_ref, three_ref)), rh, rl)
-    product = sum_ref[...] + dot3(high_ref[...], low_ref[...], rh[...], rl[...])
-    mid = product.shape[0] // 2
-    real = product[:mid, :HALF] - product[mid:, HALF:]
-    imag = product[mid:, :HALF] + product[:mid, HALF:]
-    applied = NG ** (-0.5) * jnp.concatenate(
-        [jnp.concatenate([real, imag], axis=0), jnp.concatenate([imag, -real], axis=0)], axis=1
-    )
+    )(place, *rights, *screens, *total)
+
+
+def pair_kernel(place, table, one_ref, two_ref, *refs):
+    screens, (sum_ref, left_high, left_low, keep_ref, give_ref, rh, rl, kern) = refs[:4], refs[4:]
+    load_right(place, ((one_ref, two_ref),), rh, rl)
+    half = sum_ref.shape[0] // 2
+    mid = half // 4
+    applied = []
+    for at in range(2):
+        product = dot3(screens[2 * at][...], screens[2 * at + 1][...], rh[...], rl[...])
+        product = product + sum_ref[at * half : (at + 1) * half, :]
+        for source in range(2):
+            top = product[2 * source * mid : (2 * source + 1) * mid]
+            low = product[(2 * source + 1) * mid : (2 * source + 2) * mid]
+            real = top[:, :HALF] - low[:, HALF:]
+            imag = low[:, :HALF] + top[:, HALF:]
+            applied += [jnp.concatenate([real, imag], axis=1), jnp.concatenate([imag, -real], axis=1)]
+    applied = NG ** (-0.5) * jnp.concatenate(applied, axis=0)
     kern[...] = dot3(left_high[...], left_low[...], *split(applied))
 
     lane = lax.broadcasted_iota(jnp.int32, (8, 128), 1) // BLK
@@ -216,22 +303,18 @@
     lax.fori_loop(0, table.shape[1] // 8, group, 0)
 
 
-def pair_call(place, table, one, two, three, screen_high, screen_low, total, left_high, left_low):
-    whole = lambda array: pl.BlockSpec(array.shape, lambda i: (0, 0))
+def pair_call(place, table, one, two, screens, total, left_high, left_low):
     shape = jax.ShapeDtypeStruct((2, 8, table.shape[1] * BLK), jnp.float32)
-    out = pl.BlockSpec(shape.shape, lambda i: (0, 0, 0))
     return pl.pallas_call(
         pair_kernel,
-        grid=(1,),
         out_shape=(shape, shape),
-        in_specs=[SMEM, SMEM, whole(one), whole(two), whole(three), screen_spec(3), screen_spec(3)]
-        + [whole(total), whole(left_high), whole(left_low)],
-        out_specs=(out, out),
-        scratch_shapes=[pltpu.VMEM((PAIR, 2 * HALF), jnp.bfloat16)] * 2
+        in_specs=[SMEM, SMEM] + [VMEM] * 9,
+        out_specs=(VMEM, VMEM),
+        scratch_shapes=[pltpu.VMEM((screens[0].shape[1], 2 * HALF), jnp.bfloat16)] * 2
         + [pltpu.VMEM((left_high.shape[0], 2 * HALF), jnp.float32)],
-        compiler_params=params(36),
+        compiler_params=params(44),
         name="pair",
-    )(place, table, one, two, three, screen_high, screen_low, total, left_high, left_low)
+    )(place, table, one, two, *screens, total, left_high, left_low)
 
 
 def rows_kernel(keep_ref, come_ref, out_ref):
@@ -448,41 +531,57 @@
         [left_at, local // 8, (lane - local % 8) % 8 * BLK, jnp.where(valid, lane, -1)]
     ).astype(jnp.int32)
 
-    pieces = pack_call(place, densities, lax.ppermute(densities, "core", SWAP))
+    shift = lambda array, axis, by: lax.ppermute(array, axis, ring(lax.axis_size(axis), by))
+    partner = lambda array: lax.ppermute(array, "y", ((0, 1), (1, 0), (2, 3), (3, 2)))
+    swap = lambda array: lax.ppermute(array, "core", SWAP)
+    hold = lax.optimization_barrier
+
+    screen = screened.reshape(2 * 4 * span, -1)
+    others = swap(densities)
+    chunks = give_call(place, screen, (192, 64, 64))
+    come = [partner(chunks[0])]
+
+    pieces = pack_call(place, densities, after(others, chunks[0]))
     mine = lax.all_to_all(pieces.reshape(32, 1, -1), ("z", "y"), 0, 0, tiled=True).reshape(pieces.shape)
-    mine, table, offset, held = lax.optimization_barrier((mine, table, offset, held))
-
-    screen = screened.reshape(2 * 4 * span, -1)
-    other = lax.ppermute(after(screen, pieces), "core", SWAP)
-    screen_high, screen_low = screen_call(place, screen, other)
-
+    other = swap(after(screen, pieces))
+    mine, table, offset, held, come[0], other = hold((mine, table, offset, held, come[0], other))
+
+    come.append(partner(after(chunks[1], mine)))
     columns, keep, give = unpack_call(place, used_list, mine)
-    shard = shard_call(place, keep, lax.ppermute(give, "core", SWAP))
-
-    shift = lambda array, axis, by: lax.ppermute(array, axis, ring(lax.axis_size(axis), by))
-    from_below, from_above = shift(shard, "y", 1), shift(shard, "y", -1)
-    across = shift(from_below, "y", 1)
-    plane = jnp.concatenate([shard, from_below, from_above, across], axis=0)
+    give = swap(give)
+    turned = [swap(come[0])]
+    give, come[1], turned[0] = hold((give, come[1], turned[0]))
+    shard = shard_call(place, keep, give)
+
+    come.append(partner(after(chunks[2], give)))
+    turned.append(swap(come[1]))
+    columns = after(columns, give)
+    columns = jnp.concatenate([columns, partner(columns)], axis=0)
+    plane = jnp.concatenate([shard, shift(shard, "y", 2)], axis=0)
+    plane, columns, come[2], turned[1] = hold((plane, columns, come[2], turned[1]))
+
     below, above = shift(plane, "z", 1), shift(plane, "z", -1)
-
-    below, above, screen_high, screen_low = lax.optimization_barrier((below, above, screen_high, screen_low))
+    turned.append(swap(come[2]))
+    own = screen_call(place, (screen, other))
+    around = [columns] + [shift(columns, "x", by) for by in (1, 2, 3)]
+    below, above, turned[2], *own = hold((below, above, turned[2], *own))
+
     below2, above2 = shift(below, "z", 1), shift(above, "z", -1)
-    columns = after(columns, screen_high)
-    around = [columns] + [shift(columns, "x", by) for by in (1, 2, 3)]
-    total = group_call(0, place, below, above, screen_high, screen_low, None)
-    below2, above2, total = lax.optimization_barrier((below2, above2, total))
+    paired = screen_call(None, (*come, *turned))
+    below2, above2, around[1], around[3], *paired = hold((below2, above2, around[1], around[3], *paired))
+
     below3, above3 = shift(below2, "z", 1), shift(above2, "z", -1)
-    total = group_call(1, place, below2, above2, screen_high, screen_low, total)
-    below3, above3, total = lax.optimization_barrier((below3, above3, total))
-    around = lax.optimization_barrier((*around, total))[:4]
-    swapped = lax.ppermute(jnp.concatenate(around, axis=0), "core", SWAP)
-    swapped = [swapped[at * 2 * span : (at + 1) * 2 * span] for at in range(4)]
-    left_high, left_low = left_call(place, list(around) + swapped)
+    screens = [own[2 * at : 2 * at + 2] + paired[2 * at : 2 * at + 2] for at in range(3)]
+    total = group_call(place, (plane, below, above, below2, above2), screens[0], ())
+    swapped = swap(around[0])
+    below3, above3, total, around[2], swapped = hold((below3, above3, total, around[2], swapped))
+
     middle = below3.shape[0] // 2
     far, near = shift(below3[:middle], "z", 1), shift(above3[middle:], "z", -1)
-    total = group_call(2, place, below3, above3, screen_high, screen_low, total)
-    far, near, total, left_high, left_low = lax.optimization_barrier((far, near, total, left_high, left_low))
-    keep, give = pair_call(place, table, plane, far, near, screen_high, screen_low, total, left_high, left_low)
+    total = group_call(place, (below3, above3), screens[1], (total,))
+    left_high, left_low = left_call(place, around + [swapped] + [swap(array) for array in around[1:]])
+    far, near, total, left_high, left_low = hold((far, near, total, left_high, left_low))
+    keep, give = pair_call(place, table, far, near, screens[2], total, left_high, left_low)
 
     parts = rows_call(keep, lax.ppermute(give, "core", SWAP))
     parts = lax.all_to_all(parts, "x", 0, 0, tiled=True)

time: 176 us -> 183 us (1.040)
  waiting for transfers between devices: 60.2 us -> 41.3 us
  Pallas kernels: 43.5 us -> 56 us
  starting transfers between devices: 30.5 us -> 36.3 us
  blocking collectives: 29.9 us -> 35 us
  local copies, waits for them, and re-layouts: 4.16 us -> 7.06 us
    ppermute x14 -> x12, waiting for transfers between devices: 41.1 us -> 13.7 us  [shards(): lax.ppermute(array, axis, ring(lax.axis_size(axis), by))]
    pallas_call x5 -> x6, Pallas kernels: 26.7 us -> 37.9 us  [the longest x2 14.9 us: screen_call(): pl.pallas_call(kernel, out_shape=[jax.ShapeDtypeStruct((rows, width), jnp...]
    ppermute x4 -> x14, waiting for transfers between devices: 2.84 us -> 9.64 us  [the longest x4 8.48 us: shards(): lax.ppermute(array, 'y', ((0, 1), (1, 0), (2, 3), (3, 2)))]
    all_to_all x1, blocking collectives: 12.5 us -> 17.1 us  [shards(): parts = lax.all_to_all(parts, 'x', 0, 0, tiled=True)]
    unnamed x14 -> x26, local copies, waits for them, and re-layouts: 2.62 us -> 6.37 us
    ppermute x14 -> x12, starting transfers between devices: 18.7 us -> 21.8 us  [shards(): lax.ppermute(array, axis, ring(lax.axis_size(axis), by))]
    ppermute x4 -> x14, starting transfers between devices: 0.23 us -> 3.15 us  [the longest x4 2.21 us: shards(): lax.ppermute(array, 'y', ((0, 1), (1, 0), (2, 3), (3, 2)))]
  transfers between devices with their start and end apart: 21 -> 29, of which waited for: 15 -> 10; matrix products, arithmetic and copies ran while one was open for 4% -> 3% of each run, Pallas kernels for 12% -> 20%
where the time goes in v5:
time: 183 us; the launch traced here: 180 us
  Pallas kernels  56 us (31%)
  waiting for transfers between devices  41.3 us (23%)
  starting transfers between devices  36.3 us (20%)
  blocking collectives  35 us (19%)
  local copies, waits for them, and re-layouts  7.06 us (4%)
  other arithmetic  4.27 us (2%)
    ppermute x12, starting transfers between devices, shards(): lax.ppermute(array, axis, ring(lax.axis_size(axis), by))  21.8 us
    all_to_all x1, blocking collectives, shards(): parts = lax.all_to_all(parts, ('z', 'y'), 0, 0, tiled=True)  18 us
    all_to_all x1, blocking collectives, shards(): parts = lax.all_to_all(parts, 'x', 0, 0, tiled=True)  17.1 us
    all_to_all x1, waiting for transfers between devices, shards(): lax.all_to_all(pieces.reshape(32, 1, -1), ('z', 'y'), 0, 0, tiled=True)  15.1 us
    pallas_call x2, Pallas kernels, screen_call(): pl.pallas_call(kernel, out_shape=[jax.ShapeDtypeStruct((rows, width), jnp...  14.9 us
    ppermute x12, waiting for transfers between devices, shards(): lax.ppermute(array, axis, ring(lax.axis_size(axis), by))  13.7 us
    all_to_all x1, starting transfers between devices, shards(): lax.all_to_all(pieces.reshape(32, 1, -1), ('z', 'y'), 0, 0, tiled=True)  11.3 us
    pallas_call x1, Pallas kernels, pair_call(): pl.pallas_call(pair_kernel, out_shape=(shape, shape), in_specs=[SMEM, SME...  10.5 us
  transfers between devices with their start and end apart: 29, of which 10 were waited for; matrix products, arithmetic and copies ran while one was open for 3% of the time, Pallas kernels for 20%

profile of v5, /device:TPU:2, one launch (start us, length us, event | category | flops | bytes accessed | tf_op | source)
XLA Modules:
  0.0 180.2 jit_solution(7420974198885652298)
XLA Ops:
  0.1 1.9 %copy-done = f32[2,4,40,2560]{3,2,1,0:T(8,128)S(1)} copy-done((f32[2,4,40,2560]{3,2,1,0:T(8,128)S(1)}, f32[2,4,40,2560]{3,2,1,0:T(8,128)}, u32[]{:S(2)}) %copy-start) | copy-done | bytes 3276824
  2.0 4.7 %give.1 = (f32[192,1280]{1,0:T(8,128)S(1)}, f32[64,1280]{1,0:T(8,128)S(1)}, f32[64,1280]{1,0:T(8,128)S(1)}) custom-call(s32[4]{0:T(128)S(1)} %pad_add_fusion.1.place, f32[320,2560]{1,0:T(8,128)S(1)} %bitcast.12), custom_call_target="tpu_custom_call" | custom-call | tf_op jit(solution)/shard_map/give/pallas_call | solution.py:111
  9.2 2.3 %pack.1 = f32[640,128]{1,0:T(8,128)} custom-call(s32[4]{0:T(128)} %copy-done.3, f32[2,16,2560]{2,1,0:T(8,128)} %own_ref.1, f32[2,16,2560]{2,1,0:T(8,128)} %collective-permute-done.other_ref), custom_call_target="tpu_custom_call" | custom-call | tf_op jit(solution)/shard_map/pack/pallas_call | solution.py:438
  11.9 1.6 collective-permute-start.1
  14.9 11.3 %all-to-all-start = ((f32[32,1,2560]{2,1,0:T(1,128)}), f32[32,1,2560]{2,1,0:T(1,128)}, u32[]{:S(2)}, u32[]{:S(2)}) async-start(f32[32,1,2560]{2,1,0:T(1,128)} %bitcast.15), calls=%async_computation | async-start | bytes 655360 | tf_op jit(solution)/shard_map/all_to_all | solution.py:545
  26.9 15.1 %all-to-all-done = f32[32,1,2560]{2,1,0:T(1,128)} async-done(((f32[32,1,2560]{2,1,0:T(1,128)}), f32[32,1,2560]{2,1,0:T(1,128)}, u32[]{:S(2)}, u32[]{:S(2)}) %all-to-all-start) | async-done | bytes 327712 | tf_op jit(solution)/shard_map/all_to_all | solution.py:545
  42.9 3.2 %unpack.1 = (f32[80,1024]{1,0:T(8,128)}, f32[80,256]{1,0:T(8,128)}, f32[80,256]{1,0:T(8,128)}) custom-call(s32[4]{0:T(128)} %copy-done.3, s32[32]{0:T(128)} %select_reduce_fusion.5.used, f32[640,128]{1,0:T(8,128)} %bitcast.6.in_ref), custom_call_target="tpu_custom_call" | custom-call | tf_op jit(solution)/shard_map/unpack/pallas_call | solution.py:483
  47.6 4.8 %collective-permute-done.4.refs_1_ = f32[64,1280]{1,0:T(8,128)} collective-permute-done((f32[64,1280]{1,0:T(8,128)}, f32[64,1280]{1,0:T(8,128)}, u32[]{:S(2)}, u32[]{:S(2)}) %collective-permute-start.4) | collective-permute-done | bytes 327712 | tf_op jit(solution)/shard_map/ppermute | solution.py:535
  52.7 1.6 shard.1
  54.3 1.6 collective-permute-start.6
  56.2 10.5 %collective-permute-done.6 = f32[160,256]{1,0:T(8,128)S(1)} collective-permute-done((f32[160,256]{1,0:T(8,128)}, f32[160,256]{1,0:T(8,128)S(1)}, u32[]{:S(2)}, u32[]{:S(2)}) %collective-permute-start.6) | collective-permute-done | bytes 163872 | tf_op jit(solution)/shard_map/ppermute | solution.py:534
  68.8 3.7 %collective-permute-done.8.refs_2_ = f32[64,1280]{1,0:T(8,128)S(1)} collective-permute-done((f32[64,1280]{1,0:T(8,128)}, f32[64,1280]{1,0:T(8,128)S(1)}, u32[]{:S(2)}, u32[]{:S(2)}) %collective-permute-start.8) | collective-permute-done | bytes 327712 | tf_op jit(solution)/shard_map/ppermute | solution.py:535
  73.9 1.9 %collective-permute-start.10 = (f32[320,256]{1,0:T(8,128)S(1)}, f32[320,256]{1,0:T(8,128)S(1)}, u32[]{:S(2)}, u32[]{:S(2)}) collective-permute-start(f32[320,256]{1,0:T(8,128)S(1)} %pad_maximum_fusion.1.refs_0_), channel_id=1, source_target_pairs={{0,32},{32,64},{64,96},{96,128},{128,160},{160,192},{192,224},{224... | collective-permute-start | bytes 983048 | tf_op jit(solution)/shard_map/ppermute | solution.py:534
  75.8 3.9 %collective-permute-start.11 = (f32[320,256]{1,0:T(8,128)S(1)}, f32[320,256]{1,0:T(8,128)S(1)}, u32[]{:S(2)}, u32[]{:S(2)}) collective-permute-start(f32[320,256]{1,0:T(8,128)S(1)} %pad_maximum_fusion.1.refs_0_), channel_id=1, source_target_pairs={{0,224},{32,0},{64,32},{96,64},{128,96},{160,128},{192,160},{224,1... | collective-permute-start | bytes 983048 | tf_op jit(solution)/shard_map/ppermute | solution.py:534
  80.3 10.0 %own.1 = (bf16[640,896]{1,0:T(8,128)(2,1)S(1)}, bf16[640,896]{1,0:T(8,128)(2,1)S(1)}, bf16[640,384]{1,0:T(8,128)(2,1)S(1)}, bf16[640,384]{1,0:T(8,128)(2,1)S(1)}...) custom-call(s32[4]{0:T(128)S(1)} %copy-done.4, f32[320,2560]{1,0:T(8,128)S(1)} %bitcast.14, ...), custom_call_target="tpu_custom_call" | custom-call | tf_op jit(solution)/shard_map/own/pallas_call | solution.py:180
  90.4 3.2 %collective-permute-start.14 = (f32[320,256]{1,0:T(8,128)S(1)}, f32[320,256]{1,0:T(8,128)S(1)}, u32[]{:S(2)}, u32[]{:S(2)}) collective-permute-start(f32[320,256]{1,0:T(8,128)S(1)} %collective-permute-done.11.refs_2_), channel_id=1, source_target_pairs={{0,224},{32,0},{64,32},{96,64},{128,96},{160,128},{192,160},{224,1... | collective-permute-start | bytes 983048 | tf_op jit(solution)/shard_map/ppermute | solution.py:534
  93.7 2.1 %collective-permute-start.19 = (f32[160,1024]{1,0:T(8,128)S(1)}, f32[160,1024]{1,0:T(8,128)S(1)}, u32[]{:S(2)}, u32[]{:S(2)}) collective-permute-start(f32[160,1024]{1,0:T(8,128)S(1)} %pad_maximum_fusion.refs_0_), channel_id=1, source_target_pairs={{0,2},{1,3},{2,0},{3,1},{4,6},{5,7},{6,4},{7,5},{8,10},{9,11},{10,... | collective-permute-start | bytes 1966088 | tf_op jit(solution)/shard_map/ppermute | solution.py:534
  95.8 4.9 %come.1 = (bf16[640,896]{1,0:T(8,128)(2,1)S(1)}, bf16[640,896]{1,0:T(8,128)(2,1)S(1)}, bf16[640,384]{1,0:T(8,128)(2,1)S(1)}, bf16[640,384]{1,0:T(8,128)(2,1)S(1)...) custom-call(f32[192,1280]{1,0:T(8,128)} %collective-permute-done.1.refs_0_, ...), custom_call_target="tpu_custom_call" | custom-call | tf_op jit(solution)/shard_map/come/pallas_call | solution.py:180
  101.5 3.2 %collective-permute-start.18 = (f32[320,256]{1,0:T(8,128)S(1)}, f32[320,256]{1,0:T(8,128)S(1)}, u32[]{:S(2)}, u32[]{:S(2)}) collective-permute-start(f32[320,256]{1,0:T(8,128)S(1)} %collective-permute-done.14.refs_4_), channel_id=1, source_target_pairs={{0,224},{32,0},{64,32},{96,64},{128,96},{160,128},{192,160},{224,1... | collective-permute-start | bytes 983048 | tf_op jit(solution)/shard_map/ppermute | solution.py:534
  104.7 5.0 %group.2.refs_6_ = f32[1280,512]{1,0:T(8,128)S(1)} custom-call(s32[4]{0:T(128)S(1)} %copy-done.4, f32[320,256]{1,0:T(8,128)S(1)} %pad_maximum_fusion.1.refs_0_, f32[320,256]{1,0:T(8,128)S(1)} %collective-permute-done.10.refs_1_, f32[320,256]{1,0:T(8,128)S(1)} %collective-permute-done.11.refs_2_, f32[320,256]{1,0:T(8,128)S(1)} %collective-permute-done.13.refs_3_, ...), custom_call_target="tpu_custom_call" | custom-call | tf_op jit(solution)/shard_map/group/pallas_call | solution.py:253
  109.7 1.9 %collective-permute-done.19.refs_2_ = f32[160,1024]{1,0:T(8,128)S(1)} collective-permute-done((f32[160,1024]{1,0:T(8,128)S(1)}, f32[160,1024]{1,0:T(8,128)S(1)}, u32[]{:S(2)}, u32[]{:S(2)}) %collective-permute-start.19) | collective-permute-done | bytes 655392 | tf_op jit(solution)/shard_map/ppermute | solution.py:534
  112.2 2.0 %collective-permute-start.21 = (f32[160,256]{1,0:T(8,128)S(1)}, f32[160,256]{1,0:T(8,128)S(1)}, u32[]{:S(2)}, u32[]{:S(2)}) collective-permute-start(f32[160,256]{1,0:T(8,128)S(1)} %slice.14), channel_id=1, source_target_pairs={{0,32},{32,64},{64,96},{96,128},{128,160},{160,192},{192,224},{224... | collective-permute-start | bytes 491528 | tf_op jit(solution)/shard_map/ppermute | solution.py:534
  114.2 1.6 collective-permute-start.22
  115.9 2.8 %group.3.refs_4_ = f32[1280,512]{1,0:T(8,128)S(1)} custom-call(s32[4]{0:T(128)S(1)} %copy-done.4, f32[320,256]{1,0:T(8,128)S(1)} %collective-permute-done.17.refs_0_, f32[320,256]{1,0:T(8,128)S(1)} %collective-permute-done.18.refs_1_, bf16[640,384]{1,0:T(8,128)(2,1)S(1)} %get-tuple-element.121.refs_2_, bf16[640,384]{1,0:T(8,128)(2,1)S(1)} %get-tuple-element.122.refs_3_, ...), custom_call_target="tpu_custom_call" | custom-call | tf_op jit(solution)/shard_map/group/pallas_call | solution.py:253
  118.7 3.3 %left.1 = (bf16[1024,1280]{1,0:T(8,128)(2,1)S(1)}, bf16[1024,1280]{1,0:T(8,128)(2,1)S(1)}) custom-call(s32[4]{0:T(128)S(1)} %copy-done.4, f32[160,1024]{1,0:T(8,128)S(1)} %pad_maximum_fusion.refs_0_, f32[160,1024]{1,0:T(8,128)S(1)} %collective-permute-done.15.refs_1_, f32[160,1024]{1,0:T(8,128)S(1)} %collective-permute-done.19.refs_2_, ...), custom_call_target="tpu_custom_call" | custom-call | tf_op jit(solution)/shard_map/left/pallas_call | solution.py:212
  122.0 10.5 %pair.1 = (f32[2,8,4096]{2,1,0:T(8,128)S(1)}, f32[2,8,4096]{2,1,0:T(8,128)S(1)}) custom-call(s32[4]{0:T(128)S(1)} %copy-done.4, s32[4,256]{1,0:T(4,128)S(1)} %pad_add_fusion.table, f32[160,256]{1,0:T(8,128)S(1)} %collective-permute-done.21.one_ref, f32[160,256]{1,0:T(8,128)S(1)} %collective-permute-done.22.two_ref, ...), custom_call_target="tpu_custom_call" | custom-call | tf_op jit(solution)/shard_map/pair/pallas_call | solution.py:308
  135.4 1.8 rows.1
  137.2 17.1 %all_to_all.15.parts_ref = f32[4,8,2048]{2,1,0:T(8,128)} all-to-all(f32[4,8,2048]{2,1,0:T(8,128)} %rows.1), channel_id=1, replica_groups=mesh['z'=8,'y'=4,'core'=2,'x'=4] {'x'}, dimensions={0} | all-to-all | bytes 524288 | tf_op jit(solution)/shard_map/all_to_all | solution.py:587
  154.2 2.4 %owner.1 = f32[32,8,256]{2,1,0:T(8,128)} custom-call(s32[64]{0:T(128)} %select_reduce_fusion.4.offset, f32[4,8,2048]{2,1,0:T(8,128)} %all_to_all.15.parts_ref), custom_call_target="tpu_custom_call" | custom-call | tf_op jit(solution)/shard_map/owner/pallas_call | solution.py:361
  156.6 18.0 %all_to_all.16.in_ref = f32[32,8,256]{2,1,0:T(8,128)} all-to-all(f32[32,8,256]{2,1,0:T(8,128)} %owner.1), channel_id=1, replica_groups=mesh['z'=8,'y'=4,'core'=2,'x'=4] {'z','y'}, dimensions={0} | all-to-all | bytes 524288 | tf_op jit(solution)/shard_map/all_to_all | solution.py:589
  174.6 1.6 total.1.own_ref
  178.1 2.1 %last.1 = f32[12,8,16]{2,1,0:T(8,128)} custom-call(s32[4]{0:T(128)} %copy-done.3, s32[1]{0:T(128)} %dynamic_slice.3.held_ref, f32[8,256]{1,0:T(8,128)} %total.1.own_ref, f32[8,256]{1,0:T(8,128)} %copy-done.10), custom_call_target="tpu_custom_call" | custom-call | tf_op jit(solution)/shard_map/last/pallas_call | solution.py:406
  (88 shorter events, 18.5 us)
Async XLA Ops:
  0.0 13.5 %copy-start.11 = (s32[256]{0:T(256)S(1)}, s32[256]{0:T(256)}, u32[]{:S(2)}) copy-start(s32[256]{0:T(256)} %param.7) | copy-start | bytes 3076
  0.0 14.3 %copy-start.12 = (s32[256,2]{0,1:T(2,128)S(1)}, s32[256,2]{0,1:T(2,128)}, u32[]{:S(2)}) copy-start(s32[256,2]{0,1:T(2,128)} %param.6) | copy-start | bytes 6148
  0.0 9.2 %collective-permute-start = (f32[2,16,2560]{2,1,0:T(8,128)}, f32[2,16,2560]{2,1,0:T(8,128)}, u32[]{:S(2)}, u32[]{:S(2)}) collective-permute-start(f32[2,16,2560]{2,1,0:T(8,128)} %own_ref.1), channel_id=1, source_target_pairs={{0,4},{4,0},{1,5},{5,1},{2,6},{6,2},{3,7},{7,3},{8,12},{12,8},{9,1... | collective-permute-start | bytes 983048 | tf_op jit(solution)/shard_map/ppermute | solution.py:536
  11.4 68.9 %copy-start.4 = (s32[4]{0:T(128)S(1)}, s32[4]{0:T(128)}, u32[]{:S(2)}) copy-start(s32[4]{0:T(128)} %copy-done.3) | copy-start | bytes 52
  11.4 30.5 %collective-permute-start.2 = (f32[320,2560]{1,0:T(8,128)S(1)}, f32[320,2560]{1,0:T(8,128)}, u32[]{:S(2)}, u32[]{:S(2)}) collective-permute-start(f32[320,2560]{1,0:T(8,128)S(1)} %bitcast.13), channel_id=1, source_target_pairs={{0,4},{4,0},{1,5},{5,1},{2,6},{6,2},{3,7},{7,3},{8,12},{12,8},{9,1... | collective-permute-start | bytes 9830408 | tf_op jit(solution)/shard_map/ppermute | solution.py:536
  11.9 30.0 %collective-permute-start.1 = (f32[192,1280]{1,0:T(8,128)}, f32[192,1280]{1,0:T(8,128)}, u32[]{:S(2)}, u32[]{:S(2)}) collective-permute-start(f32[192,1280]{1,0:T(8,128)} %copy-done.5), channel_id=1, source_target_pairs={{0,8},{8,0},{16,24},{24,16},{1,9},{9,1},{17,25},{25,17},{2,10},{10... | collective-permute-start | bytes 2949128 | tf_op jit(solution)/shard_map/ppermute | solution.py:535
  14.9 27.1 %all-to-all-start = ((f32[32,1,2560]{2,1,0:T(1,128)}), f32[32,1,2560]{2,1,0:T(1,128)}, u32[]{:S(2)}, u32[]{:S(2)}) async-start(f32[32,1,2560]{2,1,0:T(1,128)} %bitcast.15), calls=%async_computation | async-start | bytes 655360 | tf_op jit(solution)/shard_map/all_to_all | solution.py:545
  42.0 10.5 %collective-permute-start.5 = (f32[192,1280]{1,0:T(8,128)}, f32[192,1280]{1,0:T(8,128)}, u32[]{:S(2)}, u32[]{:S(2)}) collective-permute-start(f32[192,1280]{1,0:T(8,128)} %collective-permute-done.1.refs_0_), channel_id=1, source_target_pairs={{0,4},{4,0},{1,5},{5,1},{2,6},{6,2},{3,7},{7,3},{8,12},{12,8},{9,1... | collective-permute-start | bytes 2949128 | tf_op jit(solution)/shard_map/ppermute | solution.py:536
  42.0 10.4 %collective-permute-start.4 = (f32[64,1280]{1,0:T(8,128)}, f32[64,1280]{1,0:T(8,128)}, u32[]{:S(2)}, u32[]{:S(2)}) collective-permute-start(f32[64,1280]{1,0:T(8,128)} %copy-done.7), channel_id=1, source_target_pairs={{0,8},{8,0},{16,24},{24,16},{1,9},{9,1},{17,25},{25,17},{2,10},{10... | collective-permute-start | bytes 983048 | tf_op jit(solution)/shard_map/ppermute | solution.py:535
  46.1 1.5 collective-permute-start.3
  52.4 15.2 %collective-permute-start.7 = (f32[80,1024]{1,0:T(8,128)}, f32[80,1024]{1,0:T(8,128)}, u32[]{:S(2)}, u32[]{:S(2)}) collective-permute-start(f32[80,1024]{1,0:T(8,128)} %get-tuple-element.88), channel_id=1, source_target_pairs={{0,8},{8,0},{16,24},{24,16},{1,9},{9,1},{17,25},{25,17},{2,10},{10... | collective-permute-start | bytes 983048 | tf_op jit(solution)/shard_map/ppermute | solution.py:535
  54.3 12.4 %collective-permute-start.6 = (f32[160,256]{1,0:T(8,128)}, f32[160,256]{1,0:T(8,128)S(1)}, u32[]{:S(2)}, u32[]{:S(2)}) collective-permute-start(f32[160,256]{1,0:T(8,128)} %shard.1), channel_id=1, source_target_pairs={{0,16},{8,24},{16,0},{24,8},{1,17},{9,25},{17,1},{25,9},{2,18},{10... | collective-permute-start | bytes 491528 | tf_op jit(solution)/shard_map/ppermute | solution.py:534
  56.0 16.5 %collective-permute-start.8 = (f32[64,1280]{1,0:T(8,128)}, f32[64,1280]{1,0:T(8,128)S(1)}, u32[]{:S(2)}, u32[]{:S(2)}) collective-permute-start(f32[64,1280]{1,0:T(8,128)} %copy-done.6), channel_id=1, source_target_pairs={{0,8},{8,0},{16,24},{24,16},{1,9},{9,1},{17,25},{25,17},{2,10},{10... | collective-permute-start | bytes 983048 | tf_op jit(solution)/shard_map/ppermute | solution.py:535
  56.2 16.2 %collective-permute-start.9 = (f32[64,1280]{1,0:T(8,128)}, f32[64,1280]{1,0:T(8,128)S(1)}, u32[]{:S(2)}, u32[]{:S(2)}) collective-permute-start(f32[64,1280]{1,0:T(8,128)} %collective-permute-done.4.refs_1_), channel_id=1, source_target_pairs={{0,4},{4,0},{1,5},{5,1},{2,6},{6,2},{3,7},{7,3},{8,12},{12,8},{9,1... | collective-permute-start | bytes 983048 | tf_op jit(solution)/shard_map/ppermute | solution.py:536
  72.4 23.4 %collective-permute-start.15 = (f32[160,1024]{1,0:T(8,128)S(1)}, f32[160,1024]{1,0:T(8,128)S(1)}, u32[]{:S(2)}, u32[]{:S(2)}) collective-permute-start(f32[160,1024]{1,0:T(8,128)S(1)} %pad_maximum_fusion.refs_0_), channel_id=1, source_target_pairs={{0,1},{1,2},{2,3},{3,0},{4,5},{5,6},{6,7},{7,4},{8,9},{9,10},{10,1... | collective-permute-start | bytes 1966088 | tf_op jit(solution)/shard_map/ppermute | solution.py:534
  73.9 16.4 %collective-permute-start.10 = (f32[320,256]{1,0:T(8,128)S(1)}, f32[320,256]{1,0:T(8,128)S(1)}, u32[]{:S(2)}, u32[]{:S(2)}) collective-permute-start(f32[320,256]{1,0:T(8,128)S(1)} %pad_maximum_fusion.1.refs_0_), channel_id=1, source_target_pairs={{0,32},{32,64},{64,96},{96,128},{128,160},{160,192},{192,224},{224... | collective-permute-start | bytes 983048 | tf_op jit(solution)/shard_map/ppermute | solution.py:534
  75.8 14.5 %collective-permute-start.11 = (f32[320,256]{1,0:T(8,128)S(1)}, f32[320,256]{1,0:T(8,128)S(1)}, u32[]{:S(2)}, u32[]{:S(2)}) collective-permute-start(f32[320,256]{1,0:T(8,128)S(1)} %pad_maximum_fusion.1.refs_0_), channel_id=1, source_target_pairs={{0,224},{32,0},{64,32},{96,64},{128,96},{160,128},{192,160},{224,1... | collective-permute-start | bytes 983048 | tf_op jit(solution)/shard_map/ppermute | solution.py:534
  79.8 10.6 %collective-permute-start.12 = (f32[64,1280]{1,0:T(8,128)S(1)}, f32[64,1280]{1,0:T(8,128)S(1)}, u32[]{:S(2)}, u32[]{:S(2)}) collective-permute-start(f32[64,1280]{1,0:T(8,128)S(1)} %collective-permute-done.8.refs_2_), channel_id=1, source_target_pairs={{0,4},{4,0},{1,5},{5,1},{2,6},{6,2},{3,7},{7,3},{8,12},{12,8},{9,1... | collective-permute-start | bytes 983048 | tf_op jit(solution)/shard_map/ppermute | solution.py:536
  79.8 21.0 %collective-permute-start.16 = (f32[160,1024]{1,0:T(8,128)S(1)}, f32[160,1024]{1,0:T(8,128)S(1)}, u32[]{:S(2)}, u32[]{:S(2)}) collective-permute-start(f32[160,1024]{1,0:T(8,128)S(1)} %pad_maximum_fusion.refs_0_), channel_id=1, source_target_pairs={{0,3},{1,0},{2,1},{3,2},{4,7},{5,4},{6,5},{7,6},{8,11},{9,8},{10,9... | collective-permute-start | bytes 1966088 | tf_op jit(solution)/shard_map/ppermute | solution.py:534
  90.3 11.1 %collective-permute-start.13 = (f32[320,256]{1,0:T(8,128)S(1)}, f32[320,256]{1,0:T(8,128)S(1)}, u32[]{:S(2)}, u32[]{:S(2)}) collective-permute-start(f32[320,256]{1,0:T(8,128)S(1)} %collective-permute-done.10.refs_1_), channel_id=1, source_target_pairs={{0,32},{32,64},{64,96},{96,128},{128,160},{160,192},{192,224},{224... | collective-permute-start | bytes 983048 | tf_op jit(solution)/shard_map/ppermute | solution.py:534
  90.4 11.0 %collective-permute-start.14 = (f32[320,256]{1,0:T(8,128)S(1)}, f32[320,256]{1,0:T(8,128)S(1)}, u32[]{:S(2)}, u32[]{:S(2)}) collective-permute-start(f32[320,256]{1,0:T(8,128)S(1)} %collective-permute-done.11.refs_2_), channel_id=1, source_target_pairs={{0,224},{32,0},{64,32},{96,64},{128,96},{160,128},{192,160},{224,1... | collective-permute-start | bytes 983048 | tf_op jit(solution)/shard_map/ppermute | solution.py:534
  93.7 18.0 %collective-permute-start.19 = (f32[160,1024]{1,0:T(8,128)S(1)}, f32[160,1024]{1,0:T(8,128)S(1)}, u32[]{:S(2)}, u32[]{:S(2)}) collective-permute-start(f32[160,1024]{1,0:T(8,128)S(1)} %pad_maximum_fusion.refs_0_), channel_id=1, source_target_pairs={{0,2},{1,3},{2,0},{3,1},{4,6},{5,7},{6,4},{7,5},{8,10},{9,11},{10,... | collective-permute-start | bytes 1966088 | tf_op jit(solution)/shard_map/ppermute | solution.py:534
  95.8 15.8 %collective-permute-start.20 = (f32[160,1024]{1,0:T(8,128)S(1)}, f32[160,1024]{1,0:T(8,128)S(1)}, u32[]{:S(2)}, u32[]{:S(2)}) collective-permute-start(f32[160,1024]{1,0:T(8,128)S(1)} %pad_maximum_fusion.refs_0_), channel_id=1, source_target_pairs={{0,4},{4,0},{1,5},{5,1},{2,6},{6,2},{3,7},{7,3},{8,12},{12,8},{9,1... | collective-permute-start | bytes 1966088 | tf_op jit(solution)/shard_map/ppermute | solution.py:536
  101.5 10.7 %collective-permute-start.17 = (f32[320,256]{1,0:T(8,128)S(1)}, f32[320,256]{1,0:T(8,128)S(1)}, u32[]{:S(2)}, u32[]{:S(2)}) collective-permute-start(f32[320,256]{1,0:T(8,128)S(1)} %collective-permute-done.13.refs_3_), channel_id=1, source_target_pairs={{0,32},{32,64},{64,96},{96,128},{128,160},{160,192},{192,224},{224... | collective-permute-start | bytes 983048 | tf_op jit(solution)/shard_map/ppermute | solution.py:534
  101.5 10.7 %collective-permute-start.18 = (f32[320,256]{1,0:T(8,128)S(1)}, f32[320,256]{1,0:T(8,128)S(1)}, u32[]{:S(2)}, u32[]{:S(2)}) collective-permute-start(f32[320,256]{1,0:T(8,128)S(1)} %collective-permute-done.14.refs_4_), channel_id=1, source_target_pairs={{0,224},{32,0},{64,32},{96,64},{128,96},{160,128},{192,160},{224,1... | collective-permute-start | bytes 983048 | tf_op jit(solution)/shard_map/ppermute | solution.py:534
  104.7 14.0 %collective-permute-start.23 = (f32[160,1024]{1,0:T(8,128)S(1)}, f32[160,1024]{1,0:T(8,128)S(1)}, u32[]{:S(2)}, u32[]{:S(2)}) collective-permute-start(f32[160,1024]{1,0:T(8,128)S(1)} %collective-permute-done.15.refs_1_), channel_id=1, source_target_pairs={{0,4},{4,0},{1,5},{5,1},{2,6},{6,2},{3,7},{7,3},{8,12},{12,8},{9,1... | collective-permute-start | bytes 1966088 | tf_op jit(solution)/shard_map/ppermute | solution.py:536
  111.6 7.1 %collective-permute-start.25 = (f32[160,1024]{1,0:T(8,128)S(1)}, f32[160,1024]{1,0:T(8,128)S(1)}, u32[]{:S(2)}, u32[]{:S(2)}) collective-permute-start(f32[160,1024]{1,0:T(8,128)S(1)} %collective-permute-done.16.refs_3_), channel_id=1, source_target_pairs={{0,4},{4,0},{1,5},{5,1},{2,6},{6,2},{3,7},{7,3},{8,12},{12,8},{9,1... | collective-permute-start | bytes 1966088 | tf_op jit(solution)/shard_map/ppermute | solution.py:536
  112.2 6.5 %collective-permute-start.24 = (f32[160,1024]{1,0:T(8,128)S(1)}, f32[160,1024]{1,0:T(8,128)S(1)}, u32[]{:S(2)}, u32[]{:S(2)}) collective-permute-start(f32[160,1024]{1,0:T(8,128)S(1)} %collective-permute-done.19.refs_2_), channel_id=1, source_target_pairs={{0,4},{4,0},{1,5},{5,1},{2,6},{6,2},{3,7},{7,3},{8,12},{12,8},{9,1... | collective-permute-start | bytes 1966088 | tf_op jit(solution)/shard_map/ppermute | solution.py:536
  112.2 9.7 %collective-permute-start.21 = (f32[160,256]{1,0:T(8,128)S(1)}, f32[160,256]{1,0:T(8,128)S(1)}, u32[]{:S(2)}, u32[]{:S(2)}) collective-permute-start(f32[160,256]{1,0:T(8,128)S(1)} %slice.14), channel_id=1, source_target_pairs={{0,32},{32,64},{64,96},{96,128},{128,160},{160,192},{192,224},{224... | collective-permute-start | bytes 491528 | tf_op jit(solution)/shard_map/ppermute | solution.py:534
  114.2 7.7 %collective-permute-start.22 = (f32[160,256]{1,0:T(8,128)S(1)}, f32[160,256]{1,0:T(8,128)S(1)}, u32[]{:S(2)}, u32[]{:S(2)}) collective-permute-start(f32[160,256]{1,0:T(8,128)S(1)} %slice.15), channel_id=1, source_target_pairs={{0,224},{32,0},{64,32},{96,64},{128,96},{160,128},{192,160},{224,1... | collective-permute-start | bytes 491528 | tf_op jit(solution)/shard_map/ppermute | solution.py:534
  133.2 1.5 collective-permute-start.26
  176.2 1.4 collective-permute-start.27
  (10 other events, 29.9 us)

commit v6 on v4

--- a/solution.py
+++ b/solution.py
@@ -17,8 +17,10 @@
 SWAP = ((0, 1), (1, 0))
 SMEM = pl.BlockSpec(memory_space=pltpu.SMEM)
 VMEM = pl.BlockSpec(memory_space=pltpu.VMEM)
+SPAN = 80
 PLANE = 320
-PAIR = 2 * PLANE
+NEAR = (0, 7, 1, 6, 2)
+FAR = (5, 3, 4)
 
 
 def ring(n, shift):
@@ -66,44 +68,58 @@
     return used_list, left_at, right_at, offset, count
 
 
-def screen_kernel(place, own_ref, other_ref, high_ref, low_ref):
+def padded(planes):
+    return (len(planes) * PLANE + 127) // 128 * 128
+
+
+def screen_kernel(place, own_ref, other_ref, *outs):
     z = place[0]
     rows = 16
     lane = lax.broadcasted_iota(jnp.int32, (rows, 128), 1)
+
+    def plane_of(ref, row, delta, offset):
+        plane = lax.rem(z + delta, 8)
+        odd = lax.rem(plane, 2)
+        column = pl.multiple_of(plane * PLANE - odd * 64, 128)
+        window = ref[row, pl.ds(column, 384)]
+        turned = pltpu.roll(window, 64 if offset else 320, 1)
+        return jnp.where((odd == 1) if offset else (odd == 0), window, turned)
+
     for source, ref in enumerate((own_ref, other_ref)):
 
-        def body(step, carry):
+        def body(step, carry, source=source, ref=ref):
             part = step // 10
-            start = pl.multiple_of(step * rows, rows)
+            row = pl.ds(pl.multiple_of(step * rows, rows), rows)
             target = pl.multiple_of(part * PLANE + source * (PLANE // 2) + (step - part * 10) * rows, rows)
-            for pair, (one, two) in enumerate(((7, 1), (6, 2), (5, 3), (0, 4))):
-                parts = []
-                for place_in, delta in ((0, one), (64, two)):
-                    plane = lax.rem(z + delta, 8)
-                    odd = lax.rem(plane, 2)
-                    column = pl.multiple_of(plane * PLANE - odd * 64, 128)
-                    window = ref[pl.ds(start, rows), pl.ds(column, 384)]
-                    turned = pltpu.roll(window, 320 if place_in == 0 else 64, 1)
-                    plain = (odd == 0) if place_in == 0 else (odd == 1)
-                    parts.append(jnp.where(plain, window, turned))
-                a, b = parts
-                middle = jnp.where(lane < 64, a[:, 256:], b[:, :128])
-                whole = jnp.concatenate([a[:, :256], middle, b[:, 128:]], axis=1)
-                top, rest = split(whole)
-                high_ref[pl.ds(target, rows), pair * PAIR : (pair + 1) * PAIR] = top
-                low_ref[pl.ds(target, rows), pair * PAIR : (pair + 1) * PAIR] = rest
+            for group, planes in enumerate((NEAR, FAR)):
+                for at in range(0, len(planes), 2):
+                    a = plane_of(ref, row, planes[at], False)
+                    if at + 1 < len(planes):
+                        b = plane_of(ref, row, planes[at + 1], True)
+                        middle = jnp.where(lane < 64, a[:, 256:], b[:, :128])
+                        whole = jnp.concatenate([a[:, :256], middle, b[:, 128:]], axis=1)
+                    else:
+                        whole = jnp.concatenate([a[:, :256], jnp.where(lane < 64, a[:, 256:], 0.0)], axis=1)
+                    top, rest = split(whole)
+                    columns = slice(at * PLANE, at * PLANE + whole.shape[1])
+                    outs[2 * group][pl.ds(target, rows), columns] = top
+                    outs[2 * group + 1][pl.ds(target, rows), columns] = rest
             return carry
 
         lax.fori_loop(0, 20, body, 0)
 
 
 def screen_call(place, own, other):
-    shape = jax.ShapeDtypeStruct((2 * own.shape[0], own.shape[1]), jnp.bfloat16)
+    shapes = [
+        jax.ShapeDtypeStruct((2 * own.shape[0], padded(planes)), jnp.bfloat16)
+        for planes in (NEAR, FAR)
+        for _ in range(2)
+    ]
     return pl.pallas_call(
         screen_kernel,
-        out_shape=(shape, shape),
+        out_shape=shapes,
         in_specs=[SMEM, VMEM, VMEM],
-        out_specs=(VMEM, VMEM),
+        out_specs=[VMEM] * 4,
         compiler_params=params(20),
         name="screen",
     )(place, own, other)
@@ -140,49 +156,50 @@
     )(place, *pieces)
 
 
-def load_right(place, planes, high, low):
+def load_right(place, units, planes, high, low):
     y = place[2]
-    span = PLANE // 4
-    for plane, refs in enumerate(planes):
-        each = 4 // len(refs)
-        for at, delta in enumerate((0, 3, 1, 2)):
-            row = pl.multiple_of(plane * PLANE + lax.rem(y + delta, 4) * span, 16)
-            for part in range(2):
-                start = (at % each * 2 + part) * span
-                top, rest = split(refs[at // each][start : start + span, :])
-                high[pl.ds(row, span), part * HALF : (part + 1) * HALF] = top
-                low[pl.ds(row, span), part * HALF : (part + 1) * HALF] = rest
-
-
-def group_kernel(first, place, one_ref, two_ref, high_ref, low_ref, *refs):
-    sum_ref, (out_ref, rh, rl) = (None if first else refs[0]), refs[-3:]
-    load_right(place, ((one_ref,), (two_ref,)), rh, rl)
-    value = dot3(high_ref[...], low_ref[...], rh[...], rl[...])
-    out_ref[...] = value if first else value + sum_ref[...]
-
-
-def screen_spec(index):
-    return pl.BlockSpec((PAIR, PAIR), lambda i: (0, index))
-
-
-def group_call(index, place, one, two, screen_high, screen_low, total):
-    whole = lambda shape: pl.BlockSpec(shape, lambda i: (0, 0))
-    first = total is None
-    return pl.pallas_call(
-        functools.partial(group_kernel, first),
-        grid=(1,),
-        out_shape=jax.ShapeDtypeStruct((PAIR, 2 * HALF), jnp.float32),
-        in_specs=[SMEM, whole(one.shape), whole(two.shape), screen_spec(index), screen_spec(index)]
-        + ([] if first else [whole((PAIR, 2 * HALF))]),
-        out_specs=whole((PAIR, 2 * HALF)),
-        scratch_shapes=[pltpu.VMEM((PAIR, 2 * HALF), jnp.bfloat16)] * 2,
-        compiler_params=params(24),
+    for delta, plane, part, ref, start in units:
+        row = pl.multiple_of(plane * PLANE + lax.rem(y + delta, 4) * SPAN, 16)
+        top, rest = split(ref[start : start + SPAN, :])
+        high[pl.ds(row, SPAN), part * HALF : (part + 1) * HALF] = top
+        low[pl.ds(row, SPAN), part * HALF : (part + 1) * HALF] = rest
+    used = planes * PLANE
+    for ref in (high, low):
+        ref[used:, :] = jnp.zeros((ref.shape[0] - used, ref.shape[1]), ref.dtype)
+
+
+def units_of(planes, own, below, above, two_below, two_above):
+    units = []
+    for unit in range(2 * planes):
+        half, at = (two_below, unit) if unit < planes else (two_above, unit - planes)
+        for delta, (ref, start), index in ((0, own, unit), (3, below, unit), (1, above, unit), (2, half, at)):
+            units.append((delta, unit // 2, unit % 2, ref, start + index * SPAN))
+    return units
+
+
+def group_kernel(place, own, below, above, two_below, two_above, high_ref, low_ref, out_ref, rh, rl):
+    sources = [(ref, 0) for ref in (own, below, above, two_below, two_above)]
+    load_right(place, units_of(len(NEAR), *sources), len(NEAR), rh, rl)
+    out_ref[...] = dot3(high_ref[...], low_ref[...], rh[...], rl[...])
+
+
+def group_call(place, rights, high, low):
+    rows, width = high.shape
+    return pl.pallas_call(
+        group_kernel,
+        out_shape=jax.ShapeDtypeStruct((rows, 2 * HALF), jnp.float32),
+        in_specs=[SMEM] + [VMEM] * 7,
+        out_specs=VMEM,
+        scratch_shapes=[pltpu.VMEM((width, 2 * HALF), jnp.bfloat16)] * 2,
+        compiler_params=params(32),
         name="group",
-    )(place, one, two, screen_high, screen_low, *([] if first else [total]))
-
-
-def pair_kernel(place, table, one_ref, two_ref, three_ref, high_ref, low_ref, sum_ref, left_high, left_low, keep_ref, give_ref, rh, rl, kern):
-    load_right(place, ((one_ref,), (two_ref, three_ref)), rh, rl)
+    )(place, *rights, high, low)
+
+
+def pair_kernel(place, table, own, below, above, two_below, two_above, high_ref, low_ref, sum_ref, left_high, left_low, keep_ref, give_ref, rh, rl, kern):
+    skip = len(NEAR) * SPAN
+    sources = [(own, 0), (below, skip), (above, skip), (two_below, 0), (two_above, 0)]
+    load_right(place, units_of(len(FAR), *sources), len(FAR), rh, rl)
     product = sum_ref[...] + dot3(high_ref[...], low_ref[...], rh[...], rl[...])
     mid = product.shape[0] // 2
     real = product[:mid, :HALF] - product[mid:, HALF:]
@@ -216,22 +233,18 @@
     lax.fori_loop(0, table.shape[1] // 8, group, 0)
 
 
-def pair_call(place, table, one, two, three, screen_high, screen_low, total, left_high, left_low):
-    whole = lambda array: pl.BlockSpec(array.shape, lambda i: (0, 0))
+def pair_call(place, table, rights, high, low, total, left_high, left_low):
     shape = jax.ShapeDtypeStruct((2, 8, table.shape[1] * BLK), jnp.float32)
-    out = pl.BlockSpec(shape.shape, lambda i: (0, 0, 0))
     return pl.pallas_call(
         pair_kernel,
-        grid=(1,),
         out_shape=(shape, shape),
-        in_specs=[SMEM, SMEM, whole(one), whole(two), whole(three), screen_spec(3), screen_spec(3)]
-        + [whole(total), whole(left_high), whole(left_low)],
-        out_specs=(out, out),
-        scratch_shapes=[pltpu.VMEM((PAIR, 2 * HALF), jnp.bfloat16)] * 2
+        in_specs=[SMEM, SMEM] + [VMEM] * 10,
+        out_specs=(VMEM, VMEM),
+        scratch_shapes=[pltpu.VMEM((high.shape[1], 2 * HALF), jnp.bfloat16)] * 2
         + [pltpu.VMEM((left_high.shape[0], 2 * HALF), jnp.float32)],
-        compiler_params=params(36),
+        compiler_params=params(40),
         name="pair",
-    )(place, table, one, two, three, screen_high, screen_low, total, left_high, left_low)
+    )(place, table, *rights, high, low, total, left_high, left_low)
 
 
 def rows_kernel(keep_ref, come_ref, out_ref):
@@ -454,35 +467,42 @@
 
     screen = screened.reshape(2 * 4 * span, -1)
     other = lax.ppermute(after(screen, pieces), "core", SWAP)
-    screen_high, screen_low = screen_call(place, screen, other)
 
     columns, keep, give = unpack_call(place, used_list, mine)
     shard = shard_call(place, keep, lax.ppermute(give, "core", SWAP))
 
     shift = lambda array, axis, by: lax.ppermute(array, axis, ring(lax.axis_size(axis), by))
-    from_below, from_above = shift(shard, "y", 1), shift(shard, "y", -1)
-    across = shift(from_below, "y", 1)
-    plane = jnp.concatenate([shard, from_below, from_above, across], axis=0)
-    below, above = shift(plane, "z", 1), shift(plane, "z", -1)
-
-    below, above, screen_high, screen_low = lax.optimization_barrier((below, above, screen_high, screen_low))
+    join = lambda *arrays: jnp.concatenate(arrays, axis=0)
+    hold = lax.optimization_barrier
+    below, above = shift(shard, "z", 1), shift(shard, "z", -1)
+    around = [columns] + [shift(after(columns, shard), "x", by) for by in (1, 2, 3)]
+    below, above = hold((below, above))
     below2, above2 = shift(below, "z", 1), shift(above, "z", -1)
-    columns = after(columns, screen_high)
-    around = [columns] + [shift(columns, "x", by) for by in (1, 2, 3)]
-    total = group_call(0, place, below, above, screen_high, screen_low, None)
-    below2, above2, total = lax.optimization_barrier((below2, above2, total))
+    below2, above2, around[1], around[3] = hold((below2, above2, around[1], around[3]))
+    near = join(shard, below, above, below2, above2)
+    near_down, near_up = shift(near, "y", 1), shift(near, "y", -1)
     below3, above3 = shift(below2, "z", 1), shift(above2, "z", -1)
-    total = group_call(1, place, below2, above2, screen_high, screen_low, total)
-    below3, above3, total = lax.optimization_barrier((below3, above3, total))
-    around = lax.optimization_barrier((*around, total))[:4]
-    swapped = lax.ppermute(jnp.concatenate(around, axis=0), "core", SWAP)
+    below3, above3 = hold((below3, above3))
+    far_low, far_high = shift(below3[:SPAN], "z", 1), shift(above3[SPAN:], "z", -1)
+    far = join(below3, above3, far_low, far_high)
+    near_high, near_low, far_top, far_rest = screen_call(place, screen, other)
+    near_down, near_up, far, around[2], near_high, near_low, far_top, far_rest = hold(
+        (near_down, near_up, far, around[2], near_high, near_low, far_top, far_rest)
+    )
+
+    half = len(NEAR) * SPAN
+    down, up = shift(join(near_down[:half], far), "y", 1), shift(join(near_up[half:], far), "y", -1)
+    swapped = lax.ppermute(join(*around), "core", SWAP)
     swapped = [swapped[at * 2 * span : (at + 1) * 2 * span] for at in range(4)]
     left_high, left_low = left_call(place, list(around) + swapped)
-    middle = below3.shape[0] // 2
-    far, near = shift(below3[:middle], "z", 1), shift(above3[middle:], "z", -1)
-    total = group_call(2, place, below3, above3, screen_high, screen_low, total)
-    far, near, total, left_high, left_low = lax.optimization_barrier((far, near, total, left_high, left_low))
-    keep, give = pair_call(place, table, plane, far, near, screen_high, screen_low, total, left_high, left_low)
+    down, up, left_high, left_low = hold((down, up, left_high, left_low))
+
+    cut = half + len(FAR) * SPAN
+    last_down, last_up = shift(down[half:cut], "y", 1), shift(up[cut:], "y", -1)
+    total = group_call(place, (near, near_down, near_up, down, up), near_high, near_low)
+    last_down, last_up, total = hold((last_down, last_up, total))
+    rights = (far, down, up, last_down, last_up)
+    keep, give = pair_call(place, table, rights, far_top, far_rest, total, left_high, left_low)
 
     parts = rows_call(keep, lax.ppermute(give, "core", SWAP))
     parts = lax.all_to_all(parts, "x", 0, 0, tiled=True)

time: 176 us -> 178 us (1.011)
  starting transfers between devices: 30.5 us -> 36.8 us
  waiting for transfers between devices: 60.2 us -> 54.8 us
  local copies, waits for them, and re-layouts: 4.16 us -> 6.73 us
    ppermute x14 -> x17, starting transfers between devices: 18.7 us -> 25 us  [shards(): lax.ppermute(array, axis, ring(lax.axis_size(axis), by))]
    ppermute x14 -> x17, waiting for transfers between devices: 41.1 us -> 36.7 us  [shards(): lax.ppermute(array, axis, ring(lax.axis_size(axis), by))]
    unnamed x14 -> x22, local copies, waits for them, and re-layouts: 2.62 us -> 5.04 us
    pallas_call x5 -> x3, Pallas kernels: 26.7 us -> 25.8 us  [the longest x1 14 us: pair_call(): pl.pallas_call(pair_kernel, out_shape=(shape, shape), in_specs=[SMEM, SME...]
  transfers between devices with their start and end apart: 21 -> 24, of which waited for: 15 -> 12; matrix products, arithmetic and copies ran while one was open for 4% -> 4% of each run, Pallas kernels for 12% -> 11%
where the time goes in v6:
time: 178 us; the launch traced here: 176 us
  waiting for transfers between devices  54.8 us (31%)
  Pallas kernels  42.7 us (24%)
  starting transfers between devices  36.8 us (21%)
  blocking collectives  30.1 us (17%)
  local copies, waits for them, and re-layouts  6.73 us (4%)
  other arithmetic  4.42 us (2%)
    ppermute x17, waiting for transfers between devices, shards(): lax.ppermute(array, axis, ring(lax.axis_size(axis), by))  36.7 us
    ppermute x17, starting transfers between devices, shards(): lax.ppermute(array, axis, ring(lax.axis_size(axis), by))  25 us
    all_to_all x1, blocking collectives, shards(): parts = lax.all_to_all(parts, ('z', 'y'), 0, 0, tiled=True)  18.8 us
    pallas_call x1, Pallas kernels, pair_call(): pl.pallas_call(pair_kernel, out_shape=(shape, shape), in_specs=[SMEM, SME...  14 us
    all_to_all x1, waiting for transfers between devices, shards(): lax.all_to_all(pieces.reshape(32, 1, -1), ('z', 'y'), 0, 0, tiled=True)  13.3 us
    all_to_all x1, starting transfers between devices, shards(): lax.all_to_all(pieces.reshape(32, 1, -1), ('z', 'y'), 0, 0, tiled=True)  11.5 us
    all_to_all x1, blocking collectives, shards(): parts = lax.all_to_all(parts, 'x', 0, 0, tiled=True)  11.3 us
    pallas_call x1, Pallas kernels, screen_call(): pl.pallas_call(screen_kernel, out_shape=shapes, in_specs=[SMEM, VMEM, VME...  7.37 us
  transfers between devices with their start and end apart: 24, of which 12 were waited for; matrix products, arithmetic and copies ran while one was open for 4% of the time, Pallas kernels for 11%

profile of v6, /device:TPU:2, one launch (start us, length us, event | category | flops | bytes accessed | tf_op | source)
XLA Modules:
  0.0 175.8 jit_solution(8387951806474464582)
XLA Ops:
  2.6 2.3 %pack.1 = f32[640,128]{1,0:T(8,128)} custom-call(s32[4]{0:T(128)} %pad_add_fusion.1.place, f32[2,16,2560]{2,1,0:T(8,128)} %own_ref.1, f32[2,16,2560]{2,1,0:T(8,128)} %copy-done.5), custom_call_target="tpu_custom_call" | custom-call | tf_op jit(solution)/shard_map/pack/pallas_call | solution.py:368
  7.7 11.5 %all-to-all-start = ((f32[32,1,2560]{2,1,0:T(1,128)}), f32[32,1,2560]{2,1,0:T(1,128)S(1)}, u32[]{:S(2)}, u32[]{:S(2)}) async-start(f32[32,1,2560]{2,1,0:T(1,128)} %bitcast.14), calls=%async_computation | async-start | bytes 655360 | tf_op jit(solution)/shard_map/all_to_all | solution.py:465
  20.7 13.3 %all-to-all-done = f32[32,1,2560]{2,1,0:T(1,128)S(1)} async-done(((f32[32,1,2560]{2,1,0:T(1,128)}), f32[32,1,2560]{2,1,0:T(1,128)S(1)}, u32[]{:S(2)}, u32[]{:S(2)}) %all-to-all-start) | async-done | bytes 327712 | tf_op jit(solution)/shard_map/all_to_all | solution.py:465
  34.7 3.2 %unpack.1 = (f32[80,1024]{1,0:T(8,128)}, f32[80,256]{1,0:T(8,128)}, f32[80,256]{1,0:T(8,128)}) custom-call(s32[4]{0:T(128)} %pad_add_fusion.1.place, s32[32]{0:T(128)} %select_reduce_fusion.5.used, f32[640,128]{1,0:T(8,128)} %bitcast.15), custom_call_target="tpu_custom_call" | custom-call | tf_op jit(solution)/shard_map/unpack/pallas_call | solution.py:413
  38.0 1.5 collective-permute-done.1.take_ref
  40.1 1.8 %shard.1 = f32[160,256]{1,0:T(8,128)} custom-call(s32[4]{0:T(128)} %pad_add_fusion.1.place, f32[80,256]{1,0:T(8,128)} %get-tuple-element.49.keep_ref, f32[80,256]{1,0:T(8,128)} %copy-done.7), custom_call_target="tpu_custom_call" | custom-call | tf_op jit(solution)/shard_map/shard/pallas_call | solution.py:434
  42.7 2.3 %collective-permute-start.3 = (f32[160,256]{1,0:T(8,128)}, f32[160,256]{1,0:T(8,128)S(1)}, u32[]{:S(2)}, u32[]{:S(2)}) collective-permute-start(f32[160,256]{1,0:T(8,128)} %shard.1), channel_id=1, source_target_pairs={{0,224},{32,0},{64,32},{96,64},{128,96},{160,128},{192,160},{224,1... | collective-permute-start | bytes 491528 | tf_op jit(solution)/shard_map/ppermute | solution.py:474
  45.1 1.5 collective-permute-start.6
  48.0 1.5 collective-permute-done.2
  49.7 3.0 %collective-permute-start.5 = (f32[160,256]{1,0:T(8,128)S(1)}, f32[160,256]{1,0:T(8,128)S(1)}, u32[]{:S(2)}, u32[]{:S(2)}) collective-permute-start(f32[160,256]{1,0:T(8,128)S(1)} %collective-permute-done.3), channel_id=1, source_target_pairs={{0,224},{32,0},{64,32},{96,64},{128,96},{160,128},{192,160},{224,1... | collective-permute-start | bytes 491528 | tf_op jit(solution)/shard_map/ppermute | solution.py:474
  52.8 3.4 %collective-permute-done.4 = f32[160,256]{1,0:T(8,128)S(1)} collective-permute-done((f32[160,256]{1,0:T(8,128)S(1)}, f32[160,256]{1,0:T(8,128)S(1)}, u32[]{:S(2)}, u32[]{:S(2)}) %collective-permute-start.4) | collective-permute-done | bytes 163872 | tf_op jit(solution)/shard_map/ppermute | solution.py:474
  56.4 3.1 %collective-permute-start.9 = (f32[800,256]{1,0:T(8,128)S(1)}, f32[800,256]{1,0:T(8,128)S(1)}, u32[]{:S(2)}, u32[]{:S(2)}) collective-permute-start(f32[800,256]{1,0:T(8,128)S(1)} %constant_dynamic-update-slice_fusion.own), channel_id=1, source_target_pairs={{0,24},{8,0},{16,8},{24,16},{1,25},{9,1},{17,9},{25,17},{2,26},{10... | collective-permute-start | bytes 2457608 | tf_op jit(solution)/shard_map/ppermute | solution.py:474
  59.5 3.2 %collective-permute-start.11 = (f32[160,256]{1,0:T(8,128)S(1)}, f32[160,256]{1,0:T(8,128)S(1)}, u32[]{:S(2)}, u32[]{:S(2)}) collective-permute-start(f32[160,256]{1,0:T(8,128)S(1)} %collective-permute-done.5), channel_id=1, source_target_pairs={{0,224},{32,0},{64,32},{96,64},{128,96},{160,128},{192,160},{224,1... | collective-permute-start | bytes 491528 | tf_op jit(solution)/shard_map/ppermute | solution.py:474
  62.8 3.3 %collective-permute-done.10 = f32[160,256]{1,0:T(8,128)S(1)} collective-permute-done((f32[160,256]{1,0:T(8,128)S(1)}, f32[160,256]{1,0:T(8,128)S(1)}, u32[]{:S(2)}, u32[]{:S(2)}) %collective-permute-start.10) | collective-permute-done | bytes 163872 | tf_op jit(solution)/shard_map/ppermute | solution.py:474
  66.1 2.1 %collective-permute-start.14 = (f32[80,1024]{1,0:T(8,128)}, f32[80,1024]{1,0:T(8,128)S(1)}, u32[]{:S(2)}, u32[]{:S(2)}) collective-permute-start(f32[80,1024]{1,0:T(8,128)} %get-tuple-element.54.refs_0_), channel_id=1, source_target_pairs={{0,2},{1,3},{2,0},{3,1},{4,6},{5,7},{6,4},{7,5},{8,10},{9,11},{10,... | collective-permute-start | bytes 983048 | tf_op jit(solution)/shard_map/ppermute | solution.py:474
  68.5 5.6 %collective-permute-done.12 = f32[80,256]{1,0:T(8,128)S(1)} collective-permute-done((f32[80,256]{1,0:T(8,128)S(1)}, f32[80,256]{1,0:T(8,128)S(1)}, u32[]{:S(2)}, u32[]{:S(2)}) %collective-permute-start.12) | collective-permute-done | bytes 81952 | tf_op jit(solution)/shard_map/ppermute | solution.py:474
  74.8 3.7 %collective-permute-done.13 = f32[80,256]{1,0:T(8,128)S(1)} collective-permute-done((f32[80,256]{1,0:T(8,128)S(1)}, f32[80,256]{1,0:T(8,128)S(1)}, u32[]{:S(2)}, u32[]{:S(2)}) %collective-permute-start.13) | collective-permute-done | bytes 81952 | tf_op jit(solution)/shard_map/ppermute | solution.py:474
  78.6 7.4 %screen.1 = (bf16[640,1664]{1,0:T(8,128)(2,1)S(1)}, bf16[640,1664]{1,0:T(8,128)(2,1)S(1)}, bf16[640,1024]{1,0:T(8,128)(2,1)S(1)}, bf16[640,1024]{1,0:T(8,128)(2,1)S(1)}) custom-call(s32[4]{0:T(128)S(1)} %copy-done.3, f32[320,2560]{1,0:T(8,128)S(1)} %bitcast.13, f32[320,2560]{1,0:T(8,128)} %collective-permute-done.15.other_ref), custom_call_target="tpu_custom_call" | custom-call | tf_op jit(solution)/shard_map/screen/pallas_call | solution.py:118
  86.5 3.2 %collective-permute-start.17 = (f32[880,256]{1,0:T(8,128)S(1)}, f32[880,256]{1,0:T(8,128)S(1)}, u32[]{:S(2)}, u32[]{:S(2)}) collective-permute-start(f32[880,256]{1,0:T(8,128)S(1)} %get-tuple-element.93), channel_id=1, source_target_pairs={{0,24},{8,0},{16,8},{24,16},{1,25},{9,1},{17,9},{25,17},{2,26},{10... | collective-permute-start | bytes 2703368 | tf_op jit(solution)/shard_map/ppermute | solution.py:474
  89.9 1.8 %left.1 = (bf16[1024,640]{1,0:T(8,128)(2,1)S(1)}, bf16[1024,640]{1,0:T(8,128)(2,1)S(1)}) custom-call(s32[4]{0:T(128)S(1)} %copy-done.3, f32[80,1024]{1,0:T(8,128)S(1)} %copy-done.1, f32[80,1024]{1,0:T(8,128)S(1)} %collective-permute-done.6.refs_1_, f32[80,1024]{1,0:T(8,128)S(1)} %collective-permute-done.14.refs_2_, ...), custom_call_target="tpu_custom_call" | custom-call | tf_op jit(solution)/shard_map/left/pallas_call | solution.py:148
  91.7 18.4 %collective-permute-done.16.two_below.below = f32[880,256]{1,0:T(8,128)S(1)} collective-permute-done((f32[880,256]{1,0:T(8,128)S(1)}, f32[880,256]{1,0:T(8,128)S(1)}, u32[]{:S(2)}, u32[]{:S(2)}) %collective-permute-start.16) | collective-permute-done | bytes 901152 | tf_op jit(solution)/shard_map/ppermute | solution.py:474
  110.3 3.5 %collective-permute-start.20 = (f32[240,256]{1,0:T(8,128)S(1)}, f32[240,256]{1,0:T(8,128)S(1)}, u32[]{:S(2)}, u32[]{:S(2)}) collective-permute-start(f32[240,256]{1,0:T(8,128)S(1)} %slice.47), channel_id=1, source_target_pairs={{0,24},{8,0},{16,8},{24,16},{1,25},{9,1},{17,9},{25,17},{2,26},{10... | collective-permute-start | bytes 737288 | tf_op jit(solution)/shard_map/ppermute | solution.py:474
  113.8 4.4 %group.1.sum_ref = f32[640,512]{1,0:T(8,128)S(1)} custom-call(s32[4]{0:T(128)S(1)} %copy-done.3, f32[800,256]{1,0:T(8,128)S(1)} %constant_dynamic-update-slice_fusion.own, f32[800,256]{1,0:T(8,128)S(1)} %collective-permute-done.8.below, f32[800,256]{1,0:T(8,128)S(1)} %collective-permute-done.9.above, f32[880,256]{1,0:T(8,128)S(1)} %collective-permute-done.16.two_below.below, ...), custom_call_target="tpu_custom_call" | custom-call | tf_op jit(solution)/shard_map/group/pallas_call | solution.py:188
  119.0 14.0 %pair.1 = (f32[2,8,4096]{2,1,0:T(8,128)S(1)}, f32[2,8,4096]{2,1,0:T(8,128)S(1)}) custom-call(s32[4]{0:T(128)S(1)} %copy-done.3, s32[4,256]{1,0:T(4,128)S(1)} %pad_add_fusion.table, f32[480,256]{1,0:T(8,128)S(1)} %pad_maximum_fusion.3.own, f32[880,256]{1,0:T(8,128)S(1)} %collective-permute-done.16.two_below.below, ...), custom_call_target="tpu_custom_call" | custom-call | tf_op jit(solution)/shard_map/pair/pallas_call | solution.py:238
  133.7 1.5 collective-permute-done.21.come_ref
  135.9 1.7 rows.1
  137.7 11.3 %all_to_all.15.parts_ref = f32[4,8,2048]{2,1,0:T(8,128)} all-to-all(f32[4,8,2048]{2,1,0:T(8,128)} %rows.1), channel_id=1, replica_groups=mesh['z'=8,'y'=4,'core'=2,'x'=4] {'x'}, dimensions={0} | all-to-all | bytes 524288 | tf_op jit(solution)/shard_map/all_to_all | solution.py:508
  149.0 2.4 %owner.1 = f32[32,8,256]{2,1,0:T(8,128)} custom-call(s32[64]{0:T(128)} %select_reduce_fusion.4.offset, f32[4,8,2048]{2,1,0:T(8,128)} %all_to_all.15.parts_ref), custom_call_target="tpu_custom_call" | custom-call | tf_op jit(solution)/shard_map/owner/pallas_call | solution.py:291
  151.4 18.8 %all_to_all.16.in_ref = f32[32,8,256]{2,1,0:T(8,128)} all-to-all(f32[32,8,256]{2,1,0:T(8,128)} %owner.1), channel_id=1, replica_groups=mesh['z'=8,'y'=4,'core'=2,'x'=4] {'z','y'}, dimensions={0} | all-to-all | bytes 524288 | tf_op jit(solution)/shard_map/all_to_all | solution.py:510
  170.2 1.6 total.1.own_ref
  171.8 1.4 collective-permute-done.22.come_ref
  173.7 2.1 %last.1 = f32[12,8,16]{2,1,0:T(8,128)} custom-call(s32[4]{0:T(128)} %pad_add_fusion.1.place, s32[1]{0:T(128)} %dynamic_slice.3.held_ref, f32[8,256]{1,0:T(8,128)} %total.1.own_ref, f32[8,256]{1,0:T(8,128)} %copy-done.8), custom_call_target="tpu_custom_call" | custom-call | tf_op jit(solution)/shard_map/last/pallas_call | solution.py:336
  (78 shorter events, 15.6 us)
Async XLA Ops:
  0.0 1.8 %collective-permute-start = (f32[2,16,2560]{2,1,0:T(8,128)}, f32[2,16,2560]{2,1,0:T(8,128)S(1)}, u32[]{:S(2)}, u32[]{:S(2)}) collective-permute-start(f32[2,16,2560]{2,1,0:T(8,128)} %own_ref.1), channel_id=1, source_target_pairs={{0,4},{4,0},{1,5},{5,1},{2,6},{6,2},{3,7},{7,3},{8,12},{12,8},{9,1... | collective-permute-start | bytes 983048 | tf_op jit(solution)/shard_map/ppermute | solution.py:464
  1.8 0.7 copy-start.5
  4.8 73.8 %collective-permute-start.15 = (f32[320,2560]{1,0:T(8,128)}, f32[320,2560]{1,0:T(8,128)}, u32[]{:S(2)}, u32[]{:S(2)}) collective-permute-start(f32[320,2560]{1,0:T(8,128)} %bitcast.12), channel_id=1, source_target_pairs={{0,4},{4,0},{1,5},{5,1},{2,6},{6,2},{3,7},{7,3},{8,12},{12,8},{9,1... | collective-permute-start | bytes 9830408 | tf_op jit(solution)/shard_map/ppermute | solution.py:469
  7.7 26.3 %all-to-all-start = ((f32[32,1,2560]{2,1,0:T(1,128)}), f32[32,1,2560]{2,1,0:T(1,128)S(1)}, u32[]{:S(2)}, u32[]{:S(2)}) async-start(f32[32,1,2560]{2,1,0:T(1,128)} %bitcast.14), calls=%async_computation | async-start | bytes 655360 | tf_op jit(solution)/shard_map/all_to_all | solution.py:465
  34.0 0.7 copy-start.4
  37.9 1.5 collective-permute-start.1
  39.4 0.6 copy-start.7
  40.1 38.5 %copy-start = (f32[2,4,40,2560]{3,2,1,0:T(8,128)S(1)}, f32[2,4,40,2560]{3,2,1,0:T(8,128)}, u32[]{:S(2)}) copy-start(f32[2,4,40,2560]{3,2,1,0:T(8,128)} %param.5) | copy-start | bytes 9830404
  41.8 7.7 %collective-permute-start.2 = (f32[160,256]{1,0:T(8,128)}, f32[160,256]{1,0:T(8,128)S(1)}, u32[]{:S(2)}, u32[]{:S(2)}) collective-permute-start(f32[160,256]{1,0:T(8,128)} %shard.1), channel_id=1, source_target_pairs={{0,32},{32,64},{64,96},{96,128},{128,160},{160,192},{192,224},{224... | collective-permute-start | bytes 491528 | tf_op jit(solution)/shard_map/ppermute | solution.py:474
  42.7 6.8 %collective-permute-start.3 = (f32[160,256]{1,0:T(8,128)}, f32[160,256]{1,0:T(8,128)S(1)}, u32[]{:S(2)}, u32[]{:S(2)}) collective-permute-start(f32[160,256]{1,0:T(8,128)} %shard.1), channel_id=1, source_target_pairs={{0,224},{32,0},{64,32},{96,64},{128,96},{160,128},{192,160},{224,1... | collective-permute-start | bytes 491528 | tf_op jit(solution)/shard_map/ppermute | solution.py:474
  45.1 11.1 %collective-permute-start.6 = (f32[80,1024]{1,0:T(8,128)}, f32[80,1024]{1,0:T(8,128)S(1)}, u32[]{:S(2)}, u32[]{:S(2)}) collective-permute-start(f32[80,1024]{1,0:T(8,128)} %get-tuple-element.54.refs_0_), channel_id=1, source_target_pairs={{0,1},{1,2},{2,3},{3,0},{4,5},{5,6},{6,7},{7,4},{8,9},{9,10},{10,1... | collective-permute-start | bytes 983048 | tf_op jit(solution)/shard_map/ppermute | solution.py:474
  46.6 9.6 %collective-permute-start.7 = (f32[80,1024]{1,0:T(8,128)}, f32[80,1024]{1,0:T(8,128)S(1)}, u32[]{:S(2)}, u32[]{:S(2)}) collective-permute-start(f32[80,1024]{1,0:T(8,128)} %get-tuple-element.54.refs_0_), channel_id=1, source_target_pairs={{0,3},{1,0},{2,1},{3,2},{4,7},{5,4},{6,5},{7,6},{8,11},{9,8},{10,9... | collective-permute-start | bytes 983048 | tf_op jit(solution)/shard_map/ppermute | solution.py:474
  48.0 30.6 %copy-start.3 = (s32[4]{0:T(128)S(1)}, s32[4]{0:T(128)}, u32[]{:S(2)}) copy-start(s32[4]{0:T(128)} %pad_add_fusion.1.place) | copy-start | bytes 52
  49.5 6.6 %collective-permute-start.4 = (f32[160,256]{1,0:T(8,128)S(1)}, f32[160,256]{1,0:T(8,128)S(1)}, u32[]{:S(2)}, u32[]{:S(2)}) collective-permute-start(f32[160,256]{1,0:T(8,128)S(1)} %collective-permute-done.2), channel_id=1, source_target_pairs={{0,32},{32,64},{64,96},{96,128},{128,160},{160,192},{192,224},{224... | collective-permute-start | bytes 491528 | tf_op jit(solution)/shard_map/ppermute | solution.py:474
  49.7 6.4 %collective-permute-start.5 = (f32[160,256]{1,0:T(8,128)S(1)}, f32[160,256]{1,0:T(8,128)S(1)}, u32[]{:S(2)}, u32[]{:S(2)}) collective-permute-start(f32[160,256]{1,0:T(8,128)S(1)} %collective-permute-done.3), channel_id=1, source_target_pairs={{0,224},{32,0},{64,32},{96,64},{128,96},{160,128},{192,160},{224,1... | collective-permute-start | bytes 491528 | tf_op jit(solution)/shard_map/ppermute | solution.py:474
  56.2 29.8 %collective-permute-start.8 = (f32[800,256]{1,0:T(8,128)S(1)}, f32[800,256]{1,0:T(8,128)S(1)}, u32[]{:S(2)}, u32[]{:S(2)}) collective-permute-start(f32[800,256]{1,0:T(8,128)S(1)} %constant_dynamic-update-slice_fusion.own), channel_id=1, source_target_pairs={{0,8},{8,16},{16,24},{24,0},{1,9},{9,17},{17,25},{25,1},{2,10},{10... | collective-permute-start | bytes 2457608 | tf_op jit(solution)/shard_map/ppermute | solution.py:474
  56.4 29.6 %collective-permute-start.9 = (f32[800,256]{1,0:T(8,128)S(1)}, f32[800,256]{1,0:T(8,128)S(1)}, u32[]{:S(2)}, u32[]{:S(2)}) collective-permute-start(f32[800,256]{1,0:T(8,128)S(1)} %constant_dynamic-update-slice_fusion.own), channel_id=1, source_target_pairs={{0,24},{8,0},{16,8},{24,16},{1,25},{9,1},{17,9},{25,17},{2,26},{10... | collective-permute-start | bytes 2457608 | tf_op jit(solution)/shard_map/ppermute | solution.py:474
  59.5 6.5 %collective-permute-start.10 = (f32[160,256]{1,0:T(8,128)S(1)}, f32[160,256]{1,0:T(8,128)S(1)}, u32[]{:S(2)}, u32[]{:S(2)}) collective-permute-start(f32[160,256]{1,0:T(8,128)S(1)} %collective-permute-done.4), channel_id=1, source_target_pairs={{0,32},{32,64},{64,96},{96,128},{128,160},{160,192},{192,224},{224... | collective-permute-start | bytes 491528 | tf_op jit(solution)/shard_map/ppermute | solution.py:474
  59.5 8.7 %collective-permute-start.11 = (f32[160,256]{1,0:T(8,128)S(1)}, f32[160,256]{1,0:T(8,128)S(1)}, u32[]{:S(2)}, u32[]{:S(2)}) collective-permute-start(f32[160,256]{1,0:T(8,128)S(1)} %collective-permute-done.5), channel_id=1, source_target_pairs={{0,224},{32,0},{64,32},{96,64},{128,96},{160,128},{192,160},{224,1... | collective-permute-start | bytes 491528 | tf_op jit(solution)/shard_map/ppermute | solution.py:474
  66.1 19.9 %collective-permute-start.14 = (f32[80,1024]{1,0:T(8,128)}, f32[80,1024]{1,0:T(8,128)S(1)}, u32[]{:S(2)}, u32[]{:S(2)}) collective-permute-start(f32[80,1024]{1,0:T(8,128)} %get-tuple-element.54.refs_0_), channel_id=1, source_target_pairs={{0,2},{1,3},{2,0},{3,1},{4,6},{5,7},{6,4},{7,5},{8,10},{9,11},{10,... | collective-permute-start | bytes 983048 | tf_op jit(solution)/shard_map/ppermute | solution.py:474
  68.2 5.9 %collective-permute-start.12 = (f32[80,256]{1,0:T(8,128)S(1)}, f32[80,256]{1,0:T(8,128)S(1)}, u32[]{:S(2)}, u32[]{:S(2)}) collective-permute-start(f32[80,256]{1,0:T(8,128)S(1)} %slice.38), channel_id=1, source_target_pairs={{0,32},{32,64},{64,96},{96,128},{128,160},{160,192},{192,224},{224... | collective-permute-start | bytes 245768 | tf_op jit(solution)/shard_map/ppermute | solution.py:474
  74.1 4.4 %collective-permute-start.13 = (f32[80,256]{1,0:T(8,128)S(1)}, f32[80,256]{1,0:T(8,128)S(1)}, u32[]{:S(2)}, u32[]{:S(2)}) collective-permute-start(f32[80,256]{1,0:T(8,128)S(1)} %slice.39), channel_id=1, source_target_pairs={{0,224},{32,0},{64,32},{96,64},{128,96},{160,128},{192,160},{224,1... | collective-permute-start | bytes 245768 | tf_op jit(solution)/shard_map/ppermute | solution.py:474
  78.6 7.5 %copy-start.1 = (f32[80,1024]{1,0:T(8,128)S(1)}, f32[80,1024]{1,0:T(8,128)}, u32[]{:S(2)}) copy-start(f32[80,1024]{1,0:T(8,128)} %get-tuple-element.54.refs_0_) | copy-start | bytes 983044
  86.2 3.6 %collective-permute-start.18 = (f32[320,1024]{1,0:T(8,128)S(1)}, f32[320,1024]{1,0:T(8,128)S(1)}, u32[]{:S(2)}, u32[]{:S(2)}) collective-permute-start(f32[320,1024]{1,0:T(8,128)S(1)} %pad_maximum_fusion), channel_id=1, source_target_pairs={{0,4},{4,0},{1,5},{5,1},{2,6},{6,2},{3,7},{7,3},{8,12},{12,8},{9,1... | collective-permute-start | bytes 3932168 | tf_op jit(solution)/shard_map/ppermute | solution.py:495
  86.5 23.7 %collective-permute-start.16 = (f32[880,256]{1,0:T(8,128)S(1)}, f32[880,256]{1,0:T(8,128)S(1)}, u32[]{:S(2)}, u32[]{:S(2)}) collective-permute-start(f32[880,256]{1,0:T(8,128)S(1)} %get-tuple-element.94), channel_id=1, source_target_pairs={{0,8},{8,16},{16,24},{24,0},{1,9},{9,17},{17,25},{25,1},{2,10},{10... | collective-permute-start | bytes 2703368 | tf_op jit(solution)/shard_map/ppermute | solution.py:474
  86.5 23.6 %collective-permute-start.17 = (f32[880,256]{1,0:T(8,128)S(1)}, f32[880,256]{1,0:T(8,128)S(1)}, u32[]{:S(2)}, u32[]{:S(2)}) collective-permute-start(f32[880,256]{1,0:T(8,128)S(1)} %get-tuple-element.93), channel_id=1, source_target_pairs={{0,24},{8,0},{16,8},{24,16},{1,25},{9,1},{17,9},{25,17},{2,26},{10... | collective-permute-start | bytes 2703368 | tf_op jit(solution)/shard_map/ppermute | solution.py:474
  110.2 8.9 %collective-permute-start.19 = (f32[240,256]{1,0:T(8,128)S(1)}, f32[240,256]{1,0:T(8,128)S(1)}, u32[]{:S(2)}, u32[]{:S(2)}) collective-permute-start(f32[240,256]{1,0:T(8,128)S(1)} %slice.46), channel_id=1, source_target_pairs={{0,8},{8,16},{16,24},{24,0},{1,9},{9,17},{17,25},{25,1},{2,10},{10... | collective-permute-start | bytes 737288 | tf_op jit(solution)/shard_map/ppermute | solution.py:474
  110.3 8.7 %collective-permute-start.20 = (f32[240,256]{1,0:T(8,128)S(1)}, f32[240,256]{1,0:T(8,128)S(1)}, u32[]{:S(2)}, u32[]{:S(2)}) collective-permute-start(f32[240,256]{1,0:T(8,128)S(1)} %slice.47), channel_id=1, source_target_pairs={{0,24},{8,0},{16,8},{24,16},{1,25},{9,1},{17,9},{25,17},{2,26},{10... | collective-permute-start | bytes 737288 | tf_op jit(solution)/shard_map/ppermute | solution.py:474
  133.0 0.7 copy-start.2
  133.7 1.5 collective-permute-start.21
  135.2 0.7 copy-start.6
  171.7 1.4 collective-permute-start.22
  (1 other events, 0.6 us)

commit v7 on v6

v7 whole, which is shorter than its diff:
```python
import functools

import jax
import jax.numpy as jnp
from jax import lax
from jax.experimental import pallas as pl
from jax.experimental.pallas import tpu as pltpu
from jax.sharding import Mesh
from jax.sharding import PartitionSpec as P

NG = 10240
CAP = 12
BLK = 16
USED = 32
HALF = USED // 2 * BLK
BAND = ("z", "y", "core")
SWAP = ((0, 1), (1, 0))
SMEM = pl.BlockSpec(memory_space=pltpu.SMEM)
VMEM = pl.BlockSpec(memory_space=pltpu.VMEM)
SPAN = 80
PLANE = 320
NEAR = (0, 7, 1, 6, 2)
MIDDLE = (5, 3)
FAR = (4,)
ROOM = 224


def ring(n, shift):
    return [(i, (i + shift) % n) for i in range(n)]


def params(mib):
    return pltpu.CompilerParams(vmem_limit_bytes=mib * 1024 * 1024)


def split(x):
    high = x.astype(jnp.bfloat16)
    return high, (x - high.astype(jnp.float32)).astype(jnp.bfloat16)


def dot(former, latter):
    return jnp.dot(former, latter, preferred_element_type=jnp.float32)


def dot3(high, low, former, latter):
    return dot(high, former) + dot(high, latter) + dot(low, former)


def plan_kernel(place, pairs_ref, owners_ref, out_ref):
    size = 256
    down = lax.broadcasted_iota(jnp.int32, (size, size), 0)
    across = lax.broadcasted_iota(jnp.int32, (size, size), 1)
    one = lambda condition: jnp.where(condition, 1.0, 0.0)
    to_row = lambda column: jnp.sum(jnp.where(down == across, column, 0.0), axis=0, keepdims=True)
    to_column = lambda row: jnp.sum(jnp.where(down == across, row, 0.0), axis=1, keepdims=True)
    rows, columns = down.astype(jnp.float32), across.astype(jnp.float32)
    left, right = pairs_ref[:, 0:1].astype(jnp.float32), pairs_ref[:, 1:2].astype(jnp.float32)
    owner_row = owners_ref[...].astype(jnp.float32)
    owner = to_column(owner_row)

    used = jnp.max(one(right == columns), axis=0, keepdims=True)
    used_column = to_column(used)
    rank = jnp.sum(jnp.where(columns < rows, used, 0.0), axis=1, keepdims=True)
    used_list = jnp.sum(jnp.where((rank == columns) & (used_column > 0), rows, 0.0), axis=0, keepdims=True)
    right_rank = jnp.sum(jnp.where(columns < right, used, 0.0), axis=1, keepdims=True)

    parity = lambda value: value - 2.0 * jnp.floor(value * 0.5)
    count = jnp.sum(one(owner == columns), axis=0, keepdims=True)
    same = parity(rows) == parity(columns)
    offset = jnp.sum(jnp.where((rows < columns) & same, to_column(count), 0.0), axis=0, keepdims=True)
    ahead = (owner_row < owner) | ((owner_row == owner) & (across < down))
    ahead = ahead & (parity(owner_row) == parity(owner))
    position = jnp.sum(one(ahead), axis=1, keepdims=True)

    core = place[3].astype(jnp.float32)
    local = right_rank - core * (USED // 2)
    here = (local >= 0) & (local < USED // 2)
    local = jnp.where(here, local, 0.0)
    lane = lax.broadcasted_iota(jnp.int32, (1, size), 1)
    groups = jnp.zeros((1, size), jnp.float32)
    for half in range(2):
        hit = (position == columns) & (parity(owner) == half)
        pick = lambda column: jnp.sum(jnp.where(hit, column, 0.0), axis=0, keepdims=True).astype(jnp.int32)
        at = pick(local)
        out_ref[4 * half : 4 * half + 1, :] = pick(left) * BLK
        out_ref[4 * half + 1 : 4 * half + 2, :] = at // 8 * 128
        out_ref[4 * half + 2 : 4 * half + 3, :] = (lane + 8 - at % 8) % 8 * BLK
        out_ref[4 * half + 3 : 4 * half + 4, :] = jnp.where(pick(one(here)) > 0, lane % 8, -1)
        total = jnp.sum(one(parity(owner_row) == half))
        groups = jnp.where(lane == half, jnp.floor((total + 7.0) / 8.0), groups)
    for at, row in enumerate((offset, count, used_list, groups)):
        out_ref[8 + at : 9 + at, :] = row.astype(jnp.int32)


def plan_call(place, pairs, owners):
    return pl.pallas_call(
        plan_kernel,
        out_shape=jax.ShapeDtypeStruct((16, pairs.shape[0]), jnp.int32),
        in_specs=[SMEM, VMEM, VMEM],
        out_specs=VMEM,
        name="plan",
    )(place, pairs, owners)


def padded(planes):
    return (len(planes) * PLANE + 127) // 128 * 128


def screen_kernel(place, own_ref, other_ref, *outs):
    z = place[0]
    rows = 16
    lane = lax.broadcasted_iota(jnp.int32, (rows, 128), 1)

    def plane_of(ref, row, delta, offset):
        plane = lax.rem(z + delta, 8)
        odd = lax.rem(plane, 2)
        column = pl.multiple_of(plane * PLANE - odd * 64, 128)
        window = ref[row, pl.ds(column, 384)]
        turned = pltpu.roll(window, 64 if offset else 320, 1)
        return jnp.where((odd == 1) if offset else (odd == 0), window, turned)

    for source, ref in enumerate((own_ref, other_ref)):

        def body(step, carry, source=source, ref=ref):
            part = step // 10
            row = pl.ds(pl.multiple_of(step * rows, rows), rows)
            target = pl.multiple_of(part * PLANE + source * (PLANE // 2) + (step - part * 10) * rows, rows)
            for group, planes in enumerate((NEAR, MIDDLE, FAR)):
                for at in range(0, len(planes), 2):
                    a = plane_of(ref, row, planes[at], False)
                    if at + 1 < len(planes):
                        b = plane_of(ref, row, planes[at + 1], True)
                        middle = jnp.where(lane < 64, a[:, 256:], b[:, :128])
                        whole = jnp.concatenate([a[:, :256], middle, b[:, 128:]], axis=1)
                    else:
                        whole = jnp.concatenate([a[:, :256], jnp.where(lane < 64, a[:, 256:], 0.0)], axis=1)
                    top, rest = split(whole)
                    columns = slice(at * PLANE, at * PLANE + whole.shape[1])
                    outs[2 * group][pl.ds(target, rows), columns] = top
                    outs[2 * group + 1][pl.ds(target, rows), columns] = rest
            return carry

        lax.fori_loop(0, 20, body, 0)


def screen_call(place, own, other):
    shapes = [
        jax.ShapeDtypeStruct((2 * own.shape[0], padded(planes)), jnp.bfloat16)
        for planes in (NEAR, MIDDLE, FAR)
        for _ in range(2)
    ]
    return pl.pallas_call(
        screen_kernel,
        out_shape=shapes,
        in_specs=[SMEM, VMEM, VMEM],
        out_specs=[VMEM] * 6,
        compiler_params=params(20),
        name="screen",
    )(place, own, other)


def left_kernel(place, *refs):
    pieces, (high_ref, low_ref, work) = refs[:8], refs[8:]
    x = place[1]
    span = pieces[0].shape[0] // 2
    for core in range(2):
        for shift in range(4):
            shard = lax.rem(x - shift + 4, 4)
            for part in range(2):
                row = pl.multiple_of(part * 8 * span + core * 4 * span + shard * span, 8)
                work[pl.ds(row, span), :] = pieces[core * 4 + shift][part * span : (part + 1) * span, :]
    for block in range(work.shape[1] // 128):
        turned = work[:, block * 128 : (block + 1) * 128].T
        top, rest = split(turned)
        high_ref[block * 128 : (block + 1) * 128, :] = top
        low_ref[block * 128 : (block + 1) * 128, :] = rest


def left_call(place, pieces):
    depth, width = pieces[0].shape
    shape = jax.ShapeDtypeStruct((width, 8 * depth), jnp.bfloat16)
    return pl.pallas_call(
        left_kernel,
        out_shape=(shape, shape),
        in_specs=[SMEM] + [VMEM] * 8,
        out_specs=(VMEM, VMEM),
        scratch_shapes=[pltpu.VMEM((8 * depth, width), jnp.float32)],
        compiler_params=params(20),
        name="left",
    )(place, *pieces)


def load_right(place, units, planes, high, low):
    y = place[2]
    for delta, plane, part, ref, start in units:
        row = pl.multiple_of(plane * PLANE + lax.rem(y + delta, 4) * SPAN, 16)
        top, rest = split(ref[start : start + SPAN, :])
        high[pl.ds(row, SPAN), part * HALF : (part + 1) * HALF] = top
        low[pl.ds(row, SPAN), part * HALF : (part + 1) * HALF] = rest
    used = planes * PLANE
    if used < high.shape[0]:
        for ref in (high, low):
            ref[used:, :] = jnp.zeros((ref.shape[0] - used, ref.shape[1]), ref.dtype)


def near_units(first, first_down, first_up, second, second_down, second_up, two_down, two_up):
    units = []
    for base, planes, skip, own, below, above in (
        (0, 3, 0, first, first_down, first_up),
        (3, 2, 3, second, second_down, second_up),
    ):
        for unit in range(2 * planes):
            half, at = (two_down, unit + skip) if unit < planes else (two_up, unit - planes + skip)
            for delta, ref, index in ((0, own, unit), (3, below, unit), (1, above, unit), (2, half, at)):
                units.append((delta, base + unit // 2, unit % 2, ref, index * SPAN))
    return units


def middle_units(below, above, z_below, z_above, y_below, y_above):
    units = []
    for part in range(2):
        for plane, own, sides, across in ((0, below, z_below, y_below), (1, above, z_above, y_above)):
            for delta, ref, block in ((0, own, 0), (3, sides, 0), (1, sides, 1), (2, across, 0)):
                units.append((delta, plane, part, ref, (2 * block + part) * SPAN))
    return units


def far_units(z_below, z_above, below, above, across_low, across_high):
    units = []
    for part, own, across in ((0, z_below, across_low), (1, z_above, across_high)):
        for delta, ref, start in ((0, own, 4), (3, below, part), (1, above, part), (2, across, 0)):
            units.append((delta, 0, part, ref, start * SPAN))
    return units


def group_kernel(units, planes, place, *refs):
    count = len(refs) - 5 - (units is middle_units)
    rights, (high_ref, low_ref), rest = refs[:count], refs[count : count + 2], refs[count + 2 :]
    out_ref, rh, rl = rest[-3:]
    load_right(place, units(*rights), planes, rh, rl)
    value = dot3(high_ref[...], low_ref[...], rh[...], rl[...])
    out_ref[...] = value if len(rest) == 3 else value + rest[0][...]


def group_call(units, planes, place, rights, screens, total):
    rows, width = screens[0].shape
    return pl.pallas_call(
        functools.partial(group_kernel, units, planes),
        out_shape=jax.ShapeDtypeStruct((rows, 2 * HALF), jnp.float32),
        in_specs=[SMEM] + [VMEM] * (len(rights) + 2 + len(total)),
        out_specs=VMEM,
        scratch_shapes=[pltpu.VMEM((width, 2 * HALF), jnp.bfloat16)] * 2,
        compiler_params=params(32),
        name="group",
    )(place, *rights, *screens, *total)


def pair_kernel(place, table, *refs):
    rights, (high_ref, low_ref, sum_ref, left_high, left_low, out_ref, rh, rl, kern) = refs[:6], refs[6:]
    load_right(place, far_units(*rights), len(FAR), rh, rl)
    product = sum_ref[...] + dot3(high_ref[...], low_ref[...], rh[...], rl[...])
    mid = product.shape[0] // 2
    real = product[:mid, :HALF] - product[mid:, HALF:]
    imag = product[mid:, :HALF] + product[:mid, HALF:]
    applied = NG ** (-0.5) * jnp.concatenate(
        [jnp.concatenate([real, imag], axis=0), jnp.concatenate([imag, -real], axis=0)], axis=1
    )
    kern[...] = dot3(left_high[...], left_low[...], *split(applied))

    lane = lax.broadcasted_iota(jnp.int32, (8, 128), 1) // BLK
    upper = lax.broadcasted_iota(jnp.int32, (8, 128), 0) < 4
    out_ref[...] = jnp.zeros_like(out_ref)
    for half in range(2):

        def group(g, carry, half=half):
            tiles = [[jnp.zeros((8, 128), jnp.float32) for _ in range(2)] for _ in range(2)]
            for u in range(8):
                slot = g * 8 + u
                row = pl.multiple_of(table[4 * half, slot], BLK)
                column = pl.multiple_of(table[4 * half + 1, slot], 128)
                shift = table[4 * half + 2, slot]
                target = table[4 * half + 3, slot]
                for part in range(2):
                    for side in range(2):
                        tile = kern[pl.ds(row + side * 8, 8), pl.ds(column + part * HALF, 128)]
                        tile = pltpu.roll(tile, shift, 1)
                        tiles[part][side] = jnp.where(lane == target, tile, tiles[part][side])
            lanes = pl.ds(pl.multiple_of(g * 128, 128), 128)
            for side in range(2):
                real, imag = tiles[0][side], tiles[1][side]
                out_ref[4 * half + 2 * side, :, lanes] = jnp.where(upper, real, pltpu.roll(imag, 4, 0))
                out_ref[4 * half + 2 * side + 1, :, lanes] = jnp.where(upper, pltpu.roll(real, 4, 0), imag)
            return carry

        lax.fori_loop(0, table[11, half], group, 0)


def pair_call(place, table, rights, screens, total, left_high, left_low):
    return pl.pallas_call(
        pair_kernel,
        out_shape=jax.ShapeDtypeStruct((8, 8, ROOM * BLK), jnp.float32),
        in_specs=[SMEM, SMEM] + [VMEM] * (len(rights) + 5),
        out_specs=VMEM,
        scratch_shapes=[pltpu.VMEM((screens[0].shape[1], 2 * HALF), jnp.bfloat16)] * 2
        + [pltpu.VMEM((left_high.shape[0], 2 * HALF), jnp.float32)],
        compiler_params=params(40),
        name="pair",
    )(place, table, *rights, *screens, total, left_high, left_low)


def owner_kernel(place, table, parts_ref, out_ref, work):
    total = parts_ref[0]
    for at in range(1, parts_ref.shape[0]):
        total = total + parts_ref[at]
    width = total.shape[1]
    work[:, :width] = total
    work[:, width:] = jnp.zeros((8, work.shape[1] - width), jnp.float32)
    for chip in range(out_ref.shape[0]):
        start = table[8, chip * 2 + place[3]]
        column = pl.multiple_of(start // 8 * 128, 128)
        shift = lax.rem(384 - lax.rem(start, 8) * BLK, 384)
        out_ref[chip] = pltpu.roll(work[:, pl.ds(column, 384)], shift, 1)[:, :256]


def owner_call(place, table, parts):
    return pl.pallas_call(
        owner_kernel,
        out_shape=jax.ShapeDtypeStruct((32, 8, 256), jnp.float32),
        in_specs=[SMEM, SMEM, VMEM],
        out_specs=VMEM,
        scratch_shapes=[pltpu.VMEM((8, parts.shape[2] + 384), jnp.float32)],
        name="owner",
    )(place, table, parts)


def last_kernel(place, table, parts_ref, out_ref):
    total = parts_ref[0]
    for chip in range(1, parts_ref.shape[0]):
        total = total + parts_ref[chip]
    held = table[9, (place[0] * 4 + place[2]) * 2 + place[3]]
    for slot in range(CAP):
        tile = total[:, slot // 8 * 128 : slot // 8 * 128 + 128]
        tile = pltpu.roll(tile, (128 - slot % 8 * BLK) % 128, 1)
        out_ref[slot] = jnp.where(slot < held, tile[:, :BLK], 0.0)


def last_call(place, table, parts):
    return pl.pallas_call(
        last_kernel,
        out_shape=jax.ShapeDtypeStruct((CAP, 8, BLK), jnp.float32),
        in_specs=[SMEM, SMEM, VMEM],
        out_specs=VMEM,
        name="last",
    )(place, table, parts)


def pack_kernel(place, own_ref, other_ref, out_ref, work):
    core = place[3]
    width = own_ref.shape[2]
    for block in range(width // 128):
        lanes = pl.ds(block * 128, 128)
        rows = []
        for part in range(2):
            own, other = own_ref[part, :, lanes], other_ref[part, :, lanes]
            rows += [jnp.where(core == 0, own, other), jnp.where(core == 0, other, own)]
        rows = jnp.concatenate(rows + rows, axis=0)
        work[block * 128 : (block + 1) * 128, :] = rows.T
    half = lax.broadcasted_iota(jnp.int32, (8, 128), 1) < 64
    for chip in range(32):
        at = pl.multiple_of(chip * 80 + core * 40, 8)
        tiles = [work[pl.ds(at + 8 * t, 8), :] for t in range(5)]
        out_ref[chip * 20 : chip * 20 + 8, :] = jnp.where(half, tiles[0], tiles[1])
        out_ref[chip * 20 + 8 : chip * 20 + 16, :] = jnp.where(half, tiles[2], tiles[3])
        last = jnp.where(half, tiles[4], pltpu.roll(tiles[4], 4, 0))
        out_ref[chip * 20 + 16 : chip * 20 + 20, :] = last[:4]


def pack_call(place, own, other):
    width = own.shape[2]
    return pl.pallas_call(
        pack_kernel,
        out_shape=jax.ShapeDtypeStruct((32 * 20, 128), jnp.float32),
        in_specs=[SMEM, VMEM, VMEM],
        out_specs=VMEM,
        scratch_shapes=[pltpu.VMEM((width, 128), jnp.float32)],
        name="pack",
    )(place, own, other)


def unpack_kernel(place, table, in_ref, columns_ref, keep_ref, give_ref):
    core = place[3]
    quarter = lax.broadcasted_iota(jnp.int32, (8, 128), 1) // 32
    upper = lax.broadcasted_iota(jnp.int32, (8, 128), 0) < 4
    for group in range(8):
        tiles = [[None] * 5 for _ in range(2)]
        for u in range(4):
            at = (group * 4 + u) * 20
            one, two = in_ref[at : at + 8, :], in_ref[at + 8 : at + 16, :]
            end = in_ref[at + 12 : at + 20, :]
            end = jnp.where(upper, pltpu.roll(end, 4, 0), pltpu.roll(end, 64, 1))
            for t, (source, first) in enumerate(((one, 0), (one, 64), (two, 0), (two, 64), (end, 0))):
                for part in range(2):
                    by = (u * 32 - first - part * 32) % 128
                    turned = pltpu.roll(source, by, 1) if by else source
                    old = tiles[part][t]
                    tiles[part][t] = turned if old is None else jnp.where(quarter == u, turned, old)
        for part in range(2):
            for t in range(5):
                row = part * 40 + t * 8
                columns_ref[row : row + 8, group * 128 : (group + 1) * 128] = tiles[part][t]
    eighth = lax.broadcasted_iota(jnp.int32, (80, 128), 1) // BLK
    for ref, which in ((give_ref, 1 - core), (keep_ref, core)):
        for group in range(2):
            slab = None
            for u in range(8):
                block = table[10, which * (USED // 2) + group * 8 + u]
                column = pl.multiple_of(block // 8 * 128, 128)
                by = lax.rem(u * BLK + 128 - lax.rem(block, 8) * BLK, 128)
                turned = pltpu.roll(columns_ref[:, pl.ds(column, 128)], by, 1)
                slab = turned if slab is None else jnp.where(eighth == u, turned, slab)
            ref[:, group * 128 : (group + 1) * 128] = slab


def unpack_call(place, table, pieces):
    return pl.pallas_call(
        unpack_kernel,
        out_shape=(
            jax.ShapeDtypeStruct((80, 1024), jnp.float32),
            jax.ShapeDtypeStruct((80, HALF), jnp.float32),
            jax.ShapeDtypeStruct((80, HALF), jnp.float32),
        ),
        in_specs=[SMEM, SMEM, VMEM],
        out_specs=(VMEM, VMEM, VMEM),
        name="unpack",
    )(place, table, pieces)


def shard_kernel(place, keep_ref, take_ref, out_ref):
    core = place[3]
    for part in range(2):
        out_ref[pl.ds(pl.multiple_of(part * 80 + core * 40, 8), 40), :] = keep_ref[part * 40 : part * 40 + 40, :]
        out_ref[pl.ds(pl.multiple_of(part * 80 + 40 - core * 40, 8), 40), :] = take_ref[part * 40 : part * 40 + 40, :]


def shard_call(place, keep, take):
    return pl.pallas_call(
        shard_kernel,
        out_shape=jax.ShapeDtypeStruct((160, HALF), jnp.float32),
        in_specs=[SMEM, VMEM, VMEM],
        out_specs=VMEM,
        name="shard",
    )(place, keep, take)


def after(array, *others):
    return lax.optimization_barrier((array, *others))[0]


def shards(densities, screened, pairs, owners):
    span = screened.shape[2]
    place = jnp.stack([lax.axis_index(axis) for axis in ("z", "x", "y", "core")]).astype(jnp.int32)
    shift = lambda array, axis, by: lax.ppermute(array, axis, ring(lax.axis_size(axis), by))
    swap = lambda array: lax.ppermute(array, "core", SWAP)
    join = lambda *arrays: jnp.concatenate(arrays, axis=0)
    hold = lax.optimization_barrier

    pieces = pack_call(place, densities, swap(densities))
    table = plan_call(place, after(pairs, pieces), owners.reshape(1, -1))
    mine = lax.all_to_all(pieces.reshape(32, 1, -1), ("z", "y"), 0, 0, tiled=True).reshape(pieces.shape)

    screen = screened.reshape(2 * 4 * span, -1)
    mine, other = hold((mine, swap(after(screen, pieces))))

    columns, keep, give = unpack_call(place, table, mine)
    shard = shard_call(place, keep, swap(give))

    block = 2 * SPAN
    below, above = shift(shard, "z", 1), shift(shard, "z", -1)
    around = [columns] + [shift(columns, "x", by) for by in (1, 2, 3)]
    swapped = [swap(columns)]
    below, above, around[1], swapped[0] = hold((below, above, around[1], swapped[0]))

    first = join(shard, below, above)
    below2, above2 = shift(below, "z", 1), shift(above, "z", -1)
    first_down, first_up = shift(first, "y", 1), shift(first, "y", -1)
    screens = screen_call(place, after(screen, first), other)
    below2, above2, first_down, first_up, around[3], *screens = hold(
        (below2, above2, first_down, first_up, around[3], *screens)
    )

    second = join(below2, above2)
    below3, above3 = shift(below2, "z", 1), shift(above2, "z", -1)
    second_down, second_up = shift(second, "y", 1), shift(second, "y", -1)
    below3, above3, second_down, second_up, *around = hold((below3, above3, second_down, second_up, *around))

    two_down = shift(join(first_down[: 3 * SPAN], second_down[:block]), "y", 1)
    two_up = shift(join(first_up[3 * SPAN :], second_up[block:]), "y", -1)
    z_below = shift(join(second_down[:block], second_up[:block], below3[:SPAN]), "z", 1)
    z_above = shift(join(second_down[block:], second_up[block:], above3[SPAN:]), "z", -1)
    swapped.append(swap(around[1]))
    two_down, two_up, z_below, z_above, swapped[1] = hold((two_down, two_up, z_below, z_above, swapped[1]))

    y_below, y_above = shift(z_below[:block], "y", 1), shift(z_above[block : 2 * block], "y", -1)
    far_below, far_above = shift(z_below[:block], "z", 1), shift(z_above[block : 2 * block], "z", -1)
    rights = (first, first_down, first_up, second, second_down, second_up, two_down, two_up)
    total = group_call(near_units, len(NEAR), place, rights, screens[:2], ())
    third = swap(after(around[3], two_down))
    y_below, y_above, far_below, far_above, total, third = hold((y_below, y_above, far_below, far_above, total, third))

    across_low, across_high = shift(far_below[:SPAN], "y", 1), shift(far_above[SPAN:], "y", -1)
    rights = (below3, above3, z_below, z_above, y_below, y_above)
    total = group_call(middle_units, len(MIDDLE), place, rights, screens[2:4], (total,))
    swapped += [swap(after(around[2], third)), third]
    left_high, left_low = left_call(place, list(around) + swapped)
    across_low, across_high, total, left_high, left_low = hold((across_low, across_high, total, left_high, left_low))
    rights = (z_below, z_above, far_below, far_above, across_low, across_high)
    parts = pair_call(place, table, rights, screens[4:], total, left_high, left_low)

    parts = lax.all_to_all(parts, ("core", "x"), 0, 0, tiled=True)
    parts = owner_call(place, table, parts)
    parts = lax.all_to_all(parts, ("z", "y"), 0, 0, tiled=True)
    return last_call(place, table, parts).reshape(1, CAP, 2, 4, BLK)


def solution(mesh):
    fine = Mesh(mesh.devices.reshape(8, 4, 2, 4), ("z", "y", "core", "x"))
    in_specs = (P(None, BAND, "x"), P(None, None, BAND, "x"), P(), P())
    out_specs = P(BAND, None, None, "x", None)
    return jax.shard_map(shards, mesh=fine, in_specs=in_specs, out_specs=out_specs, check_vma=False)
```

time: 178 us -> 160 us (0.90)
  waiting for transfers between devices: 54.8 us -> 34.6 us
  blocking collectives: 30.1 us -> 37.3 us
  starting transfers between devices: 36.8 us -> 42.4 us
  local copies, waits for them, and re-layouts: 6.73 us -> 2.29 us
  other arithmetic: 4.42 us -> 1.69 us
    ppermute x17 -> x23, waiting for transfers between devices: 36.7 us -> 19 us  [shards(): lax.ppermute(array, axis, ring(lax.axis_size(axis), by))]
    all_to_all x1, blocking collectives: 11.3 us -> 17.4 us  [shards(): parts = lax.all_to_all(parts, ('core', 'x'), 0, 0, tiled=True)]
    ppermute x17 -> x23, starting transfers between devices: 25 us -> 30.4 us  [shards(): lax.ppermute(array, axis, ring(lax.axis_size(axis), by))]
    unnamed x22 -> x11, local copies, waits for them, and re-layouts: 5.04 us -> 0.65 us
    reduce_sum x7 -> x0, other arithmetic: 3.42 us -> none  [the longest x1 0.94 us: plan(): place = jnp.sum(ahead.astype(jnp.int32), axis=1)]
    all_to_all x1, waiting for transfers between devices: 13.3 us -> 11.1 us  [shards(): lax.all_to_all(pieces.reshape(32, 1, -1), ('z', 'y'), 0, 0, tiled=True)]
    ppermute x6 -> x7, waiting for transfers between devices: 4.77 us -> 4.45 us  [shards(): swap = lambda array: lax.ppermute(array, 'core', SWAP)]
  transfers between devices with their start and end apart: 24 -> 31, of which waited for: 12 -> 15; matrix products, arithmetic and copies ran while one was open for 4% -> 1% of each run, Pallas kernels for 11% -> 13%
where the time goes in v7:
time: 160 us
  starting transfers between devices  42.4 us (26%)
  Pallas kernels  41 us (26%)
  blocking collectives  37.3 us (23%)
  waiting for transfers between devices  34.6 us (22%)
  local copies, waits for them, and re-layouts  2.29 us (1%)
  other arithmetic  1.69 us (1%)
    ppermute x23, starting transfers between devices, shards(): lax.ppermute(array, axis, ring(lax.axis_size(axis), by))  30.4 us
    all_to_all x1, blocking collectives, shards(): parts = lax.all_to_all(parts, ('z', 'y'), 0, 0, tiled=True)  19.8 us
    ppermute x23, waiting for transfers between devices, shards(): lax.ppermute(array, axis, ring(lax.axis_size(axis), by))  19 us
    all_to_all x1, blocking collectives, shards(): parts = lax.all_to_all(parts, ('core', 'x'), 0, 0, tiled=True)  17.4 us
    all_to_all x1, starting transfers between devices, shards(): lax.all_to_all(pieces.reshape(32, 1, -1), ('z', 'y'), 0, 0, tiled=True)  11.6 us
    pallas_call x1, Pallas kernels, pair_call(): pl.pallas_call(pair_kernel, out_shape=jax.ShapeDtypeStruct((8, 8, ROOM *...  11.2 us
    all_to_all x1, waiting for transfers between devices, shards(): lax.all_to_all(pieces.reshape(32, 1, -1), ('z', 'y'), 0, 0, tiled=True)  11.1 us
    pallas_call x1, Pallas kernels, screen_call(): pl.pallas_call(screen_kernel, out_shape=shapes, in_specs=[SMEM, VMEM, VME...  7.35 us
  transfers between devices with their start and end apart: 31, of which 15 were waited for; matrix products, arithmetic and copies ran while one was open for 1% of the time, Pallas kernels for 13%

profile of v7, /device:TPU:2, one launch (start us, length us, event | category | flops | bytes accessed | tf_op | source)
XLA Modules:
  0.0 159.5 jit_solution(4617510680617833324)
XLA Ops:
  2.0 2.3 %pack.1 = f32[640,128]{1,0:T(8,128)} custom-call(s32[4]{0:T(128)} %pad_add_fusion.place, f32[2,16,2560]{2,1,0:T(8,128)} %own_ref.1, f32[2,16,2560]{2,1,0:T(8,128)} %collective-permute-done.other_ref), custom_call_target="tpu_custom_call" | custom-call | tf_op jit(solution)/shard_map/pack/pallas_call | solution.py:380
  4.4 11.6 %all-to-all-start = ((f32[32,1,2560]{2,1,0:T(1,128)}), f32[32,1,2560]{2,1,0:T(1,128)}, u32[]{:S(2)}, u32[]{:S(2)}) async-start(f32[32,1,2560]{2,1,0:T(1,128)} %bitcast.11), calls=%async_computation | async-start | bytes 655360 | tf_op jit(solution)/shard_map/all_to_all | solution.py:469
  17.5 2.2 %plan.1.table = s32[16,256]{1,0:T(8,128)} custom-call(s32[4]{0:T(128)} %pad_add_fusion.place, s32[256,2]{1,0:T(8,128)} %copy.6.pairs_ref, s32[1,256]{1,0:T(1,128)} %bitcast.12), custom_call_target="tpu_custom_call" | custom-call | tf_op jit(solution)/shard_map/plan/pallas_call | solution.py:96
  19.7 11.1 %all-to-all-done = f32[32,1,2560]{2,1,0:T(1,128)} async-done(((f32[32,1,2560]{2,1,0:T(1,128)}), f32[32,1,2560]{2,1,0:T(1,128)}, u32[]{:S(2)}, u32[]{:S(2)}) %all-to-all-start) | async-done | bytes 327712 | tf_op jit(solution)/shard_map/all_to_all | solution.py:469
  30.8 3.2 %unpack.1 = (f32[80,1024]{1,0:T(8,128)}, f32[80,256]{1,0:T(8,128)}, f32[80,256]{1,0:T(8,128)}) custom-call(s32[4]{0:T(128)} %pad_add_fusion.place, s32[16,256]{1,0:T(8,128)} %plan.1.table, f32[640,128]{1,0:T(8,128)} %bitcast.6.in_ref), custom_call_target="tpu_custom_call" | custom-call | tf_op jit(solution)/shard_map/unpack/pallas_call | solution.py:425
  34.0 1.5 collective-permute-start.5
  37.6 1.6 %shard.1 = f32[160,256]{1,0:T(8,128)} custom-call(s32[4]{0:T(128)} %pad_add_fusion.place, f32[80,256]{1,0:T(8,128)} %get-tuple-element.65.keep_ref, f32[80,256]{1,0:T(8,128)} %copy-done.4), custom_call_target="tpu_custom_call" | custom-call | tf_op jit(solution)/shard_map/shard/pallas_call | solution.py:446
  39.5 1.8 %collective-permute-start.3 = (f32[160,256]{1,0:T(8,128)}, f32[160,256]{1,0:T(8,128)S(1)}, u32[]{:S(2)}, u32[]{:S(2)}) collective-permute-start(f32[160,256]{1,0:T(8,128)} %shard.1), channel_id=1, source_target_pairs={{0,32},{32,64},{64,96},{96,128},{128,160},{160,192},{192,224},{224... | collective-permute-start | bytes 491528 | tf_op jit(solution)/shard_map/ppermute | solution.py:462
  41.3 4.5 %collective-permute-done.4 = f32[160,256]{1,0:T(8,128)S(1)} collective-permute-done((f32[160,256]{1,0:T(8,128)}, f32[160,256]{1,0:T(8,128)S(1)}, u32[]{:S(2)}, u32[]{:S(2)}) %collective-permute-start.4) | collective-permute-done | bytes 163872 | tf_op jit(solution)/shard_map/ppermute | solution.py:462
  51.2 2.7 %collective-permute-start.8 = (f32[160,256]{1,0:T(8,128)S(1)}, f32[160,256]{1,0:T(8,128)S(1)}, u32[]{:S(2)}, u32[]{:S(2)}) collective-permute-start(f32[160,256]{1,0:T(8,128)S(1)} %collective-permute-done.4), channel_id=1, source_target_pairs={{0,224},{32,0},{64,32},{96,64},{128,96},{160,128},{192,160},{224,1... | collective-permute-start | bytes 491528 | tf_op jit(solution)/shard_map/ppermute | solution.py:462
  53.9 7.3 %screen.1 = (bf16[640,1664]{1,0:T(8,128)(2,1)S(1)}, bf16[640,1664]{1,0:T(8,128)(2,1)S(1)}, bf16[640,640]{1,0:T(8,128)(2,1)S(1)}, bf16[640,640]{1,0:T(8,128)(2,1)...) custom-call(s32[4]{0:T(128)S(1)} %copy-done.3, f32[320,2560]{1,0:T(8,128)S(1)} %bitcast.10, ...), custom_call_target="tpu_custom_call" | custom-call | tf_op jit(solution)/shard_map/screen/pallas_call | solution.py:152
  61.2 2.2 %collective-permute-start.16 = (f32[80,1024]{1,0:T(8,128)S(1)}, f32[80,1024]{1,0:T(8,128)S(1)}, u32[]{:S(2)}, u32[]{:S(2)}) collective-permute-start(f32[80,1024]{1,0:T(8,128)S(1)} %copy-done.2), channel_id=1, source_target_pairs={{0,2},{1,3},{2,0},{3,1},{4,6},{5,7},{6,4},{7,5},{8,10},{9,11},{10,... | collective-permute-start | bytes 983048 | tf_op jit(solution)/shard_map/ppermute | solution.py:462
  63.5 2.8 %collective-permute-start.15 = (f32[320,256]{1,0:T(8,128)S(1)}, f32[320,256]{1,0:T(8,128)S(1)}, u32[]{:S(2)}, u32[]{:S(2)}) collective-permute-start(f32[320,256]{1,0:T(8,128)S(1)} %constant_dynamic-update-slice_fusion.refs_3_), channel_id=1, source_target_pairs={{0,24},{8,0},{16,8},{24,16},{1,25},{9,1},{17,9},{25,17},{2,26},{10... | collective-permute-start | bytes 983048 | tf_op jit(solution)/shard_map/ppermute | solution.py:462
  66.3 3.2 %collective-permute-start.13 = (f32[160,256]{1,0:T(8,128)S(1)}, f32[160,256]{1,0:T(8,128)S(1)}, u32[]{:S(2)}, u32[]{:S(2)}) collective-permute-start(f32[160,256]{1,0:T(8,128)S(1)} %collective-permute-done.8), channel_id=1, source_target_pairs={{0,224},{32,0},{64,32},{96,64},{128,96},{160,128},{192,160},{224,1... | collective-permute-start | bytes 491528 | tf_op jit(solution)/shard_map/ppermute | solution.py:462
  70.2 2.6 %collective-permute-done.12.refs_0_ = f32[160,256]{1,0:T(8,128)S(1)} collective-permute-done((f32[160,256]{1,0:T(8,128)S(1)}, f32[160,256]{1,0:T(8,128)S(1)}, u32[]{:S(2)}, u32[]{:S(2)}) %collective-permute-start.12) | collective-permute-done | bytes 163872 | tf_op jit(solution)/shard_map/ppermute | solution.py:462
  72.9 1.7 %collective-permute-done.14.refs_4_ = f32[320,256]{1,0:T(8,128)S(1)} collective-permute-done((f32[320,256]{1,0:T(8,128)S(1)}, f32[320,256]{1,0:T(8,128)S(1)}, u32[]{:S(2)}, u32[]{:S(2)}) %collective-permute-start.14) | collective-permute-done | bytes 327712 | tf_op jit(solution)/shard_map/ppermute | solution.py:462
  74.8 1.6 collective-permute-start.20
  76.3 3.2 %collective-permute-start.18 = (f32[400,256]{1,0:T(8,128)S(1)}, f32[400,256]{1,0:T(8,128)S(1)}, u32[]{:S(2)}, u32[]{:S(2)}) collective-permute-start(f32[400,256]{1,0:T(8,128)S(1)} %get-tuple-element.124), channel_id=1, source_target_pairs={{0,24},{8,0},{16,8},{24,16},{1,25},{9,1},{17,9},{25,17},{2,26},{10... | collective-permute-start | bytes 1228808 | tf_op jit(solution)/shard_map/ppermute | solution.py:462
  79.9 1.8 %collective-permute-done.21.refs_5_ = f32[80,1024]{1,0:T(8,128)S(1)} collective-permute-done((f32[80,1024]{1,0:T(8,128)}, f32[80,1024]{1,0:T(8,128)S(1)}, u32[]{:S(2)}, u32[]{:S(2)}) %collective-permute-start.21) | collective-permute-done | bytes 327712 | tf_op jit(solution)/shard_map/ppermute | solution.py:463
  82.8 2.3 %collective-permute-done.18.refs_7_ = f32[400,256]{1,0:T(8,128)S(1)} collective-permute-done((f32[400,256]{1,0:T(8,128)S(1)}, f32[400,256]{1,0:T(8,128)S(1)}, u32[]{:S(2)}, u32[]{:S(2)}) %collective-permute-start.18) | collective-permute-done | bytes 409632 | tf_op jit(solution)/shard_map/ppermute | solution.py:462
  85.0 3.8 %collective-permute-done.19.refs_2_.refs_0_ = f32[400,256]{1,0:T(8,128)S(1)} collective-permute-done((f32[400,256]{1,0:T(8,128)S(1)}, f32[400,256]{1,0:T(8,128)S(1)}, u32[]{:S(2)}, u32[]{:S(2)}) %collective-permute-start.19) | collective-permute-done | bytes 409632 | tf_op jit(solution)/shard_map/ppermute | solution.py:462
  89.0 3.2 %collective-permute-start.25 = (f32[160,256]{1,0:T(8,128)S(1)}, f32[160,256]{1,0:T(8,128)S(1)}, u32[]{:S(2)}, u32[]{:S(2)}) collective-permute-start(f32[160,256]{1,0:T(8,128)S(1)} %slice.49), channel_id=1, source_target_pairs={{0,224},{32,0},{64,32},{96,64},{128,96},{160,128},{192,160},{224,1... | collective-permute-start | bytes 491528 | tf_op jit(solution)/shard_map/ppermute | solution.py:462
  92.3 2.3 %collective-permute-start.22 = (f32[160,256]{1,0:T(8,128)S(1)}, f32[160,256]{1,0:T(8,128)S(1)}, u32[]{:S(2)}, u32[]{:S(2)}) collective-permute-start(f32[160,256]{1,0:T(8,128)S(1)} %slice.48), channel_id=1, source_target_pairs={{0,8},{8,16},{16,24},{24,0},{1,9},{9,17},{17,25},{25,1},{2,10},{10... | collective-permute-start | bytes 491528 | tf_op jit(solution)/shard_map/ppermute | solution.py:462
  94.7 4.4 %group.2.refs_8_ = f32[640,512]{1,0:T(8,128)S(1)} custom-call(s32[4]{0:T(128)S(1)} %copy-done.3, f32[480,256]{1,0:T(8,128)S(1)} %pad_maximum_fusion.refs_0_, f32[480,256]{1,0:T(8,128)S(1)} %collective-permute-done.9.refs_1_, f32[480,256]{1,0:T(8,128)S(1)} %collective-permute-done.10.refs_2_, f32[320,256]{1,0:T(8,128)S(1)} %constant_dynamic-update-slice_fusion.refs_3_, ...), custom_call_target="tpu_custom_call" | custom-call | tf_op jit(solution)/shard_map/group/pallas_call | solution.py:247
  100.6 1.7 %collective-permute-start.27 = (f32[80,256]{1,0:T(8,128)S(1)}, f32[80,256]{1,0:T(8,128)S(1)}, u32[]{:S(2)}, u32[]{:S(2)}) collective-permute-start(f32[80,256]{1,0:T(8,128)S(1)} %slice.50), channel_id=1, source_target_pairs={{0,8},{8,16},{16,24},{24,0},{1,9},{9,17},{17,25},{25,1},{2,10},{10... | collective-permute-start | bytes 245768 | tf_op jit(solution)/shard_map/ppermute | solution.py:462
  102.3 2.4 %group.3.refs_8_ = f32[640,512]{1,0:T(8,128)S(1)} custom-call(s32[4]{0:T(128)S(1)} %copy-done.3, f32[160,256]{1,0:T(8,128)S(1)} %collective-permute-done.12.refs_0_, f32[160,256]{1,0:T(8,128)S(1)} %collective-permute-done.13.refs_1_, f32[400,256]{1,0:T(8,128)S(1)} %collective-permute-done.19.refs_2_.refs_0_, ...), custom_call_target="tpu_custom_call" | custom-call | tf_op jit(solution)/shard_map/group/pallas_call | solution.py:247
  104.7 2.4 %left.1 = (bf16[1024,640]{1,0:T(8,128)(2,1)S(1)}, bf16[1024,640]{1,0:T(8,128)(2,1)S(1)}) custom-call(s32[4]{0:T(128)S(1)} %copy-done.3, f32[80,1024]{1,0:T(8,128)S(1)} %copy-done.2, f32[80,1024]{1,0:T(8,128)} %collective-permute-done.5.refs_1_, f32[80,1024]{1,0:T(8,128)S(1)} %collective-permute-done.16.refs_2_, ...), custom_call_target="tpu_custom_call" | custom-call | tf_op jit(solution)/shard_map/left/pallas_call | solution.py:182
  107.1 11.2 %pair.1 = f32[8,8,3584]{2,1,0:T(8,128)S(1)} custom-call(s32[4]{0:T(128)S(1)} %copy-done.3, s32[16,256]{1,0:T(8,128)S(1)} %copy-done.1, f32[400,256]{1,0:T(8,128)S(1)} %collective-permute-done.19.refs_2_.refs_0_, f32[400,256]{1,0:T(8,128)S(1)} %collective-permute-done.20.refs_3_.refs_1_, f32[160,256]{1,0:T(8,128)S(1)} %collective-permute-done.24.refs_2_, ...), custom_call_target="tpu_custom_call" | custom-call | tf_op jit(solution)/shard_map/pair/pallas_call | solution.py:299
  118.2 17.4 %all_to_all.15.parts_ref = f32[8,8,3584]{2,1,0:T(8,128)} all-to-all(f32[8,8,3584]{2,1,0:T(8,128)S(1)} %pair.1), channel_id=1, replica_groups=mesh['z'=8,'y'=4,'core'=2,'x'=4] {'core','x'}, dimensions={0} | all-to-all | bytes 1835008 | tf_op jit(solution)/shard_map/all_to_all | solution.py:519
  135.7 2.3 %owner.1 = f32[32,8,256]{2,1,0:T(8,128)} custom-call(s32[4]{0:T(128)} %pad_add_fusion.place, s32[16,256]{1,0:T(8,128)} %plan.1.table, f32[8,8,3584]{2,1,0:T(8,128)} %all_to_all.15.parts_ref), custom_call_target="tpu_custom_call" | custom-call | tf_op jit(solution)/shard_map/owner/pallas_call | solution.py:326
  138.0 19.8 %all_to_all.16.parts_ref = f32[32,8,256]{2,1,0:T(8,128)} all-to-all(f32[32,8,256]{2,1,0:T(8,128)} %owner.1), channel_id=1, replica_groups=mesh['z'=8,'y'=4,'core'=2,'x'=4] {'z','y'}, dimensions={0} | all-to-all | bytes 524288 | tf_op jit(solution)/shard_map/all_to_all | solution.py:521
  157.8 1.7 %last.1 = f32[12,8,16]{2,1,0:T(8,128)} custom-call(s32[4]{0:T(128)} %pad_add_fusion.place, s32[16,256]{1,0:T(8,128)} %plan.1.table, f32[32,8,256]{2,1,0:T(8,128)} %all_to_all.16.parts_ref), custom_call_target="tpu_custom_call" | custom-call | tf_op jit(solution)/shard_map/last/pallas_call | solution.py:348
  (69 shorter events, 15.1 us)
Async XLA Ops:
  0.0 53.9 %copy-start = (f32[2,4,40,2560]{3,2,1,0:T(8,128)S(1)}, f32[2,4,40,2560]{3,2,1,0:T(8,128)}, u32[]{:S(2)}) copy-start(f32[2,4,40,2560]{3,2,1,0:T(8,128)} %param.5) | copy-start | bytes 9830404
  0.0 2.0 %collective-permute-start = (f32[2,16,2560]{2,1,0:T(8,128)}, f32[2,16,2560]{2,1,0:T(8,128)}, u32[]{:S(2)}, u32[]{:S(2)}) collective-permute-start(f32[2,16,2560]{2,1,0:T(8,128)} %own_ref.1), channel_id=1, source_target_pairs={{0,4},{4,0},{1,5},{5,1},{2,6},{6,2},{3,7},{7,3},{8,12},{12,8},{9,1... | collective-permute-start | bytes 983048 | tf_op jit(solution)/shard_map/ppermute | solution.py:463
  4.2 26.6 %collective-permute-start.1 = (f32[320,2560]{1,0:T(8,128)}, f32[320,2560]{1,0:T(8,128)}, u32[]{:S(2)}, u32[]{:S(2)}) collective-permute-start(f32[320,2560]{1,0:T(8,128)} %bitcast.9), channel_id=1, source_target_pairs={{0,4},{4,0},{1,5},{5,1},{2,6},{6,2},{3,7},{7,3},{8,12},{12,8},{9,1... | collective-permute-start | bytes 9830408 | tf_op jit(solution)/shard_map/ppermute | solution.py:463
  4.4 26.4 %all-to-all-start = ((f32[32,1,2560]{2,1,0:T(1,128)}), f32[32,1,2560]{2,1,0:T(1,128)}, u32[]{:S(2)}, u32[]{:S(2)}) async-start(f32[32,1,2560]{2,1,0:T(1,128)} %bitcast.11), calls=%async_computation | async-start | bytes 655360 | tf_op jit(solution)/shard_map/all_to_all | solution.py:469
  34.0 13.0 %collective-permute-start.6 = (f32[80,1024]{1,0:T(8,128)}, f32[80,1024]{1,0:T(8,128)}, u32[]{:S(2)}, u32[]{:S(2)}) collective-permute-start(f32[80,1024]{1,0:T(8,128)} %get-tuple-element.104.refs_0_), channel_id=1, source_target_pairs={{0,4},{4,0},{1,5},{5,1},{2,6},{6,2},{3,7},{7,3},{8,12},{12,8},{9,1... | collective-permute-start | bytes 983048 | tf_op jit(solution)/shard_map/ppermute | solution.py:463
  34.0 13.0 %collective-permute-start.5 = (f32[80,1024]{1,0:T(8,128)}, f32[80,1024]{1,0:T(8,128)}, u32[]{:S(2)}, u32[]{:S(2)}) collective-permute-start(f32[80,1024]{1,0:T(8,128)} %get-tuple-element.104.refs_0_), channel_id=1, source_target_pairs={{0,1},{1,2},{2,3},{3,0},{4,5},{5,6},{6,7},{7,4},{8,9},{9,10},{10,1... | collective-permute-start | bytes 983048 | tf_op jit(solution)/shard_map/ppermute | solution.py:462
  35.5 1.5 collective-permute-start.2
  39.3 6.5 %collective-permute-start.4 = (f32[160,256]{1,0:T(8,128)}, f32[160,256]{1,0:T(8,128)S(1)}, u32[]{:S(2)}, u32[]{:S(2)}) collective-permute-start(f32[160,256]{1,0:T(8,128)} %shard.1), channel_id=1, source_target_pairs={{0,224},{32,0},{64,32},{96,64},{128,96},{160,128},{192,160},{224,1... | collective-permute-start | bytes 491528 | tf_op jit(solution)/shard_map/ppermute | solution.py:462
  39.5 7.6 %collective-permute-start.3 = (f32[160,256]{1,0:T(8,128)}, f32[160,256]{1,0:T(8,128)S(1)}, u32[]{:S(2)}, u32[]{:S(2)}) collective-permute-start(f32[160,256]{1,0:T(8,128)} %shard.1), channel_id=1, source_target_pairs={{0,32},{32,64},{64,96},{96,128},{128,160},{160,192},{192,224},{224... | collective-permute-start | bytes 491528 | tf_op jit(solution)/shard_map/ppermute | solution.py:462
  48.0 15.5 %collective-permute-start.10 = (f32[480,256]{1,0:T(8,128)S(1)}, f32[480,256]{1,0:T(8,128)S(1)}, u32[]{:S(2)}, u32[]{:S(2)}) collective-permute-start(f32[480,256]{1,0:T(8,128)S(1)} %pad_maximum_fusion.refs_0_), channel_id=1, source_target_pairs={{0,24},{8,0},{16,8},{24,16},{1,25},{9,1},{17,9},{25,17},{2,26},{10... | collective-permute-start | bytes 1474568 | tf_op jit(solution)/shard_map/ppermute | solution.py:462
  49.4 14.1 %collective-permute-start.9 = (f32[480,256]{1,0:T(8,128)S(1)}, f32[480,256]{1,0:T(8,128)S(1)}, u32[]{:S(2)}, u32[]{:S(2)}) collective-permute-start(f32[480,256]{1,0:T(8,128)S(1)} %pad_maximum_fusion.refs_0_), channel_id=1, source_target_pairs={{0,8},{8,16},{16,24},{24,0},{1,9},{9,17},{17,25},{25,1},{2,10},{10... | collective-permute-start | bytes 1474568 | tf_op jit(solution)/shard_map/ppermute | solution.py:462
  50.1 11.1 %collective-permute-start.11 = (f32[80,1024]{1,0:T(8,128)}, f32[80,1024]{1,0:T(8,128)S(1)}, u32[]{:S(2)}, u32[]{:S(2)}) collective-permute-start(f32[80,1024]{1,0:T(8,128)} %get-tuple-element.104.refs_0_), channel_id=1, source_target_pairs={{0,3},{1,0},{2,1},{3,2},{4,7},{5,4},{6,5},{7,6},{8,11},{9,8},{10,9... | collective-permute-start | bytes 983048 | tf_op jit(solution)/shard_map/ppermute | solution.py:462
  50.6 12.8 %collective-permute-start.7 = (f32[160,256]{1,0:T(8,128)S(1)}, f32[160,256]{1,0:T(8,128)S(1)}, u32[]{:S(2)}, u32[]{:S(2)}) collective-permute-start(f32[160,256]{1,0:T(8,128)S(1)} %collective-permute-done.3), channel_id=1, source_target_pairs={{0,32},{32,64},{64,96},{96,128},{128,160},{160,192},{192,224},{224... | collective-permute-start | bytes 491528 | tf_op jit(solution)/shard_map/ppermute | solution.py:462
  51.2 12.3 %collective-permute-start.8 = (f32[160,256]{1,0:T(8,128)S(1)}, f32[160,256]{1,0:T(8,128)S(1)}, u32[]{:S(2)}, u32[]{:S(2)}) collective-permute-start(f32[160,256]{1,0:T(8,128)S(1)} %collective-permute-done.4), channel_id=1, source_target_pairs={{0,224},{32,0},{64,32},{96,64},{128,96},{160,128},{192,160},{224,1... | collective-permute-start | bytes 491528 | tf_op jit(solution)/shard_map/ppermute | solution.py:462
  61.2 9.0 %collective-permute-start.16 = (f32[80,1024]{1,0:T(8,128)S(1)}, f32[80,1024]{1,0:T(8,128)S(1)}, u32[]{:S(2)}, u32[]{:S(2)}) collective-permute-start(f32[80,1024]{1,0:T(8,128)S(1)} %copy-done.2), channel_id=1, source_target_pairs={{0,2},{1,3},{2,0},{3,1},{4,6},{5,7},{6,4},{7,5},{8,10},{9,11},{10,... | collective-permute-start | bytes 983048 | tf_op jit(solution)/shard_map/ppermute | solution.py:462
  63.5 9.3 %collective-permute-start.15 = (f32[320,256]{1,0:T(8,128)S(1)}, f32[320,256]{1,0:T(8,128)S(1)}, u32[]{:S(2)}, u32[]{:S(2)}) collective-permute-start(f32[320,256]{1,0:T(8,128)S(1)} %constant_dynamic-update-slice_fusion.refs_3_), channel_id=1, source_target_pairs={{0,24},{8,0},{16,8},{24,16},{1,25},{9,1},{17,9},{25,17},{2,26},{10... | collective-permute-start | bytes 983048 | tf_op jit(solution)/shard_map/ppermute | solution.py:462
  66.3 8.3 %collective-permute-start.14 = (f32[320,256]{1,0:T(8,128)S(1)}, f32[320,256]{1,0:T(8,128)S(1)}, u32[]{:S(2)}, u32[]{:S(2)}) collective-permute-start(f32[320,256]{1,0:T(8,128)S(1)} %constant_dynamic-update-slice_fusion.refs_3_), channel_id=1, source_target_pairs={{0,8},{8,16},{16,24},{24,0},{1,9},{9,17},{17,25},{25,1},{2,10},{10... | collective-permute-start | bytes 983048 | tf_op jit(solution)/shard_map/ppermute | solution.py:462
  66.3 6.5 %collective-permute-start.12 = (f32[160,256]{1,0:T(8,128)S(1)}, f32[160,256]{1,0:T(8,128)S(1)}, u32[]{:S(2)}, u32[]{:S(2)}) collective-permute-start(f32[160,256]{1,0:T(8,128)S(1)} %collective-permute-done.7), channel_id=1, source_target_pairs={{0,32},{32,64},{64,96},{96,128},{128,160},{160,192},{192,224},{224... | collective-permute-start | bytes 491528 | tf_op jit(solution)/shard_map/ppermute | solution.py:462
  66.3 6.5 %collective-permute-start.13 = (f32[160,256]{1,0:T(8,128)S(1)}, f32[160,256]{1,0:T(8,128)S(1)}, u32[]{:S(2)}, u32[]{:S(2)}) collective-permute-start(f32[160,256]{1,0:T(8,128)S(1)} %collective-permute-done.8), channel_id=1, source_target_pairs={{0,224},{32,0},{64,32},{96,64},{128,96},{160,128},{192,160},{224,1... | collective-permute-start | bytes 491528 | tf_op jit(solution)/shard_map/ppermute | solution.py:462
  74.8 8.0 %collective-permute-start.20 = (f32[400,256]{1,0:T(8,128)S(1)}, f32[400,256]{1,0:T(8,128)S(1)}, u32[]{:S(2)}, u32[]{:S(2)}) collective-permute-start(f32[400,256]{1,0:T(8,128)S(1)} %get-tuple-element.123), channel_id=1, source_target_pairs={{0,224},{32,0},{64,32},{96,64},{128,96},{160,128},{192,160},{224,1... | collective-permute-start | bytes 1228808 | tf_op jit(solution)/shard_map/ppermute | solution.py:462
  76.3 8.7 %collective-permute-start.18 = (f32[400,256]{1,0:T(8,128)S(1)}, f32[400,256]{1,0:T(8,128)S(1)}, u32[]{:S(2)}, u32[]{:S(2)}) collective-permute-start(f32[400,256]{1,0:T(8,128)S(1)} %get-tuple-element.124), channel_id=1, source_target_pairs={{0,24},{8,0},{16,8},{24,16},{1,25},{9,1},{17,9},{25,17},{2,26},{10... | collective-permute-start | bytes 1228808 | tf_op jit(solution)/shard_map/ppermute | solution.py:462
  79.6 9.2 %collective-permute-start.19 = (f32[400,256]{1,0:T(8,128)S(1)}, f32[400,256]{1,0:T(8,128)S(1)}, u32[]{:S(2)}, u32[]{:S(2)}) collective-permute-start(f32[400,256]{1,0:T(8,128)S(1)} %get-tuple-element.125), channel_id=1, source_target_pairs={{0,32},{32,64},{64,96},{96,128},{128,160},{160,192},{192,224},{224... | collective-permute-start | bytes 1228808 | tf_op jit(solution)/shard_map/ppermute | solution.py:462
  79.7 9.2 %collective-permute-start.17 = (f32[400,256]{1,0:T(8,128)S(1)}, f32[400,256]{1,0:T(8,128)S(1)}, u32[]{:S(2)}, u32[]{:S(2)}) collective-permute-start(f32[400,256]{1,0:T(8,128)S(1)} %get-tuple-element.126), channel_id=1, source_target_pairs={{0,8},{8,16},{16,24},{24,0},{1,9},{9,17},{17,25},{25,1},{2,10},{10... | collective-permute-start | bytes 1228808 | tf_op jit(solution)/shard_map/ppermute | solution.py:462
  79.8 1.9 %collective-permute-start.21 = (f32[80,1024]{1,0:T(8,128)}, f32[80,1024]{1,0:T(8,128)S(1)}, u32[]{:S(2)}, u32[]{:S(2)}) collective-permute-start(f32[80,1024]{1,0:T(8,128)} %collective-permute-done.5.refs_1_), channel_id=1, source_target_pairs={{0,4},{4,0},{1,5},{5,1},{2,6},{6,2},{3,7},{7,3},{8,12},{12,8},{9,1... | collective-permute-start | bytes 983048 | tf_op jit(solution)/shard_map/ppermute | solution.py:463
  89.0 11.2 %collective-permute-start.26 = (f32[80,1024]{1,0:T(8,128)S(1)}, f32[80,1024]{1,0:T(8,128)S(1)}, u32[]{:S(2)}, u32[]{:S(2)}) collective-permute-start(f32[80,1024]{1,0:T(8,128)S(1)} %collective-permute-done.11.refs_3_), channel_id=1, source_target_pairs={{0,4},{4,0},{1,5},{5,1},{2,6},{6,2},{3,7},{7,3},{8,12},{12,8},{9,1... | collective-permute-start | bytes 983048 | tf_op jit(solution)/shard_map/ppermute | solution.py:463
  89.0 10.1 %collective-permute-start.25 = (f32[160,256]{1,0:T(8,128)S(1)}, f32[160,256]{1,0:T(8,128)S(1)}, u32[]{:S(2)}, u32[]{:S(2)}) collective-permute-start(f32[160,256]{1,0:T(8,128)S(1)} %slice.49), channel_id=1, source_target_pairs={{0,224},{32,0},{64,32},{96,64},{128,96},{160,128},{192,160},{224,1... | collective-permute-start | bytes 491528 | tf_op jit(solution)/shard_map/ppermute | solution.py:462
  92.2 6.9 %collective-permute-start.23 = (f32[160,256]{1,0:T(8,128)S(1)}, f32[160,256]{1,0:T(8,128)S(1)}, u32[]{:S(2)}, u32[]{:S(2)}) collective-permute-start(f32[160,256]{1,0:T(8,128)S(1)} %slice.49), channel_id=1, source_target_pairs={{0,24},{8,0},{16,8},{24,16},{1,25},{9,1},{17,9},{25,17},{2,26},{10... | collective-permute-start | bytes 491528 | tf_op jit(solution)/shard_map/ppermute | solution.py:462
  92.2 7.6 %collective-permute-start.24 = (f32[160,256]{1,0:T(8,128)S(1)}, f32[160,256]{1,0:T(8,128)S(1)}, u32[]{:S(2)}, u32[]{:S(2)}) collective-permute-start(f32[160,256]{1,0:T(8,128)S(1)} %slice.48), channel_id=1, source_target_pairs={{0,32},{32,64},{64,96},{96,128},{128,160},{160,192},{192,224},{224... | collective-permute-start | bytes 491528 | tf_op jit(solution)/shard_map/ppermute | solution.py:462
  92.3 7.8 %collective-permute-start.22 = (f32[160,256]{1,0:T(8,128)S(1)}, f32[160,256]{1,0:T(8,128)S(1)}, u32[]{:S(2)}, u32[]{:S(2)}) collective-permute-start(f32[160,256]{1,0:T(8,128)S(1)} %slice.48), channel_id=1, source_target_pairs={{0,8},{8,16},{16,24},{24,0},{1,9},{9,17},{17,25},{25,1},{2,10},{10... | collective-permute-start | bytes 491528 | tf_op jit(solution)/shard_map/ppermute | solution.py:462
  100.2 4.5 %collective-permute-start.29 = (f32[80,1024]{1,0:T(8,128)S(1)}, f32[80,1024]{1,0:T(8,128)S(1)}, u32[]{:S(2)}, u32[]{:S(2)}) collective-permute-start(f32[80,1024]{1,0:T(8,128)S(1)} %collective-permute-done.16.refs_2_), channel_id=1, source_target_pairs={{0,4},{4,0},{1,5},{5,1},{2,6},{6,2},{3,7},{7,3},{8,12},{12,8},{9,1... | collective-permute-start | bytes 983048 | tf_op jit(solution)/shard_map/ppermute | solution.py:463
  100.2 6.9 %collective-permute-start.28 = (f32[80,256]{1,0:T(8,128)S(1)}, f32[80,256]{1,0:T(8,128)S(1)}, u32[]{:S(2)}, u32[]{:S(2)}) collective-permute-start(f32[80,256]{1,0:T(8,128)S(1)} %slice.51), channel_id=1, source_target_pairs={{0,24},{8,0},{16,8},{24,16},{1,25},{9,1},{17,9},{25,17},{2,26},{10... | collective-permute-start | bytes 245768 | tf_op jit(solution)/shard_map/ppermute | solution.py:462
  100.6 6.5 %collective-permute-start.27 = (f32[80,256]{1,0:T(8,128)S(1)}, f32[80,256]{1,0:T(8,128)S(1)}, u32[]{:S(2)}, u32[]{:S(2)}) collective-permute-start(f32[80,256]{1,0:T(8,128)S(1)} %slice.50), channel_id=1, source_target_pairs={{0,8},{8,16},{16,24},{24,0},{1,9},{9,17},{17,25},{25,1},{2,10},{10... | collective-permute-start | bytes 245768 | tf_op jit(solution)/shard_map/ppermute | solution.py:462
  (4 other events, 69.5 us)

commit v8 on v7

--- a/solution.py
+++ b/solution.py
@@ -98,6 +98,7 @@
         out_shape=jax.ShapeDtypeStruct((16, pairs.shape[0]), jnp.int32),
         in_specs=[SMEM, VMEM, VMEM],
         out_specs=VMEM,
+        compiler_params=params(8),
         name="plan",
     )(place, pairs, owners)
 
@@ -256,7 +257,7 @@
 
 
 def pair_kernel(place, table, *refs):
-    rights, (high_ref, low_ref, sum_ref, left_high, left_low, out_ref, rh, rl, kern) = refs[:6], refs[6:]
+    rights, (high_ref, low_ref, sum_ref, left_high, left_low, give_ref, kern, rh, rl) = refs[:6], refs[6:]
     load_right(place, far_units(*rights), len(FAR), rh, rl)
     product = sum_ref[...] + dot3(high_ref[...], low_ref[...], rh[...], rl[...])
     mid = product.shape[0] // 2
@@ -267,12 +268,15 @@
     )
     kern[...] = dot3(left_high[...], left_low[...], *split(applied))
 
+    extract(table, 1 - place[3], kern, give_ref)
+
+
+def extract(table, half, kern, out_ref):
     lane = lax.broadcasted_iota(jnp.int32, (8, 128), 1) // BLK
     upper = lax.broadcasted_iota(jnp.int32, (8, 128), 0) < 4
-    out_ref[...] = jnp.zeros_like(out_ref)
-    for half in range(2):
-
-        def group(g, carry, half=half):
+
+    def groups(pair, carry):
+        for g in (pair * 2, pair * 2 + 1):
             tiles = [[jnp.zeros((8, 128), jnp.float32) for _ in range(2)] for _ in range(2)]
             for u in range(8):
                 slot = g * 8 + u
@@ -288,24 +292,58 @@
             lanes = pl.ds(pl.multiple_of(g * 128, 128), 128)
             for side in range(2):
                 real, imag = tiles[0][side], tiles[1][side]
-                out_ref[4 * half + 2 * side, :, lanes] = jnp.where(upper, real, pltpu.roll(imag, 4, 0))
-                out_ref[4 * half + 2 * side + 1, :, lanes] = jnp.where(upper, pltpu.roll(real, 4, 0), imag)
-            return carry
-
-        lax.fori_loop(0, table[11, half], group, 0)
+                out_ref[2 * side, :, lanes] = jnp.where(upper, real, pltpu.roll(imag, 4, 0))
+                out_ref[2 * side + 1, :, lanes] = jnp.where(upper, pltpu.roll(real, 4, 0), imag)
+        return carry
+
+    out_ref[...] = jnp.zeros_like(out_ref)
+    lax.fori_loop(0, (table[11, half] + 1) // 2, groups, 0)
 
 
 def pair_call(place, table, rights, screens, total, left_high, left_low):
+    rows = left_high.shape[0]
     return pl.pallas_call(
         pair_kernel,
-        out_shape=jax.ShapeDtypeStruct((8, 8, ROOM * BLK), jnp.float32),
+        out_shape=(
+            jax.ShapeDtypeStruct((4, 8, ROOM * BLK), jnp.float32),
+            jax.ShapeDtypeStruct((rows, 2 * HALF), jnp.float32),
+        ),
         in_specs=[SMEM, SMEM] + [VMEM] * (len(rights) + 5),
-        out_specs=VMEM,
-        scratch_shapes=[pltpu.VMEM((screens[0].shape[1], 2 * HALF), jnp.bfloat16)] * 2
-        + [pltpu.VMEM((left_high.shape[0], 2 * HALF), jnp.float32)],
-        compiler_params=params(40),
+        out_specs=(VMEM, VMEM),
+        scratch_shapes=[pltpu.VMEM((screens[0].shape[1], 2 * HALF), jnp.bfloat16)] * 2,
+        compiler_params=params(24),
         name="pair",
     )(place, table, *rights, *screens, total, left_high, left_low)
+
+
+def extract_kernel(place, table, kern, out_ref):
+    extract(table, place[3], kern, out_ref)
+
+
+def extract_call(place, table, kern):
+    return pl.pallas_call(
+        extract_kernel,
+        out_shape=jax.ShapeDtypeStruct((4, 8, ROOM * BLK), jnp.float32),
+        in_specs=[SMEM, SMEM, VMEM],
+        out_specs=VMEM,
+        compiler_params=params(8),
+        name="extract",
+    )(place, table, kern)
+
+
+def add_kernel(one_ref, two_ref, out_ref):
+    out_ref[...] = one_ref[...] + two_ref[...]
+
+
+def add_call(one, two):
+    return pl.pallas_call(
+        add_kernel,
+        out_shape=jax.ShapeDtypeStruct(one.shape, one.dtype),
+        in_specs=[VMEM, VMEM],
+        out_specs=VMEM,
+        compiler_params=params(8),
+        name="add",
+    )(one, two)
 
 
 def owner_kernel(place, table, parts_ref, out_ref, work):
@@ -329,6 +367,7 @@
         in_specs=[SMEM, SMEM, VMEM],
         out_specs=VMEM,
         scratch_shapes=[pltpu.VMEM((8, parts.shape[2] + 384), jnp.float32)],
+        compiler_params=params(8),
         name="owner",
     )(place, table, parts)
 
@@ -350,6 +389,7 @@
         out_shape=jax.ShapeDtypeStruct((CAP, 8, BLK), jnp.float32),
         in_specs=[SMEM, SMEM, VMEM],
         out_specs=VMEM,
+        compiler_params=params(8),
         name="last",
     )(place, table, parts)
 
@@ -408,17 +448,21 @@
             for t in range(5):
                 row = part * 40 + t * 8
                 columns_ref[row : row + 8, group * 128 : (group + 1) * 128] = tiles[part][t]
+    select(table, 1 - core, columns_ref, give_ref)
+    select(table, core, columns_ref, keep_ref)
+
+
+def select(table, which, columns_ref, out_ref):
     eighth = lax.broadcasted_iota(jnp.int32, (80, 128), 1) // BLK
-    for ref, which in ((give_ref, 1 - core), (keep_ref, core)):
-        for group in range(2):
-            slab = None
-            for u in range(8):
-                block = table[10, which * (USED // 2) + group * 8 + u]
-                column = pl.multiple_of(block // 8 * 128, 128)
-                by = lax.rem(u * BLK + 128 - lax.rem(block, 8) * BLK, 128)
-                turned = pltpu.roll(columns_ref[:, pl.ds(column, 128)], by, 1)
-                slab = turned if slab is None else jnp.where(eighth == u, turned, slab)
-            ref[:, group * 128 : (group + 1) * 128] = slab
+    for group in range(2):
+        slab = None
+        for u in range(8):
+            block = table[10, which * (USED // 2) + group * 8 + u]
+            column = pl.multiple_of(block // 8 * 128, 128)
+            by = lax.rem(u * BLK + 128 - lax.rem(block, 8) * BLK, 128)
+            turned = pltpu.roll(columns_ref[:, pl.ds(column, 128)], by, 1)
+            slab = turned if slab is None else jnp.where(eighth == u, turned, slab)
+        out_ref[:, group * 128 : (group + 1) * 128] = slab
 
 
 def unpack_call(place, table, pieces):
@@ -431,6 +475,7 @@
         ),
         in_specs=[SMEM, SMEM, VMEM],
         out_specs=(VMEM, VMEM, VMEM),
+        compiler_params=params(8),
         name="unpack",
     )(place, table, pieces)
 
@@ -448,6 +493,7 @@
         out_shape=jax.ShapeDtypeStruct((160, HALF), jnp.float32),
         in_specs=[SMEM, VMEM, VMEM],
         out_specs=VMEM,
+        compiler_params=params(8),
         name="shard",
     )(place, keep, take)
 
@@ -472,51 +518,56 @@
     mine, other = hold((mine, swap(after(screen, pieces))))
 
     columns, keep, give = unpack_call(place, table, mine)
-    shard = shard_call(place, keep, swap(give))
+    take, columns = hold((swap(give), columns))
+    shard = shard_call(place, keep, take)
 
     block = 2 * SPAN
     below, above = shift(shard, "z", 1), shift(shard, "z", -1)
     around = [columns] + [shift(columns, "x", by) for by in (1, 2, 3)]
     swapped = [swap(columns)]
-    below, above, around[1], swapped[0] = hold((below, above, around[1], swapped[0]))
+    below, above, around[1], around[3], swapped[0] = hold((below, above, around[1], around[3], swapped[0]))
 
     first = join(shard, below, above)
     below2, above2 = shift(below, "z", 1), shift(above, "z", -1)
     first_down, first_up = shift(first, "y", 1), shift(first, "y", -1)
     screens = screen_call(place, after(screen, first), other)
-    below2, above2, first_down, first_up, around[3], *screens = hold(
-        (below2, above2, first_down, first_up, around[3], *screens)
+    below2, above2, first_down, first_up, around[2], *screens = hold(
+        (below2, above2, first_down, first_up, around[2], *screens)
     )
 
     second = join(below2, above2)
     below3, above3 = shift(below2, "z", 1), shift(above2, "z", -1)
     second_down, second_up = shift(second, "y", 1), shift(second, "y", -1)
-    below3, above3, second_down, second_up, *around = hold((below3, above3, second_down, second_up, *around))
+    swapped += [swap(around[1]), swap(around[3])]
+    below3, above3, second_down, second_up, swapped[1], swapped[2] = hold(
+        (below3, above3, second_down, second_up, swapped[1], swapped[2])
+    )
 
     two_down = shift(join(first_down[: 3 * SPAN], second_down[:block]), "y", 1)
     two_up = shift(join(first_up[3 * SPAN :], second_up[block:]), "y", -1)
     z_below = shift(join(second_down[:block], second_up[:block], below3[:SPAN]), "z", 1)
     z_above = shift(join(second_down[block:], second_up[block:], above3[SPAN:]), "z", -1)
-    swapped.append(swap(around[1]))
-    two_down, two_up, z_below, z_above, swapped[1] = hold((two_down, two_up, z_below, z_above, swapped[1]))
+    swapped = [swapped[0], swapped[1], swap(around[2]), swapped[2]]
+    left_high, left_low = left_call(place, list(around) + swapped)
+    two_down, two_up, z_below, z_above, left_high, left_low = hold(
+        (two_down, two_up, z_below, z_above, left_high, left_low)
+    )
 
     y_below, y_above = shift(z_below[:block], "y", 1), shift(z_above[block : 2 * block], "y", -1)
     far_below, far_above = shift(z_below[:block], "z", 1), shift(z_above[block : 2 * block], "z", -1)
     rights = (first, first_down, first_up, second, second_down, second_up, two_down, two_up)
     total = group_call(near_units, len(NEAR), place, rights, screens[:2], ())
-    third = swap(after(around[3], two_down))
-    y_below, y_above, far_below, far_above, total, third = hold((y_below, y_above, far_below, far_above, total, third))
+    y_below, y_above, far_below, far_above, total = hold((y_below, y_above, far_below, far_above, total))
 
     across_low, across_high = shift(far_below[:SPAN], "y", 1), shift(far_above[SPAN:], "y", -1)
     rights = (below3, above3, z_below, z_above, y_below, y_above)
     total = group_call(middle_units, len(MIDDLE), place, rights, screens[2:4], (total,))
-    swapped += [swap(after(around[2], third)), third]
-    left_high, left_low = left_call(place, list(around) + swapped)
-    across_low, across_high, total, left_high, left_low = hold((across_low, across_high, total, left_high, left_low))
+    across_low, across_high, total = hold((across_low, across_high, total))
     rights = (z_below, z_above, far_below, far_above, across_low, across_high)
-    parts = pair_call(place, table, rights, screens[4:], total, left_high, left_low)
-
-    parts = lax.all_to_all(parts, ("core", "x"), 0, 0, tiled=True)
+    give, kern = pair_call(place, table, rights, screens[4:], total, left_high, left_low)
+
+    parts = add_call(extract_call(place, table, kern), swap(give))
+    parts = lax.all_to_all(parts, "x", 0, 0, tiled=True)
     parts = owner_call(place, table, parts)
     parts = lax.all_to_all(parts, ("z", "y"), 0, 0, tiled=True)
     return last_call(place, table, parts).reshape(1, CAP, 2, 4, BLK)

time: 160 us -> 154 us (0.963)
  blocking collectives: 37.3 us -> 31.1 us
  starting transfers between devices: 42.4 us -> 48.4 us
  Pallas kernels: 41 us -> 37 us
  waiting for transfers between devices: 34.6 us -> 32.1 us
    ppermute x23, starting transfers between devices: 30.4 us -> 35.9 us  [shards(): lax.ppermute(array, axis, ring(lax.axis_size(axis), by))]
    all_to_all x1, blocking collectives: 17.4 us -> 12.4 us  [shards(): parts = lax.all_to_all(parts, 'x', 0, 0, tiled=True)]
    ppermute x23, waiting for transfers between devices: 19 us -> 16.5 us  [shards(): lax.ppermute(array, axis, ring(lax.axis_size(axis), by))]
    unnamed x11 -> x13, local copies, waits for them, and re-layouts: 0.65 us -> 2.69 us
    pallas_call x1 -> x3, Pallas kernels: 11.2 us -> 11.7 us  [the longest x1 8.86 us: pair_call(): pl.pallas_call(pair_kernel, out_shape=(jax.ShapeDtypeStruct((4, 8, ROOM *...]
    ppermute x7 -> x8, waiting for transfers between devices: 4.45 us -> 4.22 us  [shards(): swap = lambda array: lax.ppermute(array, 'core', SWAP)]
  transfers between devices with their start and end apart: 31 -> 32, of which waited for: 15 -> 12; matrix products, arithmetic and copies ran while one was open for 1% -> 1% of each run, Pallas kernels for 13% -> 13%
where the time goes in v8:
time: 154 us; the launch traced here: 153 us
  starting transfers between devices  48.4 us (31%)
  Pallas kernels  37 us (24%)
  waiting for transfers between devices  32.1 us (21%)
  blocking collectives  31.1 us (20%)
  local copies, waits for them, and re-layouts  3.65 us (2%)
    ppermute x23, starting transfers between devices, shards(): lax.ppermute(array, axis, ring(lax.axis_size(axis), by))  35.9 us
    all_to_all x1, blocking collectives, shards(): parts = lax.all_to_all(parts, ('z', 'y'), 0, 0, tiled=True)  18.6 us
    ppermute x23, waiting for transfers between devices, shards(): lax.ppermute(array, axis, ring(lax.axis_size(axis), by))  16.5 us
    all_to_all x1, blocking collectives, shards(): parts = lax.all_to_all(parts, 'x', 0, 0, tiled=True)  12.4 us
    all_to_all x1, starting transfers between devices, shards(): lax.all_to_all(pieces.reshape(32, 1, -1), ('z', 'y'), 0, 0, tiled=True)  11.6 us
    all_to_all x1, waiting for transfers between devices, shards(): lax.all_to_all(pieces.reshape(32, 1, -1), ('z', 'y'), 0, 0, tiled=True)  11.4 us
    pallas_call x1, Pallas kernels, pair_call(): pl.pallas_call(pair_kernel, out_shape=(jax.ShapeDtypeStruct((4, 8, ROOM *...  8.86 us
    pallas_call x1, Pallas kernels, screen_call(): pl.pallas_call(screen_kernel, out_shape=shapes, in_specs=[SMEM, VMEM, VME...  7.35 us
  transfers between devices with their start and end apart: 32, of which 12 were waited for; matrix products, arithmetic and copies ran while one was open for 1% of the time, Pallas kernels for 13%

profile of v8, /device:TPU:2, one launch (start us, length us, event | category | flops | bytes accessed | tf_op | source)
XLA Modules:
  0.0 153.3 jit_solution(6293155938387026157)
XLA Ops:
  0.7 1.3 collective-permute-done.other_ref
  2.0 2.2 %pack.1 = f32[640,128]{1,0:T(8,128)} custom-call(s32[4]{0:T(128)} %pad_add_fusion.place, f32[2,16,2560]{2,1,0:T(8,128)} %own_ref.1, f32[2,16,2560]{2,1,0:T(8,128)} %collective-permute-done.other_ref), custom_call_target="tpu_custom_call" | custom-call | tf_op jit(solution)/shard_map/pack/pallas_call | solution.py:420
  4.4 11.6 %all-to-all-start = ((f32[32,1,2560]{2,1,0:T(1,128)}), f32[32,1,2560]{2,1,0:T(1,128)}, u32[]{:S(2)}, u32[]{:S(2)}) async-start(f32[32,1,2560]{2,1,0:T(1,128)} %bitcast.12), calls=%async_computation | async-start | bytes 655360 | tf_op jit(solution)/shard_map/all_to_all | solution.py:515
  19.4 11.4 %all-to-all-done = f32[32,1,2560]{2,1,0:T(1,128)} async-done(((f32[32,1,2560]{2,1,0:T(1,128)}), f32[32,1,2560]{2,1,0:T(1,128)}, u32[]{:S(2)}, u32[]{:S(2)}) %all-to-all-start) | async-done | bytes 327712 | tf_op jit(solution)/shard_map/all_to_all | solution.py:515
  31.4 2.5 %unpack.1 = (f32[80,1024]{1,0:T(8,128)S(1)}, f32[80,256]{1,0:T(8,128)S(1)}, f32[80,256]{1,0:T(8,128)S(1)}) custom-call(s32[4]{0:T(128)S(1)} %copy-done.2, s32[16,256]{1,0:T(8,128)S(1)} %plan.1.table, f32[640,128]{1,0:T(8,128)} %bitcast.6.in_ref), custom_call_target="tpu_custom_call" | custom-call | tf_op jit(solution)/shard_map/unpack/pallas_call | solution.py:469
  34.1 1.3 collective-permute-done.2.take_ref
  35.3 1.5 collective-permute-start.5
  38.9 2.3 %collective-permute-start.4 = (f32[160,256]{1,0:T(8,128)S(1)}, f32[160,256]{1,0:T(8,128)S(1)}, u32[]{:S(2)}, u32[]{:S(2)}) collective-permute-start(f32[160,256]{1,0:T(8,128)S(1)} %shard.1), channel_id=1, source_target_pairs={{0,224},{32,0},{64,32},{96,64},{128,96},{160,128},{192,160},{224,1... | collective-permute-start | bytes 491528 | tf_op jit(solution)/shard_map/ppermute | solution.py:508
  41.2 4.6 %collective-permute-done.3 = f32[160,256]{1,0:T(8,128)S(1)} collective-permute-done((f32[160,256]{1,0:T(8,128)S(1)}, f32[160,256]{1,0:T(8,128)S(1)}, u32[]{:S(2)}, u32[]{:S(2)}) %collective-permute-start.3) | collective-permute-done | bytes 163872 | tf_op jit(solution)/shard_map/ppermute | solution.py:508
  46.6 3.1 %collective-permute-start.11 = (f32[480,256]{1,0:T(8,128)S(1)}, f32[480,256]{1,0:T(8,128)S(1)}, u32[]{:S(2)}, u32[]{:S(2)}) collective-permute-start(f32[480,256]{1,0:T(8,128)S(1)} %pad_maximum_fusion.refs_0_), channel_id=1, source_target_pairs={{0,24},{8,0},{16,8},{24,16},{1,25},{9,1},{17,9},{25,17},{2,26},{10... | collective-permute-start | bytes 1474568 | tf_op jit(solution)/shard_map/ppermute | solution.py:508
  49.7 2.3 %collective-permute-start.12 = (f32[80,1024]{1,0:T(8,128)S(1)}, f32[80,1024]{1,0:T(8,128)S(1)}, u32[]{:S(2)}, u32[]{:S(2)}) collective-permute-start(f32[80,1024]{1,0:T(8,128)S(1)} %get-tuple-element.68.refs_0_), channel_id=1, source_target_pairs={{0,2},{1,3},{2,0},{3,1},{4,6},{5,7},{6,4},{7,5},{8,10},{9,11},{10,... | collective-permute-start | bytes 983048 | tf_op jit(solution)/shard_map/ppermute | solution.py:508
  52.9 2.3 %collective-permute-start.9 = (f32[160,256]{1,0:T(8,128)S(1)}, f32[160,256]{1,0:T(8,128)S(1)}, u32[]{:S(2)}, u32[]{:S(2)}) collective-permute-start(f32[160,256]{1,0:T(8,128)S(1)} %collective-permute-done.4), channel_id=1, source_target_pairs={{0,224},{32,0},{64,32},{96,64},{128,96},{160,128},{192,160},{224,1... | collective-permute-start | bytes 491528 | tf_op jit(solution)/shard_map/ppermute | solution.py:508
  55.9 7.3 %screen.1 = (bf16[640,1664]{1,0:T(8,128)(2,1)S(1)}, bf16[640,1664]{1,0:T(8,128)(2,1)S(1)}, bf16[640,640]{1,0:T(8,128)(2,1)S(1)}, bf16[640,640]{1,0:T(8,128)(2,1)...) custom-call(s32[4]{0:T(128)S(1)} %copy-done.3, f32[320,2560]{1,0:T(8,128)S(1)} %bitcast.10, ...), custom_call_target="tpu_custom_call" | custom-call | tf_op jit(solution)/shard_map/screen/pallas_call | solution.py:153
  64.0 3.2 %collective-permute-start.16 = (f32[320,256]{1,0:T(8,128)S(1)}, f32[320,256]{1,0:T(8,128)S(1)}, u32[]{:S(2)}, u32[]{:S(2)}) collective-permute-start(f32[320,256]{1,0:T(8,128)S(1)} %constant_dynamic-update-slice_fusion.refs_3_), channel_id=1, source_target_pairs={{0,24},{8,0},{16,8},{24,16},{1,25},{9,1},{17,9},{25,17},{2,26},{10... | collective-permute-start | bytes 983048 | tf_op jit(solution)/shard_map/ppermute | solution.py:508
  67.2 3.2 %collective-permute-start.14 = (f32[160,256]{1,0:T(8,128)S(1)}, f32[160,256]{1,0:T(8,128)S(1)}, u32[]{:S(2)}, u32[]{:S(2)}) collective-permute-start(f32[160,256]{1,0:T(8,128)S(1)} %collective-permute-done.9), channel_id=1, source_target_pairs={{0,224},{32,0},{64,32},{96,64},{128,96},{160,128},{192,160},{224,1... | collective-permute-start | bytes 491528 | tf_op jit(solution)/shard_map/ppermute | solution.py:508
  70.5 3.7 %collective-permute-done.13.refs_0_ = f32[160,256]{1,0:T(8,128)S(1)} collective-permute-done((f32[160,256]{1,0:T(8,128)S(1)}, f32[160,256]{1,0:T(8,128)S(1)}, u32[]{:S(2)}, u32[]{:S(2)}) %collective-permute-start.13) | collective-permute-done | bytes 163872 | tf_op jit(solution)/shard_map/ppermute | solution.py:508
  75.3 3.0 %collective-permute-start.20 = (f32[400,256]{1,0:T(8,128)S(1)}, f32[400,256]{1,0:T(8,128)S(1)}, u32[]{:S(2)}, u32[]{:S(2)}) collective-permute-start(f32[400,256]{1,0:T(8,128)S(1)} %get-tuple-element.122), channel_id=1, source_target_pairs={{0,24},{8,0},{16,8},{24,16},{1,25},{9,1},{17,9},{25,17},{2,26},{10... | collective-permute-start | bytes 1228808 | tf_op jit(solution)/shard_map/ppermute | solution.py:508
  80.6 1.6 %collective-permute-done.23.refs_6_ = f32[80,1024]{1,0:T(8,128)S(1)} collective-permute-done((f32[80,1024]{1,0:T(8,128)S(1)}, f32[80,1024]{1,0:T(8,128)S(1)}, u32[]{:S(2)}, u32[]{:S(2)}) %collective-permute-start.23) | collective-permute-done | bytes 327712 | tf_op jit(solution)/shard_map/ppermute | solution.py:509
  82.2 1.8 %left.1 = (bf16[1024,640]{1,0:T(8,128)(2,1)S(1)}, bf16[1024,640]{1,0:T(8,128)(2,1)S(1)}) custom-call(s32[4]{0:T(128)S(1)} %copy-done.3, f32[80,1024]{1,0:T(8,128)S(1)} %get-tuple-element.68.refs_0_, f32[80,1024]{1,0:T(8,128)S(1)} %collective-permute-done.5.refs_1_, f32[80,1024]{1,0:T(8,128)S(1)} %collective-permute-done.12.refs_2_, ...), custom_call_target="tpu_custom_call" | custom-call | tf_op jit(solution)/shard_map/left/pallas_call | solution.py:183
  84.0 2.3 %collective-permute-done.20.refs_7_ = f32[400,256]{1,0:T(8,128)S(1)} collective-permute-done((f32[400,256]{1,0:T(8,128)S(1)}, f32[400,256]{1,0:T(8,128)S(1)}, u32[]{:S(2)}, u32[]{:S(2)}) %collective-permute-start.20) | collective-permute-done | bytes 409632 | tf_op jit(solution)/shard_map/ppermute | solution.py:508
  86.3 2.2 %collective-permute-done.22.refs_3_.refs_1_ = f32[400,256]{1,0:T(8,128)S(1)} collective-permute-done((f32[400,256]{1,0:T(8,128)S(1)}, f32[400,256]{1,0:T(8,128)S(1)}, u32[]{:S(2)}, u32[]{:S(2)}) %collective-permute-start.22) | collective-permute-done | bytes 409632 | tf_op jit(solution)/shard_map/ppermute | solution.py:508
  88.5 2.2 %collective-permute-done.19.refs_6_ = f32[400,256]{1,0:T(8,128)S(1)} collective-permute-done((f32[400,256]{1,0:T(8,128)S(1)}, f32[400,256]{1,0:T(8,128)S(1)}, u32[]{:S(2)}, u32[]{:S(2)}) %collective-permute-start.19) | collective-permute-done | bytes 409632 | tf_op jit(solution)/shard_map/ppermute | solution.py:508
  90.9 3.3 %collective-permute-start.25 = (f32[160,256]{1,0:T(8,128)S(1)}, f32[160,256]{1,0:T(8,128)S(1)}, u32[]{:S(2)}, u32[]{:S(2)}) collective-permute-start(f32[160,256]{1,0:T(8,128)S(1)} %slice.49), channel_id=1, source_target_pairs={{0,24},{8,0},{16,8},{24,16},{1,25},{9,1},{17,9},{25,17},{2,26},{10... | collective-permute-start | bytes 491528 | tf_op jit(solution)/shard_map/ppermute | solution.py:508
  95.1 2.4 %collective-permute-start.27 = (f32[160,256]{1,0:T(8,128)S(1)}, f32[160,256]{1,0:T(8,128)S(1)}, u32[]{:S(2)}, u32[]{:S(2)}) collective-permute-start(f32[160,256]{1,0:T(8,128)S(1)} %slice.49), channel_id=1, source_target_pairs={{0,224},{32,0},{64,32},{96,64},{128,96},{160,128},{192,160},{224,1... | collective-permute-start | bytes 491528 | tf_op jit(solution)/shard_map/ppermute | solution.py:508
  97.5 4.4 %group.2.refs_8_ = f32[640,512]{1,0:T(8,128)S(1)} custom-call(s32[4]{0:T(128)S(1)} %copy-done.4, f32[480,256]{1,0:T(8,128)S(1)} %pad_maximum_fusion.refs_0_, f32[480,256]{1,0:T(8,128)S(1)} %collective-permute-done.10.refs_1_, f32[480,256]{1,0:T(8,128)S(1)} %collective-permute-done.11.refs_2_, f32[320,256]{1,0:T(8,128)S(1)} %constant_dynamic-update-slice_fusion.refs_3_, ...), custom_call_target="tpu_custom_call" | custom-call | tf_op jit(solution)/shard_map/group/pallas_call | solution.py:248
  102.0 3.2 %collective-permute-start.29 = (f32[80,256]{1,0:T(8,128)S(1)}, f32[80,256]{1,0:T(8,128)S(1)}, u32[]{:S(2)}, u32[]{:S(2)}) collective-permute-start(f32[80,256]{1,0:T(8,128)S(1)} %slice.51), channel_id=1, source_target_pairs={{0,24},{8,0},{16,8},{24,16},{1,25},{9,1},{17,9},{25,17},{2,26},{10... | collective-permute-start | bytes 245768 | tf_op jit(solution)/shard_map/ppermute | solution.py:508
  105.3 2.4 %group.3.refs_8_ = f32[640,512]{1,0:T(8,128)S(1)} custom-call(s32[4]{0:T(128)S(1)} %copy-done.4, f32[160,256]{1,0:T(8,128)S(1)} %collective-permute-done.13.refs_0_, f32[160,256]{1,0:T(8,128)S(1)} %collective-permute-done.14.refs_1_, f32[400,256]{1,0:T(8,128)S(1)} %collective-permute-done.21.refs_2_.refs_0_, ...), custom_call_target="tpu_custom_call" | custom-call | tf_op jit(solution)/shard_map/group/pallas_call | solution.py:248
  107.7 8.9 %pair.1 = (f32[4,8,3584]{2,1,0:T(8,128)S(1)}, f32[1024,512]{1,0:T(8,128)S(1)}) custom-call(s32[4]{0:T(128)S(1)} %copy-done.4, s32[16,256]{1,0:T(8,128)S(1)} %plan.1.table, f32[400,256]{1,0:T(8,128)S(1)} %collective-permute-done.21.refs_2_.refs_0_, f32[400,256]{1,0:T(8,128)S(1)} %collective-permute-done.22.refs_3_.refs_1_, ...), custom_call_target="tpu_custom_call" | custom-call | tf_op jit(solution)/shard_map/pair/pallas_call | solution.py:305
  116.6 2.8 %extract.1.one_ref = f32[4,8,3584]{2,1,0:T(8,128)S(1)} custom-call(s32[4]{0:T(128)S(1)} %copy-done.4, s32[16,256]{1,0:T(8,128)S(1)} %plan.1.table, f32[1024,512]{1,0:T(8,128)S(1)} %get-tuple-element.115.kern), custom_call_target="tpu_custom_call" | custom-call | tf_op jit(solution)/shard_map/extract/pallas_call | solution.py:324
  119.5 12.4 %all_to_all.15.parts_ref = f32[4,8,3584]{2,1,0:T(8,128)S(1)} all-to-all(f32[4,8,3584]{2,1,0:T(8,128)S(1)} %add.7), channel_id=1, replica_groups=mesh['z'=8,'y'=4,'core'=2,'x'=4] {'x'}, dimensions={0} | all-to-all | bytes 917504 | tf_op jit(solution)/shard_map/all_to_all | solution.py:570
  133.2 18.6 %all_to_all.16.parts_ref = f32[32,8,256]{2,1,0:T(8,128)S(1)} all-to-all(f32[32,8,256]{2,1,0:T(8,128)S(1)} %owner.1), channel_id=1, replica_groups=mesh['z'=8,'y'=4,'core'=2,'x'=4] {'z','y'}, dimensions={0} | all-to-all | bytes 524288 | tf_op jit(solution)/shard_map/all_to_all | solution.py:572
  151.8 1.5 last.1
  (75 shorter events, 15.8 us)
Async XLA Ops:
  0.0 2.0 %collective-permute-start = (f32[2,16,2560]{2,1,0:T(8,128)}, f32[2,16,2560]{2,1,0:T(8,128)}, u32[]{:S(2)}, u32[]{:S(2)}) collective-permute-start(f32[2,16,2560]{2,1,0:T(8,128)} %own_ref.1), channel_id=1, source_target_pairs={{0,4},{4,0},{1,5},{5,1},{2,6},{6,2},{3,7},{7,3},{8,12},{12,8},{9,1... | collective-permute-start | bytes 983048 | tf_op jit(solution)/shard_map/ppermute | solution.py:509
  4.2 26.6 %collective-permute-start.1 = (f32[320,2560]{1,0:T(8,128)}, f32[320,2560]{1,0:T(8,128)}, u32[]{:S(2)}, u32[]{:S(2)}) collective-permute-start(f32[320,2560]{1,0:T(8,128)} %bitcast.9), channel_id=1, source_target_pairs={{0,4},{4,0},{1,5},{5,1},{2,6},{6,2},{3,7},{7,3},{8,12},{12,8},{9,1... | collective-permute-start | bytes 9830408 | tf_op jit(solution)/shard_map/ppermute | solution.py:509
  4.4 26.4 %all-to-all-start = ((f32[32,1,2560]{2,1,0:T(1,128)}), f32[32,1,2560]{2,1,0:T(1,128)}, u32[]{:S(2)}, u32[]{:S(2)}) async-start(f32[32,1,2560]{2,1,0:T(1,128)} %bitcast.12), calls=%async_computation | async-start | bytes 655360 | tf_op jit(solution)/shard_map/all_to_all | solution.py:515
  34.0 1.4 collective-permute-start.2
  35.3 10.5 %collective-permute-start.5 = (f32[80,1024]{1,0:T(8,128)S(1)}, f32[80,1024]{1,0:T(8,128)S(1)}, u32[]{:S(2)}, u32[]{:S(2)}) collective-permute-start(f32[80,1024]{1,0:T(8,128)S(1)} %get-tuple-element.68.refs_0_), channel_id=1, source_target_pairs={{0,1},{1,2},{2,3},{3,0},{4,5},{5,6},{6,7},{7,4},{8,9},{9,10},{10,1... | collective-permute-start | bytes 983048 | tf_op jit(solution)/shard_map/ppermute | solution.py:508
  36.8 9.5 %collective-permute-start.6 = (f32[80,1024]{1,0:T(8,128)S(1)}, f32[80,1024]{1,0:T(8,128)S(1)}, u32[]{:S(2)}, u32[]{:S(2)}) collective-permute-start(f32[80,1024]{1,0:T(8,128)S(1)} %get-tuple-element.68.refs_0_), channel_id=1, source_target_pairs={{0,3},{1,0},{2,1},{3,2},{4,7},{5,4},{6,5},{7,6},{8,11},{9,8},{10,9... | collective-permute-start | bytes 983048 | tf_op jit(solution)/shard_map/ppermute | solution.py:508
  37.4 9.0 %collective-permute-start.7 = (f32[80,1024]{1,0:T(8,128)S(1)}, f32[80,1024]{1,0:T(8,128)S(1)}, u32[]{:S(2)}, u32[]{:S(2)}) collective-permute-start(f32[80,1024]{1,0:T(8,128)S(1)} %get-tuple-element.68.refs_0_), channel_id=1, source_target_pairs={{0,4},{4,0},{1,5},{5,1},{2,6},{6,2},{3,7},{7,3},{8,12},{12,8},{9,1... | collective-permute-start | bytes 983048 | tf_op jit(solution)/shard_map/ppermute | solution.py:509
  37.9 7.9 %collective-permute-start.3 = (f32[160,256]{1,0:T(8,128)S(1)}, f32[160,256]{1,0:T(8,128)S(1)}, u32[]{:S(2)}, u32[]{:S(2)}) collective-permute-start(f32[160,256]{1,0:T(8,128)S(1)} %shard.1), channel_id=1, source_target_pairs={{0,32},{32,64},{64,96},{96,128},{128,160},{160,192},{192,224},{224... | collective-permute-start | bytes 491528 | tf_op jit(solution)/shard_map/ppermute | solution.py:508
  38.9 6.9 %collective-permute-start.4 = (f32[160,256]{1,0:T(8,128)S(1)}, f32[160,256]{1,0:T(8,128)S(1)}, u32[]{:S(2)}, u32[]{:S(2)}) collective-permute-start(f32[160,256]{1,0:T(8,128)S(1)} %shard.1), channel_id=1, source_target_pairs={{0,224},{32,0},{64,32},{96,64},{128,96},{160,128},{192,160},{224,1... | collective-permute-start | bytes 491528 | tf_op jit(solution)/shard_map/ppermute | solution.py:508
  46.4 17.5 %collective-permute-start.10 = (f32[480,256]{1,0:T(8,128)S(1)}, f32[480,256]{1,0:T(8,128)S(1)}, u32[]{:S(2)}, u32[]{:S(2)}) collective-permute-start(f32[480,256]{1,0:T(8,128)S(1)} %pad_maximum_fusion.refs_0_), channel_id=1, source_target_pairs={{0,8},{8,16},{16,24},{24,0},{1,9},{9,17},{17,25},{25,1},{2,10},{10... | collective-permute-start | bytes 1474568 | tf_op jit(solution)/shard_map/ppermute | solution.py:508
  46.6 17.3 %collective-permute-start.11 = (f32[480,256]{1,0:T(8,128)S(1)}, f32[480,256]{1,0:T(8,128)S(1)}, u32[]{:S(2)}, u32[]{:S(2)}) collective-permute-start(f32[480,256]{1,0:T(8,128)S(1)} %pad_maximum_fusion.refs_0_), channel_id=1, source_target_pairs={{0,24},{8,0},{16,8},{24,16},{1,25},{9,1},{17,9},{25,17},{2,26},{10... | collective-permute-start | bytes 1474568 | tf_op jit(solution)/shard_map/ppermute | solution.py:508
  49.7 13.6 %collective-permute-start.12 = (f32[80,1024]{1,0:T(8,128)S(1)}, f32[80,1024]{1,0:T(8,128)S(1)}, u32[]{:S(2)}, u32[]{:S(2)}) collective-permute-start(f32[80,1024]{1,0:T(8,128)S(1)} %get-tuple-element.68.refs_0_), channel_id=1, source_target_pairs={{0,2},{1,3},{2,0},{3,1},{4,6},{5,7},{6,4},{7,5},{8,10},{9,11},{10,... | collective-permute-start | bytes 983048 | tf_op jit(solution)/shard_map/ppermute | solution.py:508
  52.0 11.4 %collective-permute-start.8 = (f32[160,256]{1,0:T(8,128)S(1)}, f32[160,256]{1,0:T(8,128)S(1)}, u32[]{:S(2)}, u32[]{:S(2)}) collective-permute-start(f32[160,256]{1,0:T(8,128)S(1)} %collective-permute-done.3), channel_id=1, source_target_pairs={{0,32},{32,64},{64,96},{96,128},{128,160},{160,192},{192,224},{224... | collective-permute-start | bytes 491528 | tf_op jit(solution)/shard_map/ppermute | solution.py:508
  52.9 11.0 %collective-permute-start.9 = (f32[160,256]{1,0:T(8,128)S(1)}, f32[160,256]{1,0:T(8,128)S(1)}, u32[]{:S(2)}, u32[]{:S(2)}) collective-permute-start(f32[160,256]{1,0:T(8,128)S(1)} %collective-permute-done.4), channel_id=1, source_target_pairs={{0,224},{32,0},{64,32},{96,64},{128,96},{160,128},{192,160},{224,1... | collective-permute-start | bytes 491528 | tf_op jit(solution)/shard_map/ppermute | solution.py:508
  63.3 4.0 %collective-permute-start.17 = (f32[80,1024]{1,0:T(8,128)S(1)}, f32[80,1024]{1,0:T(8,128)S(1)}, u32[]{:S(2)}, u32[]{:S(2)}) collective-permute-start(f32[80,1024]{1,0:T(8,128)S(1)} %collective-permute-done.5.refs_1_), channel_id=1, source_target_pairs={{0,4},{4,0},{1,5},{5,1},{2,6},{6,2},{3,7},{7,3},{8,12},{12,8},{9,1... | collective-permute-start | bytes 983048 | tf_op jit(solution)/shard_map/ppermute | solution.py:509
  63.4 7.1 %collective-permute-start.18 = (f32[80,1024]{1,0:T(8,128)S(1)}, f32[80,1024]{1,0:T(8,128)S(1)}, u32[]{:S(2)}, u32[]{:S(2)}) collective-permute-start(f32[80,1024]{1,0:T(8,128)S(1)} %collective-permute-done.6.refs_3_), channel_id=1, source_target_pairs={{0,4},{4,0},{1,5},{5,1},{2,6},{6,2},{3,7},{7,3},{8,12},{12,8},{9,1... | collective-permute-start | bytes 983048 | tf_op jit(solution)/shard_map/ppermute | solution.py:509
  63.9 11.2 %collective-permute-start.15 = (f32[320,256]{1,0:T(8,128)S(1)}, f32[320,256]{1,0:T(8,128)S(1)}, u32[]{:S(2)}, u32[]{:S(2)}) collective-permute-start(f32[320,256]{1,0:T(8,128)S(1)} %constant_dynamic-update-slice_fusion.refs_3_), channel_id=1, source_target_pairs={{0,8},{8,16},{16,24},{24,0},{1,9},{9,17},{17,25},{25,1},{2,10},{10... | collective-permute-start | bytes 983048 | tf_op jit(solution)/shard_map/ppermute | solution.py:508
  64.0 11.1 %collective-permute-start.16 = (f32[320,256]{1,0:T(8,128)S(1)}, f32[320,256]{1,0:T(8,128)S(1)}, u32[]{:S(2)}, u32[]{:S(2)}) collective-permute-start(f32[320,256]{1,0:T(8,128)S(1)} %constant_dynamic-update-slice_fusion.refs_3_), channel_id=1, source_target_pairs={{0,24},{8,0},{16,8},{24,16},{1,25},{9,1},{17,9},{25,17},{2,26},{10... | collective-permute-start | bytes 983048 | tf_op jit(solution)/shard_map/ppermute | solution.py:508
  67.2 7.0 %collective-permute-start.13 = (f32[160,256]{1,0:T(8,128)S(1)}, f32[160,256]{1,0:T(8,128)S(1)}, u32[]{:S(2)}, u32[]{:S(2)}) collective-permute-start(f32[160,256]{1,0:T(8,128)S(1)} %collective-permute-done.8), channel_id=1, source_target_pairs={{0,32},{32,64},{64,96},{96,128},{128,160},{160,192},{192,224},{224... | collective-permute-start | bytes 491528 | tf_op jit(solution)/shard_map/ppermute | solution.py:508
  67.2 7.0 %collective-permute-start.14 = (f32[160,256]{1,0:T(8,128)S(1)}, f32[160,256]{1,0:T(8,128)S(1)}, u32[]{:S(2)}, u32[]{:S(2)}) collective-permute-start(f32[160,256]{1,0:T(8,128)S(1)} %collective-permute-done.9), channel_id=1, source_target_pairs={{0,224},{32,0},{64,32},{96,64},{128,96},{160,128},{192,160},{224,1... | collective-permute-start | bytes 491528 | tf_op jit(solution)/shard_map/ppermute | solution.py:508
  75.3 11.1 %collective-permute-start.20 = (f32[400,256]{1,0:T(8,128)S(1)}, f32[400,256]{1,0:T(8,128)S(1)}, u32[]{:S(2)}, u32[]{:S(2)}) collective-permute-start(f32[400,256]{1,0:T(8,128)S(1)} %get-tuple-element.122), channel_id=1, source_target_pairs={{0,24},{8,0},{16,8},{24,16},{1,25},{9,1},{17,9},{25,17},{2,26},{10... | collective-permute-start | bytes 1228808 | tf_op jit(solution)/shard_map/ppermute | solution.py:508
  78.3 10.2 %collective-permute-start.22 = (f32[400,256]{1,0:T(8,128)S(1)}, f32[400,256]{1,0:T(8,128)S(1)}, u32[]{:S(2)}, u32[]{:S(2)}) collective-permute-start(f32[400,256]{1,0:T(8,128)S(1)} %get-tuple-element.121), channel_id=1, source_target_pairs={{0,224},{32,0},{64,32},{96,64},{128,96},{160,128},{192,160},{224,1... | collective-permute-start | bytes 1228808 | tf_op jit(solution)/shard_map/ppermute | solution.py:508
  79.4 11.3 %collective-permute-start.19 = (f32[400,256]{1,0:T(8,128)S(1)}, f32[400,256]{1,0:T(8,128)S(1)}, u32[]{:S(2)}, u32[]{:S(2)}) collective-permute-start(f32[400,256]{1,0:T(8,128)S(1)} %get-tuple-element.124), channel_id=1, source_target_pairs={{0,8},{8,16},{16,24},{24,0},{1,9},{9,17},{17,25},{25,1},{2,10},{10... | collective-permute-start | bytes 1228808 | tf_op jit(solution)/shard_map/ppermute | solution.py:508
  79.6 11.1 %collective-permute-start.21 = (f32[400,256]{1,0:T(8,128)S(1)}, f32[400,256]{1,0:T(8,128)S(1)}, u32[]{:S(2)}, u32[]{:S(2)}) collective-permute-start(f32[400,256]{1,0:T(8,128)S(1)} %get-tuple-element.123), channel_id=1, source_target_pairs={{0,32},{32,64},{64,96},{96,128},{128,160},{160,192},{192,224},{224... | collective-permute-start | bytes 1228808 | tf_op jit(solution)/shard_map/ppermute | solution.py:508
  80.6 1.6 %collective-permute-start.23 = (f32[80,1024]{1,0:T(8,128)S(1)}, f32[80,1024]{1,0:T(8,128)S(1)}, u32[]{:S(2)}, u32[]{:S(2)}) collective-permute-start(f32[80,1024]{1,0:T(8,128)S(1)} %collective-permute-done.12.refs_2_), channel_id=1, source_target_pairs={{0,4},{4,0},{1,5},{5,1},{2,6},{6,2},{3,7},{7,3},{8,12},{12,8},{9,1... | collective-permute-start | bytes 983048 | tf_op jit(solution)/shard_map/ppermute | solution.py:509
  90.8 11.1 %collective-permute-start.24 = (f32[160,256]{1,0:T(8,128)S(1)}, f32[160,256]{1,0:T(8,128)S(1)}, u32[]{:S(2)}, u32[]{:S(2)}) collective-permute-start(f32[160,256]{1,0:T(8,128)S(1)} %slice.48), channel_id=1, source_target_pairs={{0,8},{8,16},{16,24},{24,0},{1,9},{9,17},{17,25},{25,1},{2,10},{10... | collective-permute-start | bytes 491528 | tf_op jit(solution)/shard_map/ppermute | solution.py:508
  90.9 11.0 %collective-permute-start.25 = (f32[160,256]{1,0:T(8,128)S(1)}, f32[160,256]{1,0:T(8,128)S(1)}, u32[]{:S(2)}, u32[]{:S(2)}) collective-permute-start(f32[160,256]{1,0:T(8,128)S(1)} %slice.49), channel_id=1, source_target_pairs={{0,24},{8,0},{16,8},{24,16},{1,25},{9,1},{17,9},{25,17},{2,26},{10... | collective-permute-start | bytes 491528 | tf_op jit(solution)/shard_map/ppermute | solution.py:508
  94.2 7.7 %collective-permute-start.26 = (f32[160,256]{1,0:T(8,128)S(1)}, f32[160,256]{1,0:T(8,128)S(1)}, u32[]{:S(2)}, u32[]{:S(2)}) collective-permute-start(f32[160,256]{1,0:T(8,128)S(1)} %slice.48), channel_id=1, source_target_pairs={{0,32},{32,64},{64,96},{96,128},{128,160},{160,192},{192,224},{224... | collective-permute-start | bytes 491528 | tf_op jit(solution)/shard_map/ppermute | solution.py:508
  95.1 6.8 %collective-permute-start.27 = (f32[160,256]{1,0:T(8,128)S(1)}, f32[160,256]{1,0:T(8,128)S(1)}, u32[]{:S(2)}, u32[]{:S(2)}) collective-permute-start(f32[160,256]{1,0:T(8,128)S(1)} %slice.49), channel_id=1, source_target_pairs={{0,224},{32,0},{64,32},{96,64},{128,96},{160,128},{192,160},{224,1... | collective-permute-start | bytes 491528 | tf_op jit(solution)/shard_map/ppermute | solution.py:508
  101.9 5.7 %collective-permute-start.28 = (f32[80,256]{1,0:T(8,128)S(1)}, f32[80,256]{1,0:T(8,128)S(1)}, u32[]{:S(2)}, u32[]{:S(2)}) collective-permute-start(f32[80,256]{1,0:T(8,128)S(1)} %slice.50), channel_id=1, source_target_pairs={{0,8},{8,16},{16,24},{24,0},{1,9},{9,17},{17,25},{25,1},{2,10},{10... | collective-permute-start | bytes 245768 | tf_op jit(solution)/shard_map/ppermute | solution.py:508
  102.0 5.6 %collective-permute-start.29 = (f32[80,256]{1,0:T(8,128)S(1)}, f32[80,256]{1,0:T(8,128)S(1)}, u32[]{:S(2)}, u32[]{:S(2)}) collective-permute-start(f32[80,256]{1,0:T(8,128)S(1)} %slice.51), channel_id=1, source_target_pairs={{0,24},{8,0},{16,8},{24,16},{1,25},{9,1},{17,9},{25,17},{2,26},{10... | collective-permute-start | bytes 245768 | tf_op jit(solution)/shard_map/ppermute | solution.py:508
  116.5 2.9 %collective-permute-start.30 = (f32[4,8,3584]{2,1,0:T(8,128)S(1)}, f32[4,8,3584]{2,1,0:T(8,128)S(1)}, u32[]{:S(2)}, u32[]{:S(2)}) collective-permute-start(f32[4,8,3584]{2,1,0:T(8,128)S(1)} %get-tuple-element.116), channel_id=1, source_target_pairs={{0,4},{4,0},{1,5},{5,1},{2,6},{6,2},{3,7},{7,3},{8,12},{12,8},{9,1... | collective-permute-start | bytes 1376264 | tf_op jit(solution)/shard_map/ppermute | solution.py:509
  (6 other events, 76.0 us)

commit v9 on v8

--- a/solution.py
+++ b/solution.py
@@ -204,16 +204,12 @@
             ref[used:, :] = jnp.zeros((ref.shape[0] - used, ref.shape[1]), ref.dtype)
 
 
-def near_units(first, first_down, first_up, second, second_down, second_up, two_down, two_up):
-    units = []
-    for base, planes, skip, own, below, above in (
-        (0, 3, 0, first, first_down, first_up),
-        (3, 2, 3, second, second_down, second_up),
-    ):
-        for unit in range(2 * planes):
-            half, at = (two_down, unit + skip) if unit < planes else (two_up, unit - planes + skip)
-            for delta, ref, index in ((0, own, unit), (3, below, unit), (1, above, unit), (2, half, at)):
-                units.append((delta, base + unit // 2, unit % 2, ref, index * SPAN))
+def near_units(own, below, above, two_below, two_above):
+    units, planes = [], len(NEAR)
+    for unit in range(2 * planes):
+        half, at = (two_below, unit) if unit < planes else (two_above, unit - planes)
+        for delta, ref, index in ((0, own, unit), (3, below, unit), (1, above, unit), (2, half, at)):
+            units.append((delta, unit // 2, unit % 2, ref, index * SPAN))
     return units
 
 
@@ -518,44 +514,34 @@
     mine, other = hold((mine, swap(after(screen, pieces))))
 
     columns, keep, give = unpack_call(place, table, mine)
-    take, columns = hold((swap(give), columns))
-    shard = shard_call(place, keep, take)
-
-    block = 2 * SPAN
-    below, above = shift(shard, "z", 1), shift(shard, "z", -1)
+    shard = shard_call(place, keep, swap(give))
+
+    block, half = 2 * SPAN, len(NEAR) * SPAN
+    steps = hold((columns, *(shift(shard, "z", by) for by in (1, -1, 2, -2))))
+    columns, nearest = steps[0], steps[1:]
+    near = join(shard, *nearest)
+    near_down, near_up = shift(near, "y", 1), shift(near, "y", -1)
+    below3, above3 = shift(nearest[2], "z", 1), shift(nearest[3], "z", -1)
+    screens = screen_call(place, after(screen, near), other)
     around = [columns] + [shift(columns, "x", by) for by in (1, 2, 3)]
-    swapped = [swap(columns)]
-    below, above, around[1], around[3], swapped[0] = hold((below, above, around[1], around[3], swapped[0]))
-
-    first = join(shard, below, above)
-    below2, above2 = shift(below, "z", 1), shift(above, "z", -1)
-    first_down, first_up = shift(first, "y", 1), shift(first, "y", -1)
-    screens = screen_call(place, after(screen, first), other)
-    below2, above2, first_down, first_up, around[2], *screens = hold(
-        (below2, above2, first_down, first_up, around[2], *screens)
+    swapped = [swap(columns), swap(around[1]), None, swap(around[3])]
+    near_down, near_up, below3, above3, swapped[0], swapped[1], swapped[3], *screens = hold(
+        (near_down, near_up, below3, above3, swapped[0], swapped[1], swapped[3], *screens)
     )
 
-    second = join(below2, above2)
-    below3, above3 = shift(below2, "z", 1), shift(above2, "z", -1)
-    second_down, second_up = shift(second, "y", 1), shift(second, "y", -1)
-    swapped += [swap(around[1]), swap(around[3])]
-    below3, above3, second_down, second_up, swapped[1], swapped[2] = hold(
-        (below3, above3, second_down, second_up, swapped[1], swapped[2])
-    )
-
-    two_down = shift(join(first_down[: 3 * SPAN], second_down[:block]), "y", 1)
-    two_up = shift(join(first_up[3 * SPAN :], second_up[block:]), "y", -1)
-    z_below = shift(join(second_down[:block], second_up[:block], below3[:SPAN]), "z", 1)
-    z_above = shift(join(second_down[block:], second_up[block:], above3[SPAN:]), "z", -1)
-    swapped = [swapped[0], swapped[1], swap(around[2]), swapped[2]]
-    left_high, left_low = left_call(place, list(around) + swapped)
+    two_down, two_up = shift(near_down[:half], "y", 1), shift(near_up[half:], "y", -1)
+    third, fourth = slice(3 * block, 4 * block), slice(4 * block, 5 * block)
+    z_below = shift(join(near_down[third], near_up[third], below3[:SPAN]), "z", 1)
+    z_above = shift(join(near_down[fourth], near_up[fourth], above3[SPAN:]), "z", -1)
+    swapped[2] = swap(around[2])
+    left_high, left_low = left_call(place, around + swapped)
     two_down, two_up, z_below, z_above, left_high, left_low = hold(
         (two_down, two_up, z_below, z_above, left_high, left_low)
     )
 
     y_below, y_above = shift(z_below[:block], "y", 1), shift(z_above[block : 2 * block], "y", -1)
     far_below, far_above = shift(z_below[:block], "z", 1), shift(z_above[block : 2 * block], "z", -1)
-    rights = (first, first_down, first_up, second, second_down, second_up, two_down, two_up)
+    rights = (near, near_down, near_up, two_down, two_up)
     total = group_call(near_units, len(NEAR), place, rights, screens[:2], ())
     y_below, y_above, far_below, far_above, total = hold((y_below, y_above, far_below, far_above, total))
 

time: 154 us -> 154 us (level)
  waiting for transfers between devices: 32.1 us -> 36.5 us
  starting transfers between devices: 48.4 us -> 44.6 us
    ppermute x23 -> x21, waiting for transfers between devices: 16.5 us -> 20.9 us  [shards(): lax.ppermute(array, axis, ring(lax.axis_size(axis), by))]
    ppermute x23 -> x21, starting transfers between devices: 35.9 us -> 32.1 us  [shards(): lax.ppermute(array, axis, ring(lax.axis_size(axis), by))]
  transfers between devices with their start and end apart: 32 -> 30, of which waited for: 12 -> 12; matrix products, arithmetic and copies ran while one was open for 1% -> 1% of each run, Pallas kernels for 13% -> 13%
where the time goes in v9:
time: 154 us; the launch traced here: 153 us
  starting transfers between devices  44.6 us (29%)
  Pallas kernels  37 us (24%)
  waiting for transfers between devices  36.5 us (24%)
  blocking collectives  31.1 us (20%)
  local copies, waits for them, and re-layouts  3.04 us (2%)
    ppermute x21, starting transfers between devices, shards(): lax.ppermute(array, axis, ring(lax.axis_size(axis), by))  32.1 us
    ppermute x21, waiting for transfers between devices, shards(): lax.ppermute(array, axis, ring(lax.axis_size(axis), by))  20.9 us
    all_to_all x1, blocking collectives, shards(): parts = lax.all_to_all(parts, ('z', 'y'), 0, 0, tiled=True)  19.2 us
    all_to_all x1, blocking collectives, shards(): parts = lax.all_to_all(parts, 'x', 0, 0, tiled=True)  11.9 us
    all_to_all x1, starting transfers between devices, shards(): lax.all_to_all(pieces.reshape(32, 1, -1), ('z', 'y'), 0, 0, tiled=True)  11.6 us
    all_to_all x1, waiting for transfers between devices, shards(): lax.all_to_all(pieces.reshape(32, 1, -1), ('z', 'y'), 0, 0, tiled=True)  11.4 us
    pallas_call x1, Pallas kernels, pair_call(): pl.pallas_call(pair_kernel, out_shape=(jax.ShapeDtypeStruct((4, 8, ROOM *...  8.88 us
    pallas_call x1, Pallas kernels, screen_call(): pl.pallas_call(screen_kernel, out_shape=shapes, in_specs=[SMEM, VMEM, VME...  7.35 us
  transfers between devices with their start and end apart: 30, of which 12 were waited for; matrix products, arithmetic and copies ran while one was open for 1% of the time, Pallas kernels for 13%

profile of v9, /device:TPU:2, one launch (start us, length us, event | category | flops | bytes accessed | tf_op | source)
XLA Modules:
  0.0 153.4 jit_solution(3384421576339094391)
XLA Ops:
  0.7 1.3 collective-permute-done.other_ref
  2.0 2.2 %pack.1 = f32[640,128]{1,0:T(8,128)} custom-call(s32[4]{0:T(128)} %pad_add_fusion.place, f32[2,16,2560]{2,1,0:T(8,128)} %own_ref.1, f32[2,16,2560]{2,1,0:T(8,128)} %collective-permute-done.other_ref), custom_call_target="tpu_custom_call" | custom-call | tf_op jit(solution)/shard_map/pack/pallas_call | solution.py:416
  4.4 11.6 %all-to-all-start = ((f32[32,1,2560]{2,1,0:T(1,128)}), f32[32,1,2560]{2,1,0:T(1,128)}, u32[]{:S(2)}, u32[]{:S(2)}) async-start(f32[32,1,2560]{2,1,0:T(1,128)} %bitcast.12), calls=%async_computation | async-start | bytes 655360 | tf_op jit(solution)/shard_map/all_to_all | solution.py:511
  19.4 11.4 %all-to-all-done = f32[32,1,2560]{2,1,0:T(1,128)} async-done(((f32[32,1,2560]{2,1,0:T(1,128)}), f32[32,1,2560]{2,1,0:T(1,128)}, u32[]{:S(2)}, u32[]{:S(2)}) %all-to-all-start) | async-done | bytes 327712 | tf_op jit(solution)/shard_map/all_to_all | solution.py:511
  31.4 2.5 %unpack.1 = (f32[80,1024]{1,0:T(8,128)S(1)}, f32[80,256]{1,0:T(8,128)S(1)}, f32[80,256]{1,0:T(8,128)S(1)}) custom-call(s32[4]{0:T(128)S(1)} %copy-done.2, s32[16,256]{1,0:T(8,128)S(1)} %plan.1.table, f32[640,128]{1,0:T(8,128)} %bitcast.6.in_ref), custom_call_target="tpu_custom_call" | custom-call | tf_op jit(solution)/shard_map/unpack/pallas_call | solution.py:465
  36.9 2.3 %collective-permute-start.4 = (f32[160,256]{1,0:T(8,128)S(1)}, f32[160,256]{1,0:T(8,128)S(1)}, u32[]{:S(2)}, u32[]{:S(2)}) collective-permute-start(f32[160,256]{1,0:T(8,128)S(1)} %shard.1), channel_id=1, source_target_pairs={{0,224},{32,0},{64,32},{96,64},{128,96},{160,128},{192,160},{224,1... | collective-permute-start | bytes 491528 | tf_op jit(solution)/shard_map/ppermute | solution.py:504
  39.2 4.1 %collective-permute-start.6 = (f32[160,256]{1,0:T(8,128)S(1)}, f32[160,256]{1,0:T(8,128)S(1)}, u32[]{:S(2)}, u32[]{:S(2)}) collective-permute-start(f32[160,256]{1,0:T(8,128)S(1)} %shard.1), channel_id=1, source_target_pairs={{0,192},{32,224},{64,0},{96,32},{128,64},{160,96},{192,128},{224,1... | collective-permute-start | bytes 491528 | tf_op jit(solution)/shard_map/ppermute | solution.py:504
  43.4 2.6 %collective-permute-done.3 = f32[160,256]{1,0:T(8,128)S(1)} collective-permute-done((f32[160,256]{1,0:T(8,128)S(1)}, f32[160,256]{1,0:T(8,128)S(1)}, u32[]{:S(2)}, u32[]{:S(2)}) %collective-permute-start.3) | collective-permute-done | bytes 163872 | tf_op jit(solution)/shard_map/ppermute | solution.py:504
  46.5 3.8 %collective-permute-done.5 = f32[160,256]{1,0:T(8,128)S(1)} collective-permute-done((f32[160,256]{1,0:T(8,128)S(1)}, f32[160,256]{1,0:T(8,128)S(1)}, u32[]{:S(2)}, u32[]{:S(2)}) %collective-permute-start.5) | collective-permute-done | bytes 163872 | tf_op jit(solution)/shard_map/ppermute | solution.py:504
  50.7 3.0 %collective-permute-start.8 = (f32[800,256]{1,0:T(8,128)S(1)}, f32[800,256]{1,0:T(8,128)S(1)}, u32[]{:S(2)}, u32[]{:S(2)}) collective-permute-start(f32[800,256]{1,0:T(8,128)S(1)} %constant_dynamic-update-slice_fusion.refs_0_), channel_id=1, source_target_pairs={{0,24},{8,0},{16,8},{24,16},{1,25},{9,1},{17,9},{25,17},{2,26},{10... | collective-permute-start | bytes 2457608 | tf_op jit(solution)/shard_map/ppermute | solution.py:504
  53.8 1.5 collective-permute-start.12
  55.8 3.2 %collective-permute-done.10.refs_1_ = f32[160,256]{1,0:T(8,128)S(1)} collective-permute-done((f32[160,256]{1,0:T(8,128)S(1)}, f32[160,256]{1,0:T(8,128)S(1)}, u32[]{:S(2)}, u32[]{:S(2)}) %collective-permute-start.10) | collective-permute-done | bytes 163872 | tf_op jit(solution)/shard_map/ppermute | solution.py:504
  59.0 1.6 %collective-permute-start.9 = (f32[160,256]{1,0:T(8,128)S(1)}, f32[160,256]{1,0:T(8,128)S(1)}, u32[]{:S(2)}, u32[]{:S(2)}) collective-permute-start(f32[160,256]{1,0:T(8,128)S(1)} %collective-permute-done.5), channel_id=1, source_target_pairs={{0,32},{32,64},{64,96},{96,128},{128,160},{160,192},{192,224},{224... | collective-permute-start | bytes 491528 | tf_op jit(solution)/shard_map/ppermute | solution.py:504
  60.7 4.9 %collective-permute-done.9.refs_0_ = f32[160,256]{1,0:T(8,128)S(1)} collective-permute-done((f32[160,256]{1,0:T(8,128)S(1)}, f32[160,256]{1,0:T(8,128)S(1)}, u32[]{:S(2)}, u32[]{:S(2)}) %collective-permute-start.9) | collective-permute-done | bytes 163872 | tf_op jit(solution)/shard_map/ppermute | solution.py:504
  66.2 7.3 %screen.1 = (bf16[640,1664]{1,0:T(8,128)(2,1)S(1)}, bf16[640,1664]{1,0:T(8,128)(2,1)S(1)}, bf16[640,640]{1,0:T(8,128)(2,1)S(1)}, bf16[640,640]{1,0:T(8,128)(2,1)...) custom-call(s32[4]{0:T(128)S(1)} %copy-done.3, f32[320,2560]{1,0:T(8,128)S(1)} %bitcast.10, ...), custom_call_target="tpu_custom_call" | custom-call | tf_op jit(solution)/shard_map/screen/pallas_call | solution.py:153
  73.5 2.2 %collective-permute-start.20 = (f32[80,1024]{1,0:T(8,128)S(1)}, f32[80,1024]{1,0:T(8,128)S(1)}, u32[]{:S(2)}, u32[]{:S(2)}) collective-permute-start(f32[80,1024]{1,0:T(8,128)S(1)} %get-tuple-element.65.refs_0_), channel_id=1, source_target_pairs={{0,2},{1,3},{2,0},{3,1},{4,6},{5,7},{6,4},{7,5},{8,10},{9,11},{10,... | collective-permute-start | bytes 983048 | tf_op jit(solution)/shard_map/ppermute | solution.py:504
  75.9 2.1 %collective-permute-start.19 = (f32[400,256]{1,0:T(8,128)S(1)}, f32[400,256]{1,0:T(8,128)S(1)}, u32[]{:S(2)}, u32[]{:S(2)}) collective-permute-start(f32[400,256]{1,0:T(8,128)S(1)} %pad_maximum_fusion.1), channel_id=1, source_target_pairs={{0,224},{32,0},{64,32},{96,64},{128,96},{160,128},{192,160},{224,1... | collective-permute-start | bytes 1228808 | tf_op jit(solution)/shard_map/ppermute | solution.py:504
  78.2 3.2 %collective-permute-start.17 = (f32[400,256]{1,0:T(8,128)S(1)}, f32[400,256]{1,0:T(8,128)S(1)}, u32[]{:S(2)}, u32[]{:S(2)}) collective-permute-start(f32[400,256]{1,0:T(8,128)S(1)} %slice.39), channel_id=1, source_target_pairs={{0,24},{8,0},{16,8},{24,16},{1,25},{9,1},{17,9},{25,17},{2,26},{10... | collective-permute-start | bytes 1228808 | tf_op jit(solution)/shard_map/ppermute | solution.py:504
  81.4 3.7 %collective-permute-done.20.refs_2_ = f32[80,1024]{1,0:T(8,128)S(1)} collective-permute-done((f32[80,1024]{1,0:T(8,128)S(1)}, f32[80,1024]{1,0:T(8,128)S(1)}, u32[]{:S(2)}, u32[]{:S(2)}) %collective-permute-start.20) | collective-permute-done | bytes 327712 | tf_op jit(solution)/shard_map/ppermute | solution.py:504
  85.2 1.6 %collective-permute-done.21.refs_6_ = f32[80,1024]{1,0:T(8,128)S(1)} collective-permute-done((f32[80,1024]{1,0:T(8,128)S(1)}, f32[80,1024]{1,0:T(8,128)S(1)}, u32[]{:S(2)}, u32[]{:S(2)}) %collective-permute-start.21) | collective-permute-done | bytes 327712 | tf_op jit(solution)/shard_map/ppermute | solution.py:505
  86.8 1.8 %left.1 = (bf16[1024,640]{1,0:T(8,128)(2,1)S(1)}, bf16[1024,640]{1,0:T(8,128)(2,1)S(1)}) custom-call(s32[4]{0:T(128)S(1)} %copy-done.3, f32[80,1024]{1,0:T(8,128)S(1)} %get-tuple-element.65.refs_0_, f32[80,1024]{1,0:T(8,128)S(1)} %collective-permute-done.12.refs_1_, f32[80,1024]{1,0:T(8,128)S(1)} %collective-permute-done.20.refs_2_, ...), custom_call_target="tpu_custom_call" | custom-call | tf_op jit(solution)/shard_map/left/pallas_call | solution.py:183
  88.6 2.0 %collective-permute-done.18.refs_2_.refs_0_ = f32[400,256]{1,0:T(8,128)S(1)} collective-permute-done((f32[400,256]{1,0:T(8,128)S(1)}, f32[400,256]{1,0:T(8,128)S(1)}, u32[]{:S(2)}, u32[]{:S(2)}) %collective-permute-start.18) | collective-permute-done | bytes 409632 | tf_op jit(solution)/shard_map/ppermute | solution.py:504
  90.9 3.3 %collective-permute-start.23 = (f32[160,256]{1,0:T(8,128)S(1)}, f32[160,256]{1,0:T(8,128)S(1)}, u32[]{:S(2)}, u32[]{:S(2)}) collective-permute-start(f32[160,256]{1,0:T(8,128)S(1)} %slice.47), channel_id=1, source_target_pairs={{0,24},{8,0},{16,8},{24,16},{1,25},{9,1},{17,9},{25,17},{2,26},{10... | collective-permute-start | bytes 491528 | tf_op jit(solution)/shard_map/ppermute | solution.py:504
  94.2 3.2 %collective-permute-start.25 = (f32[160,256]{1,0:T(8,128)S(1)}, f32[160,256]{1,0:T(8,128)S(1)}, u32[]{:S(2)}, u32[]{:S(2)}) collective-permute-start(f32[160,256]{1,0:T(8,128)S(1)} %slice.47), channel_id=1, source_target_pairs={{0,224},{32,0},{64,32},{96,64},{128,96},{160,128},{192,160},{224,1... | collective-permute-start | bytes 491528 | tf_op jit(solution)/shard_map/ppermute | solution.py:504
  97.4 4.4 %group.2.refs_8_ = f32[640,512]{1,0:T(8,128)S(1)} custom-call(s32[4]{0:T(128)S(1)} %copy-done.3, f32[800,256]{1,0:T(8,128)S(1)} %constant_dynamic-update-slice_fusion.refs_0_, f32[800,256]{1,0:T(8,128)S(1)} %collective-permute-done.7.refs_1_, f32[800,256]{1,0:T(8,128)S(1)} %collective-permute-done.8.refs_2_, f32[400,256]{1,0:T(8,128)S(1)} %collective-permute-done.16.refs_3_, ...), custom_call_target="tpu_custom_call" | custom-call | tf_op jit(solution)/shard_map/group/pallas_call | solution.py:244
  102.0 3.2 %collective-permute-start.27 = (f32[80,256]{1,0:T(8,128)S(1)}, f32[80,256]{1,0:T(8,128)S(1)}, u32[]{:S(2)}, u32[]{:S(2)}) collective-permute-start(f32[80,256]{1,0:T(8,128)S(1)} %slice.49), channel_id=1, source_target_pairs={{0,24},{8,0},{16,8},{24,16},{1,25},{9,1},{17,9},{25,17},{2,26},{10... | collective-permute-start | bytes 245768 | tf_op jit(solution)/shard_map/ppermute | solution.py:504
  105.2 2.4 %group.3.refs_8_ = f32[640,512]{1,0:T(8,128)S(1)} custom-call(s32[4]{0:T(128)S(1)} %copy-done.3, f32[160,256]{1,0:T(8,128)S(1)} %collective-permute-done.9.refs_0_, f32[160,256]{1,0:T(8,128)S(1)} %collective-permute-done.10.refs_1_, f32[400,256]{1,0:T(8,128)S(1)} %collective-permute-done.18.refs_2_.refs_0_, ...), custom_call_target="tpu_custom_call" | custom-call | tf_op jit(solution)/shard_map/group/pallas_call | solution.py:244
  107.6 8.9 %pair.1 = (f32[4,8,3584]{2,1,0:T(8,128)S(1)}, f32[1024,512]{1,0:T(8,128)S(1)}) custom-call(s32[4]{0:T(128)S(1)} %copy-done.3, s32[16,256]{1,0:T(8,128)S(1)} %plan.1.table, f32[400,256]{1,0:T(8,128)S(1)} %collective-permute-done.18.refs_2_.refs_0_, f32[400,256]{1,0:T(8,128)S(1)} %collective-permute-done.19.refs_3_.refs_1_, ...), custom_call_target="tpu_custom_call" | custom-call | tf_op jit(solution)/shard_map/pair/pallas_call | solution.py:301
  116.6 2.8 %extract.1.one_ref = f32[4,8,3584]{2,1,0:T(8,128)S(1)} custom-call(s32[4]{0:T(128)S(1)} %copy-done.3, s32[16,256]{1,0:T(8,128)S(1)} %plan.1.table, f32[1024,512]{1,0:T(8,128)S(1)} %get-tuple-element.103.kern), custom_call_target="tpu_custom_call" | custom-call | tf_op jit(solution)/shard_map/extract/pallas_call | solution.py:320
  119.4 11.9 %all_to_all.15.parts_ref = f32[4,8,3584]{2,1,0:T(8,128)S(1)} all-to-all(f32[4,8,3584]{2,1,0:T(8,128)S(1)} %add.7), channel_id=1, replica_groups=mesh['z'=8,'y'=4,'core'=2,'x'=4] {'x'}, dimensions={0} | all-to-all | bytes 917504 | tf_op jit(solution)/shard_map/all_to_all | solution.py:556
  132.6 19.2 %all_to_all.16.parts_ref = f32[32,8,256]{2,1,0:T(8,128)S(1)} all-to-all(f32[32,8,256]{2,1,0:T(8,128)S(1)} %owner.1), channel_id=1, replica_groups=mesh['z'=8,'y'=4,'core'=2,'x'=4] {'z','y'}, dimensions={0} | all-to-all | bytes 524288 | tf_op jit(solution)/shard_map/all_to_all | solution.py:558
  151.8 1.5 last.1
  (71 shorter events, 12.2 us)
Async XLA Ops:
  0.0 2.0 %collective-permute-start = (f32[2,16,2560]{2,1,0:T(8,128)}, f32[2,16,2560]{2,1,0:T(8,128)}, u32[]{:S(2)}, u32[]{:S(2)}) collective-permute-start(f32[2,16,2560]{2,1,0:T(8,128)} %own_ref.1), channel_id=1, source_target_pairs={{0,4},{4,0},{1,5},{5,1},{2,6},{6,2},{3,7},{7,3},{8,12},{12,8},{9,1... | collective-permute-start | bytes 983048 | tf_op jit(solution)/shard_map/ppermute | solution.py:505
  0.7 65.5 %copy-start = (f32[2,4,40,2560]{3,2,1,0:T(8,128)S(1)}, f32[2,4,40,2560]{3,2,1,0:T(8,128)}, u32[]{:S(2)}) copy-start(f32[2,4,40,2560]{3,2,1,0:T(8,128)} %param.5) | copy-start | bytes 9830404
  4.2 26.6 %collective-permute-start.1 = (f32[320,2560]{1,0:T(8,128)}, f32[320,2560]{1,0:T(8,128)}, u32[]{:S(2)}, u32[]{:S(2)}) collective-permute-start(f32[320,2560]{1,0:T(8,128)} %bitcast.9), channel_id=1, source_target_pairs={{0,4},{4,0},{1,5},{5,1},{2,6},{6,2},{3,7},{7,3},{8,12},{12,8},{9,1... | collective-permute-start | bytes 9830408 | tf_op jit(solution)/shard_map/ppermute | solution.py:505
  4.4 26.4 %all-to-all-start = ((f32[32,1,2560]{2,1,0:T(1,128)}), f32[32,1,2560]{2,1,0:T(1,128)}, u32[]{:S(2)}, u32[]{:S(2)}) async-start(f32[32,1,2560]{2,1,0:T(1,128)} %bitcast.12), calls=%async_computation | async-start | bytes 655360 | tf_op jit(solution)/shard_map/all_to_all | solution.py:511
  31.4 34.7 %copy-start.3 = (s32[4]{0:T(128)S(1)}, s32[4]{0:T(128)}, u32[]{:S(2)}) copy-start(s32[4]{0:T(128)} %pad_add_fusion.place) | copy-start | bytes 52
  34.0 1.4 collective-permute-start.2
  35.9 10.0 %collective-permute-start.3 = (f32[160,256]{1,0:T(8,128)S(1)}, f32[160,256]{1,0:T(8,128)S(1)}, u32[]{:S(2)}, u32[]{:S(2)}) collective-permute-start(f32[160,256]{1,0:T(8,128)S(1)} %shard.1), channel_id=1, source_target_pairs={{0,32},{32,64},{64,96},{96,128},{128,160},{160,192},{192,224},{224... | collective-permute-start | bytes 491528 | tf_op jit(solution)/shard_map/ppermute | solution.py:504
  36.9 9.7 %collective-permute-start.4 = (f32[160,256]{1,0:T(8,128)S(1)}, f32[160,256]{1,0:T(8,128)S(1)}, u32[]{:S(2)}, u32[]{:S(2)}) collective-permute-start(f32[160,256]{1,0:T(8,128)S(1)} %shard.1), channel_id=1, source_target_pairs={{0,224},{32,0},{64,32},{96,64},{128,96},{160,128},{192,160},{224,1... | collective-permute-start | bytes 491528 | tf_op jit(solution)/shard_map/ppermute | solution.py:504
  39.2 11.1 %collective-permute-start.5 = (f32[160,256]{1,0:T(8,128)S(1)}, f32[160,256]{1,0:T(8,128)S(1)}, u32[]{:S(2)}, u32[]{:S(2)}) collective-permute-start(f32[160,256]{1,0:T(8,128)S(1)} %shard.1), channel_id=1, source_target_pairs={{0,64},{32,96},{64,128},{96,160},{128,192},{160,224},{192,0},{224,... | collective-permute-start | bytes 491528 | tf_op jit(solution)/shard_map/ppermute | solution.py:504
  39.2 11.1 %collective-permute-start.6 = (f32[160,256]{1,0:T(8,128)S(1)}, f32[160,256]{1,0:T(8,128)S(1)}, u32[]{:S(2)}, u32[]{:S(2)}) collective-permute-start(f32[160,256]{1,0:T(8,128)S(1)} %shard.1), channel_id=1, source_target_pairs={{0,192},{32,224},{64,0},{96,32},{128,64},{160,96},{192,128},{224,1... | collective-permute-start | bytes 491528 | tf_op jit(solution)/shard_map/ppermute | solution.py:504
  50.4 25.4 %collective-permute-start.7 = (f32[800,256]{1,0:T(8,128)S(1)}, f32[800,256]{1,0:T(8,128)S(1)}, u32[]{:S(2)}, u32[]{:S(2)}) collective-permute-start(f32[800,256]{1,0:T(8,128)S(1)} %constant_dynamic-update-slice_fusion.refs_0_), channel_id=1, source_target_pairs={{0,8},{8,16},{16,24},{24,0},{1,9},{9,17},{17,25},{25,1},{2,10},{10... | collective-permute-start | bytes 2457608 | tf_op jit(solution)/shard_map/ppermute | solution.py:504
  50.7 25.1 %collective-permute-start.8 = (f32[800,256]{1,0:T(8,128)S(1)}, f32[800,256]{1,0:T(8,128)S(1)}, u32[]{:S(2)}, u32[]{:S(2)}) collective-permute-start(f32[800,256]{1,0:T(8,128)S(1)} %constant_dynamic-update-slice_fusion.refs_0_), channel_id=1, source_target_pairs={{0,24},{8,0},{16,8},{24,16},{1,25},{9,1},{17,9},{25,17},{2,26},{10... | collective-permute-start | bytes 2457608 | tf_op jit(solution)/shard_map/ppermute | solution.py:504
  53.7 5.3 %collective-permute-start.10 = (f32[160,256]{1,0:T(8,128)S(1)}, f32[160,256]{1,0:T(8,128)S(1)}, u32[]{:S(2)}, u32[]{:S(2)}) collective-permute-start(f32[160,256]{1,0:T(8,128)S(1)} %collective-permute-done.6), channel_id=1, source_target_pairs={{0,224},{32,0},{64,32},{96,64},{128,96},{160,128},{192,160},{224,1... | collective-permute-start | bytes 491528 | tf_op jit(solution)/shard_map/ppermute | solution.py:504
  53.8 11.8 %collective-permute-start.12 = (f32[80,1024]{1,0:T(8,128)S(1)}, f32[80,1024]{1,0:T(8,128)S(1)}, u32[]{:S(2)}, u32[]{:S(2)}) collective-permute-start(f32[80,1024]{1,0:T(8,128)S(1)} %get-tuple-element.65.refs_0_), channel_id=1, source_target_pairs={{0,1},{1,2},{2,3},{3,0},{4,5},{5,6},{6,7},{7,4},{8,9},{9,10},{10,1... | collective-permute-start | bytes 983048 | tf_op jit(solution)/shard_map/ppermute | solution.py:504
  55.3 10.8 %collective-permute-start.14 = (f32[80,1024]{1,0:T(8,128)S(1)}, f32[80,1024]{1,0:T(8,128)S(1)}, u32[]{:S(2)}, u32[]{:S(2)}) collective-permute-start(f32[80,1024]{1,0:T(8,128)S(1)} %get-tuple-element.65.refs_0_), channel_id=1, source_target_pairs={{0,3},{1,0},{2,1},{3,2},{4,7},{5,4},{6,5},{7,6},{8,11},{9,8},{10,9... | collective-permute-start | bytes 983048 | tf_op jit(solution)/shard_map/ppermute | solution.py:504
  59.0 6.5 %collective-permute-start.9 = (f32[160,256]{1,0:T(8,128)S(1)}, f32[160,256]{1,0:T(8,128)S(1)}, u32[]{:S(2)}, u32[]{:S(2)}) collective-permute-start(f32[160,256]{1,0:T(8,128)S(1)} %collective-permute-done.5), channel_id=1, source_target_pairs={{0,32},{32,64},{64,96},{96,128},{128,160},{160,192},{192,224},{224... | collective-permute-start | bytes 491528 | tf_op jit(solution)/shard_map/ppermute | solution.py:504
  65.5 8.0 %collective-permute-start.11 = (f32[80,1024]{1,0:T(8,128)S(1)}, f32[80,1024]{1,0:T(8,128)S(1)}, u32[]{:S(2)}, u32[]{:S(2)}) collective-permute-start(f32[80,1024]{1,0:T(8,128)S(1)} %get-tuple-element.65.refs_0_), channel_id=1, source_target_pairs={{0,4},{4,0},{1,5},{5,1},{2,6},{6,2},{3,7},{7,3},{8,12},{12,8},{9,1... | collective-permute-start | bytes 983048 | tf_op jit(solution)/shard_map/ppermute | solution.py:505
  65.6 10.2 %collective-permute-start.13 = (f32[80,1024]{1,0:T(8,128)S(1)}, f32[80,1024]{1,0:T(8,128)S(1)}, u32[]{:S(2)}, u32[]{:S(2)}) collective-permute-start(f32[80,1024]{1,0:T(8,128)S(1)} %collective-permute-done.12.refs_1_), channel_id=1, source_target_pairs={{0,4},{4,0},{1,5},{5,1},{2,6},{6,2},{3,7},{7,3},{8,12},{12,8},{9,1... | collective-permute-start | bytes 983048 | tf_op jit(solution)/shard_map/ppermute | solution.py:505
  66.1 9.7 %collective-permute-start.15 = (f32[80,1024]{1,0:T(8,128)S(1)}, f32[80,1024]{1,0:T(8,128)S(1)}, u32[]{:S(2)}, u32[]{:S(2)}) collective-permute-start(f32[80,1024]{1,0:T(8,128)S(1)} %collective-permute-done.14.refs_3_), channel_id=1, source_target_pairs={{0,4},{4,0},{1,5},{5,1},{2,6},{6,2},{3,7},{7,3},{8,12},{12,8},{9,1... | collective-permute-start | bytes 983048 | tf_op jit(solution)/shard_map/ppermute | solution.py:505
  73.5 11.6 %collective-permute-start.20 = (f32[80,1024]{1,0:T(8,128)S(1)}, f32[80,1024]{1,0:T(8,128)S(1)}, u32[]{:S(2)}, u32[]{:S(2)}) collective-permute-start(f32[80,1024]{1,0:T(8,128)S(1)} %get-tuple-element.65.refs_0_), channel_id=1, source_target_pairs={{0,2},{1,3},{2,0},{3,1},{4,6},{5,7},{6,4},{7,5},{8,10},{9,11},{10,... | collective-permute-start | bytes 983048 | tf_op jit(solution)/shard_map/ppermute | solution.py:504
  75.9 12.7 %collective-permute-start.19 = (f32[400,256]{1,0:T(8,128)S(1)}, f32[400,256]{1,0:T(8,128)S(1)}, u32[]{:S(2)}, u32[]{:S(2)}) collective-permute-start(f32[400,256]{1,0:T(8,128)S(1)} %pad_maximum_fusion.1), channel_id=1, source_target_pairs={{0,224},{32,0},{64,32},{96,64},{128,96},{160,128},{192,160},{224,1... | collective-permute-start | bytes 1228808 | tf_op jit(solution)/shard_map/ppermute | solution.py:504
  78.0 12.6 %collective-permute-start.18 = (f32[400,256]{1,0:T(8,128)S(1)}, f32[400,256]{1,0:T(8,128)S(1)}, u32[]{:S(2)}, u32[]{:S(2)}) collective-permute-start(f32[400,256]{1,0:T(8,128)S(1)} %pad_maximum_fusion), channel_id=1, source_target_pairs={{0,32},{32,64},{64,96},{96,128},{128,160},{160,192},{192,224},{224... | collective-permute-start | bytes 1228808 | tf_op jit(solution)/shard_map/ppermute | solution.py:504
  78.2 12.6 %collective-permute-start.16 = (f32[400,256]{1,0:T(8,128)S(1)}, f32[400,256]{1,0:T(8,128)S(1)}, u32[]{:S(2)}, u32[]{:S(2)}) collective-permute-start(f32[400,256]{1,0:T(8,128)S(1)} %slice.38), channel_id=1, source_target_pairs={{0,8},{8,16},{16,24},{24,0},{1,9},{9,17},{17,25},{25,1},{2,10},{10... | collective-permute-start | bytes 1228808 | tf_op jit(solution)/shard_map/ppermute | solution.py:504
  78.2 12.5 %collective-permute-start.17 = (f32[400,256]{1,0:T(8,128)S(1)}, f32[400,256]{1,0:T(8,128)S(1)}, u32[]{:S(2)}, u32[]{:S(2)}) collective-permute-start(f32[400,256]{1,0:T(8,128)S(1)} %slice.39), channel_id=1, source_target_pairs={{0,24},{8,0},{16,8},{24,16},{1,25},{9,1},{17,9},{25,17},{2,26},{10... | collective-permute-start | bytes 1228808 | tf_op jit(solution)/shard_map/ppermute | solution.py:504
  85.2 1.6 %collective-permute-start.21 = (f32[80,1024]{1,0:T(8,128)S(1)}, f32[80,1024]{1,0:T(8,128)S(1)}, u32[]{:S(2)}, u32[]{:S(2)}) collective-permute-start(f32[80,1024]{1,0:T(8,128)S(1)} %collective-permute-done.20.refs_2_), channel_id=1, source_target_pairs={{0,4},{4,0},{1,5},{5,1},{2,6},{6,2},{3,7},{7,3},{8,12},{12,8},{9,1... | collective-permute-start | bytes 983048 | tf_op jit(solution)/shard_map/ppermute | solution.py:505
  90.7 11.1 %collective-permute-start.22 = (f32[160,256]{1,0:T(8,128)S(1)}, f32[160,256]{1,0:T(8,128)S(1)}, u32[]{:S(2)}, u32[]{:S(2)}) collective-permute-start(f32[160,256]{1,0:T(8,128)S(1)} %slice.46), channel_id=1, source_target_pairs={{0,8},{8,16},{16,24},{24,0},{1,9},{9,17},{17,25},{25,1},{2,10},{10... | collective-permute-start | bytes 491528 | tf_op jit(solution)/shard_map/ppermute | solution.py:504
  90.9 11.0 %collective-permute-start.23 = (f32[160,256]{1,0:T(8,128)S(1)}, f32[160,256]{1,0:T(8,128)S(1)}, u32[]{:S(2)}, u32[]{:S(2)}) collective-permute-start(f32[160,256]{1,0:T(8,128)S(1)} %slice.47), channel_id=1, source_target_pairs={{0,24},{8,0},{16,8},{24,16},{1,25},{9,1},{17,9},{25,17},{2,26},{10... | collective-permute-start | bytes 491528 | tf_op jit(solution)/shard_map/ppermute | solution.py:504
  94.2 7.7 %collective-permute-start.24 = (f32[160,256]{1,0:T(8,128)S(1)}, f32[160,256]{1,0:T(8,128)S(1)}, u32[]{:S(2)}, u32[]{:S(2)}) collective-permute-start(f32[160,256]{1,0:T(8,128)S(1)} %slice.46), channel_id=1, source_target_pairs={{0,32},{32,64},{64,96},{96,128},{128,160},{160,192},{192,224},{224... | collective-permute-start | bytes 491528 | tf_op jit(solution)/shard_map/ppermute | solution.py:504
  94.2 7.7 %collective-permute-start.25 = (f32[160,256]{1,0:T(8,128)S(1)}, f32[160,256]{1,0:T(8,128)S(1)}, u32[]{:S(2)}, u32[]{:S(2)}) collective-permute-start(f32[160,256]{1,0:T(8,128)S(1)} %slice.47), channel_id=1, source_target_pairs={{0,224},{32,0},{64,32},{96,64},{128,96},{160,128},{192,160},{224,1... | collective-permute-start | bytes 491528 | tf_op jit(solution)/shard_map/ppermute | solution.py:504
  101.9 5.7 %collective-permute-start.26 = (f32[80,256]{1,0:T(8,128)S(1)}, f32[80,256]{1,0:T(8,128)S(1)}, u32[]{:S(2)}, u32[]{:S(2)}) collective-permute-start(f32[80,256]{1,0:T(8,128)S(1)} %slice.48), channel_id=1, source_target_pairs={{0,8},{8,16},{16,24},{24,0},{1,9},{9,17},{17,25},{25,1},{2,10},{10... | collective-permute-start | bytes 245768 | tf_op jit(solution)/shard_map/ppermute | solution.py:504
  102.0 5.6 %collective-permute-start.27 = (f32[80,256]{1,0:T(8,128)S(1)}, f32[80,256]{1,0:T(8,128)S(1)}, u32[]{:S(2)}, u32[]{:S(2)}) collective-permute-start(f32[80,256]{1,0:T(8,128)S(1)} %slice.49), channel_id=1, source_target_pairs={{0,24},{8,0},{16,8},{24,16},{1,25},{9,1},{17,9},{25,17},{2,26},{10... | collective-permute-start | bytes 245768 | tf_op jit(solution)/shard_map/ppermute | solution.py:504
  116.5 2.9 %collective-permute-start.28 = (f32[4,8,3584]{2,1,0:T(8,128)S(1)}, f32[4,8,3584]{2,1,0:T(8,128)S(1)}, u32[]{:S(2)}, u32[]{:S(2)}) collective-permute-start(f32[4,8,3584]{2,1,0:T(8,128)S(1)} %get-tuple-element.104), channel_id=1, source_target_pairs={{0,4},{4,0},{1,5},{5,1},{2,6},{6,2},{3,7},{7,3},{8,12},{12,8},{9,1... | collective-permute-start | bytes 1376264 | tf_op jit(solution)/shard_map/ppermute | solution.py:505
  (3 other events, 2.0 us)

commit v10 on v9

--- a/solution.py
+++ b/solution.py
@@ -20,8 +20,7 @@
 SPAN = 80
 PLANE = 320
 NEAR = (0, 7, 1, 6, 2)
-MIDDLE = (5, 3)
-FAR = (4,)
+FAR = (5, 3, 4)
 ROOM = 224
 
 
@@ -126,7 +125,7 @@
             part = step // 10
             row = pl.ds(pl.multiple_of(step * rows, rows), rows)
             target = pl.multiple_of(part * PLANE + source * (PLANE // 2) + (step - part * 10) * rows, rows)
-            for group, planes in enumerate((NEAR, MIDDLE, FAR)):
+            for group, planes in enumerate((NEAR, FAR)):
                 for at in range(0, len(planes), 2):
                     a = plane_of(ref, row, planes[at], False)
                     if at + 1 < len(planes):
@@ -147,14 +146,14 @@
 def screen_call(place, own, other):
     shapes = [
         jax.ShapeDtypeStruct((2 * own.shape[0], padded(planes)), jnp.bfloat16)
-        for planes in (NEAR, MIDDLE, FAR)
+        for planes in (NEAR, FAR)
         for _ in range(2)
     ]
     return pl.pallas_call(
         screen_kernel,
         out_shape=shapes,
         in_specs=[SMEM, VMEM, VMEM],
-        out_specs=[VMEM] * 6,
+        out_specs=[VMEM] * 4,
         compiler_params=params(20),
         name="screen",
     )(place, own, other)
@@ -213,47 +212,37 @@
     return units
 
 
-def middle_units(below, above, z_below, z_above, y_below, y_above):
-    units = []
-    for part in range(2):
-        for plane, own, sides, across in ((0, below, z_below, y_below), (1, above, z_above, y_above)):
-            for delta, ref, block in ((0, own, 0), (3, sides, 0), (1, sides, 1), (2, across, 0)):
-                units.append((delta, plane, part, ref, (2 * block + part) * SPAN))
-    return units
-
-
-def far_units(z_below, z_above, below, above, across_low, across_high):
+def far_units(below, above, z_below, z_above, y_below, y_above, far_below, far_above, across_low, across_high):
     units = []
     for part, own, across in ((0, z_below, across_low), (1, z_above, across_high)):
-        for delta, ref, start in ((0, own, 4), (3, below, part), (1, above, part), (2, across, 0)):
-            units.append((delta, 0, part, ref, start * SPAN))
+        for plane, at, sides, over in ((0, below, z_below, y_below), (1, above, z_above, y_above)):
+            for delta, ref, block in ((0, at, 0), (3, sides, 0), (1, sides, 1), (2, over, 0)):
+                units.append((delta, plane, part, ref, (2 * block + part) * SPAN))
+        for delta, ref, start in ((0, own, 4), (3, far_below, part), (1, far_above, part), (2, across, 0)):
+            units.append((delta, 2, part, ref, start * SPAN))
     return units
 
 
-def group_kernel(units, planes, place, *refs):
-    count = len(refs) - 5 - (units is middle_units)
-    rights, (high_ref, low_ref), rest = refs[:count], refs[count : count + 2], refs[count + 2 :]
-    out_ref, rh, rl = rest[-3:]
-    load_right(place, units(*rights), planes, rh, rl)
-    value = dot3(high_ref[...], low_ref[...], rh[...], rl[...])
-    out_ref[...] = value if len(rest) == 3 else value + rest[0][...]
-
-
-def group_call(units, planes, place, rights, screens, total):
+def group_kernel(place, own, below, above, two_below, two_above, high_ref, low_ref, out_ref, rh, rl):
+    load_right(place, near_units(own, below, above, two_below, two_above), len(NEAR), rh, rl)
+    out_ref[...] = dot3(high_ref[...], low_ref[...], rh[...], rl[...])
+
+
+def group_call(place, rights, screens):
     rows, width = screens[0].shape
     return pl.pallas_call(
-        functools.partial(group_kernel, units, planes),
+        group_kernel,
         out_shape=jax.ShapeDtypeStruct((rows, 2 * HALF), jnp.float32),
-        in_specs=[SMEM] + [VMEM] * (len(rights) + 2 + len(total)),
+        in_specs=[SMEM] + [VMEM] * 7,
         out_specs=VMEM,
         scratch_shapes=[pltpu.VMEM((width, 2 * HALF), jnp.bfloat16)] * 2,
-        compiler_params=params(32),
+        compiler_params=params(24),
         name="group",
-    )(place, *rights, *screens, *total)
+    )(place, *rights, *screens)
 
 
 def pair_kernel(place, table, *refs):
-    rights, (high_ref, low_ref, sum_ref, left_high, left_low, give_ref, kern, rh, rl) = refs[:6], refs[6:]
+    rights, (high_ref, low_ref, sum_ref, left_high, left_low, give_ref, kern, rh, rl) = refs[:10], refs[10:]
     load_right(place, far_units(*rights), len(FAR), rh, rl)
     product = sum_ref[...] + dot3(high_ref[...], low_ref[...], rh[...], rl[...])
     mid = product.shape[0] // 2
@@ -264,10 +253,11 @@
     )
     kern[...] = dot3(left_high[...], left_low[...], *split(applied))
 
-    extract(table, 1 - place[3], kern, give_ref)
-
-
-def extract(table, half, kern, out_ref):
+    extract(place, table, 1 - place[3], kern, give_ref)
+
+
+def extract(place, table, half, kern, out_ref):
+    at = lambda x: lax.rem(x + 4 - place[1], 4)
     lane = lax.broadcasted_iota(jnp.int32, (8, 128), 1) // BLK
     upper = lax.broadcasted_iota(jnp.int32, (8, 128), 0) < 4
 
@@ -288,8 +278,8 @@
             lanes = pl.ds(pl.multiple_of(g * 128, 128), 128)
             for side in range(2):
                 real, imag = tiles[0][side], tiles[1][side]
-                out_ref[2 * side, :, lanes] = jnp.where(upper, real, pltpu.roll(imag, 4, 0))
-                out_ref[2 * side + 1, :, lanes] = jnp.where(upper, pltpu.roll(real, 4, 0), imag)
+                out_ref[at(2 * side), :, lanes] = jnp.where(upper, real, pltpu.roll(imag, 4, 0))
+                out_ref[at(2 * side + 1), :, lanes] = jnp.where(upper, pltpu.roll(real, 4, 0), imag)
         return carry
 
     out_ref[...] = jnp.zeros_like(out_ref)
@@ -313,7 +303,7 @@
 
 
 def extract_kernel(place, table, kern, out_ref):
-    extract(table, place[3], kern, out_ref)
+    extract(place, table, place[3], kern, out_ref)
 
 
 def extract_call(place, table, kern):
@@ -327,25 +317,24 @@
     )(place, table, kern)
 
 
-def add_kernel(one_ref, two_ref, out_ref):
-    out_ref[...] = one_ref[...] + two_ref[...]
+def add_kernel(one_ref, two_ref, *outs):
+    for at, out_ref in enumerate(outs):
+        out_ref[...] = one_ref[at] + two_ref[at]
 
 
 def add_call(one, two):
     return pl.pallas_call(
         add_kernel,
-        out_shape=jax.ShapeDtypeStruct(one.shape, one.dtype),
+        out_shape=[jax.ShapeDtypeStruct(one.shape[1:], one.dtype)] * one.shape[0],
         in_specs=[VMEM, VMEM],
-        out_specs=VMEM,
+        out_specs=[VMEM] * one.shape[0],
         compiler_params=params(8),
         name="add",
     )(one, two)
 
 
-def owner_kernel(place, table, parts_ref, out_ref, work):
-    total = parts_ref[0]
-    for at in range(1, parts_ref.shape[0]):
-        total = total + parts_ref[at]
+def owner_kernel(place, table, one_ref, two_ref, three_ref, four_ref, out_ref, work):
+    total = (one_ref[...] + two_ref[...]) + (three_ref[...] + four_ref[...])
     width = total.shape[1]
     work[:, :width] = total
     work[:, width:] = jnp.zeros((8, work.shape[1] - width), jnp.float32)
@@ -360,12 +349,12 @@
     return pl.pallas_call(
         owner_kernel,
         out_shape=jax.ShapeDtypeStruct((32, 8, 256), jnp.float32),
-        in_specs=[SMEM, SMEM, VMEM],
-        out_specs=VMEM,
-        scratch_shapes=[pltpu.VMEM((8, parts.shape[2] + 384), jnp.float32)],
+        in_specs=[SMEM, SMEM] + [VMEM] * 4,
+        out_specs=VMEM,
+        scratch_shapes=[pltpu.VMEM((8, parts[0].shape[1] + 384), jnp.float32)],
         compiler_params=params(8),
         name="owner",
-    )(place, table, parts)
+    )(place, table, *parts)
 
 
 def last_kernel(place, table, parts_ref, out_ref):
@@ -523,17 +512,18 @@
     near_down, near_up = shift(near, "y", 1), shift(near, "y", -1)
     below3, above3 = shift(nearest[2], "z", 1), shift(nearest[3], "z", -1)
     screens = screen_call(place, after(screen, near), other)
-    around = [columns] + [shift(columns, "x", by) for by in (1, 2, 3)]
-    swapped = [swap(columns), swap(around[1]), None, swap(around[3])]
-    near_down, near_up, below3, above3, swapped[0], swapped[1], swapped[3], *screens = hold(
-        (near_down, near_up, below3, above3, swapped[0], swapped[1], swapped[3], *screens)
+    around = [columns, shift(columns, "x", 1)]
+    columns = after(columns, screens[0])
+    around += [shift(columns, "x", 2), shift(columns, "x", 3)]
+    near_down, near_up, below3, above3, around[1], *screens = hold(
+        (near_down, near_up, below3, above3, around[1], *screens)
     )
 
     two_down, two_up = shift(near_down[:half], "y", 1), shift(near_up[half:], "y", -1)
     third, fourth = slice(3 * block, 4 * block), slice(4 * block, 5 * block)
     z_below = shift(join(near_down[third], near_up[third], below3[:SPAN]), "z", 1)
     z_above = shift(join(near_down[fourth], near_up[fourth], above3[SPAN:]), "z", -1)
-    swapped[2] = swap(around[2])
+    swapped = [swap(array) for array in around]
     left_high, left_low = left_call(place, around + swapped)
     two_down, two_up, z_below, z_above, left_high, left_low = hold(
         (two_down, two_up, z_below, z_above, left_high, left_low)
@@ -541,19 +531,14 @@
 
     y_below, y_above = shift(z_below[:block], "y", 1), shift(z_above[block : 2 * block], "y", -1)
     far_below, far_above = shift(z_below[:block], "z", 1), shift(z_above[block : 2 * block], "z", -1)
-    rights = (near, near_down, near_up, two_down, two_up)
-    total = group_call(near_units, len(NEAR), place, rights, screens[:2], ())
-    y_below, y_above, far_below, far_above, total = hold((y_below, y_above, far_below, far_above, total))
-
-    across_low, across_high = shift(far_below[:SPAN], "y", 1), shift(far_above[SPAN:], "y", -1)
-    rights = (below3, above3, z_below, z_above, y_below, y_above)
-    total = group_call(middle_units, len(MIDDLE), place, rights, screens[2:4], (total,))
-    across_low, across_high, total = hold((across_low, across_high, total))
-    rights = (z_below, z_above, far_below, far_above, across_low, across_high)
-    give, kern = pair_call(place, table, rights, screens[4:], total, left_high, left_low)
+    across_low, across_high = shift(z_below[2 * block :], "y", 2), shift(z_above[2 * block :], "y", -2)
+    total = group_call(place, (near, near_down, near_up, two_down, two_up), screens[:2])
+    *rights, total = hold((y_below, y_above, far_below, far_above, across_low, across_high, total))
+    rights = (below3, above3, z_below, z_above, *rights)
+    give, kern = pair_call(place, table, rights, screens[2:], total, left_high, left_low)
 
     parts = add_call(extract_call(place, table, kern), swap(give))
-    parts = lax.all_to_all(parts, "x", 0, 0, tiled=True)
+    parts = [parts[0]] + [shift(parts[by], "x", by) for by in (1, 2, 3)]
     parts = owner_call(place, table, parts)
     parts = lax.all_to_all(parts, ("z", "y"), 0, 0, tiled=True)
     return last_call(place, table, parts).reshape(1, CAP, 2, 4, BLK)

time: 154 us -> 158 us (1.026)
  waiting for transfers between devices: 36.5 us -> 49.5 us
  blocking collectives: 31.1 us -> 20.5 us
    ppermute x21 -> x24, waiting for transfers between devices: 20.9 us -> 33.8 us  [shards(): lax.ppermute(array, axis, ring(lax.axis_size(axis), by))]
    all_to_all x1 -> x0, blocking collectives: 11.9 us -> none  [shards(): parts = lax.all_to_all(parts, 'x', 0, 0, tiled=True)]
    pallas_call x1, Pallas kernels: 8.88 us -> 11.9 us  [pair_call(): pl.pallas_call(pair_kernel, out_shape=(jax.ShapeDtypeStruct((4, 8, ROOM *...]
    pallas_call x3 -> x2, Pallas kernels: 6.84 us -> 4.48 us  [the longest x1 4.43 us: group_call(): pl.pallas_call(group_kernel, out_shape=jax.ShapeDtypeStruct((rows, 2 * HA...]
    ppermute x21 -> x24, starting transfers between devices: 32.1 us -> 34 us  [shards(): lax.ppermute(array, axis, ring(lax.axis_size(axis), by))]
  transfers between devices with their start and end apart: 30 -> 33, of which waited for: 12 -> 16; matrix products, arithmetic and copies ran while one was open for 1% -> 1% of each run, Pallas kernels for 13% -> 11%
where the time goes in v10:
time: 158 us
  waiting for transfers between devices  49.5 us (31%)
  starting transfers between devices  45.9 us (29%)
  Pallas kernels  38.1 us (24%)
  blocking collectives  20.5 us (13%)
  local copies, waits for them, and re-layouts  2.95 us (2%)
    ppermute x24, starting transfers between devices, shards(): lax.ppermute(array, axis, ring(lax.axis_size(axis), by))  34 us
    ppermute x24, waiting for transfers between devices, shards(): lax.ppermute(array, axis, ring(lax.axis_size(axis), by))  33.8 us
    all_to_all x1, blocking collectives, shards(): parts = lax.all_to_all(parts, ('z', 'y'), 0, 0, tiled=True)  20.5 us
    pallas_call x1, Pallas kernels, pair_call(): pl.pallas_call(pair_kernel, out_shape=(jax.ShapeDtypeStruct((4, 8, ROOM *...  11.9 us
    all_to_all x1, starting transfers between devices, shards(): lax.all_to_all(pieces.reshape(32, 1, -1), ('z', 'y'), 0, 0, tiled=True)  11.6 us
    all_to_all x1, waiting for transfers between devices, shards(): lax.all_to_all(pieces.reshape(32, 1, -1), ('z', 'y'), 0, 0, tiled=True)  11.4 us
    pallas_call x1, Pallas kernels, screen_call(): pl.pallas_call(screen_kernel, out_shape=shapes, in_specs=[SMEM, VMEM, VME...  7.33 us
    pallas_call x1, Pallas kernels, group_call(): pl.pallas_call(group_kernel, out_shape=jax.ShapeDtypeStruct((rows, 2 * HA...  4.43 us
  transfers between devices with their start and end apart: 33, of which 16 were waited for; matrix products, arithmetic and copies ran while one was open for 1% of the time, Pallas kernels for 11%

profile of v10, /device:TPU:2, one launch (start us, length us, event | category | flops | bytes accessed | tf_op | source)
XLA Modules:
  0.0 157.9 jit_solution(9480221229504051889)
XLA Ops:
  2.0 2.2 %pack.1 = f32[640,128]{1,0:T(8,128)} custom-call(s32[4]{0:T(128)} %pad_add_fusion.place, f32[2,16,2560]{2,1,0:T(8,128)} %own_ref.1, f32[2,16,2560]{2,1,0:T(8,128)} %collective-permute-done.other_ref), custom_call_target="tpu_custom_call" | custom-call | tf_op jit(solution)/shard_map/pack/pallas_call | solution.py:405
  4.4 11.6 %all-to-all-start = ((f32[32,1,2560]{2,1,0:T(1,128)}), f32[32,1,2560]{2,1,0:T(1,128)}, u32[]{:S(2)}, u32[]{:S(2)}) async-start(f32[32,1,2560]{2,1,0:T(1,128)} %bitcast.12), calls=%async_computation | async-start | bytes 655360 | tf_op jit(solution)/shard_map/all_to_all | solution.py:500
  19.3 11.4 %all-to-all-done = f32[32,1,2560]{2,1,0:T(1,128)} async-done(((f32[32,1,2560]{2,1,0:T(1,128)}), f32[32,1,2560]{2,1,0:T(1,128)}, u32[]{:S(2)}, u32[]{:S(2)}) %all-to-all-start) | async-done | bytes 327712 | tf_op jit(solution)/shard_map/all_to_all | solution.py:500
  31.4 2.5 %unpack.1 = (f32[80,1024]{1,0:T(8,128)S(1)}, f32[80,256]{1,0:T(8,128)S(1)}, f32[80,256]{1,0:T(8,128)S(1)}) custom-call(s32[4]{0:T(128)S(1)} %copy-done.2, s32[16,256]{1,0:T(8,128)S(1)} %plan.1.table, f32[640,128]{1,0:T(8,128)} %bitcast.6.in_ref), custom_call_target="tpu_custom_call" | custom-call | tf_op jit(solution)/shard_map/unpack/pallas_call | solution.py:454
  36.8 2.0 %collective-permute-start.5 = (f32[160,256]{1,0:T(8,128)S(1)}, f32[160,256]{1,0:T(8,128)S(1)}, u32[]{:S(2)}, u32[]{:S(2)}) collective-permute-start(f32[160,256]{1,0:T(8,128)S(1)} %shard.1), channel_id=1, source_target_pairs={{0,64},{32,96},{64,128},{96,160},{128,192},{160,224},{192,0},{224,... | collective-permute-start | bytes 491528 | tf_op jit(solution)/shard_map/ppermute | solution.py:493
  40.9 6.1 %collective-permute-done.6 = f32[160,256]{1,0:T(8,128)S(1)} collective-permute-done((f32[160,256]{1,0:T(8,128)S(1)}, f32[160,256]{1,0:T(8,128)S(1)}, u32[]{:S(2)}, u32[]{:S(2)}) %collective-permute-start.6) | collective-permute-done | bytes 163872 | tf_op jit(solution)/shard_map/ppermute | solution.py:493
  47.0 1.7 %collective-permute-done.5 = f32[160,256]{1,0:T(8,128)S(1)} collective-permute-done((f32[160,256]{1,0:T(8,128)S(1)}, f32[160,256]{1,0:T(8,128)S(1)}, u32[]{:S(2)}, u32[]{:S(2)}) %collective-permute-start.5) | collective-permute-done | bytes 163872 | tf_op jit(solution)/shard_map/ppermute | solution.py:493
  48.9 2.3 %collective-permute-done.3 = f32[160,256]{1,0:T(8,128)S(1)} collective-permute-done((f32[160,256]{1,0:T(8,128)S(1)}, f32[160,256]{1,0:T(8,128)S(1)}, u32[]{:S(2)}, u32[]{:S(2)}) %collective-permute-start.3) | collective-permute-done | bytes 163872 | tf_op jit(solution)/shard_map/ppermute | solution.py:493
  54.1 2.6 %collective-permute-start.10 = (f32[160,256]{1,0:T(8,128)S(1)}, f32[160,256]{1,0:T(8,128)S(1)}, u32[]{:S(2)}, u32[]{:S(2)}) collective-permute-start(f32[160,256]{1,0:T(8,128)S(1)} %collective-permute-done.6), channel_id=1, source_target_pairs={{0,224},{32,0},{64,32},{96,64},{128,96},{160,128},{192,160},{224,1... | collective-permute-start | bytes 491528 | tf_op jit(solution)/shard_map/ppermute | solution.py:493
  58.1 7.3 %screen.1 = (bf16[640,1664]{1,0:T(8,128)(2,1)S(1)}, bf16[640,1664]{1,0:T(8,128)(2,1)S(1)}, bf16[640,1024]{1,0:T(8,128)(2,1)S(1)}, bf16[640,1024]{1,0:T(8,128)(2,1)S(1)}) custom-call(s32[4]{0:T(128)S(1)} %copy-done.3, f32[320,2560]{1,0:T(8,128)S(1)} %bitcast.10, f32[320,2560]{1,0:T(8,128)} %collective-permute-done.1.other_ref), custom_call_target="tpu_custom_call" | custom-call | tf_op jit(solution)/shard_map/screen/pallas_call | solution.py:152
  66.1 2.1 %collective-permute-start.16 = (f32[80,1024]{1,0:T(8,128)S(1)}, f32[80,1024]{1,0:T(8,128)S(1)}, u32[]{:S(2)}, u32[]{:S(2)}) collective-permute-start(f32[80,1024]{1,0:T(8,128)S(1)} %get-tuple-element.75.refs_0_), channel_id=1, source_target_pairs={{0,2},{1,3},{2,0},{3,1},{4,6},{5,7},{6,4},{7,5},{8,10},{9,11},{10,... | collective-permute-start | bytes 983048 | tf_op jit(solution)/shard_map/ppermute | solution.py:493
  68.2 7.3 %collective-permute-done.17.refs_3_ = f32[80,1024]{1,0:T(8,128)S(1)} collective-permute-done((f32[80,1024]{1,0:T(8,128)S(1)}, f32[80,1024]{1,0:T(8,128)S(1)}, u32[]{:S(2)}, u32[]{:S(2)}) %collective-permute-start.17) | collective-permute-done | bytes 327712 | tf_op jit(solution)/shard_map/ppermute | solution.py:493
  75.6 5.1 %collective-permute-done.16.refs_2_ = f32[80,1024]{1,0:T(8,128)S(1)} collective-permute-done((f32[80,1024]{1,0:T(8,128)S(1)}, f32[80,1024]{1,0:T(8,128)S(1)}, u32[]{:S(2)}, u32[]{:S(2)}) %collective-permute-start.16) | collective-permute-done | bytes 327712 | tf_op jit(solution)/shard_map/ppermute | solution.py:493
  80.8 2.2 %collective-permute-start.13 = (f32[400,256]{1,0:T(8,128)S(1)}, f32[400,256]{1,0:T(8,128)S(1)}, u32[]{:S(2)}, u32[]{:S(2)}) collective-permute-start(f32[400,256]{1,0:T(8,128)S(1)} %slice.39), channel_id=1, source_target_pairs={{0,24},{8,0},{16,8},{24,16},{1,25},{9,1},{17,9},{25,17},{2,26},{10... | collective-permute-start | bytes 1228808 | tf_op jit(solution)/shard_map/ppermute | solution.py:493
  83.3 3.2 %collective-permute-start.15 = (f32[400,256]{1,0:T(8,128)S(1)}, f32[400,256]{1,0:T(8,128)S(1)}, u32[]{:S(2)}, u32[]{:S(2)}) collective-permute-start(f32[400,256]{1,0:T(8,128)S(1)} %pad_maximum_fusion.1), channel_id=1, source_target_pairs={{0,224},{32,0},{64,32},{96,64},{128,96},{160,128},{192,160},{224,1... | collective-permute-start | bytes 1228808 | tf_op jit(solution)/shard_map/ppermute | solution.py:493
  86.5 1.6 %collective-permute-done.19.refs_5_ = f32[80,1024]{1,0:T(8,128)S(1)} collective-permute-done((f32[80,1024]{1,0:T(8,128)S(1)}, f32[80,1024]{1,0:T(8,128)S(1)}, u32[]{:S(2)}, u32[]{:S(2)}) %collective-permute-start.19) | collective-permute-done | bytes 327712 | tf_op jit(solution)/shard_map/ppermute | solution.py:494
  88.1 1.8 %left.1 = (bf16[1024,640]{1,0:T(8,128)(2,1)S(1)}, bf16[1024,640]{1,0:T(8,128)(2,1)S(1)}) custom-call(s32[4]{0:T(128)S(1)} %copy-done.3, f32[80,1024]{1,0:T(8,128)S(1)} %get-tuple-element.75.refs_0_, f32[80,1024]{1,0:T(8,128)S(1)} %collective-permute-done.11.refs_1_, f32[80,1024]{1,0:T(8,128)S(1)} %collective-permute-done.16.refs_2_, ...), custom_call_target="tpu_custom_call" | custom-call | tf_op jit(solution)/shard_map/left/pallas_call | solution.py:182
  89.9 2.9 %collective-permute-done.13.two_above = f32[400,256]{1,0:T(8,128)S(1)} collective-permute-done((f32[400,256]{1,0:T(8,128)S(1)}, f32[400,256]{1,0:T(8,128)S(1)}, u32[]{:S(2)}, u32[]{:S(2)}) %collective-permute-start.13) | collective-permute-done | bytes 409632 | tf_op jit(solution)/shard_map/ppermute | solution.py:493
  92.8 3.1 %collective-permute-done.12.two_below = f32[400,256]{1,0:T(8,128)S(1)} collective-permute-done((f32[400,256]{1,0:T(8,128)S(1)}, f32[400,256]{1,0:T(8,128)S(1)}, u32[]{:S(2)}, u32[]{:S(2)}) %collective-permute-start.12) | collective-permute-done | bytes 409632 | tf_op jit(solution)/shard_map/ppermute | solution.py:493
  96.1 1.6 %collective-permute-start.27 = (f32[80,256]{1,0:T(8,128)S(1)}, f32[80,256]{1,0:T(8,128)S(1)}, u32[]{:S(2)}, u32[]{:S(2)}) collective-permute-start(f32[80,256]{1,0:T(8,128)S(1)} %slice.49), channel_id=1, source_target_pairs={{0,16},{8,24},{16,0},{24,8},{1,17},{9,25},{17,1},{25,9},{2,18},{10... | collective-permute-start | bytes 245768 | tf_op jit(solution)/shard_map/ppermute | solution.py:493
  97.7 2.9 %collective-permute-start.25 = (f32[160,256]{1,0:T(8,128)S(1)}, f32[160,256]{1,0:T(8,128)S(1)}, u32[]{:S(2)}, u32[]{:S(2)}) collective-permute-start(f32[160,256]{1,0:T(8,128)S(1)} %slice.47), channel_id=1, source_target_pairs={{0,224},{32,0},{64,32},{96,64},{128,96},{160,128},{192,160},{224,1... | collective-permute-start | bytes 491528 | tf_op jit(solution)/shard_map/ppermute | solution.py:493
  100.7 1.5 collective-permute-start.23
  103.1 2.4 %collective-permute-start.26 = (f32[80,256]{1,0:T(8,128)S(1)}, f32[80,256]{1,0:T(8,128)S(1)}, u32[]{:S(2)}, u32[]{:S(2)}) collective-permute-start(f32[80,256]{1,0:T(8,128)S(1)} %slice.48), channel_id=1, source_target_pairs={{0,16},{8,24},{16,0},{24,8},{1,17},{9,25},{17,1},{25,9},{2,18},{10... | collective-permute-start | bytes 245768 | tf_op jit(solution)/shard_map/ppermute | solution.py:493
  105.5 4.4 %group.1.refs_12_ = f32[640,512]{1,0:T(8,128)S(1)} custom-call(s32[4]{0:T(128)S(1)} %copy-done.3, f32[800,256]{1,0:T(8,128)S(1)} %constant_dynamic-update-slice_fusion.own, f32[800,256]{1,0:T(8,128)S(1)} %collective-permute-done.7.below, f32[800,256]{1,0:T(8,128)S(1)} %collective-permute-done.8.above, f32[400,256]{1,0:T(8,128)S(1)} %collective-permute-done.12.two_below, ...), custom_call_target="tpu_custom_call" | custom-call | tf_op jit(solution)/shard_map/group/pallas_call | solution.py:233
  110.0 11.9 %pair.1 = (f32[4,8,3584]{2,1,0:T(8,128)S(1)}, f32[1024,512]{1,0:T(8,128)S(1)}) custom-call(s32[4]{0:T(128)S(1)} %copy-done.3, s32[16,256]{1,0:T(8,128)S(1)} %plan.1.table, f32[160,256]{1,0:T(8,128)S(1)} %collective-permute-done.9.refs_0_, f32[160,256]{1,0:T(8,128)S(1)} %collective-permute-done.10.refs_1_, f32[400,256]{1,0:T(8,128)S(1)} %collective-permute-done.14.refs_2_, ...), custom_call_target="tpu_custom_call" | custom-call | tf_op jit(solution)/shard_map/pair/pallas_call | solution.py:291
  122.0 3.2 %extract.1.one_ref = f32[4,8,3584]{2,1,0:T(8,128)S(1)} custom-call(s32[4]{0:T(128)S(1)} %copy-done.3, s32[16,256]{1,0:T(8,128)S(1)} %plan.1.table, f32[1024,512]{1,0:T(8,128)S(1)} %get-tuple-element.95.kern), custom_call_target="tpu_custom_call" | custom-call | tf_op jit(solution)/shard_map/extract/pallas_call | solution.py:310
  125.4 1.8 %collective-permute-start.30 = (f32[8,3584]{1,0:T(8,128)S(1)}, f32[8,3584]{1,0:T(8,128)S(1)}, u32[]{:S(2)}, u32[]{:S(2)}) collective-permute-start(f32[8,3584]{1,0:T(8,128)S(1)} %get-tuple-element.99), channel_id=1, source_target_pairs={{0,2},{1,3},{2,0},{3,1},{4,6},{5,7},{6,4},{7,5},{8,10},{9,11},{10,... | collective-permute-start | bytes 344072 | tf_op jit(solution)/shard_map/ppermute | solution.py:493
  127.2 2.5 %collective-permute-start.31 = (f32[8,3584]{1,0:T(8,128)S(1)}, f32[8,3584]{1,0:T(8,128)S(1)}, u32[]{:S(2)}, u32[]{:S(2)}) collective-permute-start(f32[8,3584]{1,0:T(8,128)S(1)} %get-tuple-element.100), channel_id=1, source_target_pairs={{0,3},{1,0},{2,1},{3,2},{4,7},{5,4},{6,5},{7,6},{8,11},{9,8},{10,9... | collective-permute-start | bytes 344072 | tf_op jit(solution)/shard_map/ppermute | solution.py:493
  131.1 2.0 %collective-permute-done.30.three_ref = f32[8,3584]{1,0:T(8,128)S(1)} collective-permute-done((f32[8,3584]{1,0:T(8,128)S(1)}, f32[8,3584]{1,0:T(8,128)S(1)}, u32[]{:S(2)}, u32[]{:S(2)}) %collective-permute-start.30) | collective-permute-done | bytes 114720 | tf_op jit(solution)/shard_map/ppermute | solution.py:493
  133.0 1.6 %collective-permute-done.31.four_ref = f32[8,3584]{1,0:T(8,128)S(1)} collective-permute-done((f32[8,3584]{1,0:T(8,128)S(1)}, f32[8,3584]{1,0:T(8,128)S(1)}, u32[]{:S(2)}, u32[]{:S(2)}) %collective-permute-start.31) | collective-permute-done | bytes 114720 | tf_op jit(solution)/shard_map/ppermute | solution.py:493
  135.9 20.5 %all_to_all.10.parts_ref = f32[32,8,256]{2,1,0:T(8,128)S(1)} all-to-all(f32[32,8,256]{2,1,0:T(8,128)S(1)} %owner.1), channel_id=1, replica_groups=mesh['z'=8,'y'=4,'core'=2,'x'=4] {'z','y'}, dimensions={0} | all-to-all | bytes 524288 | tf_op jit(solution)/shard_map/all_to_all | solution.py:543
  156.4 1.5 last.1
  (75 shorter events, 20.4 us)
Async XLA Ops:
  0.0 2.0 %collective-permute-start = (f32[2,16,2560]{2,1,0:T(8,128)}, f32[2,16,2560]{2,1,0:T(8,128)}, u32[]{:S(2)}, u32[]{:S(2)}) collective-permute-start(f32[2,16,2560]{2,1,0:T(8,128)} %own_ref.1), channel_id=1, source_target_pairs={{0,4},{4,0},{1,5},{5,1},{2,6},{6,2},{3,7},{7,3},{8,12},{12,8},{9,1... | collective-permute-start | bytes 983048 | tf_op jit(solution)/shard_map/ppermute | solution.py:494
  4.2 26.6 %collective-permute-start.1 = (f32[320,2560]{1,0:T(8,128)}, f32[320,2560]{1,0:T(8,128)}, u32[]{:S(2)}, u32[]{:S(2)}) collective-permute-start(f32[320,2560]{1,0:T(8,128)} %bitcast.9), channel_id=1, source_target_pairs={{0,4},{4,0},{1,5},{5,1},{2,6},{6,2},{3,7},{7,3},{8,12},{12,8},{9,1... | collective-permute-start | bytes 9830408 | tf_op jit(solution)/shard_map/ppermute | solution.py:494
  4.4 26.4 %all-to-all-start = ((f32[32,1,2560]{2,1,0:T(1,128)}), f32[32,1,2560]{2,1,0:T(1,128)}, u32[]{:S(2)}, u32[]{:S(2)}) async-start(f32[32,1,2560]{2,1,0:T(1,128)} %bitcast.12), calls=%async_computation | async-start | bytes 655360 | tf_op jit(solution)/shard_map/all_to_all | solution.py:500
  35.9 11.1 %collective-permute-start.6 = (f32[160,256]{1,0:T(8,128)S(1)}, f32[160,256]{1,0:T(8,128)S(1)}, u32[]{:S(2)}, u32[]{:S(2)}) collective-permute-start(f32[160,256]{1,0:T(8,128)S(1)} %shard.1), channel_id=1, source_target_pairs={{0,192},{32,224},{64,0},{96,32},{128,64},{160,96},{192,128},{224,1... | collective-permute-start | bytes 491528 | tf_op jit(solution)/shard_map/ppermute | solution.py:493
  36.8 11.8 %collective-permute-start.5 = (f32[160,256]{1,0:T(8,128)S(1)}, f32[160,256]{1,0:T(8,128)S(1)}, u32[]{:S(2)}, u32[]{:S(2)}) collective-permute-start(f32[160,256]{1,0:T(8,128)S(1)} %shard.1), channel_id=1, source_target_pairs={{0,64},{32,96},{64,128},{96,160},{128,192},{160,224},{192,0},{224,... | collective-permute-start | bytes 491528 | tf_op jit(solution)/shard_map/ppermute | solution.py:493
  38.9 10.0 %collective-permute-start.4 = (f32[160,256]{1,0:T(8,128)S(1)}, f32[160,256]{1,0:T(8,128)S(1)}, u32[]{:S(2)}, u32[]{:S(2)}) collective-permute-start(f32[160,256]{1,0:T(8,128)S(1)} %shard.1), channel_id=1, source_target_pairs={{0,224},{32,0},{64,32},{96,64},{128,96},{160,128},{192,160},{224,1... | collective-permute-start | bytes 491528 | tf_op jit(solution)/shard_map/ppermute | solution.py:493
  40.3 11.0 %collective-permute-start.3 = (f32[160,256]{1,0:T(8,128)S(1)}, f32[160,256]{1,0:T(8,128)S(1)}, u32[]{:S(2)}, u32[]{:S(2)}) collective-permute-start(f32[160,256]{1,0:T(8,128)S(1)} %shard.1), channel_id=1, source_target_pairs={{0,32},{32,64},{64,96},{96,128},{128,160},{160,192},{192,224},{224... | collective-permute-start | bytes 491528 | tf_op jit(solution)/shard_map/ppermute | solution.py:493
  51.3 29.4 %collective-permute-start.8 = (f32[800,256]{1,0:T(8,128)S(1)}, f32[800,256]{1,0:T(8,128)S(1)}, u32[]{:S(2)}, u32[]{:S(2)}) collective-permute-start(f32[800,256]{1,0:T(8,128)S(1)} %constant_dynamic-update-slice_fusion.own), channel_id=1, source_target_pairs={{0,24},{8,0},{16,8},{24,16},{1,25},{9,1},{17,9},{25,17},{2,26},{10... | collective-permute-start | bytes 2457608 | tf_op jit(solution)/shard_map/ppermute | solution.py:493
  52.5 28.2 %collective-permute-start.7 = (f32[800,256]{1,0:T(8,128)S(1)}, f32[800,256]{1,0:T(8,128)S(1)}, u32[]{:S(2)}, u32[]{:S(2)}) collective-permute-start(f32[800,256]{1,0:T(8,128)S(1)} %constant_dynamic-update-slice_fusion.own), channel_id=1, source_target_pairs={{0,8},{8,16},{16,24},{24,0},{1,9},{9,17},{17,25},{25,1},{2,10},{10... | collective-permute-start | bytes 2457608 | tf_op jit(solution)/shard_map/ppermute | solution.py:493
  53.4 12.1 %collective-permute-start.9 = (f32[160,256]{1,0:T(8,128)S(1)}, f32[160,256]{1,0:T(8,128)S(1)}, u32[]{:S(2)}, u32[]{:S(2)}) collective-permute-start(f32[160,256]{1,0:T(8,128)S(1)} %collective-permute-done.5), channel_id=1, source_target_pairs={{0,32},{32,64},{64,96},{96,128},{128,160},{160,192},{192,224},{224... | collective-permute-start | bytes 491528 | tf_op jit(solution)/shard_map/ppermute | solution.py:493
  54.1 12.0 %collective-permute-start.10 = (f32[160,256]{1,0:T(8,128)S(1)}, f32[160,256]{1,0:T(8,128)S(1)}, u32[]{:S(2)}, u32[]{:S(2)}) collective-permute-start(f32[160,256]{1,0:T(8,128)S(1)} %collective-permute-done.6), channel_id=1, source_target_pairs={{0,224},{32,0},{64,32},{96,64},{128,96},{160,128},{192,160},{224,1... | collective-permute-start | bytes 491528 | tf_op jit(solution)/shard_map/ppermute | solution.py:493
  56.7 11.6 %collective-permute-start.11 = (f32[80,1024]{1,0:T(8,128)S(1)}, f32[80,1024]{1,0:T(8,128)S(1)}, u32[]{:S(2)}, u32[]{:S(2)}) collective-permute-start(f32[80,1024]{1,0:T(8,128)S(1)} %get-tuple-element.75.refs_0_), channel_id=1, source_target_pairs={{0,1},{1,2},{2,3},{3,0},{4,5},{5,6},{6,7},{7,4},{8,9},{9,10},{10,1... | collective-permute-start | bytes 983048 | tf_op jit(solution)/shard_map/ppermute | solution.py:493
  65.5 10.1 %collective-permute-start.17 = (f32[80,1024]{1,0:T(8,128)S(1)}, f32[80,1024]{1,0:T(8,128)S(1)}, u32[]{:S(2)}, u32[]{:S(2)}) collective-permute-start(f32[80,1024]{1,0:T(8,128)S(1)} %get-tuple-element.75.refs_0_), channel_id=1, source_target_pairs={{0,3},{1,0},{2,1},{3,2},{4,7},{5,4},{6,5},{7,6},{8,11},{9,8},{10,9... | collective-permute-start | bytes 983048 | tf_op jit(solution)/shard_map/ppermute | solution.py:493
  66.1 14.5 %collective-permute-start.16 = (f32[80,1024]{1,0:T(8,128)S(1)}, f32[80,1024]{1,0:T(8,128)S(1)}, u32[]{:S(2)}, u32[]{:S(2)}) collective-permute-start(f32[80,1024]{1,0:T(8,128)S(1)} %get-tuple-element.75.refs_0_), channel_id=1, source_target_pairs={{0,2},{1,3},{2,0},{3,1},{4,6},{5,7},{6,4},{7,5},{8,10},{9,11},{10,... | collective-permute-start | bytes 983048 | tf_op jit(solution)/shard_map/ppermute | solution.py:493
  68.2 14.9 %collective-permute-start.18 = (f32[80,1024]{1,0:T(8,128)S(1)}, f32[80,1024]{1,0:T(8,128)S(1)}, u32[]{:S(2)}, u32[]{:S(2)}) collective-permute-start(f32[80,1024]{1,0:T(8,128)S(1)} %get-tuple-element.75.refs_0_), channel_id=1, source_target_pairs={{0,4},{4,0},{1,5},{5,1},{2,6},{6,2},{3,7},{7,3},{8,12},{12,8},{9,1... | collective-permute-start | bytes 983048 | tf_op jit(solution)/shard_map/ppermute | solution.py:494
  75.6 7.7 %collective-permute-start.21 = (f32[80,1024]{1,0:T(8,128)S(1)}, f32[80,1024]{1,0:T(8,128)S(1)}, u32[]{:S(2)}, u32[]{:S(2)}) collective-permute-start(f32[80,1024]{1,0:T(8,128)S(1)} %collective-permute-done.17.refs_3_), channel_id=1, source_target_pairs={{0,4},{4,0},{1,5},{5,1},{2,6},{6,2},{3,7},{7,3},{8,12},{12,8},{9,1... | collective-permute-start | bytes 983048 | tf_op jit(solution)/shard_map/ppermute | solution.py:494
  80.7 5.8 %collective-permute-start.20 = (f32[80,1024]{1,0:T(8,128)S(1)}, f32[80,1024]{1,0:T(8,128)S(1)}, u32[]{:S(2)}, u32[]{:S(2)}) collective-permute-start(f32[80,1024]{1,0:T(8,128)S(1)} %collective-permute-done.16.refs_2_), channel_id=1, source_target_pairs={{0,4},{4,0},{1,5},{5,1},{2,6},{6,2},{3,7},{7,3},{8,12},{12,8},{9,1... | collective-permute-start | bytes 983048 | tf_op jit(solution)/shard_map/ppermute | solution.py:494
  80.8 12.0 %collective-permute-start.13 = (f32[400,256]{1,0:T(8,128)S(1)}, f32[400,256]{1,0:T(8,128)S(1)}, u32[]{:S(2)}, u32[]{:S(2)}) collective-permute-start(f32[400,256]{1,0:T(8,128)S(1)} %slice.39), channel_id=1, source_target_pairs={{0,24},{8,0},{16,8},{24,16},{1,25},{9,1},{17,9},{25,17},{2,26},{10... | collective-permute-start | bytes 1228808 | tf_op jit(solution)/shard_map/ppermute | solution.py:493
  83.1 12.8 %collective-permute-start.12 = (f32[400,256]{1,0:T(8,128)S(1)}, f32[400,256]{1,0:T(8,128)S(1)}, u32[]{:S(2)}, u32[]{:S(2)}) collective-permute-start(f32[400,256]{1,0:T(8,128)S(1)} %slice.38), channel_id=1, source_target_pairs={{0,8},{8,16},{16,24},{24,0},{1,9},{9,17},{17,25},{25,1},{2,10},{10... | collective-permute-start | bytes 1228808 | tf_op jit(solution)/shard_map/ppermute | solution.py:493
  83.2 12.9 %collective-permute-start.14 = (f32[400,256]{1,0:T(8,128)S(1)}, f32[400,256]{1,0:T(8,128)S(1)}, u32[]{:S(2)}, u32[]{:S(2)}) collective-permute-start(f32[400,256]{1,0:T(8,128)S(1)} %pad_maximum_fusion), channel_id=1, source_target_pairs={{0,32},{32,64},{64,96},{96,128},{128,160},{160,192},{192,224},{224... | collective-permute-start | bytes 1228808 | tf_op jit(solution)/shard_map/ppermute | solution.py:493
  83.3 12.8 %collective-permute-start.15 = (f32[400,256]{1,0:T(8,128)S(1)}, f32[400,256]{1,0:T(8,128)S(1)}, u32[]{:S(2)}, u32[]{:S(2)}) collective-permute-start(f32[400,256]{1,0:T(8,128)S(1)} %pad_maximum_fusion.1), channel_id=1, source_target_pairs={{0,224},{32,0},{64,32},{96,64},{128,96},{160,128},{192,160},{224,1... | collective-permute-start | bytes 1228808 | tf_op jit(solution)/shard_map/ppermute | solution.py:493
  86.5 1.6 %collective-permute-start.19 = (f32[80,1024]{1,0:T(8,128)S(1)}, f32[80,1024]{1,0:T(8,128)S(1)}, u32[]{:S(2)}, u32[]{:S(2)}) collective-permute-start(f32[80,1024]{1,0:T(8,128)S(1)} %collective-permute-done.11.refs_1_), channel_id=1, source_target_pairs={{0,4},{4,0},{1,5},{5,1},{2,6},{6,2},{3,7},{7,3},{8,12},{12,8},{9,1... | collective-permute-start | bytes 983048 | tf_op jit(solution)/shard_map/ppermute | solution.py:494
  96.1 7.0 %collective-permute-start.27 = (f32[80,256]{1,0:T(8,128)S(1)}, f32[80,256]{1,0:T(8,128)S(1)}, u32[]{:S(2)}, u32[]{:S(2)}) collective-permute-start(f32[80,256]{1,0:T(8,128)S(1)} %slice.49), channel_id=1, source_target_pairs={{0,16},{8,24},{16,0},{24,8},{1,17},{9,25},{17,1},{25,9},{2,18},{10... | collective-permute-start | bytes 245768 | tf_op jit(solution)/shard_map/ppermute | solution.py:493
  97.7 12.3 %collective-permute-start.25 = (f32[160,256]{1,0:T(8,128)S(1)}, f32[160,256]{1,0:T(8,128)S(1)}, u32[]{:S(2)}, u32[]{:S(2)}) collective-permute-start(f32[160,256]{1,0:T(8,128)S(1)} %slice.47), channel_id=1, source_target_pairs={{0,224},{32,0},{64,32},{96,64},{128,96},{160,128},{192,160},{224,1... | collective-permute-start | bytes 491528 | tf_op jit(solution)/shard_map/ppermute | solution.py:493
  100.7 9.3 %collective-permute-start.23 = (f32[160,256]{1,0:T(8,128)S(1)}, f32[160,256]{1,0:T(8,128)S(1)}, u32[]{:S(2)}, u32[]{:S(2)}) collective-permute-start(f32[160,256]{1,0:T(8,128)S(1)} %slice.47), channel_id=1, source_target_pairs={{0,24},{8,0},{16,8},{24,16},{1,25},{9,1},{17,9},{25,17},{2,26},{10... | collective-permute-start | bytes 491528 | tf_op jit(solution)/shard_map/ppermute | solution.py:493
  102.2 7.8 %collective-permute-start.24 = (f32[160,256]{1,0:T(8,128)S(1)}, f32[160,256]{1,0:T(8,128)S(1)}, u32[]{:S(2)}, u32[]{:S(2)}) collective-permute-start(f32[160,256]{1,0:T(8,128)S(1)} %slice.46), channel_id=1, source_target_pairs={{0,32},{32,64},{64,96},{96,128},{128,160},{160,192},{192,224},{224... | collective-permute-start | bytes 491528 | tf_op jit(solution)/shard_map/ppermute | solution.py:493
  102.3 7.7 %collective-permute-start.22 = (f32[160,256]{1,0:T(8,128)S(1)}, f32[160,256]{1,0:T(8,128)S(1)}, u32[]{:S(2)}, u32[]{:S(2)}) collective-permute-start(f32[160,256]{1,0:T(8,128)S(1)} %slice.46), channel_id=1, source_target_pairs={{0,8},{8,16},{16,24},{24,0},{1,9},{9,17},{17,25},{25,1},{2,10},{10... | collective-permute-start | bytes 491528 | tf_op jit(solution)/shard_map/ppermute | solution.py:493
  103.1 6.8 %collective-permute-start.26 = (f32[80,256]{1,0:T(8,128)S(1)}, f32[80,256]{1,0:T(8,128)S(1)}, u32[]{:S(2)}, u32[]{:S(2)}) collective-permute-start(f32[80,256]{1,0:T(8,128)S(1)} %slice.48), channel_id=1, source_target_pairs={{0,16},{8,24},{16,0},{24,8},{1,17},{9,25},{17,1},{25,9},{2,18},{10... | collective-permute-start | bytes 245768 | tf_op jit(solution)/shard_map/ppermute | solution.py:493
  121.9 3.3 %collective-permute-start.28 = (f32[4,8,3584]{2,1,0:T(8,128)S(1)}, f32[4,8,3584]{2,1,0:T(8,128)S(1)}, u32[]{:S(2)}, u32[]{:S(2)}) collective-permute-start(f32[4,8,3584]{2,1,0:T(8,128)S(1)} %get-tuple-element.96), channel_id=1, source_target_pairs={{0,4},{4,0},{1,5},{5,1},{2,6},{6,2},{3,7},{7,3},{8,12},{12,8},{9,1... | collective-permute-start | bytes 1376264 | tf_op jit(solution)/shard_map/ppermute | solution.py:494
  125.3 5.7 %collective-permute-start.29 = (f32[8,3584]{1,0:T(8,128)S(1)}, f32[8,3584]{1,0:T(8,128)S(1)}, u32[]{:S(2)}, u32[]{:S(2)}) collective-permute-start(f32[8,3584]{1,0:T(8,128)S(1)} %get-tuple-element.98), channel_id=1, source_target_pairs={{0,1},{1,2},{2,3},{3,0},{4,5},{5,6},{6,7},{7,4},{8,9},{9,10},{10,1... | collective-permute-start | bytes 344072 | tf_op jit(solution)/shard_map/ppermute | solution.py:493
  125.4 7.6 %collective-permute-start.30 = (f32[8,3584]{1,0:T(8,128)S(1)}, f32[8,3584]{1,0:T(8,128)S(1)}, u32[]{:S(2)}, u32[]{:S(2)}) collective-permute-start(f32[8,3584]{1,0:T(8,128)S(1)} %get-tuple-element.99), channel_id=1, source_target_pairs={{0,2},{1,3},{2,0},{3,1},{4,6},{5,7},{6,4},{7,5},{8,10},{9,11},{10,... | collective-permute-start | bytes 344072 | tf_op jit(solution)/shard_map/ppermute | solution.py:493
  127.2 7.5 %collective-permute-start.31 = (f32[8,3584]{1,0:T(8,128)S(1)}, f32[8,3584]{1,0:T(8,128)S(1)}, u32[]{:S(2)}, u32[]{:S(2)}) collective-permute-start(f32[8,3584]{1,0:T(8,128)S(1)} %get-tuple-element.100), channel_id=1, source_target_pairs={{0,3},{1,0},{2,1},{3,2},{4,7},{5,4},{6,5},{7,6},{8,11},{9,8},{10,9... | collective-permute-start | bytes 344072 | tf_op jit(solution)/shard_map/ppermute | solution.py:493
  (6 other events, 87.6 us)
